TPU v7x, 32 devices: a whole 2x2x4 slice. The times are simulated.
32 devices in a mesh: seq: 8 (over z, y), head: 4 (over x, core).
Axes of the slice: x: 2, y: 2, z: 4, core: 2. Of those that a mesh axis runs over, the one named last changes fastest.
Arguments:
- queries: bfloat16 [4096, 2048], P('seq', 'head'), may hold values from -4 to 4
- keys: bfloat16 [4096, 2048], P('seq', 'head'), may hold values from -4 to 4
- values: bfloat16 [4096, 2048], P('seq', 'head'), may hold values from -6 to 6
- rates: float32 [4096, 4], P('seq', 'head'), may hold values from 0.02 to 0.3
- fast: bfloat16 [4, 3, 512, 512], P('head'), may hold values from -0.25 to 0.25
- momentum: float32 [4, 3, 512, 512], P('head', None, 'seq'), may hold values from -0.24 to 0.24
- out_proj: bfloat16 [2048, 2048], P('seq', 'head'), may hold values from -0.125 to 0.125
Outputs:
- mixed: bfloat16 [4096, 2048], P('seq', 'head')
- new_momentum: float32 [4, 3, 512, 512], P('head', None, 'seq')
All inputs are finite; a program needn't handle non-finite values.
Results may differ from a plain program's by a relative error of at most 0.0094.
Values may be sent and summed in bfloat16 or wider, within the bound.
No kernel may reach another device: no remote copies, remote signals or barrier semaphores. Data moves between devices by JAX's collectives and lax.ppermute only.
A program may use at most 64 MiB of HBM per device.

v0:
```python
import functools
import math

import jax
import jax.numpy as jnp
import numpy as np
from jax import lax
from jax.experimental import pallas as pl
from jax.experimental.pallas import tpu as pltpu
from jax.sharding import PartitionSpec as P

HD = 512
WINDOW = 512

MOMENTUM_DECAY = 0.9
NORM_EPS = 1e-06
NEG_LARGE = -1e30
MIB = 1024 * 1024
ORIGINS = 4
BRIEF = pl.CostEstimate(flops=1, bytes_accessed=1, transcendentals=0)


def times_transposed(left, right):
    return lax.dot_general(
        left, right, (((1,), (1,)), ((), ())), preferred_element_type=jnp.float32
    )


def contract_rows(left, right):
    return lax.dot_general(
        left, right, (((0,), (0,)), ((), ())), preferred_element_type=jnp.float32
    )


def matmul(left, right):
    return jnp.dot(left, right, preferred_element_type=jnp.float32)


def swap(array, axis, mask):
    devices = lax.axis_size(axis)
    return lax.ppermute(array, axis, [(i, i ^ mask) for i in range(devices)])


def params(mib):
    return pltpu.CompilerParams(vmem_limit_bytes=mib * MIB)


def whole_spec():
    return pl.BlockSpec(memory_space=pltpu.VMEM)


def gradient_rows(outer, side, k, e, w, eye, hg_s, hu_s, err_s, dg_s, du_s):
    tokens, hidden = k.shape
    own = hidden // (2 * outer)
    hg = times_transposed(w[0], k)
    hu = times_transposed(w[1], k)
    hg_s[...] = hg
    hu_s[...] = hu
    gated = (hg * jax.nn.sigmoid(hg) * hu).astype(jnp.bfloat16)
    err_s[...] = times_transposed(eye, e).astype(jnp.bfloat16)
    down_t = times_transposed(eye, w[2]).astype(jnp.bfloat16)
    back = matmul(down_t, err_s[...])
    dg_s[2] = back
    errors = []
    for z in range(outer):
        rows = pl.ds(pl.multiple_of((2 * z + side) * own, own), own)
        to = pl.ds(z * own, own)
        g, u, b = hg_s[rows], hu_s[rows], dg_s[2, rows]
        s = jax.nn.sigmoid(g)
        du_s[0, to] = (b * u * s * (1.0 + g * (1.0 - s))).astype(jnp.bfloat16)
        du_s[1, to] = (b * g * s).astype(jnp.bfloat16)
        du_s[2, to] = err_s[rows]
    return (
        matmul(du_s[0], k),
        matmul(du_s[1], k),
        times_transposed(du_s[2], gated),
    )


def identity(size):
    rows = lax.broadcasted_iota(jnp.int32, (size, size), 0)
    columns = lax.broadcasted_iota(jnp.int32, (size, size), 1)
    return jnp.where(rows == columns, 1.0, 0.0).astype(jnp.bfloat16)


def own_kernel(outer, place, k, e, w, acc, *scratch):
    eye = identity(e.shape[1])
    parts = gradient_rows(outer, place[0], k[...], e[...], w[0], eye, *scratch)
    own = acc.shape[2]
    for i, part in enumerate(parts):
        acc[:, i] = part.reshape(outer, own, part.shape[1])


def both_kernel(outer, place, k, e, w, acc, mine, *rest):
    sent, scratch = rest[: outer - 1], rest[outer - 1 :]
    eye = identity(e.shape[1])
    parts = gradient_rows(outer, place[0], k[...], e[...], w[0], eye, *scratch)
    own = acc.shape[2]
    total = scratch[1]
    for i, part in enumerate(parts):
        total[pl.ds(0, outer * own), :] = part + acc[:, i].reshape(outer * own, part.shape[1])
        mine[i] = total[pl.ds(pl.multiple_of(place[1] * own, own), own), :]
        for step in range(1, outer):
            other = place[1] ^ step
            block = total[pl.ds(pl.multiple_of(other * own, own), own), :]
            sent[step - 1][i] = block.astype(jnp.bfloat16)


def gradient_scratch(tokens, hidden):
    return [
        pltpu.VMEM((hidden, tokens), jnp.float32),
        pltpu.VMEM((hidden, tokens), jnp.float32),
        pltpu.VMEM((hidden, tokens), jnp.bfloat16),
        pltpu.VMEM((3, hidden, tokens), jnp.float32),
        pltpu.VMEM((3, hidden // 2, tokens), jnp.bfloat16),
    ]


def own_gradients(place, k, e, w, outer):
    tokens, hidden = k.shape
    own = hidden // (2 * outer)
    return pl.pallas_call(
        functools.partial(own_kernel, outer),
        out_shape=jax.ShapeDtypeStruct((outer, 3, own, hidden), jnp.float32),
        in_specs=[pl.BlockSpec(memory_space=pltpu.SMEM)] + [whole_spec()] * 3,
        out_specs=whole_spec(),
        scratch_shapes=gradient_scratch(tokens, hidden),
        compiler_params=params(12),
        cost_estimate=BRIEF,
        name="own_gradients",
    )(place, k, e, w)


def both_gradients(place, k, e, w, acc, outer):
    tokens, hidden = k.shape
    own = hidden // (2 * outer)
    return pl.pallas_call(
        functools.partial(both_kernel, outer),
        out_shape=[jax.ShapeDtypeStruct((3, own, hidden), jnp.float32)]
        + [jax.ShapeDtypeStruct((3, own, hidden), jnp.bfloat16)] * (outer - 1),
        in_specs=[pl.BlockSpec(memory_space=pltpu.SMEM)] + [whole_spec()] * 4,
        out_specs=[whole_spec()] * outer,
        scratch_shapes=gradient_scratch(tokens, hidden),
        compiler_params=params(12),
        cost_estimate=BRIEF,
        name="both_gradients",
    )(place, k, e, w, acc)


def attend_kernel(blocks, place, q, k, v, pair_k, up_k, early_v, out):
    early_k = jnp.where(place[0] == 0, up_k[...], pair_k[...])
    early_v = early_v[...]
    early_v = jnp.where(place[2] > 0, early_v, jnp.zeros_like(early_v))
    tokens = q.shape[0]
    rows = tokens // blocks
    scale = 1.0 / math.sqrt(q.shape[1])
    for b in range(blocks):
        first, last = b * rows, (b + 1) * rows
        own = times_transposed(q[first:last], k[:last]) * scale
        old = times_transposed(q[first:last], early_k[first:]) * scale
        row = first + lax.broadcasted_iota(jnp.int32, own.shape, 0)
        column = lax.broadcasted_iota(jnp.int32, own.shape, 1)
        own = jnp.where(column <= row, own, NEG_LARGE)
        row = first + lax.broadcasted_iota(jnp.int32, old.shape, 0)
        column = first + lax.broadcasted_iota(jnp.int32, old.shape, 1)
        old = jnp.where((column > row) & (place[2] > 0), old, NEG_LARGE)
        highest = jnp.maximum(
            jnp.max(own, axis=1, keepdims=True), jnp.max(old, axis=1, keepdims=True)
        )
        own, old = jnp.exp(own - highest), jnp.exp(old - highest)
        total = jnp.sum(own, axis=1, keepdims=True) + jnp.sum(old, axis=1, keepdims=True)
        own = (own / total).astype(jnp.bfloat16)
        old = (old / total).astype(jnp.bfloat16)
        out[first:last] = matmul(own, v[:last]) + matmul(old, early_v[first:])


def window_attention(place, q, k, v, *early):
    tokens, hidden = q.shape
    return pl.pallas_call(
        functools.partial(attend_kernel, 2),
        out_shape=jax.ShapeDtypeStruct((tokens, hidden), jnp.float32),
        in_specs=[pl.BlockSpec(memory_space=pltpu.SMEM)] + [whole_spec()] * 6,
        out_specs=whole_spec(),
        compiler_params=params(12),
        cost_estimate=BRIEF,
        name="window_attention",
    )(place, q, k, v, *early)


def pick_kernel(place, even, odd, out):
    @pl.when(place[0] == 0)
    def _():
        out[...] = even[...]

    @pl.when(place[0] == 1)
    def _():
        out[...] = odd[...]


def pick(place, even, odd):
    return pl.pallas_call(
        pick_kernel,
        out_shape=jax.ShapeDtypeStruct(even.shape, even.dtype),
        in_specs=[pl.BlockSpec(memory_space=pltpu.SMEM)] + [whole_spec()] * 2,
        out_specs=whole_spec(),
        compiler_params=params(12),
        cost_estimate=BRIEF,
        name="pick",
    )(place, even, odd)


def renew_kernel(place, w, momentum, mine, *rest):
    pieces, (moment, renewed) = rest[:-2], rest[-2:]
    own = mine.shape[1]
    total = mine[...]
    for piece in pieces:
        total = total + piece[...].astype(jnp.float32)
    new = MOMENTUM_DECAY * momentum[0] + total
    moment[0] = new
    rows = pl.ds(pl.multiple_of(place[2] * own, own), own)
    for i in range(w.shape[1]):
        base = w[0, i, rows, :].astype(jnp.float32)
        renewed[i] = renormalize(base, new[i])


def renew(place, w, momentum, mine, pieces):
    return pl.pallas_call(
        renew_kernel,
        out_shape=[
            jax.ShapeDtypeStruct(momentum.shape, jnp.float32),
            jax.ShapeDtypeStruct(mine.shape, jnp.bfloat16),
        ],
        in_specs=[pl.BlockSpec(memory_space=pltpu.SMEM)] + [whole_spec()] * (3 + len(pieces)),
        out_specs=[whole_spec()] * 2,
        compiler_params=params(12),
        cost_estimate=BRIEF,
        name="renew",
    )(place, w, momentum, mine, *pieces)


def apply_kernel(count, place, q, attended, *rest):
    units, combined, full = rest[:count], rest[count], rest[count + 1]
    own = units[0].shape[1]
    for i in range(count):
        rows = pl.ds(pl.multiple_of(place[ORIGINS + i] * own, own), own)
        full[:, rows, :] = units[i][...]
    b1 = times_transposed(q[...], full[0])
    b3 = times_transposed(q[...], full[1])
    fast_in = (b1 * jax.nn.sigmoid(b1) * b3).astype(jnp.bfloat16)
    out = times_transposed(fast_in, full[2])
    combined[...] = (attended[...] + out).astype(jnp.bfloat16)


def apply_fast(place, q, attended, units):
    tokens, hidden = q.shape
    return pl.pallas_call(
        functools.partial(apply_kernel, len(units)),
        out_shape=jax.ShapeDtypeStruct((tokens, hidden), jnp.bfloat16),
        in_specs=[pl.BlockSpec(memory_space=pltpu.SMEM)] + [whole_spec()] * (2 + len(units)),
        out_specs=whole_spec(),
        scratch_shapes=[pltpu.VMEM((3, hidden, hidden), jnp.bfloat16)],
        compiler_params=params(12),
        cost_estimate=BRIEF,
        name="apply_fast",
    )(place, q, attended, *units)


def project_kernel(tags, rows_in, place, *rest):
    blocks, units = rest[: len(tags)], rest[len(tags) : -2]
    mixed, full = rest[-2:]
    at = 0
    for unit in units:
        for part in range(unit.shape[0] // rows_in):
            rows = pl.ds(pl.multiple_of(place[ORIGINS + at] * rows_in, rows_in), rows_in)
            full[rows, :] = unit[part * rows_in : (part + 1) * rows_in, :]
            at += 1
    width = blocks[0].shape[1]
    value = None
    for block, tag in zip(blocks, tags):
        rows = pl.ds(pl.multiple_of((place[3] ^ tag) * width, width), width)
        part = matmul(block[...], full[rows, :])
        value = part if value is None else value + part
    mixed[...] = value.astype(mixed.dtype)


def project(place, blocks, tags, near, far, rows_in):
    tokens = blocks[0].shape[0]
    units = near + far
    depth, width = sum(unit.shape[0] for unit in units), units[0].shape[1]
    return pl.pallas_call(
        functools.partial(project_kernel, tags, rows_in),
        out_shape=jax.ShapeDtypeStruct((tokens, width), jnp.bfloat16),
        in_specs=[pl.BlockSpec(memory_space=pltpu.SMEM)]
        + [whole_spec()] * (len(units) + len(blocks)),
        out_specs=whole_spec(),
        scratch_shapes=[pltpu.VMEM((depth, width), jnp.bfloat16)],
        compiler_params=params(12),
        cost_estimate=BRIEF,
        name="project",
    )(place, *blocks, *units)


def ring_order(outer):
    return [0] + list(range(1, outer, 2)) + list(range(outer - 2 + outer % 2, 0, -2))


def ring_step(unit, outer):
    order = ring_order(outer)
    pairs = []
    for place, z in enumerate(order):
        to = order[(place + 1) % outer]
        pairs += [(2 * z + y, 2 * to + y) for y in range(2)]
    return lax.ppermute(unit, "seq", pairs)


def after(array, *others):
    return lax.optimization_barrier((array,) + others)[0]


def place_table(outer, heads):
    order = ring_order(outer)
    table = []
    for s in range(2 * outer):
        place = order.index(s // 2)
        sources = [order[(place - step) % outer] for step in range(outer)]
        near = [2 * z + s % 2 for z in sources]
        far = [2 * z + 1 - s % 2 for z in sources]
        table += [[s % 2, s // 2, s, head] + near + far for head in range(heads)]
    return np.array(table, np.int32)


def renormalize(base, moment):
    updated = base - moment
    base_rms = jnp.sqrt(jnp.mean(base * base, axis=-1, keepdims=True) + NORM_EPS)
    new_rms = jnp.sqrt(jnp.mean(updated * updated, axis=-1, keepdims=True) + NORM_EPS)
    return (updated * (base_rms / new_rms)).astype(jnp.bfloat16)


def attention(queries, keys, values, early_keys, early_values, position):
    tok_rows = queries.shape[0]
    all_keys = jnp.concatenate([early_keys, keys], axis=0)
    all_values = jnp.concatenate([early_values, values], axis=0)
    key_pos = (position - 1) * tok_rows + jnp.arange(all_keys.shape[0])
    query_pos = position * tok_rows + jnp.arange(tok_rows)
    spacing = query_pos[:, None] - key_pos[None, :]
    allowed = (spacing >= 0) & (spacing < WINDOW) & (key_pos[None, :] >= 0)
    scores = times_transposed(queries, all_keys) * (1.0 / math.sqrt(HD))
    scores = jnp.where(allowed, scores, NEG_LARGE)
    highest = jnp.max(scores, axis=1, keepdims=True)
    expo = jnp.exp(scores - highest)
    probs = (expo / jnp.sum(expo, axis=1, keepdims=True)).astype(jnp.bfloat16)
    return jnp.dot(probs, all_values, preferred_element_type=jnp.float32)


def shards(queries, keys, values, rates, fast, momentum, out_proj):
    tok_rows = queries.shape[0]
    ranks = lax.axis_size("seq")
    heads = lax.axis_size("head")
    own_rows = momentum.shape[2]
    if own_rows % 16 or ranks != 8 or heads % 2 or tok_rows != WINDOW:
        return plain(queries, keys, values, rates, fast, momentum, out_proj)
    outer = ranks // 2
    grad_scale = 1.0 / math.sqrt(tok_rows * ranks)
    index = lax.axis_index("seq") * heads + lax.axis_index("head")
    place = lax.dynamic_index_in_dim(jnp.asarray(place_table(outer, heads)), index, 0, False)

    pair_keys = swap(keys, "seq", 1)
    errors = (-grad_scale * rates * values.astype(jnp.float32)).astype(jnp.bfloat16)
    pair_errors = swap(errors, "seq", 1)

    up_values = lax.ppermute(values, "seq", [(s, s + 2) for s in range(1, ranks - 2, 2)])
    up_keys = lax.ppermute(pair_keys, "seq", [(s, s + 2) for s in range(0, ranks - 2, 2)])

    wide = [after(out_proj, errors)]
    for _ in range(2, outer):
        wide.append(ring_step(wide[-1], outer))

    acc = own_gradients(place, keys, errors, fast, outer)
    across = pick(place, values, up_values)
    pair_errors = after(pair_errors, up_keys, wide[-1], across)
    summed = both_gradients(place, pair_keys, pair_errors, fast, acc, outer)
    pieces = [swap(summed[step], "seq", step * 2) for step in range(1, outer)]
    early_values = swap(after(across, summed[1]), "seq", 1)
    pieces[2] = after(pieces[2], early_values)
    moment, renewed = renew(place, fast, momentum, summed[0], pieces)

    wide_far = [swap(after(wide[0], pieces[1]), "seq", 1)]
    wide.append(ring_step(after(wide[-1], renewed), outer))

    near, far = [renewed], [swap(renewed, "seq", 1)]
    for step in range(1, outer):
        near.append(ring_step(near[-1], outer))
        if step == 2:
            near[-1] = after(near[-1], far[0], wide[-1], wide_far[0])
            wide_far.append(swap(after(wide[1], near[-2]), "seq", 1))
            attended = window_attention(
                place, queries, keys, values, pair_keys, up_keys, early_values
            )
        if step == 3:
            near[-1] = after(near[-1], far[1], attended, wide_far[1])
        far.append(swap(near[-1], "seq", 1))
    rest = jnp.concatenate(wide[2:])
    wide_far.append(swap(after(rest, far[-2]), "seq", 1))
    combined = apply_fast(place, queries, attended, near + far)

    blocks = [(combined, 0)]
    mask = heads // 2
    while mask:
        blocks = blocks + [(swap(block, "head", mask), tag ^ mask) for block, tag in blocks]
        mask //= 2
    mixed = project(
        place, [b for b, _ in blocks], [t for _, t in blocks], wide, wide_far, out_proj.shape[0]
    )
    return (mixed, moment)


def plain(queries, keys, values, rates, fast, momentum, out_proj):
    tok_rows = queries.shape[0]
    ranks = lax.axis_size("seq")
    position = lax.axis_index("seq")
    own_rows = momentum.shape[2]
    grad_scale = 1.0 / math.sqrt(tok_rows * ranks)
    weights = fast[0]
    h_gate = times_transposed(keys, weights[0])
    h_up = times_transposed(keys, weights[1])
    sigma = jax.nn.sigmoid(h_gate)
    gated = (h_gate * sigma * h_up).astype(jnp.bfloat16)
    errors = (-grad_scale * rates * values.astype(jnp.float32)).astype(jnp.bfloat16)
    grad_down = contract_rows(errors, gated)
    back = matmul(errors, weights[2])
    d_gate = (back * h_up * sigma * (1.0 + h_gate * (1.0 - sigma))).astype(jnp.bfloat16)
    d_up = (back * h_gate * sigma).astype(jnp.bfloat16)
    grads = jnp.stack([contract_rows(d_gate, keys), contract_rows(d_up, keys), grad_down])
    summed_rows = lax.psum_scatter(grads, "seq", scatter_dimension=1, tiled=True)
    moment_own = MOMENTUM_DECAY * momentum[0] + summed_rows
    base_rows = lax.dynamic_slice_in_dim(weights, position * own_rows, own_rows, 1).astype(jnp.float32)
    renewed = lax.all_gather(renormalize(base_rows, moment_own), "seq", axis=1, tiled=True)
    q_gate = times_transposed(queries, renewed[0])
    q_up = times_transposed(queries, renewed[1])
    fast_in = (q_gate * jax.nn.sigmoid(q_gate) * q_up).astype(jnp.bfloat16)
    fast_out = times_transposed(fast_in, renewed[2])
    behind = [(i, i + 1) for i in range(ranks - 1)]
    early_keys = lax.ppermute(keys, "seq", behind)
    early_values = lax.ppermute(values, "seq", behind)
    attended = attention(queries, keys, values, early_keys, early_values, position)
    combined = (attended + fast_out).astype(jnp.bfloat16)
    all_heads = lax.all_gather(combined, "head", axis=1, tiled=True)
    projection = lax.all_gather(out_proj, "seq", axis=0, tiled=True)
    return (matmul(all_heads, projection).astype(jnp.bfloat16), moment_own[None])


def solution(mesh):
    return jax.shard_map(
        shards,
        mesh=mesh,
        in_specs=(
            P("seq", "head"),
            P("seq", "head"),
            P("seq", "head"),
            P("seq", "head"),
            P("head", None, None, None),
            P("head", None, "seq", None),
            P("seq", "head"),
        ),
        out_specs=(P("seq", "head"), P("head", None, "seq", None)),
        check_vma=False,
    )
```

profile of v0, /device:TPU:0, one launch (start us, length us, event | category | flops | bytes accessed | tf_op | source)
XLA Modules:
  0.0 107.4 jit_solution(2062723527493748567)
XLA Ops:
  0.6 3.0 %collective-permute-start = (bf16[512,512]{1,0:T(8,128)(2,1)}, bf16[512,512]{1,0:T(8,128)(2,1)S(1)}, u32[]{:S(2)}, u32[]{:S(2)}) collective-permute-start(bf16[512,512]{1,0:T(8,128)(2,1)} %k.3), channel_id=1, source_target_pairs={{0,4},{4,0},{8,12},{12,8},{16,20},{20,16},{24,28},{28,24},{1,5},{5... | collective-permute-start | bytes 1572872 | tf_op jit(solution)/shard_map/ppermute | solution.py:41
  6.2 1.6 %collective-permute-start.4 = (bf16[256,512]{1,0:T(8,128)(2,1)}, bf16[256,512]{1,0:T(8,128)(2,1)S(1)}, u32[]{:S(2)}, u32[]{:S(2)}) collective-permute-start(bf16[256,512]{1,0:T(8,128)(2,1)} %rest_4_), channel_id=1, source_target_pairs={{0,8},{4,12},{8,24},{12,28},{24,16},{28,20},{16,0},{20,4},{1,9},{5... | collective-permute-start | bytes 786440 | tf_op jit(solution)/shard_map/ppermute | solution.py:313
  7.9 3.3 %collective-permute-start.3 = (bf16[512,512]{1,0:T(8,128)(2,1)S(1)}, bf16[512,512]{1,0:T(8,128)(2,1)S(1)}, u32[]{:S(2)}, u32[]{:S(2)}) collective-permute-start(bf16[512,512]{1,0:T(8,128)(2,1)S(1)} %multiply_convert_fusion.e), channel_id=1, source_target_pairs={{0,4},{4,0},{8,12},{12,8},{16,20},{20,16},{24,28},{28,24},{1,5},{5... | collective-permute-start | bytes 1572872 | tf_op jit(solution)/shard_map/ppermute | solution.py:41
  11.2 5.4 %collective-permute-done.k.pair_k = bf16[512,512]{1,0:T(8,128)(2,1)S(1)} collective-permute-done((bf16[512,512]{1,0:T(8,128)(2,1)}, bf16[512,512]{1,0:T(8,128)(2,1)S(1)}, u32[]{:S(2)}, u32[]{:S(2)}) %collective-permute-start) | collective-permute-done | bytes 524320 | tf_op jit(solution)/shard_map/ppermute | solution.py:41
  16.6 4.0 %collective-permute-start.1 = (bf16[512,512]{1,0:T(8,128)(2,1)S(1)}, bf16[512,512]{1,0:T(8,128)(2,1)S(1)}, u32[]{:S(2)}, u32[]{:S(2)}) collective-permute-start(bf16[512,512]{1,0:T(8,128)(2,1)S(1)} %collective-permute-done.k.pair_k), channel_id=1, source_target_pairs={{0,8},{8,16},{16,24},{1,9},{9,17},{17,25},{2,10},{10,18},{18,26},{... | collective-permute-start | bytes 1572872 | tf_op jit(solution)/shard_map/ppermute | solution.py:372
  20.7 1.6 %collective-permute-start.5 = (bf16[256,512]{1,0:T(8,128)(2,1)S(1)}, bf16[256,512]{1,0:T(8,128)(2,1)S(1)}, u32[]{:S(2)}, u32[]{:S(2)}) collective-permute-start(bf16[256,512]{1,0:T(8,128)(2,1)S(1)} %collective-permute-done.4.rest_5_), channel_id=1, source_target_pairs={{0,8},{4,12},{8,24},{12,28},{24,16},{28,20},{16,0},{20,4},{1,9},{5... | collective-permute-start | bytes 786440 | tf_op jit(solution)/shard_map/ppermute | solution.py:313
  23.0 1.4 %copy-done = bf16[1,3,512,512]{3,2,1,0:T(8,128)(2,1)S(1)} copy-done((bf16[1,3,512,512]{3,2,1,0:T(8,128)(2,1)S(1)}, bf16[1,3,512,512]{3,2,1,0:T(8,128)(2,1)}, u32[]{:S(2)}) %copy-start) | copy-done | bytes 1572888
  25.4 2.8 %own_gradients.1.acc = f32[4,3,64,512]{3,2,1,0:T(8,128)S(1)} custom-call(s32[12]{0:T(128)S(1)} %dynamic-slice_bitcast_fusion.place, bf16[512,512]{1,0:T(8,128)(2,1)S(1)} %copy-done.3, bf16[512,512]{1,0:T(8,128)(2,1)S(1)} %multiply_convert_fusion.e, bf16[1,3,512,512]{3,2,1,0:T(8,128)(2,1)S(1)} %copy-done), custom_call_target="tpu_custom_call" | custom-call | flops 1 | bytes 1 | tf_op jit(solution)/shard_map/own_gradients/pallas_call | solution.py:122
  28.8 6.6 %collective-permute-done.5.rest_6_ = bf16[256,512]{1,0:T(8,128)(2,1)S(1)} collective-permute-done((bf16[256,512]{1,0:T(8,128)(2,1)S(1)}, bf16[256,512]{1,0:T(8,128)(2,1)S(1)}, u32[]{:S(2)}, u32[]{:S(2)}) %collective-permute-start.5) | collective-permute-done | bytes 262176 | tf_op jit(solution)/shard_map/ppermute | solution.py:313
  35.4 2.8 %both_gradients.1 = (f32[3,64,512]{2,1,0:T(8,128)S(1)}, bf16[3,64,512]{2,1,0:T(8,128)(2,1)S(1)}, bf16[3,64,512]{2,1,0:T(8,128)(2,1)S(1)}, bf16[3,64,512]{2,1,0:T(8,128)(2,1)S(1)}) custom-call(s32[12]{0:T(128)S(1)} %dynamic-slice_bitcast_fusion.place, bf16[512,512]{1,0:T(8,128)(2,1)S(1)} %collective-permute-done.k.pair_k, ...), custom_call_target="tpu_custom_call" | custom-call | flops 1 | bytes 1 | tf_op jit(solution)/shard_map/both_gradients/pallas_call | solution.py:137
  38.4 4.6 %collective-permute-start.9 = (bf16[3,64,512]{2,1,0:T(8,128)(2,1)S(1)}, bf16[3,64,512]{2,1,0:T(8,128)(2,1)S(1)}, u32[]{:S(2)}, u32[]{:S(2)}) collective-permute-start(bf16[3,64,512]{2,1,0:T(8,128)(2,1)S(1)} %get-tuple-element.24), channel_id=1, source_target_pairs={{0,24},{4,28},{8,16},{12,20},{16,8},{20,12},{24,0},{28,4},{1,25},{... | collective-permute-start | bytes 589832 | tf_op jit(solution)/shard_map/ppermute | solution.py:41
  43.6 5.2 %collective-permute-done.9.rest_2_ = bf16[3,64,512]{2,1,0:T(8,128)(2,1)S(1)} collective-permute-done((bf16[3,64,512]{2,1,0:T(8,128)(2,1)S(1)}, bf16[3,64,512]{2,1,0:T(8,128)(2,1)S(1)}, u32[]{:S(2)}, u32[]{:S(2)}) %collective-permute-start.9) | collective-permute-done | bytes 196640 | tf_op jit(solution)/shard_map/ppermute | solution.py:41
  49.1 7.6 %collective-permute-done.8.rest_1_ = bf16[3,64,512]{2,1,0:T(8,128)(2,1)S(1)} collective-permute-done((bf16[3,64,512]{2,1,0:T(8,128)(2,1)S(1)}, bf16[3,64,512]{2,1,0:T(8,128)(2,1)S(1)}, u32[]{:S(2)}, u32[]{:S(2)}) %collective-permute-start.8) | collective-permute-done | bytes 196640 | tf_op jit(solution)/shard_map/ppermute | solution.py:41
  56.7 1.4 %renew.1 = (f32[1,3,64,512]{3,2,1,0:T(8,128)}, bf16[3,64,512]{2,1,0:T(8,128)(2,1)S(1)}) custom-call(s32[12]{0:T(128)S(1)} %dynamic-slice_bitcast_fusion.place, bf16[1,3,512,512]{3,2,1,0:T(8,128)(2,1)S(1)} %copy-done.1, f32[1,3,64,512]{3,2,1,0:T(8,128)S(1)} %copy-done.6, f32[3,64,512]{2,1,0:T(8,128)S(1)} %get-tuple-element.22.mine, ...), custom_call_target="tpu_custom_call" | custom-call | flops 1 | bytes 1 | tf_op jit(solution)/shard_map/renew/pallas_call | solution.py:227
  58.1 1.7 %collective-permute-start.14 = (bf16[256,512]{1,0:T(8,128)(2,1)S(1)}, bf16[256,512]{1,0:T(8,128)(2,1)S(1)}, u32[]{:S(2)}, u32[]{:S(2)}) collective-permute-start(bf16[256,512]{1,0:T(8,128)(2,1)S(1)} %copy-done.7), channel_id=1, source_target_pairs={{0,4},{4,0},{8,12},{12,8},{16,20},{20,16},{24,28},{28,24},{1,5},{5... | collective-permute-start | bytes 786440 | tf_op jit(solution)/shard_map/ppermute | solution.py:41
  59.8 1.8 %collective-permute-start.13 = (bf16[256,512]{1,0:T(8,128)(2,1)S(1)}, bf16[256,512]{1,0:T(8,128)(2,1)S(1)}, u32[]{:S(2)}, u32[]{:S(2)}) collective-permute-start(bf16[256,512]{1,0:T(8,128)(2,1)S(1)} %collective-permute-done.5.rest_6_), channel_id=1, source_target_pairs={{0,8},{4,12},{8,24},{12,28},{24,16},{28,20},{16,0},{20,4},{1,9},{5... | collective-permute-start | bytes 786440 | tf_op jit(solution)/shard_map/ppermute | solution.py:313
  62.0 4.9 %collective-permute-done.10.rest_1_ = bf16[3,64,512]{2,1,0:T(8,128)(2,1)S(1)} collective-permute-done((bf16[3,64,512]{2,1,0:T(8,128)(2,1)S(1)}, bf16[3,64,512]{2,1,0:T(8,128)(2,1)S(1)}, u32[]{:S(2)}, u32[]{:S(2)}) %collective-permute-start.10) | collective-permute-done | bytes 196640 | tf_op jit(solution)/shard_map/ppermute | solution.py:313
  66.9 1.7 %collective-permute-start.17 = (bf16[256,512]{1,0:T(8,128)(2,1)S(1)}, bf16[256,512]{1,0:T(8,128)(2,1)S(1)}, u32[]{:S(2)}, u32[]{:S(2)}) collective-permute-start(bf16[256,512]{1,0:T(8,128)(2,1)S(1)} %collective-permute-done.4.rest_5_), channel_id=1, source_target_pairs={{0,4},{4,0},{8,12},{12,8},{16,20},{20,16},{24,28},{28,24},{1,5},{5... | collective-permute-start | bytes 786440 | tf_op jit(solution)/shard_map/ppermute | solution.py:41
  69.0 2.6 %collective-permute-done.12.rest_4_ = bf16[3,64,512]{2,1,0:T(8,128)(2,1)S(1)} collective-permute-done((bf16[3,64,512]{2,1,0:T(8,128)(2,1)S(1)}, bf16[3,64,512]{2,1,0:T(8,128)(2,1)S(1)}, u32[]{:S(2)}, u32[]{:S(2)}) %collective-permute-start.12) | collective-permute-done | bytes 196640 | tf_op jit(solution)/shard_map/ppermute | solution.py:41
  72.5 2.7 %collective-permute-done.11.rest_2_ = bf16[3,64,512]{2,1,0:T(8,128)(2,1)S(1)} collective-permute-done((bf16[3,64,512]{2,1,0:T(8,128)(2,1)S(1)}, bf16[3,64,512]{2,1,0:T(8,128)(2,1)S(1)}, u32[]{:S(2)}, u32[]{:S(2)}) %collective-permute-start.11) | collective-permute-done | bytes 196640 | tf_op jit(solution)/shard_map/ppermute | solution.py:313
  75.2 2.3 %window_attention.1.attended = f32[512,512]{1,0:T(8,128)S(1)} custom-call(s32[12]{0:T(128)S(1)} %dynamic-slice_bitcast_fusion.place, bf16[512,512]{1,0:T(8,128)(2,1)S(1)} %copy-done.5, bf16[512,512]{1,0:T(8,128)(2,1)S(1)} %copy-done.4, bf16[512,512]{1,0:T(8,128)(2,1)S(1)} %copy-done.2, bf16[512,512]{1,0:T(8,128)(2,1)S(1)} %collective-permute-done.k.pair_k, ...), custom_call_target="tpu_custom_call" | custom-call | flops 1 | bytes 1 | tf_op jit(solution)/shard_map/window_attention/pallas_call | solution.py:179
  77.5 1.7 %collective-permute-start.18 = (bf16[3,64,512]{2,1,0:T(8,128)(2,1)S(1)}, bf16[3,64,512]{2,1,0:T(8,128)(2,1)S(1)}, u32[]{:S(2)}, u32[]{:S(2)}) collective-permute-start(bf16[3,64,512]{2,1,0:T(8,128)(2,1)S(1)} %collective-permute-done.11.rest_2_), channel_id=1, source_target_pairs={{0,4},{4,0},{8,12},{12,8},{16,20},{20,16},{24,28},{28,24},{1,5},{5... | collective-permute-start | bytes 589832 | tf_op jit(solution)/shard_map/ppermute | solution.py:41
  79.2 1.8 %collective-permute-done.16.rest_5_ = bf16[3,64,512]{2,1,0:T(8,128)(2,1)S(1)} collective-permute-done((bf16[3,64,512]{2,1,0:T(8,128)(2,1)S(1)}, bf16[3,64,512]{2,1,0:T(8,128)(2,1)S(1)}, u32[]{:S(2)}, u32[]{:S(2)}) %collective-permute-start.16) | collective-permute-done | bytes 196640 | tf_op jit(solution)/shard_map/ppermute | solution.py:41
  81.7 1.7 %collective-permute-start.19 = (bf16[3,64,512]{2,1,0:T(8,128)(2,1)S(1)}, bf16[3,64,512]{2,1,0:T(8,128)(2,1)S(1)}, u32[]{:S(2)}, u32[]{:S(2)}) collective-permute-start(bf16[3,64,512]{2,1,0:T(8,128)(2,1)S(1)} %collective-permute-done.15.rest_3_), channel_id=1, source_target_pairs={{0,4},{4,0},{8,12},{12,8},{16,20},{20,16},{24,28},{28,24},{1,5},{5... | collective-permute-start | bytes 589832 | tf_op jit(solution)/shard_map/ppermute | solution.py:41
  83.4 2.0 %collective-permute-done.18.rest_6_ = bf16[3,64,512]{2,1,0:T(8,128)(2,1)S(1)} collective-permute-done((bf16[3,64,512]{2,1,0:T(8,128)(2,1)S(1)}, bf16[3,64,512]{2,1,0:T(8,128)(2,1)S(1)}, u32[]{:S(2)}, u32[]{:S(2)}) %collective-permute-start.18) | collective-permute-done | bytes 196640 | tf_op jit(solution)/shard_map/ppermute | solution.py:41
  85.4 2.9 %collective-permute-done.19.rest_7_ = bf16[3,64,512]{2,1,0:T(8,128)(2,1)S(1)} collective-permute-done((bf16[3,64,512]{2,1,0:T(8,128)(2,1)S(1)}, bf16[3,64,512]{2,1,0:T(8,128)(2,1)S(1)}, u32[]{:S(2)}, u32[]{:S(2)}) %collective-permute-start.19) | collective-permute-done | bytes 196640 | tf_op jit(solution)/shard_map/ppermute | solution.py:41
  88.3 1.7 %apply_fast.1.rest_0_ = bf16[512,512]{1,0:T(8,128)(2,1)S(1)} custom-call(s32[12]{0:T(128)S(1)} %dynamic-slice_bitcast_fusion.place, bf16[512,512]{1,0:T(8,128)(2,1)S(1)} %copy-done.5, f32[512,512]{1,0:T(8,128)S(1)} %window_attention.1.attended, bf16[3,64,512]{2,1,0:T(8,128)(2,1)S(1)} %get-tuple-element.26.rest_0_, ...), custom_call_target="tpu_custom_call" | custom-call | flops 1 | bytes 1 | tf_op jit(solution)/shard_map/apply_fast/pallas_call | solution.py:256
  90.0 1.6 %collective-permute-start.20 = (bf16[512,512]{1,0:T(8,128)(2,1)S(1)}, bf16[512,512]{1,0:T(8,128)(2,1)S(1)}, u32[]{:S(2)}, u32[]{:S(2)}) collective-permute-start(bf16[512,512]{1,0:T(8,128)(2,1)S(1)} %apply_fast.1.rest_0_), channel_id=1, source_target_pairs={{0,2},{1,3},{2,0},{3,1},{4,6},{5,7},{6,4},{7,5},{8,10},{9,11},{10,... | collective-permute-start | bytes 1572872 | tf_op jit(solution)/shard_map/ppermute | solution.py:41
  91.6 1.7 %collective-permute-start.23 = (bf16[512,512]{1,0:T(8,128)(2,1)S(1)}, bf16[512,512]{1,0:T(8,128)(2,1)S(1)}, u32[]{:S(2)}, u32[]{:S(2)}) collective-permute-start(bf16[512,512]{1,0:T(8,128)(2,1)S(1)} %pad_maximum_fusion), channel_id=1, source_target_pairs={{0,4},{4,0},{8,12},{12,8},{16,20},{20,16},{24,28},{28,24},{1,5},{5... | collective-permute-start | bytes 1572872 | tf_op jit(solution)/shard_map/ppermute | solution.py:41
  93.3 9.4 %collective-permute-done.20.rest_1_ = bf16[512,512]{1,0:T(8,128)(2,1)S(1)} collective-permute-done((bf16[512,512]{1,0:T(8,128)(2,1)S(1)}, bf16[512,512]{1,0:T(8,128)(2,1)S(1)}, u32[]{:S(2)}, u32[]{:S(2)}) %collective-permute-start.20) | collective-permute-done | bytes 524320 | tf_op jit(solution)/shard_map/ppermute | solution.py:41
  102.7 1.3 %collective-permute-done.23.rest_10_ = bf16[512,512]{1,0:T(8,128)(2,1)S(1)} collective-permute-done((bf16[512,512]{1,0:T(8,128)(2,1)S(1)}, bf16[512,512]{1,0:T(8,128)(2,1)S(1)}, u32[]{:S(2)}, u32[]{:S(2)}) %collective-permute-start.23) | collective-permute-done | bytes 524320 | tf_op jit(solution)/shard_map/ppermute | solution.py:41
  104.6 2.7 %project.1 = bf16[512,512]{1,0:T(8,128)(2,1)} custom-call(s32[12]{0:T(128)S(1)} %dynamic-slice_bitcast_fusion.place, bf16[512,512]{1,0:T(8,128)(2,1)S(1)} %apply_fast.1.rest_0_, bf16[512,512]{1,0:T(8,128)(2,1)S(1)} %collective-permute-done.20.rest_1_, bf16[512,512]{1,0:T(8,128)(2,1)S(1)} %collective-permute-done.21.rest_2_, ...), custom_call_target="tpu_custom_call" | custom-call | flops 1 | bytes 1 | tf_op jit(solution)/shard_map/project/pallas_call | solution.py:290
  (43 shorter events, 9.1 us)
Async XLA Ops:
  0.6 16.0 %collective-permute-start = (bf16[512,512]{1,0:T(8,128)(2,1)}, bf16[512,512]{1,0:T(8,128)(2,1)S(1)}, u32[]{:S(2)}, u32[]{:S(2)}) collective-permute-start(bf16[512,512]{1,0:T(8,128)(2,1)} %k.3), channel_id=1, source_target_pairs={{0,4},{4,0},{8,12},{12,8},{16,20},{20,16},{24,28},{28,24},{1,5},{5... | collective-permute-start | bytes 1572872 | tf_op jit(solution)/shard_map/ppermute | solution.py:41
  3.7 24.6 %collective-permute-start.2 = (bf16[512,512]{1,0:T(8,128)(2,1)}, bf16[512,512]{1,0:T(8,128)(2,1)S(1)}, u32[]{:S(2)}, u32[]{:S(2)}) collective-permute-start(bf16[512,512]{1,0:T(8,128)(2,1)} %v.1), channel_id=1, source_target_pairs={{4,12},{12,20},{20,28},{5,13},{13,21},{21,29},{6,14},{14,22},{22,3... | collective-permute-start | bytes 1572872 | tf_op jit(solution)/shard_map/ppermute | solution.py:371
  6.2 14.4 %collective-permute-start.4 = (bf16[256,512]{1,0:T(8,128)(2,1)}, bf16[256,512]{1,0:T(8,128)(2,1)S(1)}, u32[]{:S(2)}, u32[]{:S(2)}) collective-permute-start(bf16[256,512]{1,0:T(8,128)(2,1)} %rest_4_), channel_id=1, source_target_pairs={{0,8},{4,12},{8,24},{12,28},{24,16},{28,20},{16,0},{20,4},{1,9},{5... | collective-permute-start | bytes 786440 | tf_op jit(solution)/shard_map/ppermute | solution.py:313
  7.9 27.5 %collective-permute-start.3 = (bf16[512,512]{1,0:T(8,128)(2,1)S(1)}, bf16[512,512]{1,0:T(8,128)(2,1)S(1)}, u32[]{:S(2)}, u32[]{:S(2)}) collective-permute-start(bf16[512,512]{1,0:T(8,128)(2,1)S(1)} %multiply_convert_fusion.e), channel_id=1, source_target_pairs={{0,4},{4,0},{8,12},{12,8},{16,20},{20,16},{24,28},{28,24},{1,5},{5... | collective-permute-start | bytes 1572872 | tf_op jit(solution)/shard_map/ppermute | solution.py:41
  16.6 18.8 %collective-permute-start.1 = (bf16[512,512]{1,0:T(8,128)(2,1)S(1)}, bf16[512,512]{1,0:T(8,128)(2,1)S(1)}, u32[]{:S(2)}, u32[]{:S(2)}) collective-permute-start(bf16[512,512]{1,0:T(8,128)(2,1)S(1)} %collective-permute-done.k.pair_k), channel_id=1, source_target_pairs={{0,8},{8,16},{16,24},{1,9},{9,17},{17,25},{2,10},{10,18},{18,26},{... | collective-permute-start | bytes 1572872 | tf_op jit(solution)/shard_map/ppermute | solution.py:372
  20.7 14.7 %collective-permute-start.5 = (bf16[256,512]{1,0:T(8,128)(2,1)S(1)}, bf16[256,512]{1,0:T(8,128)(2,1)S(1)}, u32[]{:S(2)}, u32[]{:S(2)}) collective-permute-start(bf16[256,512]{1,0:T(8,128)(2,1)S(1)} %collective-permute-done.4.rest_5_), channel_id=1, source_target_pairs={{0,8},{4,12},{8,24},{12,28},{24,16},{28,20},{16,0},{20,4},{1,9},{5... | collective-permute-start | bytes 786440 | tf_op jit(solution)/shard_map/ppermute | solution.py:313
  23.0 1.4 %copy-start = (bf16[1,3,512,512]{3,2,1,0:T(8,128)(2,1)S(1)}, bf16[1,3,512,512]{3,2,1,0:T(8,128)(2,1)}, u32[]{:S(2)}) copy-start(bf16[1,3,512,512]{3,2,1,0:T(8,128)(2,1)} %w.5) | copy-start | bytes 4718596
  24.4 1.0 copy-start.3
  25.4 2.8 %copy-start.2 = (bf16[512,512]{1,0:T(8,128)(2,1)S(1)}, bf16[512,512]{1,0:T(8,128)(2,1)}, u32[]{:S(2)}) copy-start(bf16[512,512]{1,0:T(8,128)(2,1)} %v.1) | copy-start | bytes 1572868
  28.2 7.2 %copy-start.1 = (bf16[1,3,512,512]{3,2,1,0:T(8,128)(2,1)S(1)}, bf16[1,3,512,512]{3,2,1,0:T(8,128)(2,1)}, u32[]{:S(2)}) copy-start(bf16[1,3,512,512]{3,2,1,0:T(8,128)(2,1)} %w.5) | copy-start | bytes 4718596
  28.8 27.9 %copy-start.6 = (f32[1,3,64,512]{3,2,1,0:T(8,128)S(1)}, f32[1,3,64,512]{3,2,1,0:T(8,128)}, u32[]{:S(2)}) copy-start(f32[1,3,64,512]{3,2,1,0:T(8,128)} %momentum.1) | copy-start | bytes 1179652
  38.2 19.9 %copy-start.7 = (bf16[256,512]{1,0:T(8,128)(2,1)S(1)}, bf16[256,512]{1,0:T(8,128)(2,1)}, u32[]{:S(2)}) copy-start(bf16[256,512]{1,0:T(8,128)(2,1)} %rest_4_) | copy-start | bytes 786436
  38.3 36.9 %copy-start.4 = (bf16[512,512]{1,0:T(8,128)(2,1)S(1)}, bf16[512,512]{1,0:T(8,128)(2,1)}, u32[]{:S(2)}) copy-start(bf16[512,512]{1,0:T(8,128)(2,1)} %k.3) | copy-start | bytes 1572868
  38.3 36.9 %copy-start.5 = (bf16[512,512]{1,0:T(8,128)(2,1)S(1)}, bf16[512,512]{1,0:T(8,128)(2,1)}, u32[]{:S(2)}) copy-start(bf16[512,512]{1,0:T(8,128)(2,1)} %q.3) | copy-start | bytes 1572868
  38.3 10.8 %collective-permute-start.6 = (bf16[512,512]{1,0:T(8,128)(2,1)S(1)}, bf16[512,512]{1,0:T(8,128)(2,1)S(1)}, u32[]{:S(2)}, u32[]{:S(2)}) collective-permute-start(bf16[512,512]{1,0:T(8,128)(2,1)S(1)} %pick.1), channel_id=1, source_target_pairs={{0,4},{4,0},{8,12},{12,8},{16,20},{20,16},{24,28},{28,24},{1,5},{5... | collective-permute-start | bytes 1572872 | tf_op jit(solution)/shard_map/ppermute | solution.py:41
  38.4 10.4 %collective-permute-start.9 = (bf16[3,64,512]{2,1,0:T(8,128)(2,1)S(1)}, bf16[3,64,512]{2,1,0:T(8,128)(2,1)S(1)}, u32[]{:S(2)}, u32[]{:S(2)}) collective-permute-start(bf16[3,64,512]{2,1,0:T(8,128)(2,1)S(1)} %get-tuple-element.24), channel_id=1, source_target_pairs={{0,24},{4,28},{8,16},{12,20},{16,8},{20,12},{24,0},{28,4},{1,25},{... | collective-permute-start | bytes 589832 | tf_op jit(solution)/shard_map/ppermute | solution.py:41
  42.9 13.8 %collective-permute-start.8 = (bf16[3,64,512]{2,1,0:T(8,128)(2,1)S(1)}, bf16[3,64,512]{2,1,0:T(8,128)(2,1)S(1)}, u32[]{:S(2)}, u32[]{:S(2)}) collective-permute-start(bf16[3,64,512]{2,1,0:T(8,128)(2,1)S(1)} %get-tuple-element.23), channel_id=1, source_target_pairs={{0,16},{4,20},{8,24},{12,28},{16,0},{20,4},{24,8},{28,12},{1,17},{... | collective-permute-start | bytes 589832 | tf_op jit(solution)/shard_map/ppermute | solution.py:41
  42.9 13.8 %collective-permute-start.7 = (bf16[3,64,512]{2,1,0:T(8,128)(2,1)S(1)}, bf16[3,64,512]{2,1,0:T(8,128)(2,1)S(1)}, u32[]{:S(2)}, u32[]{:S(2)}) collective-permute-start(bf16[3,64,512]{2,1,0:T(8,128)(2,1)S(1)} %get-tuple-element.20), channel_id=1, source_target_pairs={{0,8},{4,12},{8,0},{12,4},{16,24},{20,28},{24,16},{28,20},{1,9},{5... | collective-permute-start | bytes 589832 | tf_op jit(solution)/shard_map/ppermute | solution.py:41
  58.1 8.7 %collective-permute-start.10 = (bf16[3,64,512]{2,1,0:T(8,128)(2,1)S(1)}, bf16[3,64,512]{2,1,0:T(8,128)(2,1)S(1)}, u32[]{:S(2)}, u32[]{:S(2)}) collective-permute-start(bf16[3,64,512]{2,1,0:T(8,128)(2,1)S(1)} %get-tuple-element.26.rest_0_), channel_id=1, source_target_pairs={{0,8},{4,12},{8,24},{12,28},{24,16},{28,20},{16,0},{20,4},{1,9},{5... | collective-permute-start | bytes 589832 | tf_op jit(solution)/shard_map/ppermute | solution.py:313
  58.1 10.4 %collective-permute-start.14 = (bf16[256,512]{1,0:T(8,128)(2,1)S(1)}, bf16[256,512]{1,0:T(8,128)(2,1)S(1)}, u32[]{:S(2)}, u32[]{:S(2)}) collective-permute-start(bf16[256,512]{1,0:T(8,128)(2,1)S(1)} %copy-done.7), channel_id=1, source_target_pairs={{0,4},{4,0},{8,12},{12,8},{16,20},{20,16},{24,28},{28,24},{1,5},{5... | collective-permute-start | bytes 786440 | tf_op jit(solution)/shard_map/ppermute | solution.py:41
  59.8 12.7 %collective-permute-start.13 = (bf16[256,512]{1,0:T(8,128)(2,1)S(1)}, bf16[256,512]{1,0:T(8,128)(2,1)S(1)}, u32[]{:S(2)}, u32[]{:S(2)}) collective-permute-start(bf16[256,512]{1,0:T(8,128)(2,1)S(1)} %collective-permute-done.5.rest_6_), channel_id=1, source_target_pairs={{0,8},{4,12},{8,24},{12,28},{24,16},{28,20},{16,0},{20,4},{1,9},{5... | collective-permute-start | bytes 786440 | tf_op jit(solution)/shard_map/ppermute | solution.py:313
  61.6 10.0 %collective-permute-start.12 = (bf16[3,64,512]{2,1,0:T(8,128)(2,1)S(1)}, bf16[3,64,512]{2,1,0:T(8,128)(2,1)S(1)}, u32[]{:S(2)}, u32[]{:S(2)}) collective-permute-start(bf16[3,64,512]{2,1,0:T(8,128)(2,1)S(1)} %get-tuple-element.26.rest_0_), channel_id=1, source_target_pairs={{0,4},{4,0},{8,12},{12,8},{16,20},{20,16},{24,28},{28,24},{1,5},{5... | collective-permute-start | bytes 589832 | tf_op jit(solution)/shard_map/ppermute | solution.py:41
  66.9 8.3 %collective-permute-start.11 = (bf16[3,64,512]{2,1,0:T(8,128)(2,1)S(1)}, bf16[3,64,512]{2,1,0:T(8,128)(2,1)S(1)}, u32[]{:S(2)}, u32[]{:S(2)}) collective-permute-start(bf16[3,64,512]{2,1,0:T(8,128)(2,1)S(1)} %collective-permute-done.10.rest_1_), channel_id=1, source_target_pairs={{0,8},{4,12},{8,24},{12,28},{24,16},{28,20},{16,0},{20,4},{1,9},{5... | collective-permute-start | bytes 589832 | tf_op jit(solution)/shard_map/ppermute | solution.py:313
  66.9 14.1 %collective-permute-start.17 = (bf16[256,512]{1,0:T(8,128)(2,1)S(1)}, bf16[256,512]{1,0:T(8,128)(2,1)S(1)}, u32[]{:S(2)}, u32[]{:S(2)}) collective-permute-start(bf16[256,512]{1,0:T(8,128)(2,1)S(1)} %collective-permute-done.4.rest_5_), channel_id=1, source_target_pairs={{0,4},{4,0},{8,12},{12,8},{16,20},{20,16},{24,28},{28,24},{1,5},{5... | collective-permute-start | bytes 786440 | tf_op jit(solution)/shard_map/ppermute | solution.py:41
  68.5 12.5 %collective-permute-start.16 = (bf16[3,64,512]{2,1,0:T(8,128)(2,1)S(1)}, bf16[3,64,512]{2,1,0:T(8,128)(2,1)S(1)}, u32[]{:S(2)}, u32[]{:S(2)}) collective-permute-start(bf16[3,64,512]{2,1,0:T(8,128)(2,1)S(1)} %collective-permute-done.10.rest_1_), channel_id=1, source_target_pairs={{0,4},{4,0},{8,12},{12,8},{16,20},{20,16},{24,28},{28,24},{1,5},{5... | collective-permute-start | bytes 589832 | tf_op jit(solution)/shard_map/ppermute | solution.py:41
  75.2 6.6 %collective-permute-start.15 = (bf16[3,64,512]{2,1,0:T(8,128)(2,1)S(1)}, bf16[3,64,512]{2,1,0:T(8,128)(2,1)S(1)}, u32[]{:S(2)}, u32[]{:S(2)}) collective-permute-start(bf16[3,64,512]{2,1,0:T(8,128)(2,1)S(1)} %collective-permute-done.11.rest_2_), channel_id=1, source_target_pairs={{0,8},{4,12},{8,24},{12,28},{24,16},{28,20},{16,0},{20,4},{1,9},{5... | collective-permute-start | bytes 589832 | tf_op jit(solution)/shard_map/ppermute | solution.py:313
  77.5 7.9 %collective-permute-start.18 = (bf16[3,64,512]{2,1,0:T(8,128)(2,1)S(1)}, bf16[3,64,512]{2,1,0:T(8,128)(2,1)S(1)}, u32[]{:S(2)}, u32[]{:S(2)}) collective-permute-start(bf16[3,64,512]{2,1,0:T(8,128)(2,1)S(1)} %collective-permute-done.11.rest_2_), channel_id=1, source_target_pairs={{0,4},{4,0},{8,12},{12,8},{16,20},{20,16},{24,28},{28,24},{1,5},{5... | collective-permute-start | bytes 589832 | tf_op jit(solution)/shard_map/ppermute | solution.py:41
  81.7 6.6 %collective-permute-start.19 = (bf16[3,64,512]{2,1,0:T(8,128)(2,1)S(1)}, bf16[3,64,512]{2,1,0:T(8,128)(2,1)S(1)}, u32[]{:S(2)}, u32[]{:S(2)}) collective-permute-start(bf16[3,64,512]{2,1,0:T(8,128)(2,1)S(1)} %collective-permute-done.15.rest_3_), channel_id=1, source_target_pairs={{0,4},{4,0},{8,12},{12,8},{16,20},{20,16},{24,28},{28,24},{1,5},{5... | collective-permute-start | bytes 589832 | tf_op jit(solution)/shard_map/ppermute | solution.py:41
  90.0 12.7 %collective-permute-start.20 = (bf16[512,512]{1,0:T(8,128)(2,1)S(1)}, bf16[512,512]{1,0:T(8,128)(2,1)S(1)}, u32[]{:S(2)}, u32[]{:S(2)}) collective-permute-start(bf16[512,512]{1,0:T(8,128)(2,1)S(1)} %apply_fast.1.rest_0_), channel_id=1, source_target_pairs={{0,2},{1,3},{2,0},{3,1},{4,6},{5,7},{6,4},{7,5},{8,10},{9,11},{10,... | collective-permute-start | bytes 1572872 | tf_op jit(solution)/shard_map/ppermute | solution.py:41
  91.6 12.4 %collective-permute-start.23 = (bf16[512,512]{1,0:T(8,128)(2,1)S(1)}, bf16[512,512]{1,0:T(8,128)(2,1)S(1)}, u32[]{:S(2)}, u32[]{:S(2)}) collective-permute-start(bf16[512,512]{1,0:T(8,128)(2,1)S(1)} %pad_maximum_fusion), channel_id=1, source_target_pairs={{0,4},{4,0},{8,12},{12,8},{16,20},{20,16},{24,28},{28,24},{1,5},{5... | collective-permute-start | bytes 1572872 | tf_op jit(solution)/shard_map/ppermute | solution.py:41
  93.3 10.7 %collective-permute-start.21 = (bf16[512,512]{1,0:T(8,128)(2,1)S(1)}, bf16[512,512]{1,0:T(8,128)(2,1)S(1)}, u32[]{:S(2)}, u32[]{:S(2)}) collective-permute-start(bf16[512,512]{1,0:T(8,128)(2,1)S(1)} %apply_fast.1.rest_0_), channel_id=1, source_target_pairs={{0,1},{1,0},{2,3},{3,2},{4,5},{5,4},{6,7},{7,6},{8,9},{9,8},{10,11... | collective-permute-start | bytes 1572872 | tf_op jit(solution)/shard_map/ppermute | solution.py:41
  102.7 1.9 %collective-permute-start.22 = (bf16[512,512]{1,0:T(8,128)(2,1)S(1)}, bf16[512,512]{1,0:T(8,128)(2,1)S(1)}, u32[]{:S(2)}, u32[]{:S(2)}) collective-permute-start(bf16[512,512]{1,0:T(8,128)(2,1)S(1)} %collective-permute-done.20.rest_1_), channel_id=1, source_target_pairs={{0,1},{1,0},{2,3},{3,2},{4,5},{5,4},{6,7},{7,6},{8,9},{9,8},{10,11... | collective-permute-start | bytes 1572872 | tf_op jit(solution)/shard_map/ppermute | solution.py:41
where the time goes:
time: 108 us; the launch traced here: 107 us
  waiting for transfers between devices  54.9 us (51%)
  starting transfers between devices  32.3 us (30%)
  Pallas kernels  14.3 us (13%)
  local copies, waits for them, and re-layouts  3.17 us (3%)
  other arithmetic  1.92 us (2%)
    ppermute x16, waiting for transfers between devices, swap(): return lax.ppermute(array, axis, [(i, i ^ mask) for i in range(devices)])  39.1 us
    ppermute x16, starting transfers between devices, swap(): return lax.ppermute(array, axis, [(i, i ^ mask) for i in range(devices)])  22.5 us
    ppermute x6, waiting for transfers between devices, ring_step(): return lax.ppermute(unit, 'seq', pairs)  15.8 us
    ppermute x6, starting transfers between devices, ring_step(): return lax.ppermute(unit, 'seq', pairs)  5.02 us
    ppermute x1, starting transfers between devices, shards(): lax.ppermute(pair_keys, 'seq', [(s, s + 2) for s in range(0, ranks - 2, 2)])  4.04 us
    pallas_call x1, Pallas kernels, both_gradients(): pl.pallas_call(functools.partial(both_kernel, outer), out_shape=[jax.Shap...  2.82 us
    pallas_call x1, Pallas kernels, own_gradients(): pl.pallas_call(functools.partial(own_kernel, outer), out_shape=jax.ShapeD...  2.77 us
    pallas_call x1, Pallas kernels, project(): pl.pallas_call(functools.partial(project_kernel, tags, rows_in), out_shap...  2.72 us
  transfers between devices with their start and end apart: 24, of which 16 were waited for; matrix products, arithmetic and copies ran while one was open for 2% of the time, Pallas kernels for 5%

commit v1 on v0

--- a/solution.py
+++ b/solution.py
@@ -149,7 +149,7 @@
 
 def attend_kernel(blocks, place, q, k, v, pair_k, up_k, early_v, out):
     early_k = jnp.where(place[0] == 0, up_k[...], pair_k[...])
-    early_v = early_v[...]
+    early_v = early_v[: v.shape[0]]
     early_v = jnp.where(place[2] > 0, early_v, jnp.zeros_like(early_v))
     tokens = q.shape[0]
     rows = tokens // blocks
@@ -187,26 +187,31 @@
     )(place, q, k, v, *early)
 
 
-def pick_kernel(place, even, odd, out):
+def crossing_kernel(place, even, odd, rows, out):
+    tokens = even.shape[0]
+
     @pl.when(place[0] == 0)
     def _():
-        out[...] = even[...]
+        out[:tokens] = even[...]
 
     @pl.when(place[0] == 1)
     def _():
-        out[...] = odd[...]
-
-
-def pick(place, even, odd):
-    return pl.pallas_call(
-        pick_kernel,
-        out_shape=jax.ShapeDtypeStruct(even.shape, even.dtype),
-        in_specs=[pl.BlockSpec(memory_space=pltpu.SMEM)] + [whole_spec()] * 2,
+        out[:tokens] = odd[...]
+
+    out[tokens:] = rows[...]
+
+
+def crossing(place, even, odd, rows):
+    shape = (even.shape[0] + rows.shape[0], even.shape[1])
+    return pl.pallas_call(
+        crossing_kernel,
+        out_shape=jax.ShapeDtypeStruct(shape, even.dtype),
+        in_specs=[pl.BlockSpec(memory_space=pltpu.SMEM)] + [whole_spec()] * 3,
         out_specs=whole_spec(),
         compiler_params=params(12),
         cost_estimate=BRIEF,
-        name="pick",
-    )(place, even, odd)
+        name="crossing",
+    )(place, even, odd, rows)
 
 
 def renew_kernel(place, w, momentum, mine, *rest):
@@ -242,7 +247,8 @@
     units, combined, full = rest[:count], rest[count], rest[count + 1]
     own = units[0].shape[1]
     for i in range(count):
-        rows = pl.ds(pl.multiple_of(place[ORIGINS + i] * own, own), own)
+        step, across = i % (count // 2), i // (count // 2)
+        rows = pl.ds(pl.multiple_of((place[2] ^ (2 * step + across)) * own, own), own)
         full[:, rows, :] = units[i][...]
     b1 = times_transposed(q[...], full[0])
     b3 = times_transposed(q[...], full[1])
@@ -268,12 +274,9 @@
 def project_kernel(tags, rows_in, place, *rest):
     blocks, units = rest[: len(tags)], rest[len(tags) : -2]
     mixed, full = rest[-2:]
-    at = 0
-    for unit in units:
-        for part in range(unit.shape[0] // rows_in):
-            rows = pl.ds(pl.multiple_of(place[ORIGINS + at] * rows_in, rows_in), rows_in)
-            full[rows, :] = unit[part * rows_in : (part + 1) * rows_in, :]
-            at += 1
+    for at, unit in enumerate(units):
+        rows = pl.ds(pl.multiple_of(place[ORIGINS + at] * rows_in, rows_in), rows_in)
+        full[rows, :] = unit[unit.shape[0] - rows_in :, :]
     width = blocks[0].shape[1]
     value = None
     for block, tag in zip(blocks, tags):
@@ -286,7 +289,7 @@
 def project(place, blocks, tags, near, far, rows_in):
     tokens = blocks[0].shape[0]
     units = near + far
-    depth, width = sum(unit.shape[0] for unit in units), units[0].shape[1]
+    depth, width = rows_in * len(units), units[0].shape[1]
     return pl.pallas_call(
         functools.partial(project_kernel, tags, rows_in),
         out_shape=jax.ShapeDtypeStruct((tokens, width), jnp.bfloat16),
@@ -369,44 +372,45 @@
     pair_errors = swap(errors, "seq", 1)
 
     up_values = lax.ppermute(values, "seq", [(s, s + 2) for s in range(1, ranks - 2, 2)])
-    up_keys = lax.ppermute(pair_keys, "seq", [(s, s + 2) for s in range(0, ranks - 2, 2)])
 
     wide = [after(out_proj, errors)]
-    for _ in range(2, outer):
-        wide.append(ring_step(wide[-1], outer))
+    wide.append(ring_step(wide[-1], outer))
+    up_keys = after(pair_keys, wide[-1])
+    up_keys = lax.ppermute(up_keys, "seq", [(s, s + 2) for s in range(0, ranks - 2, 2)])
+    wide.append(ring_step(wide[-1], outer))
 
     acc = own_gradients(place, keys, errors, fast, outer)
-    across = pick(place, values, up_values)
+    across = crossing(place, values, up_values, wide[0])
     pair_errors = after(pair_errors, up_keys, wide[-1], across)
     summed = both_gradients(place, pair_keys, pair_errors, fast, acc, outer)
     pieces = [swap(summed[step], "seq", step * 2) for step in range(1, outer)]
-    early_values = swap(after(across, summed[1]), "seq", 1)
-    pieces[2] = after(pieces[2], early_values)
+    crossed = swap(after(across, summed[1]), "seq", 1)
+    pieces[2] = after(pieces[2], crossed)
     moment, renewed = renew(place, fast, momentum, summed[0], pieces)
 
-    wide_far = [swap(after(wide[0], pieces[1]), "seq", 1)]
-    wide.append(ring_step(after(wide[-1], renewed), outer))
-
-    near, far = [renewed], [swap(renewed, "seq", 1)]
+    near = [renewed]
     for step in range(1, outer):
-        near.append(ring_step(near[-1], outer))
-        if step == 2:
-            near[-1] = after(near[-1], far[0], wide[-1], wide_far[0])
-            wide_far.append(swap(after(wide[1], near[-2]), "seq", 1))
-            attended = window_attention(
-                place, queries, keys, values, pair_keys, up_keys, early_values
-            )
-        if step == 3:
-            near[-1] = after(near[-1], far[1], attended, wide_far[1])
-        far.append(swap(near[-1], "seq", 1))
-    rest = jnp.concatenate(wide[2:])
-    wide_far.append(swap(after(rest, far[-2]), "seq", 1))
+        near.append(swap(renewed, "seq", step * 2))
+    far = [swap(renewed, "seq", 1)]
+    near[1] = after(near[1], far[0])
+    far += [swap(unit, "seq", 1) for unit in near[1:]]
+    attended = window_attention(
+        place, queries, keys, values, pair_keys, up_keys, after(crossed, near[1])
+    )
+    far[1] = after(far[1], attended)
+    wide_far = [crossed, swap(after(wide[1], near[1]), "seq", 1)]
+    wide.append(ring_step(after(wide[2], near[1], near[2]), outer))
+    far[-1] = after(far[-1], wide_far[1], wide[3])
+    wide_far += [swap(after(unit, far[1]), "seq", 1) for unit in wide[2:]]
     combined = apply_fast(place, queries, attended, near + far)
 
     blocks = [(combined, 0)]
     mask = heads // 2
     while mask:
-        blocks = blocks + [(swap(block, "head", mask), tag ^ mask) for block, tag in blocks]
+        moved = [(swap(block, "head", mask), tag ^ mask) for block, tag in blocks]
+        if mask > 1:
+            moved = [(after(block, *wide_far[2:]), tag) for block, tag in moved]
+        blocks = blocks + moved
         mask //= 2
     mixed = project(
         place, [b for b, _ in blocks], [t for _, t in blocks], wide, wide_far, out_proj.shape[0]

time: 108 us -> 104 us (0.963)
  waiting for transfers between devices: 54.9 us -> 47.2 us
  starting transfers between devices: 32.3 us -> 35.7 us
    ppermute x6 -> x3, waiting for transfers between devices: 15.8 us -> 8.74 us  [ring_step(): return lax.ppermute(unit, 'seq', pairs)]
    ppermute x16 -> x19, starting transfers between devices: 22.5 us -> 27.7 us  [swap(): return lax.ppermute(array, axis, [(i, i ^ mask) for i in range(devices)])]
    ppermute x6 -> x3, starting transfers between devices: 5.02 us -> 3.23 us  [ring_step(): return lax.ppermute(unit, 'seq', pairs)]
    ppermute x16 -> x19, waiting for transfers between devices: 39.1 us -> 38.5 us  [swap(): return lax.ppermute(array, axis, [(i, i ^ mask) for i in range(devices)])]
  transfers between devices with their start and end apart: 24 -> 24, of which waited for: 16 -> 14; matrix products, arithmetic and copies ran while one was open for 2% -> 2% of each run, Pallas kernels for 5% -> 5%
where the time goes in v1:
time: 104 us; the launch traced here: 103 us
  waiting for transfers between devices  47.2 us (45%)
  starting transfers between devices  35.7 us (34%)
  Pallas kernels  14.3 us (14%)
  local copies, waits for them, and re-layouts  3.17 us (3%)
  other arithmetic  1.89 us (2%)
    ppermute x19, waiting for transfers between devices, swap(): return lax.ppermute(array, axis, [(i, i ^ mask) for i in range(devices)])  38.5 us
    ppermute x19, starting transfers between devices, swap(): return lax.ppermute(array, axis, [(i, i ^ mask) for i in range(devices)])  27.7 us
    ppermute x3, waiting for transfers between devices, ring_step(): return lax.ppermute(unit, 'seq', pairs)  8.74 us
    ppermute x1, starting transfers between devices, shards(): lax.ppermute(up_keys, 'seq', [(s, s + 2) for s in range(0, ranks - 2, 2)])  4.04 us
    ppermute x3, starting transfers between devices, ring_step(): return lax.ppermute(unit, 'seq', pairs)  3.23 us
    pallas_call x1, Pallas kernels, both_gradients(): pl.pallas_call(functools.partial(both_kernel, outer), out_shape=[jax.Shap...  2.82 us
    pallas_call x1, Pallas kernels, own_gradients(): pl.pallas_call(functools.partial(own_kernel, outer), out_shape=jax.ShapeD...  2.77 us
    pallas_call x1, Pallas kernels, project(): pl.pallas_call(functools.partial(project_kernel, tags, rows_in), out_shap...  2.72 us
  transfers between devices with their start and end apart: 24, of which 14 were waited for; matrix products, arithmetic and copies ran while one was open for 2% of the time, Pallas kernels for 5%

profile of v1, /device:TPU:0, one launch (start us, length us, event | category | flops | bytes accessed | tf_op | source)
XLA Modules:
  0.0 103.1 jit_solution(7616719747365989080)
XLA Ops:
  0.6 3.0 %collective-permute-start = (bf16[512,512]{1,0:T(8,128)(2,1)}, bf16[512,512]{1,0:T(8,128)(2,1)S(1)}, u32[]{:S(2)}, u32[]{:S(2)}) collective-permute-start(bf16[512,512]{1,0:T(8,128)(2,1)} %k.3), channel_id=1, source_target_pairs={{0,4},{4,0},{8,12},{12,8},{16,20},{20,16},{24,28},{28,24},{1,5},{5... | collective-permute-start | bytes 1572872 | tf_op jit(solution)/shard_map/ppermute | solution.py:41
  4.3 1.2 %multiply_convert_fusion.e = bf16[512,512]{1,0:T(8,128)(2,1)S(1)} fusion(bf16[512,512]{1,0:T(8,128)(2,1)} %v.1, f32[512]{0:T(512)S(1)} %bitcast.3), kind=kLoop, calls=%fused_computation | loop fusion | flops 786432 | bytes 1050624 | tf_op jit(solution)/shard_map/convert_element_type | solution.py:371
  5.6 1.6 %collective-permute-start.1 = (bf16[256,512]{1,0:T(8,128)(2,1)}, bf16[256,512]{1,0:T(8,128)(2,1)S(1)}, u32[]{:S(2)}, u32[]{:S(2)}) collective-permute-start(bf16[256,512]{1,0:T(8,128)(2,1)} %rest_4_), channel_id=1, source_target_pairs={{0,8},{4,12},{8,24},{12,28},{24,16},{28,20},{16,0},{20,4},{1,9},{5... | collective-permute-start | bytes 786440 | tf_op jit(solution)/shard_map/ppermute | solution.py:316
  7.9 4.4 %collective-permute-start.4 = (bf16[512,512]{1,0:T(8,128)(2,1)S(1)}, bf16[512,512]{1,0:T(8,128)(2,1)S(1)}, u32[]{:S(2)}, u32[]{:S(2)}) collective-permute-start(bf16[512,512]{1,0:T(8,128)(2,1)S(1)} %multiply_convert_fusion.e), channel_id=1, source_target_pairs={{0,4},{4,0},{8,12},{12,8},{16,20},{20,16},{24,28},{28,24},{1,5},{5... | collective-permute-start | bytes 1572872 | tf_op jit(solution)/shard_map/ppermute | solution.py:41
  12.3 2.2 %collective-permute-done.1.rest_5_ = bf16[256,512]{1,0:T(8,128)(2,1)S(1)} collective-permute-done((bf16[256,512]{1,0:T(8,128)(2,1)}, bf16[256,512]{1,0:T(8,128)(2,1)S(1)}, u32[]{:S(2)}, u32[]{:S(2)}) %collective-permute-start.1) | collective-permute-done | bytes 262176 | tf_op jit(solution)/shard_map/ppermute | solution.py:316
  14.5 2.1 %collective-permute-done.k.pair_k = bf16[512,512]{1,0:T(8,128)(2,1)S(1)} collective-permute-done((bf16[512,512]{1,0:T(8,128)(2,1)}, bf16[512,512]{1,0:T(8,128)(2,1)S(1)}, u32[]{:S(2)}, u32[]{:S(2)}) %collective-permute-start) | collective-permute-done | bytes 524320 | tf_op jit(solution)/shard_map/ppermute | solution.py:41
  16.6 4.0 %collective-permute-start.2 = (bf16[512,512]{1,0:T(8,128)(2,1)S(1)}, bf16[512,512]{1,0:T(8,128)(2,1)S(1)}, u32[]{:S(2)}, u32[]{:S(2)}) collective-permute-start(bf16[512,512]{1,0:T(8,128)(2,1)S(1)} %collective-permute-done.k.pair_k), channel_id=1, source_target_pairs={{0,8},{8,16},{16,24},{1,9},{9,17},{17,25},{2,10},{10,18},{18,26},{... | collective-permute-start | bytes 1572872 | tf_op jit(solution)/shard_map/ppermute | solution.py:379
  20.7 1.6 %collective-permute-start.5 = (bf16[256,512]{1,0:T(8,128)(2,1)S(1)}, bf16[256,512]{1,0:T(8,128)(2,1)S(1)}, u32[]{:S(2)}, u32[]{:S(2)}) collective-permute-start(bf16[256,512]{1,0:T(8,128)(2,1)S(1)} %collective-permute-done.1.rest_5_), channel_id=1, source_target_pairs={{0,8},{4,12},{8,24},{12,28},{24,16},{28,20},{16,0},{20,4},{1,9},{5... | collective-permute-start | bytes 786440 | tf_op jit(solution)/shard_map/ppermute | solution.py:316
  23.0 1.4 %copy-done = bf16[1,3,512,512]{3,2,1,0:T(8,128)(2,1)S(1)} copy-done((bf16[1,3,512,512]{3,2,1,0:T(8,128)(2,1)S(1)}, bf16[1,3,512,512]{3,2,1,0:T(8,128)(2,1)}, u32[]{:S(2)}) %copy-start) | copy-done | bytes 1572888
  25.4 2.8 %own_gradients.1.acc = f32[4,3,64,512]{3,2,1,0:T(8,128)S(1)} custom-call(s32[12]{0:T(128)S(1)} %dynamic-slice_bitcast_fusion.place, bf16[512,512]{1,0:T(8,128)(2,1)S(1)} %copy-done.3, bf16[512,512]{1,0:T(8,128)(2,1)S(1)} %multiply_convert_fusion.e, bf16[1,3,512,512]{3,2,1,0:T(8,128)(2,1)S(1)} %copy-done), custom_call_target="tpu_custom_call" | custom-call | flops 1 | bytes 1 | tf_op jit(solution)/shard_map/own_gradients/pallas_call | solution.py:122
  28.9 6.5 %collective-permute-done.5.rest_6_ = bf16[256,512]{1,0:T(8,128)(2,1)S(1)} collective-permute-done((bf16[256,512]{1,0:T(8,128)(2,1)S(1)}, bf16[256,512]{1,0:T(8,128)(2,1)S(1)}, u32[]{:S(2)}, u32[]{:S(2)}) %collective-permute-start.5) | collective-permute-done | bytes 262176 | tf_op jit(solution)/shard_map/ppermute | solution.py:316
  35.4 2.8 %both_gradients.1 = (f32[3,64,512]{2,1,0:T(8,128)S(1)}, bf16[3,64,512]{2,1,0:T(8,128)(2,1)S(1)}, bf16[3,64,512]{2,1,0:T(8,128)(2,1)S(1)}, bf16[3,64,512]{2,1,0:T(8,128)(2,1)S(1)}) custom-call(s32[12]{0:T(128)S(1)} %dynamic-slice_bitcast_fusion.place, bf16[512,512]{1,0:T(8,128)(2,1)S(1)} %collective-permute-done.k.pair_k, ...), custom_call_target="tpu_custom_call" | custom-call | flops 1 | bytes 1 | tf_op jit(solution)/shard_map/both_gradients/pallas_call | solution.py:137
  38.3 4.6 %collective-permute-start.9 = (bf16[3,64,512]{2,1,0:T(8,128)(2,1)S(1)}, bf16[3,64,512]{2,1,0:T(8,128)(2,1)S(1)}, u32[]{:S(2)}, u32[]{:S(2)}) collective-permute-start(bf16[3,64,512]{2,1,0:T(8,128)(2,1)S(1)} %get-tuple-element.29), channel_id=1, source_target_pairs={{0,24},{4,28},{8,16},{12,20},{16,8},{20,12},{24,0},{28,4},{1,25},{... | collective-permute-start | bytes 589832 | tf_op jit(solution)/shard_map/ppermute | solution.py:41
  43.6 5.3 %collective-permute-done.9.rest_2_ = bf16[3,64,512]{2,1,0:T(8,128)(2,1)S(1)} collective-permute-done((bf16[3,64,512]{2,1,0:T(8,128)(2,1)S(1)}, bf16[3,64,512]{2,1,0:T(8,128)(2,1)S(1)}, u32[]{:S(2)}, u32[]{:S(2)}) %collective-permute-start.9) | collective-permute-done | bytes 196640 | tf_op jit(solution)/shard_map/ppermute | solution.py:41
  48.8 5.8 %collective-permute-done.6.early_v.rest_8_ = bf16[768,512]{1,0:T(8,128)(2,1)S(1)} collective-permute-done((bf16[768,512]{1,0:T(8,128)(2,1)S(1)}, bf16[768,512]{1,0:T(8,128)(2,1)S(1)}, u32[]{:S(2)}, u32[]{:S(2)}) %collective-permute-start.6) | collective-permute-done | bytes 786464 | tf_op jit(solution)/shard_map/ppermute | solution.py:41
  54.7 2.0 %collective-permute-done.8.rest_1_ = bf16[3,64,512]{2,1,0:T(8,128)(2,1)S(1)} collective-permute-done((bf16[3,64,512]{2,1,0:T(8,128)(2,1)S(1)}, bf16[3,64,512]{2,1,0:T(8,128)(2,1)S(1)}, u32[]{:S(2)}, u32[]{:S(2)}) %collective-permute-start.8) | collective-permute-done | bytes 196640 | tf_op jit(solution)/shard_map/ppermute | solution.py:41
  56.7 1.4 %renew.1 = (f32[1,3,64,512]{3,2,1,0:T(8,128)}, bf16[3,64,512]{2,1,0:T(8,128)(2,1)S(1)}) custom-call(s32[12]{0:T(128)S(1)} %dynamic-slice_bitcast_fusion.place, bf16[1,3,512,512]{3,2,1,0:T(8,128)(2,1)S(1)} %copy-done.1, f32[1,3,64,512]{3,2,1,0:T(8,128)S(1)} %copy-done.7, f32[3,64,512]{2,1,0:T(8,128)S(1)} %get-tuple-element.27.mine, ...), custom_call_target="tpu_custom_call" | custom-call | flops 1 | bytes 1 | tf_op jit(solution)/shard_map/renew/pallas_call | solution.py:232
  59.8 2.5 %collective-permute-start.12 = (bf16[3,64,512]{2,1,0:T(8,128)(2,1)S(1)}, bf16[3,64,512]{2,1,0:T(8,128)(2,1)S(1)}, u32[]{:S(2)}, u32[]{:S(2)}) collective-permute-start(bf16[3,64,512]{2,1,0:T(8,128)(2,1)S(1)} %get-tuple-element.31.rest_0_), channel_id=1, source_target_pairs={{0,16},{4,20},{8,24},{12,28},{16,0},{20,4},{24,8},{28,12},{1,17},{... | collective-permute-start | bytes 589832 | tf_op jit(solution)/shard_map/ppermute | solution.py:41
  62.3 1.9 %collective-permute-start.13 = (bf16[3,64,512]{2,1,0:T(8,128)(2,1)S(1)}, bf16[3,64,512]{2,1,0:T(8,128)(2,1)S(1)}, u32[]{:S(2)}, u32[]{:S(2)}) collective-permute-start(bf16[3,64,512]{2,1,0:T(8,128)(2,1)S(1)} %get-tuple-element.31.rest_0_), channel_id=1, source_target_pairs={{0,24},{4,28},{8,16},{12,20},{16,8},{20,12},{24,0},{28,4},{1,25},{... | collective-permute-start | bytes 589832 | tf_op jit(solution)/shard_map/ppermute | solution.py:41
  65.3 2.2 %collective-permute-start.17 = (bf16[256,512]{1,0:T(8,128)(2,1)S(1)}, bf16[256,512]{1,0:T(8,128)(2,1)S(1)}, u32[]{:S(2)}, u32[]{:S(2)}) collective-permute-start(bf16[256,512]{1,0:T(8,128)(2,1)S(1)} %collective-permute-done.1.rest_5_), channel_id=1, source_target_pairs={{0,4},{4,0},{8,12},{12,8},{16,20},{20,16},{24,28},{28,24},{1,5},{5... | collective-permute-start | bytes 786440 | tf_op jit(solution)/shard_map/ppermute | solution.py:41
  67.6 8.0 %collective-permute-done.12.rest_2_ = bf16[3,64,512]{2,1,0:T(8,128)(2,1)S(1)} collective-permute-done((bf16[3,64,512]{2,1,0:T(8,128)(2,1)S(1)}, bf16[3,64,512]{2,1,0:T(8,128)(2,1)S(1)}, u32[]{:S(2)}, u32[]{:S(2)}) %collective-permute-start.12) | collective-permute-done | bytes 196640 | tf_op jit(solution)/shard_map/ppermute | solution.py:41
  76.2 1.4 %collective-permute-start.16 = (bf16[3,64,512]{2,1,0:T(8,128)(2,1)S(1)}, bf16[3,64,512]{2,1,0:T(8,128)(2,1)S(1)}, u32[]{:S(2)}, u32[]{:S(2)}) collective-permute-start(bf16[3,64,512]{2,1,0:T(8,128)(2,1)S(1)} %collective-permute-done.13.rest_3_), channel_id=1, source_target_pairs={{0,4},{4,0},{8,12},{12,8},{16,20},{20,16},{24,28},{28,24},{1,5},{5... | collective-permute-start | bytes 589832 | tf_op jit(solution)/shard_map/ppermute | solution.py:41
  78.3 2.3 %window_attention.1.attended = f32[512,512]{1,0:T(8,128)S(1)} custom-call(s32[12]{0:T(128)S(1)} %dynamic-slice_bitcast_fusion.place, bf16[512,512]{1,0:T(8,128)(2,1)S(1)} %copy-done.5, bf16[512,512]{1,0:T(8,128)(2,1)S(1)} %copy-done.4, bf16[512,512]{1,0:T(8,128)(2,1)S(1)} %copy-done.2, bf16[512,512]{1,0:T(8,128)(2,1)S(1)} %collective-permute-done.k.pair_k, ...), custom_call_target="tpu_custom_call" | custom-call | flops 1 | bytes 1 | tf_op jit(solution)/shard_map/window_attention/pallas_call | solution.py:179
  81.3 2.1 %collective-permute-done.16.rest_7_ = bf16[3,64,512]{2,1,0:T(8,128)(2,1)S(1)} collective-permute-done((bf16[3,64,512]{2,1,0:T(8,128)(2,1)S(1)}, bf16[3,64,512]{2,1,0:T(8,128)(2,1)S(1)}, u32[]{:S(2)}, u32[]{:S(2)}) %collective-permute-start.16) | collective-permute-done | bytes 196640 | tf_op jit(solution)/shard_map/ppermute | solution.py:41
  83.4 2.1 %collective-permute-done.15.rest_6_ = bf16[3,64,512]{2,1,0:T(8,128)(2,1)S(1)} collective-permute-done((bf16[3,64,512]{2,1,0:T(8,128)(2,1)S(1)}, bf16[3,64,512]{2,1,0:T(8,128)(2,1)S(1)}, u32[]{:S(2)}, u32[]{:S(2)}) %collective-permute-start.15) | collective-permute-done | bytes 196640 | tf_op jit(solution)/shard_map/ppermute | solution.py:41
  85.5 1.7 %apply_fast.1.rest_0_ = bf16[512,512]{1,0:T(8,128)(2,1)S(1)} custom-call(s32[12]{0:T(128)S(1)} %dynamic-slice_bitcast_fusion.place, bf16[512,512]{1,0:T(8,128)(2,1)S(1)} %copy-done.5, f32[512,512]{1,0:T(8,128)S(1)} %window_attention.1.attended, bf16[3,64,512]{2,1,0:T(8,128)(2,1)S(1)} %get-tuple-element.31.rest_0_, ...), custom_call_target="tpu_custom_call" | custom-call | flops 1 | bytes 1 | tf_op jit(solution)/shard_map/apply_fast/pallas_call | solution.py:262
  87.2 2.1 %collective-permute-start.19 = (bf16[512,512]{1,0:T(8,128)(2,1)S(1)}, bf16[512,512]{1,0:T(8,128)(2,1)S(1)}, u32[]{:S(2)}, u32[]{:S(2)}) collective-permute-start(bf16[512,512]{1,0:T(8,128)(2,1)S(1)} %apply_fast.1.rest_0_), channel_id=1, source_target_pairs={{0,2},{1,3},{2,0},{3,1},{4,6},{5,7},{6,4},{7,5},{8,10},{9,11},{10,... | collective-permute-start | bytes 1572872 | tf_op jit(solution)/shard_map/ppermute | solution.py:41
  89.4 1.9 %collective-permute-start.21 = (bf16[256,512]{1,0:T(8,128)(2,1)S(1)}, bf16[256,512]{1,0:T(8,128)(2,1)S(1)}, u32[]{:S(2)}, u32[]{:S(2)}) collective-permute-start(bf16[256,512]{1,0:T(8,128)(2,1)S(1)} %collective-permute-done.18.rest_7_), channel_id=1, source_target_pairs={{0,4},{4,0},{8,12},{12,8},{16,20},{20,16},{24,28},{28,24},{1,5},{5... | collective-permute-start | bytes 786440 | tf_op jit(solution)/shard_map/ppermute | solution.py:41
  91.3 4.3 %collective-permute-done.20.rest_10_ = bf16[256,512]{1,0:T(8,128)(2,1)S(1)} collective-permute-done((bf16[256,512]{1,0:T(8,128)(2,1)S(1)}, bf16[256,512]{1,0:T(8,128)(2,1)S(1)}, u32[]{:S(2)}, u32[]{:S(2)}) %collective-permute-start.20) | collective-permute-done | bytes 262176 | tf_op jit(solution)/shard_map/ppermute | solution.py:41
  95.6 2.8 %collective-permute-done.21.rest_11_ = bf16[256,512]{1,0:T(8,128)(2,1)S(1)} collective-permute-done((bf16[256,512]{1,0:T(8,128)(2,1)S(1)}, bf16[256,512]{1,0:T(8,128)(2,1)S(1)}, u32[]{:S(2)}, u32[]{:S(2)}) %collective-permute-start.21) | collective-permute-done | bytes 262176 | tf_op jit(solution)/shard_map/ppermute | solution.py:41
  98.4 1.9 %collective-permute-done.23.rest_3_ = bf16[512,512]{1,0:T(8,128)(2,1)S(1)} collective-permute-done((bf16[512,512]{1,0:T(8,128)(2,1)S(1)}, bf16[512,512]{1,0:T(8,128)(2,1)S(1)}, u32[]{:S(2)}, u32[]{:S(2)}) %collective-permute-start.23) | collective-permute-done | bytes 524320 | tf_op jit(solution)/shard_map/ppermute | solution.py:41
  100.3 2.7 %project.1 = bf16[512,512]{1,0:T(8,128)(2,1)} custom-call(s32[12]{0:T(128)S(1)} %dynamic-slice_bitcast_fusion.place, bf16[512,512]{1,0:T(8,128)(2,1)S(1)} %apply_fast.1.rest_0_, bf16[512,512]{1,0:T(8,128)(2,1)S(1)} %collective-permute-done.19.rest_1_, bf16[512,512]{1,0:T(8,128)(2,1)S(1)} %collective-permute-done.22.rest_2_, ...), custom_call_target="tpu_custom_call" | custom-call | flops 1 | bytes 1 | tf_op jit(solution)/shard_map/project/pallas_call | solution.py:293
  (42 shorter events, 9.4 us)
Async XLA Ops:
  0.6 16.0 %collective-permute-start = (bf16[512,512]{1,0:T(8,128)(2,1)}, bf16[512,512]{1,0:T(8,128)(2,1)S(1)}, u32[]{:S(2)}, u32[]{:S(2)}) collective-permute-start(bf16[512,512]{1,0:T(8,128)(2,1)} %k.3), channel_id=1, source_target_pairs={{0,4},{4,0},{8,12},{12,8},{16,20},{20,16},{24,28},{28,24},{1,5},{5... | collective-permute-start | bytes 1572872 | tf_op jit(solution)/shard_map/ppermute | solution.py:41
  5.6 8.9 %collective-permute-start.1 = (bf16[256,512]{1,0:T(8,128)(2,1)}, bf16[256,512]{1,0:T(8,128)(2,1)S(1)}, u32[]{:S(2)}, u32[]{:S(2)}) collective-permute-start(bf16[256,512]{1,0:T(8,128)(2,1)} %rest_4_), channel_id=1, source_target_pairs={{0,8},{4,12},{8,24},{12,28},{24,16},{28,20},{16,0},{20,4},{1,9},{5... | collective-permute-start | bytes 786440 | tf_op jit(solution)/shard_map/ppermute | solution.py:316
  7.2 21.0 %collective-permute-start.3 = (bf16[512,512]{1,0:T(8,128)(2,1)}, bf16[512,512]{1,0:T(8,128)(2,1)S(1)}, u32[]{:S(2)}, u32[]{:S(2)}) collective-permute-start(bf16[512,512]{1,0:T(8,128)(2,1)} %v.1), channel_id=1, source_target_pairs={{4,12},{12,20},{20,28},{5,13},{13,21},{21,29},{6,14},{14,22},{22,3... | collective-permute-start | bytes 1572872 | tf_op jit(solution)/shard_map/ppermute | solution.py:374
  7.9 21.0 %collective-permute-start.4 = (bf16[512,512]{1,0:T(8,128)(2,1)S(1)}, bf16[512,512]{1,0:T(8,128)(2,1)S(1)}, u32[]{:S(2)}, u32[]{:S(2)}) collective-permute-start(bf16[512,512]{1,0:T(8,128)(2,1)S(1)} %multiply_convert_fusion.e), channel_id=1, source_target_pairs={{0,4},{4,0},{8,12},{12,8},{16,20},{20,16},{24,28},{28,24},{1,5},{5... | collective-permute-start | bytes 1572872 | tf_op jit(solution)/shard_map/ppermute | solution.py:41
  16.6 18.8 %collective-permute-start.2 = (bf16[512,512]{1,0:T(8,128)(2,1)S(1)}, bf16[512,512]{1,0:T(8,128)(2,1)S(1)}, u32[]{:S(2)}, u32[]{:S(2)}) collective-permute-start(bf16[512,512]{1,0:T(8,128)(2,1)S(1)} %collective-permute-done.k.pair_k), channel_id=1, source_target_pairs={{0,8},{8,16},{16,24},{1,9},{9,17},{17,25},{2,10},{10,18},{18,26},{... | collective-permute-start | bytes 1572872 | tf_op jit(solution)/shard_map/ppermute | solution.py:379
  20.7 14.7 %collective-permute-start.5 = (bf16[256,512]{1,0:T(8,128)(2,1)S(1)}, bf16[256,512]{1,0:T(8,128)(2,1)S(1)}, u32[]{:S(2)}, u32[]{:S(2)}) collective-permute-start(bf16[256,512]{1,0:T(8,128)(2,1)S(1)} %collective-permute-done.1.rest_5_), channel_id=1, source_target_pairs={{0,8},{4,12},{8,24},{12,28},{24,16},{28,20},{16,0},{20,4},{1,9},{5... | collective-permute-start | bytes 786440 | tf_op jit(solution)/shard_map/ppermute | solution.py:316
  23.0 1.4 %copy-start = (bf16[1,3,512,512]{3,2,1,0:T(8,128)(2,1)S(1)}, bf16[1,3,512,512]{3,2,1,0:T(8,128)(2,1)}, u32[]{:S(2)}) copy-start(bf16[1,3,512,512]{3,2,1,0:T(8,128)(2,1)} %w.5) | copy-start | bytes 4718596
  24.4 1.0 %copy-start.3 = (bf16[512,512]{1,0:T(8,128)(2,1)S(1)}, bf16[512,512]{1,0:T(8,128)(2,1)}, u32[]{:S(2)}) copy-start(bf16[512,512]{1,0:T(8,128)(2,1)} %k.3) | copy-start | bytes 1572868
  25.4 2.8 %copy-start.2 = (bf16[512,512]{1,0:T(8,128)(2,1)S(1)}, bf16[512,512]{1,0:T(8,128)(2,1)}, u32[]{:S(2)}) copy-start(bf16[512,512]{1,0:T(8,128)(2,1)} %v.1) | copy-start | bytes 1572868
  25.4 2.8 %copy-start.6 = (bf16[256,512]{1,0:T(8,128)(2,1)S(1)}, bf16[256,512]{1,0:T(8,128)(2,1)}, u32[]{:S(2)}) copy-start(bf16[256,512]{1,0:T(8,128)(2,1)} %rest_4_) | copy-start | bytes 786436
  28.2 7.2 %copy-start.1 = (bf16[1,3,512,512]{3,2,1,0:T(8,128)(2,1)S(1)}, bf16[1,3,512,512]{3,2,1,0:T(8,128)(2,1)}, u32[]{:S(2)}) copy-start(bf16[1,3,512,512]{3,2,1,0:T(8,128)(2,1)} %w.5) | copy-start | bytes 4718596
  28.9 27.8 %copy-start.7 = (f32[1,3,64,512]{3,2,1,0:T(8,128)S(1)}, f32[1,3,64,512]{3,2,1,0:T(8,128)}, u32[]{:S(2)}) copy-start(f32[1,3,64,512]{3,2,1,0:T(8,128)} %momentum.1) | copy-start | bytes 1179652
  38.2 40.0 %copy-start.4 = (bf16[512,512]{1,0:T(8,128)(2,1)S(1)}, bf16[512,512]{1,0:T(8,128)(2,1)}, u32[]{:S(2)}) copy-start(bf16[512,512]{1,0:T(8,128)(2,1)} %k.3) | copy-start | bytes 1572868
  38.3 40.0 %copy-start.5 = (bf16[512,512]{1,0:T(8,128)(2,1)S(1)}, bf16[512,512]{1,0:T(8,128)(2,1)}, u32[]{:S(2)}) copy-start(bf16[512,512]{1,0:T(8,128)(2,1)} %q.3) | copy-start | bytes 1572868
  38.3 16.4 %collective-permute-start.6 = (bf16[768,512]{1,0:T(8,128)(2,1)S(1)}, bf16[768,512]{1,0:T(8,128)(2,1)S(1)}, u32[]{:S(2)}, u32[]{:S(2)}) collective-permute-start(bf16[768,512]{1,0:T(8,128)(2,1)S(1)} %crossing.1), channel_id=1, source_target_pairs={{0,4},{4,0},{8,12},{12,8},{16,20},{20,16},{24,28},{28,24},{1,5},{5... | collective-permute-start | bytes 2359304 | tf_op jit(solution)/shard_map/ppermute | solution.py:41
  38.3 10.5 %collective-permute-start.9 = (bf16[3,64,512]{2,1,0:T(8,128)(2,1)S(1)}, bf16[3,64,512]{2,1,0:T(8,128)(2,1)S(1)}, u32[]{:S(2)}, u32[]{:S(2)}) collective-permute-start(bf16[3,64,512]{2,1,0:T(8,128)(2,1)S(1)} %get-tuple-element.29), channel_id=1, source_target_pairs={{0,24},{4,28},{8,16},{12,20},{16,8},{20,12},{24,0},{28,4},{1,25},{... | collective-permute-start | bytes 589832 | tf_op jit(solution)/shard_map/ppermute | solution.py:41
  42.9 11.8 %collective-permute-start.7 = (bf16[3,64,512]{2,1,0:T(8,128)(2,1)S(1)}, bf16[3,64,512]{2,1,0:T(8,128)(2,1)S(1)}, u32[]{:S(2)}, u32[]{:S(2)}) collective-permute-start(bf16[3,64,512]{2,1,0:T(8,128)(2,1)S(1)} %get-tuple-element.25), channel_id=1, source_target_pairs={{0,8},{4,12},{8,0},{12,4},{16,24},{20,28},{24,16},{28,20},{1,9},{5... | collective-permute-start | bytes 589832 | tf_op jit(solution)/shard_map/ppermute | solution.py:41
  42.9 13.7 %collective-permute-start.8 = (bf16[3,64,512]{2,1,0:T(8,128)(2,1)S(1)}, bf16[3,64,512]{2,1,0:T(8,128)(2,1)S(1)}, u32[]{:S(2)}, u32[]{:S(2)}) collective-permute-start(bf16[3,64,512]{2,1,0:T(8,128)(2,1)S(1)} %get-tuple-element.28), channel_id=1, source_target_pairs={{0,16},{4,20},{8,24},{12,28},{16,0},{20,4},{24,8},{28,12},{1,17},{... | collective-permute-start | bytes 589832 | tf_op jit(solution)/shard_map/ppermute | solution.py:41
  58.1 7.2 %collective-permute-start.10 = (bf16[3,64,512]{2,1,0:T(8,128)(2,1)S(1)}, bf16[3,64,512]{2,1,0:T(8,128)(2,1)S(1)}, u32[]{:S(2)}, u32[]{:S(2)}) collective-permute-start(bf16[3,64,512]{2,1,0:T(8,128)(2,1)S(1)} %get-tuple-element.31.rest_0_), channel_id=1, source_target_pairs={{0,8},{4,12},{8,0},{12,4},{16,24},{20,28},{24,16},{28,20},{1,9},{5... | collective-permute-start | bytes 589832 | tf_op jit(solution)/shard_map/ppermute | solution.py:41
  58.6 6.7 %collective-permute-start.11 = (bf16[3,64,512]{2,1,0:T(8,128)(2,1)S(1)}, bf16[3,64,512]{2,1,0:T(8,128)(2,1)S(1)}, u32[]{:S(2)}, u32[]{:S(2)}) collective-permute-start(bf16[3,64,512]{2,1,0:T(8,128)(2,1)S(1)} %get-tuple-element.31.rest_0_), channel_id=1, source_target_pairs={{0,4},{4,0},{8,12},{12,8},{16,20},{20,16},{24,28},{28,24},{1,5},{5... | collective-permute-start | bytes 589832 | tf_op jit(solution)/shard_map/ppermute | solution.py:41
  59.8 15.8 %collective-permute-start.12 = (bf16[3,64,512]{2,1,0:T(8,128)(2,1)S(1)}, bf16[3,64,512]{2,1,0:T(8,128)(2,1)S(1)}, u32[]{:S(2)}, u32[]{:S(2)}) collective-permute-start(bf16[3,64,512]{2,1,0:T(8,128)(2,1)S(1)} %get-tuple-element.31.rest_0_), channel_id=1, source_target_pairs={{0,16},{4,20},{8,24},{12,28},{16,0},{20,4},{24,8},{28,12},{1,17},{... | collective-permute-start | bytes 589832 | tf_op jit(solution)/shard_map/ppermute | solution.py:41
  62.3 13.9 %collective-permute-start.13 = (bf16[3,64,512]{2,1,0:T(8,128)(2,1)S(1)}, bf16[3,64,512]{2,1,0:T(8,128)(2,1)S(1)}, u32[]{:S(2)}, u32[]{:S(2)}) collective-permute-start(bf16[3,64,512]{2,1,0:T(8,128)(2,1)S(1)} %get-tuple-element.31.rest_0_), channel_id=1, source_target_pairs={{0,24},{4,28},{8,16},{12,20},{16,8},{20,12},{24,0},{28,4},{1,25},{... | collective-permute-start | bytes 589832 | tf_op jit(solution)/shard_map/ppermute | solution.py:41
  65.3 18.1 %collective-permute-start.17 = (bf16[256,512]{1,0:T(8,128)(2,1)S(1)}, bf16[256,512]{1,0:T(8,128)(2,1)S(1)}, u32[]{:S(2)}, u32[]{:S(2)}) collective-permute-start(bf16[256,512]{1,0:T(8,128)(2,1)S(1)} %collective-permute-done.1.rest_5_), channel_id=1, source_target_pairs={{0,4},{4,0},{8,12},{12,8},{16,20},{20,16},{24,28},{28,24},{1,5},{5... | collective-permute-start | bytes 786440 | tf_op jit(solution)/shard_map/ppermute | solution.py:41
  75.6 7.8 %collective-permute-start.18 = (bf16[256,512]{1,0:T(8,128)(2,1)S(1)}, bf16[256,512]{1,0:T(8,128)(2,1)S(1)}, u32[]{:S(2)}, u32[]{:S(2)}) collective-permute-start(bf16[256,512]{1,0:T(8,128)(2,1)S(1)} %collective-permute-done.5.rest_6_), channel_id=1, source_target_pairs={{0,8},{4,12},{8,24},{12,28},{24,16},{28,20},{16,0},{20,4},{1,9},{5... | collective-permute-start | bytes 786440 | tf_op jit(solution)/shard_map/ppermute | solution.py:316
  75.6 5.7 %collective-permute-start.14 = (bf16[3,64,512]{2,1,0:T(8,128)(2,1)S(1)}, bf16[3,64,512]{2,1,0:T(8,128)(2,1)S(1)}, u32[]{:S(2)}, u32[]{:S(2)}) collective-permute-start(bf16[3,64,512]{2,1,0:T(8,128)(2,1)S(1)} %collective-permute-done.10.rest_1_), channel_id=1, source_target_pairs={{0,4},{4,0},{8,12},{12,8},{16,20},{20,16},{24,28},{28,24},{1,5},{5... | collective-permute-start | bytes 589832 | tf_op jit(solution)/shard_map/ppermute | solution.py:41
  76.2 7.2 %collective-permute-start.16 = (bf16[3,64,512]{2,1,0:T(8,128)(2,1)S(1)}, bf16[3,64,512]{2,1,0:T(8,128)(2,1)S(1)}, u32[]{:S(2)}, u32[]{:S(2)}) collective-permute-start(bf16[3,64,512]{2,1,0:T(8,128)(2,1)S(1)} %collective-permute-done.13.rest_3_), channel_id=1, source_target_pairs={{0,4},{4,0},{8,12},{12,8},{16,20},{20,16},{24,28},{28,24},{1,5},{5... | collective-permute-start | bytes 589832 | tf_op jit(solution)/shard_map/ppermute | solution.py:41
  77.6 7.9 %collective-permute-start.15 = (bf16[3,64,512]{2,1,0:T(8,128)(2,1)S(1)}, bf16[3,64,512]{2,1,0:T(8,128)(2,1)S(1)}, u32[]{:S(2)}, u32[]{:S(2)}) collective-permute-start(bf16[3,64,512]{2,1,0:T(8,128)(2,1)S(1)} %collective-permute-done.12.rest_2_), channel_id=1, source_target_pairs={{0,4},{4,0},{8,12},{12,8},{16,20},{20,16},{24,28},{28,24},{1,5},{5... | collective-permute-start | bytes 589832 | tf_op jit(solution)/shard_map/ppermute | solution.py:41
  87.2 11.2 %collective-permute-start.19 = (bf16[512,512]{1,0:T(8,128)(2,1)S(1)}, bf16[512,512]{1,0:T(8,128)(2,1)S(1)}, u32[]{:S(2)}, u32[]{:S(2)}) collective-permute-start(bf16[512,512]{1,0:T(8,128)(2,1)S(1)} %apply_fast.1.rest_0_), channel_id=1, source_target_pairs={{0,2},{1,3},{2,0},{3,1},{4,6},{5,7},{6,4},{7,5},{8,10},{9,11},{10,... | collective-permute-start | bytes 1572872 | tf_op jit(solution)/shard_map/ppermute | solution.py:41
  89.2 6.4 %collective-permute-start.20 = (bf16[256,512]{1,0:T(8,128)(2,1)S(1)}, bf16[256,512]{1,0:T(8,128)(2,1)S(1)}, u32[]{:S(2)}, u32[]{:S(2)}) collective-permute-start(bf16[256,512]{1,0:T(8,128)(2,1)S(1)} %collective-permute-done.5.rest_6_), channel_id=1, source_target_pairs={{0,4},{4,0},{8,12},{12,8},{16,20},{20,16},{24,28},{28,24},{1,5},{5... | collective-permute-start | bytes 786440 | tf_op jit(solution)/shard_map/ppermute | solution.py:41
  89.4 9.0 %collective-permute-start.21 = (bf16[256,512]{1,0:T(8,128)(2,1)S(1)}, bf16[256,512]{1,0:T(8,128)(2,1)S(1)}, u32[]{:S(2)}, u32[]{:S(2)}) collective-permute-start(bf16[256,512]{1,0:T(8,128)(2,1)S(1)} %collective-permute-done.18.rest_7_), channel_id=1, source_target_pairs={{0,4},{4,0},{8,12},{12,8},{16,20},{20,16},{24,28},{28,24},{1,5},{5... | collective-permute-start | bytes 786440 | tf_op jit(solution)/shard_map/ppermute | solution.py:41
  91.3 7.2 %collective-permute-start.22 = (bf16[512,512]{1,0:T(8,128)(2,1)S(1)}, bf16[512,512]{1,0:T(8,128)(2,1)S(1)}, u32[]{:S(2)}, u32[]{:S(2)}) collective-permute-start(bf16[512,512]{1,0:T(8,128)(2,1)S(1)} %apply_fast.1.rest_0_), channel_id=1, source_target_pairs={{0,1},{1,0},{2,3},{3,2},{4,5},{5,4},{6,7},{7,6},{8,9},{9,8},{10,11... | collective-permute-start | bytes 1572872 | tf_op jit(solution)/shard_map/ppermute | solution.py:41
  98.4 1.9 %collective-permute-start.23 = (bf16[512,512]{1,0:T(8,128)(2,1)S(1)}, bf16[512,512]{1,0:T(8,128)(2,1)S(1)}, u32[]{:S(2)}, u32[]{:S(2)}) collective-permute-start(bf16[512,512]{1,0:T(8,128)(2,1)S(1)} %collective-permute-done.19.rest_1_), channel_id=1, source_target_pairs={{0,1},{1,0},{2,3},{3,2},{4,5},{5,4},{6,7},{7,6},{8,9},{9,8},{10,11... | collective-permute-start | bytes 1572872 | tf_op jit(solution)/shard_map/ppermute | solution.py:41

commit v2 on v1

--- a/solution.py
+++ b/solution.py
@@ -373,15 +373,15 @@
 
     up_values = lax.ppermute(values, "seq", [(s, s + 2) for s in range(1, ranks - 2, 2)])
 
-    wide = [after(out_proj, errors)]
-    wide.append(ring_step(wide[-1], outer))
+    wide = [out_proj]
+    for _ in range(2):
+        wide.append(ring_step(wide[-1], outer))
     up_keys = after(pair_keys, wide[-1])
     up_keys = lax.ppermute(up_keys, "seq", [(s, s + 2) for s in range(0, ranks - 2, 2)])
-    wide.append(ring_step(wide[-1], outer))
 
     acc = own_gradients(place, keys, errors, fast, outer)
     across = crossing(place, values, up_values, wide[0])
-    pair_errors = after(pair_errors, up_keys, wide[-1], across)
+    pair_errors = after(pair_errors, up_keys, across)
     summed = both_gradients(place, pair_keys, pair_errors, fast, acc, outer)
     pieces = [swap(summed[step], "seq", step * 2) for step in range(1, outer)]
     crossed = swap(after(across, summed[1]), "seq", 1)
@@ -393,11 +393,13 @@
         near.append(swap(renewed, "seq", step * 2))
     far = [swap(renewed, "seq", 1)]
     near[1] = after(near[1], far[0])
-    far += [swap(unit, "seq", 1) for unit in near[1:]]
+    far.append(swap(near[1], "seq", 1))
+    near[2] = after(near[2], far[1])
+    far += [swap(unit, "seq", 1) for unit in near[2:]]
     attended = window_attention(
         place, queries, keys, values, pair_keys, up_keys, after(crossed, near[1])
     )
-    far[1] = after(far[1], attended)
+    far[2] = after(far[2], attended)
     wide_far = [crossed, swap(after(wide[1], near[1]), "seq", 1)]
     wide.append(ring_step(after(wide[2], near[1], near[2]), outer))
     far[-1] = after(far[-1], wide_far[1], wide[3])

time: 104 us -> 108 us (1.038)
  waiting for transfers between devices: 47.2 us -> 51.3 us
    ppermute x19, waiting for transfers between devices: 38.5 us -> 42.9 us  [swap(): return lax.ppermute(array, axis, [(i, i ^ mask) for i in range(devices)])]
    ppermute x3, waiting for transfers between devices: 8.74 us -> 6.19 us  [ring_step(): return lax.ppermute(unit, 'seq', pairs)]
    ppermute x1, waiting for transfers between devices: 0.01 us -> 2.19 us  [shards(): lax.ppermute(up_keys, 'seq', [(s, s + 2) for s in range(0, ranks - 2, 2)])]
  transfers between devices with their start and end apart: 24 -> 24, of which waited for: 14 -> 16; matrix products, arithmetic and copies ran while one was open for 2% -> 2% of each run, Pallas kernels for 5% -> 5%
where the time goes in v2:
time: 108 us
  waiting for transfers between devices  51.3 us (48%)
  starting transfers between devices  36.1 us (33%)
  Pallas kernels  14.3 us (13%)
  local copies, waits for them, and re-layouts  3.18 us (3%)
  other arithmetic  1.89 us (2%)
    ppermute x19, waiting for transfers between devices, swap(): return lax.ppermute(array, axis, [(i, i ^ mask) for i in range(devices)])  42.9 us
    ppermute x19, starting transfers between devices, swap(): return lax.ppermute(array, axis, [(i, i ^ mask) for i in range(devices)])  28.1 us
    ppermute x3, waiting for transfers between devices, ring_step(): return lax.ppermute(unit, 'seq', pairs)  6.19 us
    ppermute x3, starting transfers between devices, ring_step(): return lax.ppermute(unit, 'seq', pairs)  4.02 us
    ppermute x1, starting transfers between devices, shards(): lax.ppermute(up_keys, 'seq', [(s, s + 2) for s in range(0, ranks - 2, 2)])  3.33 us
    pallas_call x1, Pallas kernels, both_gradients(): pl.pallas_call(functools.partial(both_kernel, outer), out_shape=[jax.Shap...  2.82 us
    pallas_call x1, Pallas kernels, own_gradients(): pl.pallas_call(functools.partial(own_kernel, outer), out_shape=jax.ShapeD...  2.77 us
    pallas_call x1, Pallas kernels, project(): pl.pallas_call(functools.partial(project_kernel, tags, rows_in), out_shap...  2.72 us
  transfers between devices with their start and end apart: 24, of which 16 were waited for; matrix products, arithmetic and copies ran while one was open for 2% of the time, Pallas kernels for 5%

profile of v2, /device:TPU:0, one launch (start us, length us, event | category | flops | bytes accessed | tf_op | source)
XLA Modules:
  0.0 107.5 jit_solution(11013354037732111494)
XLA Ops:
  0.6 3.1 %collective-permute-start.1 = (bf16[256,512]{1,0:T(8,128)(2,1)}, bf16[256,512]{1,0:T(8,128)(2,1)S(1)}, u32[]{:S(2)}, u32[]{:S(2)}) collective-permute-start(bf16[256,512]{1,0:T(8,128)(2,1)} %rest_4_.1), channel_id=1, source_target_pairs={{0,8},{4,12},{8,24},{12,28},{24,16},{28,20},{16,0},{20,4},{1,9},{5... | collective-permute-start | bytes 786440 | tf_op jit(solution)/shard_map/ppermute | solution.py:316
  3.7 1.5 %collective-permute-start = (bf16[512,512]{1,0:T(8,128)(2,1)}, bf16[512,512]{1,0:T(8,128)(2,1)S(1)}, u32[]{:S(2)}, u32[]{:S(2)}) collective-permute-start(bf16[512,512]{1,0:T(8,128)(2,1)} %k.3), channel_id=1, source_target_pairs={{0,4},{4,0},{8,12},{12,8},{16,20},{20,16},{24,28},{28,24},{1,5},{5... | collective-permute-start | bytes 1572872 | tf_op jit(solution)/shard_map/ppermute | solution.py:41
  5.9 5.3 %collective-permute-done.1.rest_5_ = bf16[256,512]{1,0:T(8,128)(2,1)S(1)} collective-permute-done((bf16[256,512]{1,0:T(8,128)(2,1)}, bf16[256,512]{1,0:T(8,128)(2,1)S(1)}, u32[]{:S(2)}, u32[]{:S(2)}) %collective-permute-start.1) | collective-permute-done | bytes 262176 | tf_op jit(solution)/shard_map/ppermute | solution.py:316
  14.1 2.8 %collective-permute-start.5 = (bf16[512,512]{1,0:T(8,128)(2,1)S(1)}, bf16[512,512]{1,0:T(8,128)(2,1)S(1)}, u32[]{:S(2)}, u32[]{:S(2)}) collective-permute-start(bf16[512,512]{1,0:T(8,128)(2,1)S(1)} %multiply_convert_fusion.e), channel_id=1, source_target_pairs={{0,4},{4,0},{8,12},{12,8},{16,20},{20,16},{24,28},{28,24},{1,5},{5... | collective-permute-start | bytes 1572872 | tf_op jit(solution)/shard_map/ppermute | solution.py:41
  16.8 1.9 %collective-permute-done.k.pair_k = bf16[512,512]{1,0:T(8,128)(2,1)S(1)} collective-permute-done((bf16[512,512]{1,0:T(8,128)(2,1)}, bf16[512,512]{1,0:T(8,128)(2,1)S(1)}, u32[]{:S(2)}, u32[]{:S(2)}) %collective-permute-start) | collective-permute-done | bytes 524320 | tf_op jit(solution)/shard_map/ppermute | solution.py:41
  19.6 3.3 %collective-permute-start.3 = (bf16[512,512]{1,0:T(8,128)(2,1)S(1)}, bf16[512,512]{1,0:T(8,128)(2,1)S(1)}, u32[]{:S(2)}, u32[]{:S(2)}) collective-permute-start(bf16[512,512]{1,0:T(8,128)(2,1)S(1)} %collective-permute-done.k.pair_k), channel_id=1, source_target_pairs={{0,8},{8,16},{16,24},{1,9},{9,17},{17,25},{2,10},{10,18},{18,26},{... | collective-permute-start | bytes 1572872 | tf_op jit(solution)/shard_map/ppermute | solution.py:380
  23.7 1.4 %copy-done = bf16[1,3,512,512]{3,2,1,0:T(8,128)(2,1)S(1)} copy-done((bf16[1,3,512,512]{3,2,1,0:T(8,128)(2,1)S(1)}, bf16[1,3,512,512]{3,2,1,0:T(8,128)(2,1)}, u32[]{:S(2)}) %copy-start) | copy-done | bytes 1572888
  26.1 2.8 %own_gradients.1.acc = f32[4,3,64,512]{3,2,1,0:T(8,128)S(1)} custom-call(s32[12]{0:T(128)S(1)} %dynamic-slice_bitcast_fusion.place, bf16[512,512]{1,0:T(8,128)(2,1)S(1)} %copy-done.3, bf16[512,512]{1,0:T(8,128)(2,1)S(1)} %multiply_convert_fusion.e, bf16[1,3,512,512]{3,2,1,0:T(8,128)(2,1)S(1)} %copy-done), custom_call_target="tpu_custom_call" | custom-call | flops 1 | bytes 1 | tf_op jit(solution)/shard_map/own_gradients/pallas_call | solution.py:122
  29.6 2.2 %collective-permute-done.3.up_k = bf16[512,512]{1,0:T(8,128)(2,1)S(1)} collective-permute-done((bf16[512,512]{1,0:T(8,128)(2,1)S(1)}, bf16[512,512]{1,0:T(8,128)(2,1)S(1)}, u32[]{:S(2)}, u32[]{:S(2)}) %collective-permute-start.3) | collective-permute-done | bytes 524320 | tf_op jit(solution)/shard_map/ppermute | solution.py:380
  31.8 2.8 %both_gradients.1 = (f32[3,64,512]{2,1,0:T(8,128)S(1)}, bf16[3,64,512]{2,1,0:T(8,128)(2,1)S(1)}, bf16[3,64,512]{2,1,0:T(8,128)(2,1)S(1)}, bf16[3,64,512]{2,1,0:T(8,128)(2,1)S(1)}) custom-call(s32[12]{0:T(128)S(1)} %dynamic-slice_bitcast_fusion.place, bf16[512,512]{1,0:T(8,128)(2,1)S(1)} %collective-permute-done.k.pair_k, ...), custom_call_target="tpu_custom_call" | custom-call | flops 1 | bytes 1 | tf_op jit(solution)/shard_map/both_gradients/pallas_call | solution.py:137
  34.6 4.2 %collective-permute-start.6 = (bf16[768,512]{1,0:T(8,128)(2,1)S(1)}, bf16[768,512]{1,0:T(8,128)(2,1)S(1)}, u32[]{:S(2)}, u32[]{:S(2)}) collective-permute-start(bf16[768,512]{1,0:T(8,128)(2,1)S(1)} %crossing.1), channel_id=1, source_target_pairs={{0,4},{4,0},{8,12},{12,8},{16,20},{20,16},{24,28},{28,24},{1,5},{5... | collective-permute-start | bytes 2359304 | tf_op jit(solution)/shard_map/ppermute | solution.py:41
  38.8 5.4 %collective-permute-start.9 = (bf16[3,64,512]{2,1,0:T(8,128)(2,1)S(1)}, bf16[3,64,512]{2,1,0:T(8,128)(2,1)S(1)}, u32[]{:S(2)}, u32[]{:S(2)}) collective-permute-start(bf16[3,64,512]{2,1,0:T(8,128)(2,1)S(1)} %get-tuple-element.28), channel_id=1, source_target_pairs={{0,24},{4,28},{8,16},{12,20},{16,8},{20,12},{24,0},{28,4},{1,25},{... | collective-permute-start | bytes 589832 | tf_op jit(solution)/shard_map/ppermute | solution.py:41
  44.8 5.3 %collective-permute-done.9.rest_2_ = bf16[3,64,512]{2,1,0:T(8,128)(2,1)S(1)} collective-permute-done((bf16[3,64,512]{2,1,0:T(8,128)(2,1)S(1)}, bf16[3,64,512]{2,1,0:T(8,128)(2,1)S(1)}, u32[]{:S(2)}, u32[]{:S(2)}) %collective-permute-start.9) | collective-permute-done | bytes 196640 | tf_op jit(solution)/shard_map/ppermute | solution.py:41
  50.1 5.4 %collective-permute-done.6.early_v.rest_8_ = bf16[768,512]{1,0:T(8,128)(2,1)S(1)} collective-permute-done((bf16[768,512]{1,0:T(8,128)(2,1)S(1)}, bf16[768,512]{1,0:T(8,128)(2,1)S(1)}, u32[]{:S(2)}, u32[]{:S(2)}) %collective-permute-start.6) | collective-permute-done | bytes 786464 | tf_op jit(solution)/shard_map/ppermute | solution.py:41
  55.5 3.5 %collective-permute-done.8.rest_1_ = bf16[3,64,512]{2,1,0:T(8,128)(2,1)S(1)} collective-permute-done((bf16[3,64,512]{2,1,0:T(8,128)(2,1)S(1)}, bf16[3,64,512]{2,1,0:T(8,128)(2,1)S(1)}, u32[]{:S(2)}, u32[]{:S(2)}) %collective-permute-start.8) | collective-permute-done | bytes 196640 | tf_op jit(solution)/shard_map/ppermute | solution.py:41
  59.0 1.4 %renew.1 = (f32[1,3,64,512]{3,2,1,0:T(8,128)}, bf16[3,64,512]{2,1,0:T(8,128)(2,1)S(1)}) custom-call(s32[12]{0:T(128)S(1)} %dynamic-slice_bitcast_fusion.place, bf16[1,3,512,512]{3,2,1,0:T(8,128)(2,1)S(1)} %copy-done.1, f32[1,3,64,512]{3,2,1,0:T(8,128)S(1)} %copy-done.7, f32[3,64,512]{2,1,0:T(8,128)S(1)} %get-tuple-element.26.mine, ...), custom_call_target="tpu_custom_call" | custom-call | flops 1 | bytes 1 | tf_op jit(solution)/shard_map/renew/pallas_call | solution.py:232
  61.3 3.4 %collective-permute-start.12 = (bf16[3,64,512]{2,1,0:T(8,128)(2,1)S(1)}, bf16[3,64,512]{2,1,0:T(8,128)(2,1)S(1)}, u32[]{:S(2)}, u32[]{:S(2)}) collective-permute-start(bf16[3,64,512]{2,1,0:T(8,128)(2,1)S(1)} %get-tuple-element.30.rest_0_), channel_id=1, source_target_pairs={{0,16},{4,20},{8,24},{12,28},{16,0},{20,4},{24,8},{28,12},{1,17},{... | collective-permute-start | bytes 589832 | tf_op jit(solution)/shard_map/ppermute | solution.py:41
  64.7 3.6 %collective-permute-done.10.rest_1_ = bf16[3,64,512]{2,1,0:T(8,128)(2,1)S(1)} collective-permute-done((bf16[3,64,512]{2,1,0:T(8,128)(2,1)S(1)}, bf16[3,64,512]{2,1,0:T(8,128)(2,1)S(1)}, u32[]{:S(2)}, u32[]{:S(2)}) %collective-permute-start.10) | collective-permute-done | bytes 196640 | tf_op jit(solution)/shard_map/ppermute | solution.py:41
  69.0 2.8 %collective-permute-start.14 = (bf16[3,64,512]{2,1,0:T(8,128)(2,1)S(1)}, bf16[3,64,512]{2,1,0:T(8,128)(2,1)S(1)}, u32[]{:S(2)}, u32[]{:S(2)}) collective-permute-start(bf16[3,64,512]{2,1,0:T(8,128)(2,1)S(1)} %get-tuple-element.30.rest_0_), channel_id=1, source_target_pairs={{0,24},{4,28},{8,16},{12,20},{16,8},{20,12},{24,0},{28,4},{1,25},{... | collective-permute-start | bytes 589832 | tf_op jit(solution)/shard_map/ppermute | solution.py:41
  72.0 3.6 %collective-permute-done.12.rest_2_ = bf16[3,64,512]{2,1,0:T(8,128)(2,1)S(1)} collective-permute-done((bf16[3,64,512]{2,1,0:T(8,128)(2,1)S(1)}, bf16[3,64,512]{2,1,0:T(8,128)(2,1)S(1)}, u32[]{:S(2)}, u32[]{:S(2)}) %collective-permute-start.12) | collective-permute-done | bytes 196640 | tf_op jit(solution)/shard_map/ppermute | solution.py:41
  76.7 1.8 %collective-permute-done.14.rest_3_ = bf16[3,64,512]{2,1,0:T(8,128)(2,1)S(1)} collective-permute-done((bf16[3,64,512]{2,1,0:T(8,128)(2,1)S(1)}, bf16[3,64,512]{2,1,0:T(8,128)(2,1)S(1)}, u32[]{:S(2)}, u32[]{:S(2)}) %collective-permute-start.14) | collective-permute-done | bytes 196640 | tf_op jit(solution)/shard_map/ppermute | solution.py:41
  78.5 1.4 %collective-permute-start.16 = (bf16[3,64,512]{2,1,0:T(8,128)(2,1)S(1)}, bf16[3,64,512]{2,1,0:T(8,128)(2,1)S(1)}, u32[]{:S(2)}, u32[]{:S(2)}) collective-permute-start(bf16[3,64,512]{2,1,0:T(8,128)(2,1)S(1)} %collective-permute-done.14.rest_3_), channel_id=1, source_target_pairs={{0,4},{4,0},{8,12},{12,8},{16,20},{20,16},{24,28},{28,24},{1,5},{5... | collective-permute-start | bytes 589832 | tf_op jit(solution)/shard_map/ppermute | solution.py:41
  79.9 2.3 %window_attention.1.attended = f32[512,512]{1,0:T(8,128)S(1)} custom-call(s32[12]{0:T(128)S(1)} %dynamic-slice_bitcast_fusion.place, bf16[512,512]{1,0:T(8,128)(2,1)S(1)} %copy-done.5, bf16[512,512]{1,0:T(8,128)(2,1)S(1)} %copy-done.4, bf16[512,512]{1,0:T(8,128)(2,1)S(1)} %copy-done.2, bf16[512,512]{1,0:T(8,128)(2,1)S(1)} %collective-permute-done.k.pair_k, ...), custom_call_target="tpu_custom_call" | custom-call | flops 1 | bytes 1 | tf_op jit(solution)/shard_map/window_attention/pallas_call | solution.py:179
  82.2 3.7 %collective-permute-done.15.rest_6_ = bf16[3,64,512]{2,1,0:T(8,128)(2,1)S(1)} collective-permute-done((bf16[3,64,512]{2,1,0:T(8,128)(2,1)S(1)}, bf16[3,64,512]{2,1,0:T(8,128)(2,1)S(1)}, u32[]{:S(2)}, u32[]{:S(2)}) %collective-permute-start.15) | collective-permute-done | bytes 196640 | tf_op jit(solution)/shard_map/ppermute | solution.py:41
  85.9 2.1 %collective-permute-done.16.rest_7_ = bf16[3,64,512]{2,1,0:T(8,128)(2,1)S(1)} collective-permute-done((bf16[3,64,512]{2,1,0:T(8,128)(2,1)S(1)}, bf16[3,64,512]{2,1,0:T(8,128)(2,1)S(1)}, u32[]{:S(2)}, u32[]{:S(2)}) %collective-permute-start.16) | collective-permute-done | bytes 196640 | tf_op jit(solution)/shard_map/ppermute | solution.py:41
  88.0 1.7 %apply_fast.1.rest_0_ = bf16[512,512]{1,0:T(8,128)(2,1)S(1)} custom-call(s32[12]{0:T(128)S(1)} %dynamic-slice_bitcast_fusion.place, bf16[512,512]{1,0:T(8,128)(2,1)S(1)} %copy-done.5, f32[512,512]{1,0:T(8,128)S(1)} %window_attention.1.attended, bf16[3,64,512]{2,1,0:T(8,128)(2,1)S(1)} %get-tuple-element.30.rest_0_, ...), custom_call_target="tpu_custom_call" | custom-call | flops 1 | bytes 1 | tf_op jit(solution)/shard_map/apply_fast/pallas_call | solution.py:262
  89.7 1.6 %collective-permute-start.19 = (bf16[512,512]{1,0:T(8,128)(2,1)S(1)}, bf16[512,512]{1,0:T(8,128)(2,1)S(1)}, u32[]{:S(2)}, u32[]{:S(2)}) collective-permute-start(bf16[512,512]{1,0:T(8,128)(2,1)S(1)} %apply_fast.1.rest_0_), channel_id=1, source_target_pairs={{0,2},{1,3},{2,0},{3,1},{4,6},{5,7},{6,4},{7,5},{8,10},{9,11},{10,... | collective-permute-start | bytes 1572872 | tf_op jit(solution)/shard_map/ppermute | solution.py:41
  91.6 1.7 %collective-permute-start.21 = (bf16[256,512]{1,0:T(8,128)(2,1)S(1)}, bf16[256,512]{1,0:T(8,128)(2,1)S(1)}, u32[]{:S(2)}, u32[]{:S(2)}) collective-permute-start(bf16[256,512]{1,0:T(8,128)(2,1)S(1)} %collective-permute-done.18.rest_7_), channel_id=1, source_target_pairs={{0,4},{4,0},{8,12},{12,8},{16,20},{20,16},{24,28},{28,24},{1,5},{5... | collective-permute-start | bytes 786440 | tf_op jit(solution)/shard_map/ppermute | solution.py:41
  93.3 6.7 %collective-permute-done.20.rest_10_ = bf16[256,512]{1,0:T(8,128)(2,1)S(1)} collective-permute-done((bf16[256,512]{1,0:T(8,128)(2,1)S(1)}, bf16[256,512]{1,0:T(8,128)(2,1)S(1)}, u32[]{:S(2)}, u32[]{:S(2)}) %collective-permute-start.20) | collective-permute-done | bytes 262176 | tf_op jit(solution)/shard_map/ppermute | solution.py:41
  100.1 2.8 %collective-permute-done.21.rest_11_ = bf16[256,512]{1,0:T(8,128)(2,1)S(1)} collective-permute-done((bf16[256,512]{1,0:T(8,128)(2,1)S(1)}, bf16[256,512]{1,0:T(8,128)(2,1)S(1)}, u32[]{:S(2)}, u32[]{:S(2)}) %collective-permute-start.21) | collective-permute-done | bytes 262176 | tf_op jit(solution)/shard_map/ppermute | solution.py:41
  102.9 1.9 %collective-permute-done.23.rest_3_ = bf16[512,512]{1,0:T(8,128)(2,1)S(1)} collective-permute-done((bf16[512,512]{1,0:T(8,128)(2,1)S(1)}, bf16[512,512]{1,0:T(8,128)(2,1)S(1)}, u32[]{:S(2)}, u32[]{:S(2)}) %collective-permute-start.23) | collective-permute-done | bytes 524320 | tf_op jit(solution)/shard_map/ppermute | solution.py:41
  104.8 2.7 %project.1 = bf16[512,512]{1,0:T(8,128)(2,1)} custom-call(s32[12]{0:T(128)S(1)} %dynamic-slice_bitcast_fusion.place, bf16[512,512]{1,0:T(8,128)(2,1)S(1)} %apply_fast.1.rest_0_, bf16[512,512]{1,0:T(8,128)(2,1)S(1)} %collective-permute-done.19.rest_1_, bf16[512,512]{1,0:T(8,128)(2,1)S(1)} %collective-permute-done.22.rest_2_, ...), custom_call_target="tpu_custom_call" | custom-call | flops 1 | bytes 1 | tf_op jit(solution)/shard_map/project/pallas_call | solution.py:293
  (42 shorter events, 10.5 us)
Async XLA Ops:
  0.6 10.6 %collective-permute-start.1 = (bf16[256,512]{1,0:T(8,128)(2,1)}, bf16[256,512]{1,0:T(8,128)(2,1)S(1)}, u32[]{:S(2)}, u32[]{:S(2)}) collective-permute-start(bf16[256,512]{1,0:T(8,128)(2,1)} %rest_4_.1), channel_id=1, source_target_pairs={{0,8},{4,12},{8,24},{12,28},{24,16},{28,20},{16,0},{20,4},{1,9},{5... | collective-permute-start | bytes 786440 | tf_op jit(solution)/shard_map/ppermute | solution.py:316
  3.7 15.1 %collective-permute-start = (bf16[512,512]{1,0:T(8,128)(2,1)}, bf16[512,512]{1,0:T(8,128)(2,1)S(1)}, u32[]{:S(2)}, u32[]{:S(2)}) collective-permute-start(bf16[512,512]{1,0:T(8,128)(2,1)} %k.3), channel_id=1, source_target_pairs={{0,4},{4,0},{8,12},{12,8},{16,20},{20,16},{24,28},{28,24},{1,5},{5... | collective-permute-start | bytes 1572872 | tf_op jit(solution)/shard_map/ppermute | solution.py:41
  5.2 23.7 %collective-permute-start.4 = (bf16[512,512]{1,0:T(8,128)(2,1)}, bf16[512,512]{1,0:T(8,128)(2,1)S(1)}, u32[]{:S(2)}, u32[]{:S(2)}) collective-permute-start(bf16[512,512]{1,0:T(8,128)(2,1)} %v.1), channel_id=1, source_target_pairs={{4,12},{12,20},{20,28},{5,13},{13,21},{21,29},{6,14},{14,22},{22,3... | collective-permute-start | bytes 1572872 | tf_op jit(solution)/shard_map/ppermute | solution.py:374
  11.2 8.4 %collective-permute-start.2 = (bf16[256,512]{1,0:T(8,128)(2,1)S(1)}, bf16[256,512]{1,0:T(8,128)(2,1)S(1)}, u32[]{:S(2)}, u32[]{:S(2)}) collective-permute-start(bf16[256,512]{1,0:T(8,128)(2,1)S(1)} %collective-permute-done.1.rest_5_), channel_id=1, source_target_pairs={{0,8},{4,12},{8,24},{12,28},{24,16},{28,20},{16,0},{20,4},{1,9},{5... | collective-permute-start | bytes 786440 | tf_op jit(solution)/shard_map/ppermute | solution.py:316
  14.1 15.5 %collective-permute-start.5 = (bf16[512,512]{1,0:T(8,128)(2,1)S(1)}, bf16[512,512]{1,0:T(8,128)(2,1)S(1)}, u32[]{:S(2)}, u32[]{:S(2)}) collective-permute-start(bf16[512,512]{1,0:T(8,128)(2,1)S(1)} %multiply_convert_fusion.e), channel_id=1, source_target_pairs={{0,4},{4,0},{8,12},{12,8},{16,20},{20,16},{24,28},{28,24},{1,5},{5... | collective-permute-start | bytes 1572872 | tf_op jit(solution)/shard_map/ppermute | solution.py:41
  19.6 12.1 %collective-permute-start.3 = (bf16[512,512]{1,0:T(8,128)(2,1)S(1)}, bf16[512,512]{1,0:T(8,128)(2,1)S(1)}, u32[]{:S(2)}, u32[]{:S(2)}) collective-permute-start(bf16[512,512]{1,0:T(8,128)(2,1)S(1)} %collective-permute-done.k.pair_k), channel_id=1, source_target_pairs={{0,8},{8,16},{16,24},{1,9},{9,17},{17,25},{2,10},{10,18},{18,26},{... | collective-permute-start | bytes 1572872 | tf_op jit(solution)/shard_map/ppermute | solution.py:380
  23.7 1.4 %copy-start = (bf16[1,3,512,512]{3,2,1,0:T(8,128)(2,1)S(1)}, bf16[1,3,512,512]{3,2,1,0:T(8,128)(2,1)}, u32[]{:S(2)}) copy-start(bf16[1,3,512,512]{3,2,1,0:T(8,128)(2,1)} %w.5) | copy-start | bytes 4718596
  25.1 1.0 copy-start.3
  26.1 2.8 %copy-start.2 = (bf16[512,512]{1,0:T(8,128)(2,1)S(1)}, bf16[512,512]{1,0:T(8,128)(2,1)}, u32[]{:S(2)}) copy-start(bf16[512,512]{1,0:T(8,128)(2,1)} %v.1) | copy-start | bytes 1572868
  26.1 2.8 %copy-start.6 = (bf16[256,512]{1,0:T(8,128)(2,1)S(1)}, bf16[256,512]{1,0:T(8,128)(2,1)}, u32[]{:S(2)}) copy-start(bf16[256,512]{1,0:T(8,128)(2,1)} %rest_4_.1) | copy-start | bytes 786436
  28.9 2.9 %copy-start.1 = (bf16[1,3,512,512]{3,2,1,0:T(8,128)(2,1)S(1)}, bf16[1,3,512,512]{3,2,1,0:T(8,128)(2,1)}, u32[]{:S(2)}) copy-start(bf16[1,3,512,512]{3,2,1,0:T(8,128)(2,1)} %w.5) | copy-start | bytes 4718596
  29.6 29.5 %copy-start.7 = (f32[1,3,64,512]{3,2,1,0:T(8,128)S(1)}, f32[1,3,64,512]{3,2,1,0:T(8,128)}, u32[]{:S(2)}) copy-start(f32[1,3,64,512]{3,2,1,0:T(8,128)} %momentum.1) | copy-start | bytes 1179652
  34.6 45.3 %copy-start.4 = (bf16[512,512]{1,0:T(8,128)(2,1)S(1)}, bf16[512,512]{1,0:T(8,128)(2,1)}, u32[]{:S(2)}) copy-start(bf16[512,512]{1,0:T(8,128)(2,1)} %k.3) | copy-start | bytes 1572868
  34.6 45.3 %copy-start.5 = (bf16[512,512]{1,0:T(8,128)(2,1)S(1)}, bf16[512,512]{1,0:T(8,128)(2,1)}, u32[]{:S(2)}) copy-start(bf16[512,512]{1,0:T(8,128)(2,1)} %q.3) | copy-start | bytes 1572868
  34.6 20.9 %collective-permute-start.6 = (bf16[768,512]{1,0:T(8,128)(2,1)S(1)}, bf16[768,512]{1,0:T(8,128)(2,1)S(1)}, u32[]{:S(2)}, u32[]{:S(2)}) collective-permute-start(bf16[768,512]{1,0:T(8,128)(2,1)S(1)} %crossing.1), channel_id=1, source_target_pairs={{0,4},{4,0},{8,12},{12,8},{16,20},{20,16},{24,28},{28,24},{1,5},{5... | collective-permute-start | bytes 2359304 | tf_op jit(solution)/shard_map/ppermute | solution.py:41
  38.8 11.3 %collective-permute-start.9 = (bf16[3,64,512]{2,1,0:T(8,128)(2,1)S(1)}, bf16[3,64,512]{2,1,0:T(8,128)(2,1)S(1)}, u32[]{:S(2)}, u32[]{:S(2)}) collective-permute-start(bf16[3,64,512]{2,1,0:T(8,128)(2,1)S(1)} %get-tuple-element.28), channel_id=1, source_target_pairs={{0,24},{4,28},{8,16},{12,20},{16,8},{20,12},{24,0},{28,4},{1,25},{... | collective-permute-start | bytes 589832 | tf_op jit(solution)/shard_map/ppermute | solution.py:41
  44.3 11.2 %collective-permute-start.7 = (bf16[3,64,512]{2,1,0:T(8,128)(2,1)S(1)}, bf16[3,64,512]{2,1,0:T(8,128)(2,1)S(1)}, u32[]{:S(2)}, u32[]{:S(2)}) collective-permute-start(bf16[3,64,512]{2,1,0:T(8,128)(2,1)S(1)} %get-tuple-element.24), channel_id=1, source_target_pairs={{0,8},{4,12},{8,0},{12,4},{16,24},{20,28},{24,16},{28,20},{1,9},{5... | collective-permute-start | bytes 589832 | tf_op jit(solution)/shard_map/ppermute | solution.py:41
  44.3 14.7 %collective-permute-start.8 = (bf16[3,64,512]{2,1,0:T(8,128)(2,1)S(1)}, bf16[3,64,512]{2,1,0:T(8,128)(2,1)S(1)}, u32[]{:S(2)}, u32[]{:S(2)}) collective-permute-start(bf16[3,64,512]{2,1,0:T(8,128)(2,1)S(1)} %get-tuple-element.27), channel_id=1, source_target_pairs={{0,16},{4,20},{8,24},{12,28},{16,0},{20,4},{24,8},{28,12},{1,17},{... | collective-permute-start | bytes 589832 | tf_op jit(solution)/shard_map/ppermute | solution.py:41
  60.4 7.9 %collective-permute-start.10 = (bf16[3,64,512]{2,1,0:T(8,128)(2,1)S(1)}, bf16[3,64,512]{2,1,0:T(8,128)(2,1)S(1)}, u32[]{:S(2)}, u32[]{:S(2)}) collective-permute-start(bf16[3,64,512]{2,1,0:T(8,128)(2,1)S(1)} %get-tuple-element.30.rest_0_), channel_id=1, source_target_pairs={{0,8},{4,12},{8,0},{12,4},{16,24},{20,28},{24,16},{28,20},{1,9},{5... | collective-permute-start | bytes 589832 | tf_op jit(solution)/shard_map/ppermute | solution.py:41
  60.5 7.9 %collective-permute-start.11 = (bf16[3,64,512]{2,1,0:T(8,128)(2,1)S(1)}, bf16[3,64,512]{2,1,0:T(8,128)(2,1)S(1)}, u32[]{:S(2)}, u32[]{:S(2)}) collective-permute-start(bf16[3,64,512]{2,1,0:T(8,128)(2,1)S(1)} %get-tuple-element.30.rest_0_), channel_id=1, source_target_pairs={{0,4},{4,0},{8,12},{12,8},{16,20},{20,16},{24,28},{28,24},{1,5},{5... | collective-permute-start | bytes 589832 | tf_op jit(solution)/shard_map/ppermute | solution.py:41
  61.3 14.3 %collective-permute-start.12 = (bf16[3,64,512]{2,1,0:T(8,128)(2,1)S(1)}, bf16[3,64,512]{2,1,0:T(8,128)(2,1)S(1)}, u32[]{:S(2)}, u32[]{:S(2)}) collective-permute-start(bf16[3,64,512]{2,1,0:T(8,128)(2,1)S(1)} %get-tuple-element.30.rest_0_), channel_id=1, source_target_pairs={{0,16},{4,20},{8,24},{12,28},{16,0},{20,4},{24,8},{28,12},{1,17},{... | collective-permute-start | bytes 589832 | tf_op jit(solution)/shard_map/ppermute | solution.py:41
  68.3 7.7 %collective-permute-start.13 = (bf16[3,64,512]{2,1,0:T(8,128)(2,1)S(1)}, bf16[3,64,512]{2,1,0:T(8,128)(2,1)S(1)}, u32[]{:S(2)}, u32[]{:S(2)}) collective-permute-start(bf16[3,64,512]{2,1,0:T(8,128)(2,1)S(1)} %collective-permute-done.10.rest_1_), channel_id=1, source_target_pairs={{0,4},{4,0},{8,12},{12,8},{16,20},{20,16},{24,28},{28,24},{1,5},{5... | collective-permute-start | bytes 589832 | tf_op jit(solution)/shard_map/ppermute | solution.py:41
  69.0 9.5 %collective-permute-start.14 = (bf16[3,64,512]{2,1,0:T(8,128)(2,1)S(1)}, bf16[3,64,512]{2,1,0:T(8,128)(2,1)S(1)}, u32[]{:S(2)}, u32[]{:S(2)}) collective-permute-start(bf16[3,64,512]{2,1,0:T(8,128)(2,1)S(1)} %get-tuple-element.30.rest_0_), channel_id=1, source_target_pairs={{0,24},{4,28},{8,16},{12,20},{16,8},{20,12},{24,0},{28,4},{1,25},{... | collective-permute-start | bytes 589832 | tf_op jit(solution)/shard_map/ppermute | solution.py:41
  71.8 16.3 %collective-permute-start.17 = (bf16[256,512]{1,0:T(8,128)(2,1)S(1)}, bf16[256,512]{1,0:T(8,128)(2,1)S(1)}, u32[]{:S(2)}, u32[]{:S(2)}) collective-permute-start(bf16[256,512]{1,0:T(8,128)(2,1)S(1)} %collective-permute-done.1.rest_5_), channel_id=1, source_target_pairs={{0,4},{4,0},{8,12},{12,8},{16,20},{20,16},{24,28},{28,24},{1,5},{5... | collective-permute-start | bytes 786440 | tf_op jit(solution)/shard_map/ppermute | solution.py:41
  76.1 12.0 %collective-permute-start.18 = (bf16[256,512]{1,0:T(8,128)(2,1)S(1)}, bf16[256,512]{1,0:T(8,128)(2,1)S(1)}, u32[]{:S(2)}, u32[]{:S(2)}) collective-permute-start(bf16[256,512]{1,0:T(8,128)(2,1)S(1)} %collective-permute-done.2.rest_6_), channel_id=1, source_target_pairs={{0,8},{4,12},{8,24},{12,28},{24,16},{28,20},{16,0},{20,4},{1,9},{5... | collective-permute-start | bytes 786440 | tf_op jit(solution)/shard_map/ppermute | solution.py:316
  76.1 9.8 %collective-permute-start.15 = (bf16[3,64,512]{2,1,0:T(8,128)(2,1)S(1)}, bf16[3,64,512]{2,1,0:T(8,128)(2,1)S(1)}, u32[]{:S(2)}, u32[]{:S(2)}) collective-permute-start(bf16[3,64,512]{2,1,0:T(8,128)(2,1)S(1)} %collective-permute-done.12.rest_2_), channel_id=1, source_target_pairs={{0,4},{4,0},{8,12},{12,8},{16,20},{20,16},{24,28},{28,24},{1,5},{5... | collective-permute-start | bytes 589832 | tf_op jit(solution)/shard_map/ppermute | solution.py:41
  78.5 9.5 %collective-permute-start.16 = (bf16[3,64,512]{2,1,0:T(8,128)(2,1)S(1)}, bf16[3,64,512]{2,1,0:T(8,128)(2,1)S(1)}, u32[]{:S(2)}, u32[]{:S(2)}) collective-permute-start(bf16[3,64,512]{2,1,0:T(8,128)(2,1)S(1)} %collective-permute-done.14.rest_3_), channel_id=1, source_target_pairs={{0,4},{4,0},{8,12},{12,8},{16,20},{20,16},{24,28},{28,24},{1,5},{5... | collective-permute-start | bytes 589832 | tf_op jit(solution)/shard_map/ppermute | solution.py:41
  89.7 13.2 %collective-permute-start.19 = (bf16[512,512]{1,0:T(8,128)(2,1)S(1)}, bf16[512,512]{1,0:T(8,128)(2,1)S(1)}, u32[]{:S(2)}, u32[]{:S(2)}) collective-permute-start(bf16[512,512]{1,0:T(8,128)(2,1)S(1)} %apply_fast.1.rest_0_), channel_id=1, source_target_pairs={{0,2},{1,3},{2,0},{3,1},{4,6},{5,7},{6,4},{7,5},{8,10},{9,11},{10,... | collective-permute-start | bytes 1572872 | tf_op jit(solution)/shard_map/ppermute | solution.py:41
  91.3 8.8 %collective-permute-start.20 = (bf16[256,512]{1,0:T(8,128)(2,1)S(1)}, bf16[256,512]{1,0:T(8,128)(2,1)S(1)}, u32[]{:S(2)}, u32[]{:S(2)}) collective-permute-start(bf16[256,512]{1,0:T(8,128)(2,1)S(1)} %collective-permute-done.2.rest_6_), channel_id=1, source_target_pairs={{0,4},{4,0},{8,12},{12,8},{16,20},{20,16},{24,28},{28,24},{1,5},{5... | collective-permute-start | bytes 786440 | tf_op jit(solution)/shard_map/ppermute | solution.py:41
  91.6 11.3 %collective-permute-start.21 = (bf16[256,512]{1,0:T(8,128)(2,1)S(1)}, bf16[256,512]{1,0:T(8,128)(2,1)S(1)}, u32[]{:S(2)}, u32[]{:S(2)}) collective-permute-start(bf16[256,512]{1,0:T(8,128)(2,1)S(1)} %collective-permute-done.18.rest_7_), channel_id=1, source_target_pairs={{0,4},{4,0},{8,12},{12,8},{16,20},{20,16},{24,28},{28,24},{1,5},{5... | collective-permute-start | bytes 786440 | tf_op jit(solution)/shard_map/ppermute | solution.py:41
  93.3 9.6 %collective-permute-start.22 = (bf16[512,512]{1,0:T(8,128)(2,1)S(1)}, bf16[512,512]{1,0:T(8,128)(2,1)S(1)}, u32[]{:S(2)}, u32[]{:S(2)}) collective-permute-start(bf16[512,512]{1,0:T(8,128)(2,1)S(1)} %apply_fast.1.rest_0_), channel_id=1, source_target_pairs={{0,1},{1,0},{2,3},{3,2},{4,5},{5,4},{6,7},{7,6},{8,9},{9,8},{10,11... | collective-permute-start | bytes 1572872 | tf_op jit(solution)/shard_map/ppermute | solution.py:41
  102.9 1.9 %collective-permute-start.23 = (bf16[512,512]{1,0:T(8,128)(2,1)S(1)}, bf16[512,512]{1,0:T(8,128)(2,1)S(1)}, u32[]{:S(2)}, u32[]{:S(2)}) collective-permute-start(bf16[512,512]{1,0:T(8,128)(2,1)S(1)} %collective-permute-done.19.rest_1_), channel_id=1, source_target_pairs={{0,1},{1,0},{2,3},{3,2},{4,5},{5,4},{6,7},{7,6},{8,9},{9,8},{10,11... | collective-permute-start | bytes 1572872 | tf_op jit(solution)/shard_map/ppermute | solution.py:41

commit v3 on v2

--- a/solution.py
+++ b/solution.py
@@ -187,6 +187,28 @@
     )(place, q, k, v, *early)
 
 
+def pick_kernel(place, even, odd, out):
+    @pl.when(place[0] == 0)
+    def _():
+        out[...] = even[...]
+
+    @pl.when(place[0] == 1)
+    def _():
+        out[...] = odd[...]
+
+
+def pick(place, even, odd):
+    return pl.pallas_call(
+        pick_kernel,
+        out_shape=jax.ShapeDtypeStruct(even.shape, even.dtype),
+        in_specs=[pl.BlockSpec(memory_space=pltpu.SMEM)] + [whole_spec()] * 2,
+        out_specs=whole_spec(),
+        compiler_params=params(12),
+        cost_estimate=BRIEF,
+        name="pick",
+    )(place, even, odd)
+
+
 def crossing_kernel(place, even, odd, rows, out):
     tokens = even.shape[0]
 
@@ -371,17 +393,16 @@
     errors = (-grad_scale * rates * values.astype(jnp.float32)).astype(jnp.bfloat16)
     pair_errors = swap(errors, "seq", 1)
 
-    up_values = lax.ppermute(values, "seq", [(s, s + 2) for s in range(1, ranks - 2, 2)])
-
     wide = [out_proj]
     for _ in range(2):
         wide.append(ring_step(wide[-1], outer))
-    up_keys = after(pair_keys, wide[-1])
-    up_keys = lax.ppermute(up_keys, "seq", [(s, s + 2) for s in range(0, ranks - 2, 2)])
+
+    up = pick(place, after(pair_keys, wide[-1]), values)
+    up = lax.ppermute(up, "seq", [(s, s + 2) for s in range(ranks - 2)])
 
     acc = own_gradients(place, keys, errors, fast, outer)
-    across = crossing(place, values, up_values, wide[0])
-    pair_errors = after(pair_errors, up_keys, across)
+    across = crossing(place, values, up, wide[0])
+    pair_errors = after(pair_errors, up)
     summed = both_gradients(place, pair_keys, pair_errors, fast, acc, outer)
     pieces = [swap(summed[step], "seq", step * 2) for step in range(1, outer)]
     crossed = swap(after(across, summed[1]), "seq", 1)
@@ -397,13 +418,13 @@
     near[2] = after(near[2], far[1])
     far += [swap(unit, "seq", 1) for unit in near[2:]]
     attended = window_attention(
-        place, queries, keys, values, pair_keys, up_keys, after(crossed, near[1])
+        place, queries, keys, values, pair_keys, up, after(crossed, near[1])
     )
     far[2] = after(far[2], attended)
-    wide_far = [crossed, swap(after(wide[1], near[1]), "seq", 1)]
+    wide_far = [crossed] + [swap(after(unit, near[1]), "seq", 1) for unit in wide[1:]]
     wide.append(ring_step(after(wide[2], near[1], near[2]), outer))
-    far[-1] = after(far[-1], wide_far[1], wide[3])
-    wide_far += [swap(after(unit, far[1]), "seq", 1) for unit in wide[2:]]
+    far[-1] = after(far[-1], wide_far[1], wide_far[2], wide[3])
+    wide_far.append(swap(wide[3], "seq", 1))
     combined = apply_fast(place, queries, attended, near + far)
 
     blocks = [(combined, 0)]
@@ -411,7 +432,7 @@
     while mask:
         moved = [(swap(block, "head", mask), tag ^ mask) for block, tag in blocks]
         if mask > 1:
-            moved = [(after(block, *wide_far[2:]), tag) for block, tag in moved]
+            moved = [(after(block, wide_far[3]), tag) for block, tag in moved]
         blocks = blocks + moved
         mask //= 2
     mixed = project(

time: 108 us -> 105 us (0.972)
  starting transfers between devices: 36.1 us -> 33.4 us
  local copies, waits for them, and re-layouts: 3.18 us -> 1.77 us
    ppermute x19, starting transfers between devices: 28.1 us -> 24.4 us  [swap(): return lax.ppermute(array, axis, [(i, i ^ mask) for i in range(devices)])]
    ppermute x19, waiting for transfers between devices: 42.9 us -> 39.3 us  [swap(): return lax.ppermute(array, axis, [(i, i ^ mask) for i in range(devices)])]
    ppermute x2 -> x1, waiting for transfers between devices: 2.19 us -> 5.14 us  [shards(): up = lax.ppermute(up, 'seq', [(s, s + 2) for s in range(ranks - 2)])]
    unnamed x16 -> x14, local copies, waits for them, and re-layouts: 2.48 us -> 1.07 us
    ppermute x3, starting transfers between devices: 4.02 us -> 5.33 us  [ring_step(): return lax.ppermute(unit, 'seq', pairs)]
    ppermute x2 -> x1, starting transfers between devices: 4.01 us -> 3.69 us  [shards(): up = lax.ppermute(up, 'seq', [(s, s + 2) for s in range(ranks - 2)])]
  transfers between devices with their start and end apart: 24 -> 23, of which waited for: 16 -> 16; matrix products, arithmetic and copies ran while one was open for 2% -> 2% of each run, Pallas kernels for 5% -> 5%
where the time goes in v3:
time: 105 us; the launch traced here: 104 us
  waiting for transfers between devices  50.7 us (48%)
  starting transfers between devices  33.4 us (32%)
  Pallas kernels  15.3 us (15%)
  other arithmetic  1.89 us (2%)
  local copies, waits for them, and re-layouts  1.77 us (2%)
    ppermute x19, waiting for transfers between devices, swap(): return lax.ppermute(array, axis, [(i, i ^ mask) for i in range(devices)])  39.3 us
    ppermute x19, starting transfers between devices, swap(): return lax.ppermute(array, axis, [(i, i ^ mask) for i in range(devices)])  24.4 us
    ppermute x3, waiting for transfers between devices, ring_step(): return lax.ppermute(unit, 'seq', pairs)  6.3 us
    ppermute x3, starting transfers between devices, ring_step(): return lax.ppermute(unit, 'seq', pairs)  5.33 us
    ppermute x1, waiting for transfers between devices, shards(): up = lax.ppermute(up, 'seq', [(s, s + 2) for s in range(ranks - 2)])  5.14 us
    ppermute x1, starting transfers between devices, shards(): up = lax.ppermute(up, 'seq', [(s, s + 2) for s in range(ranks - 2)])  3.69 us
    pallas_call x1, Pallas kernels, project(): pl.pallas_call(functools.partial(project_kernel, tags, rows_in), out_shap...  3.14 us
    pallas_call x1, Pallas kernels, both_gradients(): pl.pallas_call(functools.partial(both_kernel, outer), out_shape=[jax.Shap...  2.81 us
  transfers between devices with their start and end apart: 23, of which 16 were waited for; matrix products, arithmetic and copies ran while one was open for 2% of the time, Pallas kernels for 5%

profile of v3, /device:TPU:0, one launch (start us, length us, event | category | flops | bytes accessed | tf_op | source)
XLA Modules:
  0.0 103.9 jit_solution(17284881817843593100)
XLA Ops:
  0.6 3.1 %collective-permute-start.1 = (bf16[256,512]{1,0:T(8,128)(2,1)}, bf16[256,512]{1,0:T(8,128)(2,1)S(1)}, u32[]{:S(2)}, u32[]{:S(2)}) collective-permute-start(bf16[256,512]{1,0:T(8,128)(2,1)} %rest_4_.1), channel_id=1, source_target_pairs={{0,8},{4,12},{8,24},{12,28},{24,16},{28,20},{16,0},{20,4},{1,9},{5... | collective-permute-start | bytes 786440 | tf_op jit(solution)/shard_map/ppermute | solution.py:338
  3.7 1.5 %collective-permute-start = (bf16[512,512]{1,0:T(8,128)(2,1)}, bf16[512,512]{1,0:T(8,128)(2,1)S(1)}, u32[]{:S(2)}, u32[]{:S(2)}) collective-permute-start(bf16[512,512]{1,0:T(8,128)(2,1)} %k.3), channel_id=1, source_target_pairs={{0,4},{4,0},{8,12},{12,8},{16,20},{20,16},{24,28},{28,24},{1,5},{5... | collective-permute-start | bytes 1572872 | tf_op jit(solution)/shard_map/ppermute | solution.py:41
  5.9 5.3 %collective-permute-done.1.rest_5_ = bf16[256,512]{1,0:T(8,128)(2,1)S(1)} collective-permute-done((bf16[256,512]{1,0:T(8,128)(2,1)}, bf16[256,512]{1,0:T(8,128)(2,1)S(1)}, u32[]{:S(2)}, u32[]{:S(2)}) %collective-permute-start.1) | collective-permute-done | bytes 262176 | tf_op jit(solution)/shard_map/ppermute | solution.py:338
  12.2 1.2 %multiply_convert_fusion.e = bf16[512,512]{1,0:T(8,128)(2,1)S(1)} fusion(bf16[512,512]{1,0:T(8,128)(2,1)} %v.1, f32[512]{0:T(512)S(1)} %bitcast.3), kind=kLoop, calls=%fused_computation | loop fusion | flops 786432 | bytes 1050624 | tf_op jit(solution)/shard_map/convert_element_type | solution.py:393
  13.4 1.6 %collective-permute-start.4 = (bf16[512,512]{1,0:T(8,128)(2,1)S(1)}, bf16[512,512]{1,0:T(8,128)(2,1)S(1)}, u32[]{:S(2)}, u32[]{:S(2)}) collective-permute-start(bf16[512,512]{1,0:T(8,128)(2,1)S(1)} %multiply_convert_fusion.e), channel_id=1, source_target_pairs={{0,4},{4,0},{8,12},{12,8},{16,20},{20,16},{24,28},{28,24},{1,5},{5... | collective-permute-start | bytes 1572872 | tf_op jit(solution)/shard_map/ppermute | solution.py:41
  15.7 3.1 %collective-permute-done.even.k.pair_k = bf16[512,512]{1,0:T(8,128)(2,1)S(1)} collective-permute-done((bf16[512,512]{1,0:T(8,128)(2,1)}, bf16[512,512]{1,0:T(8,128)(2,1)S(1)}, u32[]{:S(2)}, u32[]{:S(2)}) %collective-permute-start) | collective-permute-done | bytes 524320 | tf_op jit(solution)/shard_map/ppermute | solution.py:41
  21.4 3.7 %collective-permute-start.3 = (bf16[512,512]{1,0:T(8,128)(2,1)S(1)}, bf16[512,512]{1,0:T(8,128)(2,1)S(1)}, u32[]{:S(2)}, u32[]{:S(2)}) collective-permute-start(bf16[512,512]{1,0:T(8,128)(2,1)S(1)} %pick.1), channel_id=1, source_target_pairs={{0,8},{4,12},{8,16},{12,20},{16,24},{20,28},{1,9},{5,13},{9,17},{1... | collective-permute-start | bytes 1572872 | tf_op jit(solution)/shard_map/ppermute | solution.py:401
  25.1 2.8 %own_gradients.1.acc = f32[4,3,64,512]{3,2,1,0:T(8,128)S(1)} custom-call(s32[12]{0:T(128)S(1)} %dynamic-slice_bitcast_fusion.place, bf16[512,512]{1,0:T(8,128)(2,1)S(1)} %copy-done.3, bf16[512,512]{1,0:T(8,128)(2,1)S(1)} %multiply_convert_fusion.e, bf16[1,3,512,512]{3,2,1,0:T(8,128)(2,1)S(1)} %copy-done), custom_call_target="tpu_custom_call" | custom-call | flops 1 | bytes 1 | tf_op jit(solution)/shard_map/own_gradients/pallas_call | solution.py:122
  28.5 5.1 %collective-permute-done.3.odd.up_k = bf16[512,512]{1,0:T(8,128)(2,1)S(1)} collective-permute-done((bf16[512,512]{1,0:T(8,128)(2,1)S(1)}, bf16[512,512]{1,0:T(8,128)(2,1)S(1)}, u32[]{:S(2)}, u32[]{:S(2)}) %collective-permute-start.3) | collective-permute-done | bytes 524320 | tf_op jit(solution)/shard_map/ppermute | solution.py:401
  34.3 2.8 %both_gradients.1 = (f32[3,64,512]{2,1,0:T(8,128)S(1)}, bf16[3,64,512]{2,1,0:T(8,128)(2,1)S(1)}, bf16[3,64,512]{2,1,0:T(8,128)(2,1)S(1)}, bf16[3,64,512]{2,1,0:T(8,128)(2,1)S(1)}) custom-call(s32[12]{0:T(128)S(1)} %dynamic-slice_bitcast_fusion.place, bf16[512,512]{1,0:T(8,128)(2,1)S(1)} %collective-permute-done.even.k.pair_k, ...), custom_call_target="tpu_custom_call" | custom-call | flops 1 | bytes 1 | tf_op jit(solution)/shard_map/both_gradients/pallas_call | solution.py:137
  37.1 1.6 %collective-permute-start.5 = (bf16[768,512]{1,0:T(8,128)(2,1)S(1)}, bf16[768,512]{1,0:T(8,128)(2,1)S(1)}, u32[]{:S(2)}, u32[]{:S(2)}) collective-permute-start(bf16[768,512]{1,0:T(8,128)(2,1)S(1)} %crossing.1), channel_id=1, source_target_pairs={{0,4},{4,0},{8,12},{12,8},{16,20},{20,16},{24,28},{28,24},{1,5},{5... | collective-permute-start | bytes 2359304 | tf_op jit(solution)/shard_map/ppermute | solution.py:41
  38.7 4.9 %collective-permute-start.8 = (bf16[3,64,512]{2,1,0:T(8,128)(2,1)S(1)}, bf16[3,64,512]{2,1,0:T(8,128)(2,1)S(1)}, u32[]{:S(2)}, u32[]{:S(2)}) collective-permute-start(bf16[3,64,512]{2,1,0:T(8,128)(2,1)S(1)} %get-tuple-element.27), channel_id=1, source_target_pairs={{0,24},{4,28},{8,16},{12,20},{16,8},{20,12},{24,0},{28,4},{1,25},{... | collective-permute-start | bytes 589832 | tf_op jit(solution)/shard_map/ppermute | solution.py:41
  44.2 5.3 %collective-permute-done.8.rest_2_ = bf16[3,64,512]{2,1,0:T(8,128)(2,1)S(1)} collective-permute-done((bf16[3,64,512]{2,1,0:T(8,128)(2,1)S(1)}, bf16[3,64,512]{2,1,0:T(8,128)(2,1)S(1)}, u32[]{:S(2)}, u32[]{:S(2)}) %collective-permute-start.8) | collective-permute-done | bytes 196640 | tf_op jit(solution)/shard_map/ppermute | solution.py:41
  49.6 3.4 %collective-permute-done.5.early_v.rest_8_ = bf16[768,512]{1,0:T(8,128)(2,1)S(1)} collective-permute-done((bf16[768,512]{1,0:T(8,128)(2,1)S(1)}, bf16[768,512]{1,0:T(8,128)(2,1)S(1)}, u32[]{:S(2)}, u32[]{:S(2)}) %collective-permute-start.5) | collective-permute-done | bytes 786464 | tf_op jit(solution)/shard_map/ppermute | solution.py:41
  53.0 3.7 %collective-permute-done.7.rest_1_ = bf16[3,64,512]{2,1,0:T(8,128)(2,1)S(1)} collective-permute-done((bf16[3,64,512]{2,1,0:T(8,128)(2,1)S(1)}, bf16[3,64,512]{2,1,0:T(8,128)(2,1)S(1)}, u32[]{:S(2)}, u32[]{:S(2)}) %collective-permute-start.7) | collective-permute-done | bytes 196640 | tf_op jit(solution)/shard_map/ppermute | solution.py:41
  56.7 1.4 %renew.1 = (f32[1,3,64,512]{3,2,1,0:T(8,128)}, bf16[3,64,512]{2,1,0:T(8,128)(2,1)S(1)}) custom-call(s32[12]{0:T(128)S(1)} %dynamic-slice_bitcast_fusion.place, bf16[1,3,512,512]{3,2,1,0:T(8,128)(2,1)S(1)} %copy-done, f32[1,3,64,512]{3,2,1,0:T(8,128)S(1)} %copy-done.6, f32[3,64,512]{2,1,0:T(8,128)S(1)} %get-tuple-element.25.mine, ...), custom_call_target="tpu_custom_call" | custom-call | flops 1 | bytes 1 | tf_op jit(solution)/shard_map/renew/pallas_call | solution.py:254
  58.8 3.4 %collective-permute-start.11 = (bf16[3,64,512]{2,1,0:T(8,128)(2,1)S(1)}, bf16[3,64,512]{2,1,0:T(8,128)(2,1)S(1)}, u32[]{:S(2)}, u32[]{:S(2)}) collective-permute-start(bf16[3,64,512]{2,1,0:T(8,128)(2,1)S(1)} %get-tuple-element.29.rest_0_), channel_id=1, source_target_pairs={{0,16},{4,20},{8,24},{12,28},{16,0},{20,4},{24,8},{28,12},{1,17},{... | collective-permute-start | bytes 589832 | tf_op jit(solution)/shard_map/ppermute | solution.py:41
  62.3 3.3 %collective-permute-done.9.rest_1_ = bf16[3,64,512]{2,1,0:T(8,128)(2,1)S(1)} collective-permute-done((bf16[3,64,512]{2,1,0:T(8,128)(2,1)S(1)}, bf16[3,64,512]{2,1,0:T(8,128)(2,1)S(1)}, u32[]{:S(2)}, u32[]{:S(2)}) %collective-permute-start.9) | collective-permute-done | bytes 196640 | tf_op jit(solution)/shard_map/ppermute | solution.py:41
  65.6 3.4 %collective-permute-start.13 = (bf16[3,64,512]{2,1,0:T(8,128)(2,1)S(1)}, bf16[3,64,512]{2,1,0:T(8,128)(2,1)S(1)}, u32[]{:S(2)}, u32[]{:S(2)}) collective-permute-start(bf16[3,64,512]{2,1,0:T(8,128)(2,1)S(1)} %get-tuple-element.29.rest_0_), channel_id=1, source_target_pairs={{0,24},{4,28},{8,16},{12,20},{16,8},{20,12},{24,0},{28,4},{1,25},{... | collective-permute-start | bytes 589832 | tf_op jit(solution)/shard_map/ppermute | solution.py:41
  68.9 1.5 %collective-permute-start.16 = (bf16[256,512]{1,0:T(8,128)(2,1)S(1)}, bf16[256,512]{1,0:T(8,128)(2,1)S(1)}, u32[]{:S(2)}, u32[]{:S(2)}) collective-permute-start(bf16[256,512]{1,0:T(8,128)(2,1)S(1)} %collective-permute-done.1.rest_5_), channel_id=1, source_target_pairs={{0,4},{4,0},{8,12},{12,8},{16,20},{20,16},{24,28},{28,24},{1,5},{5... | collective-permute-start | bytes 786440 | tf_op jit(solution)/shard_map/ppermute | solution.py:41
  71.0 1.4 %collective-permute-done.11.rest_2_ = bf16[3,64,512]{2,1,0:T(8,128)(2,1)S(1)} collective-permute-done((bf16[3,64,512]{2,1,0:T(8,128)(2,1)S(1)}, bf16[3,64,512]{2,1,0:T(8,128)(2,1)S(1)}, u32[]{:S(2)}, u32[]{:S(2)}) %collective-permute-start.11) | collective-permute-done | bytes 196640 | tf_op jit(solution)/shard_map/ppermute | solution.py:41
  72.3 1.1 %collective-permute-done.12.rest_5_ = bf16[3,64,512]{2,1,0:T(8,128)(2,1)S(1)} collective-permute-done((bf16[3,64,512]{2,1,0:T(8,128)(2,1)S(1)}, bf16[3,64,512]{2,1,0:T(8,128)(2,1)S(1)}, u32[]{:S(2)}, u32[]{:S(2)}) %collective-permute-start.12) | collective-permute-done | bytes 196640 | tf_op jit(solution)/shard_map/ppermute | solution.py:41
  73.4 1.3 %collective-permute-start.18 = (bf16[256,512]{1,0:T(8,128)(2,1)}, bf16[256,512]{1,0:T(8,128)(2,1)S(1)}, u32[]{:S(2)}, u32[]{:S(2)}) collective-permute-start(bf16[256,512]{1,0:T(8,128)(2,1)} %collective-permute-done.2.rest_6_), channel_id=1, source_target_pairs={{0,8},{4,12},{8,24},{12,28},{24,16},{28,20},{16,0},{20,4},{1,9},{5... | collective-permute-start | bytes 786440 | tf_op jit(solution)/shard_map/ppermute | solution.py:338
  75.2 1.5 %collective-permute-start.15 = (bf16[3,64,512]{2,1,0:T(8,128)(2,1)S(1)}, bf16[3,64,512]{2,1,0:T(8,128)(2,1)S(1)}, u32[]{:S(2)}, u32[]{:S(2)}) collective-permute-start(bf16[3,64,512]{2,1,0:T(8,128)(2,1)S(1)} %collective-permute-done.13.rest_3_), channel_id=1, source_target_pairs={{0,4},{4,0},{8,12},{12,8},{16,20},{20,16},{24,28},{28,24},{1,5},{5... | collective-permute-start | bytes 589832 | tf_op jit(solution)/shard_map/ppermute | solution.py:41
  76.8 2.3 %window_attention.1.attended = f32[512,512]{1,0:T(8,128)S(1)} custom-call(s32[12]{0:T(128)S(1)} %dynamic-slice_bitcast_fusion.place, bf16[512,512]{1,0:T(8,128)(2,1)S(1)} %copy-done.4, bf16[512,512]{1,0:T(8,128)(2,1)S(1)} %copy-done.3, bf16[512,512]{1,0:T(8,128)(2,1)S(1)} %copy-done.2, bf16[512,512]{1,0:T(8,128)(2,1)S(1)} %collective-permute-done.even.k.pair_k, ...), custom_call_target="tpu_custom_call" | custom-call | flops 1 | bytes 1 | tf_op jit(solution)/shard_map/window_attention/pallas_call | solution.py:179
  79.0 6.7 %collective-permute-done.14.rest_6_ = bf16[3,64,512]{2,1,0:T(8,128)(2,1)S(1)} collective-permute-done((bf16[3,64,512]{2,1,0:T(8,128)(2,1)S(1)}, bf16[3,64,512]{2,1,0:T(8,128)(2,1)S(1)}, u32[]{:S(2)}, u32[]{:S(2)}) %collective-permute-start.14) | collective-permute-done | bytes 196640 | tf_op jit(solution)/shard_map/ppermute | solution.py:41
  85.8 2.1 %collective-permute-done.15.rest_7_ = bf16[3,64,512]{2,1,0:T(8,128)(2,1)S(1)} collective-permute-done((bf16[3,64,512]{2,1,0:T(8,128)(2,1)S(1)}, bf16[3,64,512]{2,1,0:T(8,128)(2,1)S(1)}, u32[]{:S(2)}, u32[]{:S(2)}) %collective-permute-start.15) | collective-permute-done | bytes 196640 | tf_op jit(solution)/shard_map/ppermute | solution.py:41
  87.9 1.7 %apply_fast.1.rest_0_ = bf16[512,512]{1,0:T(8,128)(2,1)S(1)} custom-call(s32[12]{0:T(128)S(1)} %dynamic-slice_bitcast_fusion.place, bf16[512,512]{1,0:T(8,128)(2,1)S(1)} %copy-done.4, f32[512,512]{1,0:T(8,128)S(1)} %window_attention.1.attended, bf16[3,64,512]{2,1,0:T(8,128)(2,1)S(1)} %get-tuple-element.29.rest_0_, ...), custom_call_target="tpu_custom_call" | custom-call | flops 1 | bytes 1 | tf_op jit(solution)/shard_map/apply_fast/pallas_call | solution.py:284
  89.6 2.0 %collective-permute-start.19 = (bf16[512,512]{1,0:T(8,128)(2,1)S(1)}, bf16[512,512]{1,0:T(8,128)(2,1)S(1)}, u32[]{:S(2)}, u32[]{:S(2)}) collective-permute-start(bf16[512,512]{1,0:T(8,128)(2,1)S(1)} %apply_fast.1.rest_0_), channel_id=1, source_target_pairs={{0,2},{1,3},{2,0},{3,1},{4,6},{5,7},{6,4},{7,5},{8,10},{9,11},{10,... | collective-permute-start | bytes 1572872 | tf_op jit(solution)/shard_map/ppermute | solution.py:41
  92.2 5.7 %collective-permute-done.20.rest_11_ = bf16[256,512]{1,0:T(8,128)(2,1)S(1)} collective-permute-done((bf16[256,512]{1,0:T(8,128)(2,1)S(1)}, bf16[256,512]{1,0:T(8,128)(2,1)S(1)}, u32[]{:S(2)}, u32[]{:S(2)}) %collective-permute-start.20) | collective-permute-done | bytes 262176 | tf_op jit(solution)/shard_map/ppermute | solution.py:41
  98.8 1.9 %collective-permute-done.22.rest_3_ = bf16[512,512]{1,0:T(8,128)(2,1)S(1)} collective-permute-done((bf16[512,512]{1,0:T(8,128)(2,1)S(1)}, bf16[512,512]{1,0:T(8,128)(2,1)S(1)}, u32[]{:S(2)}, u32[]{:S(2)}) %collective-permute-start.22) | collective-permute-done | bytes 524320 | tf_op jit(solution)/shard_map/ppermute | solution.py:41
  100.7 3.1 %project.1 = bf16[512,512]{1,0:T(8,128)(2,1)} custom-call(s32[12]{0:T(128)S(1)} %dynamic-slice_bitcast_fusion.place, bf16[512,512]{1,0:T(8,128)(2,1)S(1)} %apply_fast.1.rest_0_, bf16[512,512]{1,0:T(8,128)(2,1)S(1)} %collective-permute-done.19.rest_1_, bf16[512,512]{1,0:T(8,128)(2,1)S(1)} %collective-permute-done.21.rest_2_, ...), custom_call_target="tpu_custom_call" | custom-call | flops 1 | bytes 1 | tf_op jit(solution)/shard_map/project/pallas_call | solution.py:315
  (39 shorter events, 10.1 us)
Async XLA Ops:
  0.6 24.5 %copy-start = (bf16[1,3,512,512]{3,2,1,0:T(8,128)(2,1)S(1)}, bf16[1,3,512,512]{3,2,1,0:T(8,128)(2,1)}, u32[]{:S(2)}) copy-start(bf16[1,3,512,512]{3,2,1,0:T(8,128)(2,1)} %w.5) | copy-start | bytes 4718596
  0.6 10.6 %collective-permute-start.1 = (bf16[256,512]{1,0:T(8,128)(2,1)}, bf16[256,512]{1,0:T(8,128)(2,1)S(1)}, u32[]{:S(2)}, u32[]{:S(2)}) collective-permute-start(bf16[256,512]{1,0:T(8,128)(2,1)} %rest_4_.1), channel_id=1, source_target_pairs={{0,8},{4,12},{8,24},{12,28},{24,16},{28,20},{16,0},{20,4},{1,9},{5... | collective-permute-start | bytes 786440 | tf_op jit(solution)/shard_map/ppermute | solution.py:338
  3.7 15.1 %collective-permute-start = (bf16[512,512]{1,0:T(8,128)(2,1)}, bf16[512,512]{1,0:T(8,128)(2,1)S(1)}, u32[]{:S(2)}, u32[]{:S(2)}) collective-permute-start(bf16[512,512]{1,0:T(8,128)(2,1)} %k.3), channel_id=1, source_target_pairs={{0,4},{4,0},{8,12},{12,8},{16,20},{20,16},{24,28},{28,24},{1,5},{5... | collective-permute-start | bytes 1572872 | tf_op jit(solution)/shard_map/ppermute | solution.py:41
  11.2 8.5 %collective-permute-start.2 = (bf16[256,512]{1,0:T(8,128)(2,1)S(1)}, bf16[256,512]{1,0:T(8,128)(2,1)}, u32[]{:S(2)}, u32[]{:S(2)}) collective-permute-start(bf16[256,512]{1,0:T(8,128)(2,1)S(1)} %collective-permute-done.1.rest_5_), channel_id=1, source_target_pairs={{0,8},{4,12},{8,24},{12,28},{24,16},{28,20},{16,0},{20,4},{1,9},{5... | collective-permute-start | bytes 786440 | tf_op jit(solution)/shard_map/ppermute | solution.py:338
  13.4 15.1 %collective-permute-start.4 = (bf16[512,512]{1,0:T(8,128)(2,1)S(1)}, bf16[512,512]{1,0:T(8,128)(2,1)S(1)}, u32[]{:S(2)}, u32[]{:S(2)}) collective-permute-start(bf16[512,512]{1,0:T(8,128)(2,1)S(1)} %multiply_convert_fusion.e), channel_id=1, source_target_pairs={{0,4},{4,0},{8,12},{12,8},{16,20},{20,16},{24,28},{28,24},{1,5},{5... | collective-permute-start | bytes 1572872 | tf_op jit(solution)/shard_map/ppermute | solution.py:41
  19.7 1.0 %copy-start.1 = (bf16[512,512]{1,0:T(8,128)(2,1)S(1)}, bf16[512,512]{1,0:T(8,128)(2,1)}, u32[]{:S(2)}) copy-start(bf16[512,512]{1,0:T(8,128)(2,1)} %v.1) | copy-start | bytes 1572868
  20.8 4.3 %copy-start.3 = (bf16[512,512]{1,0:T(8,128)(2,1)S(1)}, bf16[512,512]{1,0:T(8,128)(2,1)}, u32[]{:S(2)}) copy-start(bf16[512,512]{1,0:T(8,128)(2,1)} %k.3) | copy-start | bytes 1572868
  21.4 12.3 %copy-start.2 = (bf16[512,512]{1,0:T(8,128)(2,1)S(1)}, bf16[512,512]{1,0:T(8,128)(2,1)}, u32[]{:S(2)}) copy-start(bf16[512,512]{1,0:T(8,128)(2,1)} %v.1) | copy-start | bytes 1572868
  21.4 12.3 %copy-start.5 = (bf16[256,512]{1,0:T(8,128)(2,1)S(1)}, bf16[256,512]{1,0:T(8,128)(2,1)}, u32[]{:S(2)}) copy-start(bf16[256,512]{1,0:T(8,128)(2,1)} %rest_4_.1) | copy-start | bytes 786436
  21.4 12.3 %collective-permute-start.3 = (bf16[512,512]{1,0:T(8,128)(2,1)S(1)}, bf16[512,512]{1,0:T(8,128)(2,1)S(1)}, u32[]{:S(2)}, u32[]{:S(2)}) collective-permute-start(bf16[512,512]{1,0:T(8,128)(2,1)S(1)} %pick.1), channel_id=1, source_target_pairs={{0,8},{4,12},{8,16},{12,20},{16,24},{20,28},{1,9},{5,13},{9,17},{1... | collective-permute-start | bytes 1572872 | tf_op jit(solution)/shard_map/ppermute | solution.py:401
  34.3 22.4 %copy-start.6 = (f32[1,3,64,512]{3,2,1,0:T(8,128)S(1)}, f32[1,3,64,512]{3,2,1,0:T(8,128)}, u32[]{:S(2)}) copy-start(f32[1,3,64,512]{3,2,1,0:T(8,128)} %momentum.1) | copy-start | bytes 1179652
  37.1 39.6 %copy-start.4 = (bf16[512,512]{1,0:T(8,128)(2,1)S(1)}, bf16[512,512]{1,0:T(8,128)(2,1)}, u32[]{:S(2)}) copy-start(bf16[512,512]{1,0:T(8,128)(2,1)} %q.3) | copy-start | bytes 1572868
  37.1 15.9 %collective-permute-start.5 = (bf16[768,512]{1,0:T(8,128)(2,1)S(1)}, bf16[768,512]{1,0:T(8,128)(2,1)S(1)}, u32[]{:S(2)}, u32[]{:S(2)}) collective-permute-start(bf16[768,512]{1,0:T(8,128)(2,1)S(1)} %crossing.1), channel_id=1, source_target_pairs={{0,4},{4,0},{8,12},{12,8},{16,20},{20,16},{24,28},{28,24},{1,5},{5... | collective-permute-start | bytes 2359304 | tf_op jit(solution)/shard_map/ppermute | solution.py:41
  38.7 10.9 %collective-permute-start.8 = (bf16[3,64,512]{2,1,0:T(8,128)(2,1)S(1)}, bf16[3,64,512]{2,1,0:T(8,128)(2,1)S(1)}, u32[]{:S(2)}, u32[]{:S(2)}) collective-permute-start(bf16[3,64,512]{2,1,0:T(8,128)(2,1)S(1)} %get-tuple-element.27), channel_id=1, source_target_pairs={{0,24},{4,28},{8,16},{12,20},{16,8},{20,12},{24,0},{28,4},{1,25},{... | collective-permute-start | bytes 589832 | tf_op jit(solution)/shard_map/ppermute | solution.py:41
  43.7 9.4 %collective-permute-start.6 = (bf16[3,64,512]{2,1,0:T(8,128)(2,1)S(1)}, bf16[3,64,512]{2,1,0:T(8,128)(2,1)S(1)}, u32[]{:S(2)}, u32[]{:S(2)}) collective-permute-start(bf16[3,64,512]{2,1,0:T(8,128)(2,1)S(1)} %get-tuple-element.23), channel_id=1, source_target_pairs={{0,8},{4,12},{8,0},{12,4},{16,24},{20,28},{24,16},{28,20},{1,9},{5... | collective-permute-start | bytes 589832 | tf_op jit(solution)/shard_map/ppermute | solution.py:41
  43.7 13.0 %collective-permute-start.7 = (bf16[3,64,512]{2,1,0:T(8,128)(2,1)S(1)}, bf16[3,64,512]{2,1,0:T(8,128)(2,1)S(1)}, u32[]{:S(2)}, u32[]{:S(2)}) collective-permute-start(bf16[3,64,512]{2,1,0:T(8,128)(2,1)S(1)} %get-tuple-element.26), channel_id=1, source_target_pairs={{0,16},{4,20},{8,24},{12,28},{16,0},{20,4},{24,8},{28,12},{1,17},{... | collective-permute-start | bytes 589832 | tf_op jit(solution)/shard_map/ppermute | solution.py:41
  58.1 7.4 %collective-permute-start.9 = (bf16[3,64,512]{2,1,0:T(8,128)(2,1)S(1)}, bf16[3,64,512]{2,1,0:T(8,128)(2,1)S(1)}, u32[]{:S(2)}, u32[]{:S(2)}) collective-permute-start(bf16[3,64,512]{2,1,0:T(8,128)(2,1)S(1)} %get-tuple-element.29.rest_0_), channel_id=1, source_target_pairs={{0,8},{4,12},{8,0},{12,4},{16,24},{20,28},{24,16},{28,20},{1,9},{5... | collective-permute-start | bytes 589832 | tf_op jit(solution)/shard_map/ppermute | solution.py:41
  58.3 7.2 %collective-permute-start.10 = (bf16[3,64,512]{2,1,0:T(8,128)(2,1)S(1)}, bf16[3,64,512]{2,1,0:T(8,128)(2,1)S(1)}, u32[]{:S(2)}, u32[]{:S(2)}) collective-permute-start(bf16[3,64,512]{2,1,0:T(8,128)(2,1)S(1)} %get-tuple-element.29.rest_0_), channel_id=1, source_target_pairs={{0,4},{4,0},{8,12},{12,8},{16,20},{20,16},{24,28},{28,24},{1,5},{5... | collective-permute-start | bytes 589832 | tf_op jit(solution)/shard_map/ppermute | solution.py:41
  58.8 13.5 %collective-permute-start.11 = (bf16[3,64,512]{2,1,0:T(8,128)(2,1)S(1)}, bf16[3,64,512]{2,1,0:T(8,128)(2,1)S(1)}, u32[]{:S(2)}, u32[]{:S(2)}) collective-permute-start(bf16[3,64,512]{2,1,0:T(8,128)(2,1)S(1)} %get-tuple-element.29.rest_0_), channel_id=1, source_target_pairs={{0,16},{4,20},{8,24},{12,28},{16,0},{20,4},{24,8},{28,12},{1,17},{... | collective-permute-start | bytes 589832 | tf_op jit(solution)/shard_map/ppermute | solution.py:41
  65.6 7.8 %collective-permute-start.12 = (bf16[3,64,512]{2,1,0:T(8,128)(2,1)S(1)}, bf16[3,64,512]{2,1,0:T(8,128)(2,1)S(1)}, u32[]{:S(2)}, u32[]{:S(2)}) collective-permute-start(bf16[3,64,512]{2,1,0:T(8,128)(2,1)S(1)} %collective-permute-done.9.rest_1_), channel_id=1, source_target_pairs={{0,4},{4,0},{8,12},{12,8},{16,20},{20,16},{24,28},{28,24},{1,5},{5... | collective-permute-start | bytes 589832 | tf_op jit(solution)/shard_map/ppermute | solution.py:41
  65.6 9.7 %collective-permute-start.13 = (bf16[3,64,512]{2,1,0:T(8,128)(2,1)S(1)}, bf16[3,64,512]{2,1,0:T(8,128)(2,1)S(1)}, u32[]{:S(2)}, u32[]{:S(2)}) collective-permute-start(bf16[3,64,512]{2,1,0:T(8,128)(2,1)S(1)} %get-tuple-element.29.rest_0_), channel_id=1, source_target_pairs={{0,24},{4,28},{8,16},{12,20},{16,8},{20,12},{24,0},{28,4},{1,25},{... | collective-permute-start | bytes 589832 | tf_op jit(solution)/shard_map/ppermute | solution.py:41
  68.9 18.9 %collective-permute-start.16 = (bf16[256,512]{1,0:T(8,128)(2,1)S(1)}, bf16[256,512]{1,0:T(8,128)(2,1)S(1)}, u32[]{:S(2)}, u32[]{:S(2)}) collective-permute-start(bf16[256,512]{1,0:T(8,128)(2,1)S(1)} %collective-permute-done.1.rest_5_), channel_id=1, source_target_pairs={{0,4},{4,0},{8,12},{12,8},{16,20},{20,16},{24,28},{28,24},{1,5},{5... | collective-permute-start | bytes 786440 | tf_op jit(solution)/shard_map/ppermute | solution.py:41
  70.4 17.4 %collective-permute-start.17 = (bf16[256,512]{1,0:T(8,128)(2,1)}, bf16[256,512]{1,0:T(8,128)(2,1)S(1)}, u32[]{:S(2)}, u32[]{:S(2)}) collective-permute-start(bf16[256,512]{1,0:T(8,128)(2,1)} %collective-permute-done.2.rest_6_), channel_id=1, source_target_pairs={{0,4},{4,0},{8,12},{12,8},{16,20},{20,16},{24,28},{28,24},{1,5},{5... | collective-permute-start | bytes 786440 | tf_op jit(solution)/shard_map/ppermute | solution.py:41
  73.4 14.5 %collective-permute-start.18 = (bf16[256,512]{1,0:T(8,128)(2,1)}, bf16[256,512]{1,0:T(8,128)(2,1)S(1)}, u32[]{:S(2)}, u32[]{:S(2)}) collective-permute-start(bf16[256,512]{1,0:T(8,128)(2,1)} %collective-permute-done.2.rest_6_), channel_id=1, source_target_pairs={{0,8},{4,12},{8,24},{12,28},{24,16},{28,20},{16,0},{20,4},{1,9},{5... | collective-permute-start | bytes 786440 | tf_op jit(solution)/shard_map/ppermute | solution.py:338
  74.7 11.1 %collective-permute-start.14 = (bf16[3,64,512]{2,1,0:T(8,128)(2,1)S(1)}, bf16[3,64,512]{2,1,0:T(8,128)(2,1)S(1)}, u32[]{:S(2)}, u32[]{:S(2)}) collective-permute-start(bf16[3,64,512]{2,1,0:T(8,128)(2,1)S(1)} %collective-permute-done.11.rest_2_), channel_id=1, source_target_pairs={{0,4},{4,0},{8,12},{12,8},{16,20},{20,16},{24,28},{28,24},{1,5},{5... | collective-permute-start | bytes 589832 | tf_op jit(solution)/shard_map/ppermute | solution.py:41
  75.2 12.7 %collective-permute-start.15 = (bf16[3,64,512]{2,1,0:T(8,128)(2,1)S(1)}, bf16[3,64,512]{2,1,0:T(8,128)(2,1)S(1)}, u32[]{:S(2)}, u32[]{:S(2)}) collective-permute-start(bf16[3,64,512]{2,1,0:T(8,128)(2,1)S(1)} %collective-permute-done.13.rest_3_), channel_id=1, source_target_pairs={{0,4},{4,0},{8,12},{12,8},{16,20},{20,16},{24,28},{28,24},{1,5},{5... | collective-permute-start | bytes 589832 | tf_op jit(solution)/shard_map/ppermute | solution.py:41
  89.6 9.2 %collective-permute-start.19 = (bf16[512,512]{1,0:T(8,128)(2,1)S(1)}, bf16[512,512]{1,0:T(8,128)(2,1)S(1)}, u32[]{:S(2)}, u32[]{:S(2)}) collective-permute-start(bf16[512,512]{1,0:T(8,128)(2,1)S(1)} %apply_fast.1.rest_0_), channel_id=1, source_target_pairs={{0,2},{1,3},{2,0},{3,1},{4,6},{5,7},{6,4},{7,5},{8,10},{9,11},{10,... | collective-permute-start | bytes 1572872 | tf_op jit(solution)/shard_map/ppermute | solution.py:41
  91.5 6.4 %collective-permute-start.20 = (bf16[256,512]{1,0:T(8,128)(2,1)S(1)}, bf16[256,512]{1,0:T(8,128)(2,1)S(1)}, u32[]{:S(2)}, u32[]{:S(2)}) collective-permute-start(bf16[256,512]{1,0:T(8,128)(2,1)S(1)} %collective-permute-done.18.rest_7_), channel_id=1, source_target_pairs={{0,4},{4,0},{8,12},{12,8},{16,20},{20,16},{24,28},{28,24},{1,5},{5... | collective-permute-start | bytes 786440 | tf_op jit(solution)/shard_map/ppermute | solution.py:41
  92.2 6.6 %collective-permute-start.21 = (bf16[512,512]{1,0:T(8,128)(2,1)S(1)}, bf16[512,512]{1,0:T(8,128)(2,1)S(1)}, u32[]{:S(2)}, u32[]{:S(2)}) collective-permute-start(bf16[512,512]{1,0:T(8,128)(2,1)S(1)} %apply_fast.1.rest_0_), channel_id=1, source_target_pairs={{0,1},{1,0},{2,3},{3,2},{4,5},{5,4},{6,7},{7,6},{8,9},{9,8},{10,11... | collective-permute-start | bytes 1572872 | tf_op jit(solution)/shard_map/ppermute | solution.py:41
  98.8 1.9 %collective-permute-start.22 = (bf16[512,512]{1,0:T(8,128)(2,1)S(1)}, bf16[512,512]{1,0:T(8,128)(2,1)S(1)}, u32[]{:S(2)}, u32[]{:S(2)}) collective-permute-start(bf16[512,512]{1,0:T(8,128)(2,1)S(1)} %collective-permute-done.19.rest_1_), channel_id=1, source_target_pairs={{0,1},{1,0},{2,3},{3,2},{4,5},{5,4},{6,7},{7,6},{8,9},{9,8},{10,11... | collective-permute-start | bytes 1572872 | tf_op jit(solution)/shard_map/ppermute | solution.py:41

commit v4 on v2

--- a/solution.py
+++ b/solution.py
@@ -371,12 +371,13 @@
     errors = (-grad_scale * rates * values.astype(jnp.float32)).astype(jnp.bfloat16)
     pair_errors = swap(errors, "seq", 1)
 
-    up_values = lax.ppermute(values, "seq", [(s, s + 2) for s in range(1, ranks - 2, 2)])
-
     wide = [out_proj]
     for _ in range(2):
         wide.append(ring_step(wide[-1], outer))
-    up_keys = after(pair_keys, wide[-1])
+
+    up_values = after(values, wide[1])
+    up_values = lax.ppermute(up_values, "seq", [(s, s + 2) for s in range(1, ranks - 2, 2)])
+    up_keys = after(pair_keys, wide[2])
     up_keys = lax.ppermute(up_keys, "seq", [(s, s + 2) for s in range(0, ranks - 2, 2)])
 
     acc = own_gradients(place, keys, errors, fast, outer)
@@ -393,13 +394,11 @@
         near.append(swap(renewed, "seq", step * 2))
     far = [swap(renewed, "seq", 1)]
     near[1] = after(near[1], far[0])
-    far.append(swap(near[1], "seq", 1))
-    near[2] = after(near[2], far[1])
-    far += [swap(unit, "seq", 1) for unit in near[2:]]
+    far += [swap(unit, "seq", 1) for unit in near[1:]]
     attended = window_attention(
         place, queries, keys, values, pair_keys, up_keys, after(crossed, near[1])
     )
-    far[2] = after(far[2], attended)
+    far[1] = after(far[1], attended)
     wide_far = [crossed, swap(after(wide[1], near[1]), "seq", 1)]
     wide.append(ring_step(after(wide[2], near[1], near[2]), outer))
     far[-1] = after(far[-1], wide_far[1], wide[3])

time: 108 us -> 102 us (0.944)
  starting transfers between devices: 36.1 us -> 29.3 us
    ppermute x19, starting transfers between devices: 28.1 us -> 21 us  [swap(): return lax.ppermute(array, axis, [(i, i ^ mask) for i in range(devices)])]
  transfers between devices with their start and end apart: 24 -> 24, of which waited for: 16 -> 15; matrix products, arithmetic and copies ran while one was open for 2% -> 3% of each run, Pallas kernels for 5% -> 6%
where the time goes in v4:
time: 102 us; the launch traced here: 101 us
  waiting for transfers between devices  51.4 us (50%)
  starting transfers between devices  29.3 us (29%)
  Pallas kernels  14.3 us (14%)
  local copies, waits for them, and re-layouts  3.18 us (3%)
  other arithmetic  1.89 us (2%)
    ppermute x19, waiting for transfers between devices, swap(): return lax.ppermute(array, axis, [(i, i ^ mask) for i in range(devices)])  42.2 us
    ppermute x19, starting transfers between devices, swap(): return lax.ppermute(array, axis, [(i, i ^ mask) for i in range(devices)])  21 us
    ppermute x3, waiting for transfers between devices, ring_step(): return lax.ppermute(unit, 'seq', pairs)  7.02 us
    ppermute x3, starting transfers between devices, ring_step(): return lax.ppermute(unit, 'seq', pairs)  4.3 us
    ppermute x1, starting transfers between devices, shards(): lax.ppermute(up_keys, 'seq', [(s, s + 2) for s in range(0, ranks - 2, 2)])  3.33 us
    pallas_call x1, Pallas kernels, both_gradients(): pl.pallas_call(functools.partial(both_kernel, outer), out_shape=[jax.Shap...  2.82 us
    pallas_call x1, Pallas kernels, own_gradients(): pl.pallas_call(functools.partial(own_kernel, outer), out_shape=jax.ShapeD...  2.77 us
    pallas_call x1, Pallas kernels, project(): pl.pallas_call(functools.partial(project_kernel, tags, rows_in), out_shap...  2.72 us
  transfers between devices with their start and end apart: 24, of which 15 were waited for; matrix products, arithmetic and copies ran while one was open for 3% of the time, Pallas kernels for 6%

profile of v4, /device:TPU:0, one launch (start us, length us, event | category | flops | bytes accessed | tf_op | source)
XLA Modules:
  0.0 100.9 jit_solution(17321445881383954352)
XLA Ops:
  0.6 3.1 %collective-permute-start.1 = (bf16[256,512]{1,0:T(8,128)(2,1)}, bf16[256,512]{1,0:T(8,128)(2,1)S(1)}, u32[]{:S(2)}, u32[]{:S(2)}) collective-permute-start(bf16[256,512]{1,0:T(8,128)(2,1)} %rest_4_.1), channel_id=1, source_target_pairs={{0,8},{4,12},{8,24},{12,28},{24,16},{28,20},{16,0},{20,4},{1,9},{5... | collective-permute-start | bytes 786440 | tf_op jit(solution)/shard_map/ppermute | solution.py:316
  3.7 1.5 %collective-permute-start = (bf16[512,512]{1,0:T(8,128)(2,1)}, bf16[512,512]{1,0:T(8,128)(2,1)S(1)}, u32[]{:S(2)}, u32[]{:S(2)}) collective-permute-start(bf16[512,512]{1,0:T(8,128)(2,1)} %k.3), channel_id=1, source_target_pairs={{0,4},{4,0},{8,12},{12,8},{16,20},{20,16},{24,28},{28,24},{1,5},{5... | collective-permute-start | bytes 1572872 | tf_op jit(solution)/shard_map/ppermute | solution.py:41
  5.2 6.0 %collective-permute-done.1.rest_5_ = bf16[256,512]{1,0:T(8,128)(2,1)S(1)} collective-permute-done((bf16[256,512]{1,0:T(8,128)(2,1)}, bf16[256,512]{1,0:T(8,128)(2,1)S(1)}, u32[]{:S(2)}, u32[]{:S(2)}) %collective-permute-start.1) | collective-permute-done | bytes 262176 | tf_op jit(solution)/shard_map/ppermute | solution.py:316
  12.9 1.2 %multiply_convert_fusion.e = bf16[512,512]{1,0:T(8,128)(2,1)S(1)} fusion(bf16[512,512]{1,0:T(8,128)(2,1)} %v.1, f32[512]{0:T(512)S(1)} %bitcast.3), kind=kLoop, calls=%fused_computation | loop fusion | flops 786432 | bytes 1050624 | tf_op jit(solution)/shard_map/convert_element_type | solution.py:371
  14.1 1.6 %collective-permute-start.5 = (bf16[512,512]{1,0:T(8,128)(2,1)S(1)}, bf16[512,512]{1,0:T(8,128)(2,1)S(1)}, u32[]{:S(2)}, u32[]{:S(2)}) collective-permute-start(bf16[512,512]{1,0:T(8,128)(2,1)S(1)} %multiply_convert_fusion.e), channel_id=1, source_target_pairs={{0,4},{4,0},{8,12},{12,8},{16,20},{20,16},{24,28},{28,24},{1,5},{5... | collective-permute-start | bytes 1572872 | tf_op jit(solution)/shard_map/ppermute | solution.py:41
  16.3 2.4 %collective-permute-done.k.pair_k = bf16[512,512]{1,0:T(8,128)(2,1)S(1)} collective-permute-done((bf16[512,512]{1,0:T(8,128)(2,1)}, bf16[512,512]{1,0:T(8,128)(2,1)S(1)}, u32[]{:S(2)}, u32[]{:S(2)}) %collective-permute-start) | collective-permute-done | bytes 524320 | tf_op jit(solution)/shard_map/ppermute | solution.py:41
  19.6 3.3 %collective-permute-start.3 = (bf16[512,512]{1,0:T(8,128)(2,1)S(1)}, bf16[512,512]{1,0:T(8,128)(2,1)S(1)}, u32[]{:S(2)}, u32[]{:S(2)}) collective-permute-start(bf16[512,512]{1,0:T(8,128)(2,1)S(1)} %collective-permute-done.k.pair_k), channel_id=1, source_target_pairs={{0,8},{8,16},{16,24},{1,9},{9,17},{17,25},{2,10},{10,18},{18,26},{... | collective-permute-start | bytes 1572872 | tf_op jit(solution)/shard_map/ppermute | solution.py:381
  23.7 1.4 %copy-done = bf16[1,3,512,512]{3,2,1,0:T(8,128)(2,1)S(1)} copy-done((bf16[1,3,512,512]{3,2,1,0:T(8,128)(2,1)S(1)}, bf16[1,3,512,512]{3,2,1,0:T(8,128)(2,1)}, u32[]{:S(2)}) %copy-start) | copy-done | bytes 1572888
  25.1 1.0 %copy-done.3 = bf16[512,512]{1,0:T(8,128)(2,1)S(1)} copy-done((bf16[512,512]{1,0:T(8,128)(2,1)S(1)}, bf16[512,512]{1,0:T(8,128)(2,1)}, u32[]{:S(2)}) %copy-start.3) | copy-done | bytes 524312
  26.1 2.8 %own_gradients.1.acc = f32[4,3,64,512]{3,2,1,0:T(8,128)S(1)} custom-call(s32[12]{0:T(128)S(1)} %dynamic-slice_bitcast_fusion.place, bf16[512,512]{1,0:T(8,128)(2,1)S(1)} %copy-done.3, bf16[512,512]{1,0:T(8,128)(2,1)S(1)} %multiply_convert_fusion.e, bf16[1,3,512,512]{3,2,1,0:T(8,128)(2,1)S(1)} %copy-done), custom_call_target="tpu_custom_call" | custom-call | flops 1 | bytes 1 | tf_op jit(solution)/shard_map/own_gradients/pallas_call | solution.py:122
  29.6 2.2 %collective-permute-done.3.up_k = bf16[512,512]{1,0:T(8,128)(2,1)S(1)} collective-permute-done((bf16[512,512]{1,0:T(8,128)(2,1)S(1)}, bf16[512,512]{1,0:T(8,128)(2,1)S(1)}, u32[]{:S(2)}, u32[]{:S(2)}) %collective-permute-start.3) | collective-permute-done | bytes 524320 | tf_op jit(solution)/shard_map/ppermute | solution.py:381
  31.8 2.8 %both_gradients.1 = (f32[3,64,512]{2,1,0:T(8,128)S(1)}, bf16[3,64,512]{2,1,0:T(8,128)(2,1)S(1)}, bf16[3,64,512]{2,1,0:T(8,128)(2,1)S(1)}, bf16[3,64,512]{2,1,0:T(8,128)(2,1)S(1)}) custom-call(s32[12]{0:T(128)S(1)} %dynamic-slice_bitcast_fusion.place, bf16[512,512]{1,0:T(8,128)(2,1)S(1)} %collective-permute-done.k.pair_k, ...), custom_call_target="tpu_custom_call" | custom-call | flops 1 | bytes 1 | tf_op jit(solution)/shard_map/both_gradients/pallas_call | solution.py:137
  35.0 4.7 %collective-permute-start.9 = (bf16[3,64,512]{2,1,0:T(8,128)(2,1)S(1)}, bf16[3,64,512]{2,1,0:T(8,128)(2,1)S(1)}, u32[]{:S(2)}, u32[]{:S(2)}) collective-permute-start(bf16[3,64,512]{2,1,0:T(8,128)(2,1)S(1)} %get-tuple-element.29), channel_id=1, source_target_pairs={{0,24},{4,28},{8,16},{12,20},{16,8},{20,12},{24,0},{28,4},{1,25},{... | collective-permute-start | bytes 589832 | tf_op jit(solution)/shard_map/ppermute | solution.py:41
  40.4 5.2 %collective-permute-done.9.rest_2_ = bf16[3,64,512]{2,1,0:T(8,128)(2,1)S(1)} collective-permute-done((bf16[3,64,512]{2,1,0:T(8,128)(2,1)S(1)}, bf16[3,64,512]{2,1,0:T(8,128)(2,1)S(1)}, u32[]{:S(2)}, u32[]{:S(2)}) %collective-permute-start.9) | collective-permute-done | bytes 196640 | tf_op jit(solution)/shard_map/ppermute | solution.py:41
  45.5 5.2 %collective-permute-done.6.early_v.rest_8_ = bf16[768,512]{1,0:T(8,128)(2,1)S(1)} collective-permute-done((bf16[768,512]{1,0:T(8,128)(2,1)S(1)}, bf16[768,512]{1,0:T(8,128)(2,1)S(1)}, u32[]{:S(2)}, u32[]{:S(2)}) %collective-permute-start.6) | collective-permute-done | bytes 786464 | tf_op jit(solution)/shard_map/ppermute | solution.py:41
  50.7 3.9 %collective-permute-done.8.rest_1_ = bf16[3,64,512]{2,1,0:T(8,128)(2,1)S(1)} collective-permute-done((bf16[3,64,512]{2,1,0:T(8,128)(2,1)S(1)}, bf16[3,64,512]{2,1,0:T(8,128)(2,1)S(1)}, u32[]{:S(2)}, u32[]{:S(2)}) %collective-permute-start.8) | collective-permute-done | bytes 196640 | tf_op jit(solution)/shard_map/ppermute | solution.py:41
  54.7 1.4 %renew.1 = (f32[1,3,64,512]{3,2,1,0:T(8,128)}, bf16[3,64,512]{2,1,0:T(8,128)(2,1)S(1)}) custom-call(s32[12]{0:T(128)S(1)} %dynamic-slice_bitcast_fusion.place, bf16[1,3,512,512]{3,2,1,0:T(8,128)(2,1)S(1)} %copy-done.1, f32[1,3,64,512]{3,2,1,0:T(8,128)S(1)} %copy-done.7, f32[3,64,512]{2,1,0:T(8,128)S(1)} %get-tuple-element.27.mine, ...), custom_call_target="tpu_custom_call" | custom-call | flops 1 | bytes 1 | tf_op jit(solution)/shard_map/renew/pallas_call | solution.py:232
  56.6 3.6 %collective-permute-start.12 = (bf16[3,64,512]{2,1,0:T(8,128)(2,1)S(1)}, bf16[3,64,512]{2,1,0:T(8,128)(2,1)S(1)}, u32[]{:S(2)}, u32[]{:S(2)}) collective-permute-start(bf16[3,64,512]{2,1,0:T(8,128)(2,1)S(1)} %get-tuple-element.31.rest_0_), channel_id=1, source_target_pairs={{0,16},{4,20},{8,24},{12,28},{16,0},{20,4},{24,8},{28,12},{1,17},{... | collective-permute-start | bytes 589832 | tf_op jit(solution)/shard_map/ppermute | solution.py:41
  60.9 5.3 %collective-permute-done.10.rest_1_ = bf16[3,64,512]{2,1,0:T(8,128)(2,1)S(1)} collective-permute-done((bf16[3,64,512]{2,1,0:T(8,128)(2,1)S(1)}, bf16[3,64,512]{2,1,0:T(8,128)(2,1)S(1)}, u32[]{:S(2)}, u32[]{:S(2)}) %collective-permute-start.10) | collective-permute-done | bytes 196640 | tf_op jit(solution)/shard_map/ppermute | solution.py:41
  66.1 6.5 %collective-permute-done.12.rest_2_ = bf16[3,64,512]{2,1,0:T(8,128)(2,1)S(1)} collective-permute-done((bf16[3,64,512]{2,1,0:T(8,128)(2,1)S(1)}, bf16[3,64,512]{2,1,0:T(8,128)(2,1)S(1)}, u32[]{:S(2)}, u32[]{:S(2)}) %collective-permute-start.12) | collective-permute-done | bytes 196640 | tf_op jit(solution)/shard_map/ppermute | solution.py:41
  73.0 1.8 %collective-permute-start.14 = (bf16[3,64,512]{2,1,0:T(8,128)(2,1)S(1)}, bf16[3,64,512]{2,1,0:T(8,128)(2,1)S(1)}, u32[]{:S(2)}, u32[]{:S(2)}) collective-permute-start(bf16[3,64,512]{2,1,0:T(8,128)(2,1)S(1)} %collective-permute-done.10.rest_1_), channel_id=1, source_target_pairs={{0,4},{4,0},{8,12},{12,8},{16,20},{20,16},{24,28},{28,24},{1,5},{5... | collective-permute-start | bytes 589832 | tf_op jit(solution)/shard_map/ppermute | solution.py:41
  75.0 1.8 %collective-permute-start.15 = (bf16[3,64,512]{2,1,0:T(8,128)(2,1)S(1)}, bf16[3,64,512]{2,1,0:T(8,128)(2,1)S(1)}, u32[]{:S(2)}, u32[]{:S(2)}) collective-permute-start(bf16[3,64,512]{2,1,0:T(8,128)(2,1)S(1)} %collective-permute-done.12.rest_2_), channel_id=1, source_target_pairs={{0,4},{4,0},{8,12},{12,8},{16,20},{20,16},{24,28},{28,24},{1,5},{5... | collective-permute-start | bytes 589832 | tf_op jit(solution)/shard_map/ppermute | solution.py:41
  76.8 2.3 %window_attention.1.attended = f32[512,512]{1,0:T(8,128)S(1)} custom-call(s32[12]{0:T(128)S(1)} %dynamic-slice_bitcast_fusion.place, bf16[512,512]{1,0:T(8,128)(2,1)S(1)} %copy-done.5, bf16[512,512]{1,0:T(8,128)(2,1)S(1)} %copy-done.4, bf16[512,512]{1,0:T(8,128)(2,1)S(1)} %copy-done.2, bf16[512,512]{1,0:T(8,128)(2,1)S(1)} %collective-permute-done.k.pair_k, ...), custom_call_target="tpu_custom_call" | custom-call | flops 1 | bytes 1 | tf_op jit(solution)/shard_map/window_attention/pallas_call | solution.py:179
  79.1 1.9 %collective-permute-done.16.rest_7_ = bf16[3,64,512]{2,1,0:T(8,128)(2,1)S(1)} collective-permute-done((bf16[3,64,512]{2,1,0:T(8,128)(2,1)S(1)}, bf16[3,64,512]{2,1,0:T(8,128)(2,1)S(1)}, u32[]{:S(2)}, u32[]{:S(2)}) %collective-permute-start.16) | collective-permute-done | bytes 196640 | tf_op jit(solution)/shard_map/ppermute | solution.py:41
  81.1 2.0 %collective-permute-done.15.rest_6_ = bf16[3,64,512]{2,1,0:T(8,128)(2,1)S(1)} collective-permute-done((bf16[3,64,512]{2,1,0:T(8,128)(2,1)S(1)}, bf16[3,64,512]{2,1,0:T(8,128)(2,1)S(1)}, u32[]{:S(2)}, u32[]{:S(2)}) %collective-permute-start.15) | collective-permute-done | bytes 196640 | tf_op jit(solution)/shard_map/ppermute | solution.py:41
  83.1 1.7 %apply_fast.1.rest_0_ = bf16[512,512]{1,0:T(8,128)(2,1)S(1)} custom-call(s32[12]{0:T(128)S(1)} %dynamic-slice_bitcast_fusion.place, bf16[512,512]{1,0:T(8,128)(2,1)S(1)} %copy-done.5, f32[512,512]{1,0:T(8,128)S(1)} %window_attention.1.attended, bf16[3,64,512]{2,1,0:T(8,128)(2,1)S(1)} %get-tuple-element.31.rest_0_, ...), custom_call_target="tpu_custom_call" | custom-call | flops 1 | bytes 1 | tf_op jit(solution)/shard_map/apply_fast/pallas_call | solution.py:262
  84.7 1.6 %collective-permute-start.19 = (bf16[512,512]{1,0:T(8,128)(2,1)S(1)}, bf16[512,512]{1,0:T(8,128)(2,1)S(1)}, u32[]{:S(2)}, u32[]{:S(2)}) collective-permute-start(bf16[512,512]{1,0:T(8,128)(2,1)S(1)} %apply_fast.1.rest_0_), channel_id=1, source_target_pairs={{0,2},{1,3},{2,0},{3,1},{4,6},{5,7},{6,4},{7,5},{8,10},{9,11},{10,... | collective-permute-start | bytes 1572872 | tf_op jit(solution)/shard_map/ppermute | solution.py:41
  86.3 1.6 %collective-permute-start.20 = (bf16[256,512]{1,0:T(8,128)(2,1)S(1)}, bf16[256,512]{1,0:T(8,128)(2,1)S(1)}, u32[]{:S(2)}, u32[]{:S(2)}) collective-permute-start(bf16[256,512]{1,0:T(8,128)(2,1)S(1)} %collective-permute-done.2.rest_6_), channel_id=1, source_target_pairs={{0,4},{4,0},{8,12},{12,8},{16,20},{20,16},{24,28},{28,24},{1,5},{5... | collective-permute-start | bytes 786440 | tf_op jit(solution)/shard_map/ppermute | solution.py:41
  88.3 5.1 %collective-permute-done.20.rest_10_ = bf16[256,512]{1,0:T(8,128)(2,1)S(1)} collective-permute-done((bf16[256,512]{1,0:T(8,128)(2,1)S(1)}, bf16[256,512]{1,0:T(8,128)(2,1)S(1)}, u32[]{:S(2)}, u32[]{:S(2)}) %collective-permute-start.20) | collective-permute-done | bytes 262176 | tf_op jit(solution)/shard_map/ppermute | solution.py:41
  93.4 2.8 %collective-permute-done.21.rest_11_ = bf16[256,512]{1,0:T(8,128)(2,1)S(1)} collective-permute-done((bf16[256,512]{1,0:T(8,128)(2,1)S(1)}, bf16[256,512]{1,0:T(8,128)(2,1)S(1)}, u32[]{:S(2)}, u32[]{:S(2)}) %collective-permute-start.21) | collective-permute-done | bytes 262176 | tf_op jit(solution)/shard_map/ppermute | solution.py:41
  96.3 1.9 %collective-permute-done.23.rest_3_ = bf16[512,512]{1,0:T(8,128)(2,1)S(1)} collective-permute-done((bf16[512,512]{1,0:T(8,128)(2,1)S(1)}, bf16[512,512]{1,0:T(8,128)(2,1)S(1)}, u32[]{:S(2)}, u32[]{:S(2)}) %collective-permute-start.23) | collective-permute-done | bytes 524320 | tf_op jit(solution)/shard_map/ppermute | solution.py:41
  98.2 2.7 %project.1 = bf16[512,512]{1,0:T(8,128)(2,1)} custom-call(s32[12]{0:T(128)S(1)} %dynamic-slice_bitcast_fusion.place, bf16[512,512]{1,0:T(8,128)(2,1)S(1)} %apply_fast.1.rest_0_, bf16[512,512]{1,0:T(8,128)(2,1)S(1)} %collective-permute-done.19.rest_1_, bf16[512,512]{1,0:T(8,128)(2,1)S(1)} %collective-permute-done.22.rest_2_, ...), custom_call_target="tpu_custom_call" | custom-call | flops 1 | bytes 1 | tf_op jit(solution)/shard_map/project/pallas_call | solution.py:293
  (42 shorter events, 7.8 us)
Async XLA Ops:
  0.6 10.6 %collective-permute-start.1 = (bf16[256,512]{1,0:T(8,128)(2,1)}, bf16[256,512]{1,0:T(8,128)(2,1)S(1)}, u32[]{:S(2)}, u32[]{:S(2)}) collective-permute-start(bf16[256,512]{1,0:T(8,128)(2,1)} %rest_4_.1), channel_id=1, source_target_pairs={{0,8},{4,12},{8,24},{12,28},{24,16},{28,20},{16,0},{20,4},{1,9},{5... | collective-permute-start | bytes 786440 | tf_op jit(solution)/shard_map/ppermute | solution.py:316
  3.7 15.1 %collective-permute-start = (bf16[512,512]{1,0:T(8,128)(2,1)}, bf16[512,512]{1,0:T(8,128)(2,1)S(1)}, u32[]{:S(2)}, u32[]{:S(2)}) collective-permute-start(bf16[512,512]{1,0:T(8,128)(2,1)} %k.3), channel_id=1, source_target_pairs={{0,4},{4,0},{8,12},{12,8},{16,20},{20,16},{24,28},{28,24},{1,5},{5... | collective-permute-start | bytes 1572872 | tf_op jit(solution)/shard_map/ppermute | solution.py:41
  11.2 8.4 %collective-permute-start.2 = (bf16[256,512]{1,0:T(8,128)(2,1)S(1)}, bf16[256,512]{1,0:T(8,128)(2,1)S(1)}, u32[]{:S(2)}, u32[]{:S(2)}) collective-permute-start(bf16[256,512]{1,0:T(8,128)(2,1)S(1)} %collective-permute-done.1.rest_5_), channel_id=1, source_target_pairs={{0,8},{4,12},{8,24},{12,28},{24,16},{28,20},{16,0},{20,4},{1,9},{5... | collective-permute-start | bytes 786440 | tf_op jit(solution)/shard_map/ppermute | solution.py:316
  14.1 15.5 %collective-permute-start.5 = (bf16[512,512]{1,0:T(8,128)(2,1)S(1)}, bf16[512,512]{1,0:T(8,128)(2,1)S(1)}, u32[]{:S(2)}, u32[]{:S(2)}) collective-permute-start(bf16[512,512]{1,0:T(8,128)(2,1)S(1)} %multiply_convert_fusion.e), channel_id=1, source_target_pairs={{0,4},{4,0},{8,12},{12,8},{16,20},{20,16},{24,28},{28,24},{1,5},{5... | collective-permute-start | bytes 1572872 | tf_op jit(solution)/shard_map/ppermute | solution.py:41
  15.7 13.3 %collective-permute-start.4 = (bf16[512,512]{1,0:T(8,128)(2,1)}, bf16[512,512]{1,0:T(8,128)(2,1)S(1)}, u32[]{:S(2)}, u32[]{:S(2)}) collective-permute-start(bf16[512,512]{1,0:T(8,128)(2,1)} %v.1), channel_id=1, source_target_pairs={{4,12},{12,20},{20,28},{5,13},{13,21},{21,29},{6,14},{14,22},{22,3... | collective-permute-start | bytes 1572872 | tf_op jit(solution)/shard_map/ppermute | solution.py:379
  19.6 12.1 %collective-permute-start.3 = (bf16[512,512]{1,0:T(8,128)(2,1)S(1)}, bf16[512,512]{1,0:T(8,128)(2,1)S(1)}, u32[]{:S(2)}, u32[]{:S(2)}) collective-permute-start(bf16[512,512]{1,0:T(8,128)(2,1)S(1)} %collective-permute-done.k.pair_k), channel_id=1, source_target_pairs={{0,8},{8,16},{16,24},{1,9},{9,17},{17,25},{2,10},{10,18},{18,26},{... | collective-permute-start | bytes 1572872 | tf_op jit(solution)/shard_map/ppermute | solution.py:381
  23.7 1.4 %copy-start = (bf16[1,3,512,512]{3,2,1,0:T(8,128)(2,1)S(1)}, bf16[1,3,512,512]{3,2,1,0:T(8,128)(2,1)}, u32[]{:S(2)}) copy-start(bf16[1,3,512,512]{3,2,1,0:T(8,128)(2,1)} %w.5) | copy-start | bytes 4718596
  25.1 1.0 %copy-start.3 = (bf16[512,512]{1,0:T(8,128)(2,1)S(1)}, bf16[512,512]{1,0:T(8,128)(2,1)}, u32[]{:S(2)}) copy-start(bf16[512,512]{1,0:T(8,128)(2,1)} %k.3) | copy-start | bytes 1572868
  26.1 2.8 %copy-start.2 = (bf16[512,512]{1,0:T(8,128)(2,1)S(1)}, bf16[512,512]{1,0:T(8,128)(2,1)}, u32[]{:S(2)}) copy-start(bf16[512,512]{1,0:T(8,128)(2,1)} %v.1) | copy-start | bytes 1572868
  26.1 2.8 %copy-start.6 = (bf16[256,512]{1,0:T(8,128)(2,1)S(1)}, bf16[256,512]{1,0:T(8,128)(2,1)}, u32[]{:S(2)}) copy-start(bf16[256,512]{1,0:T(8,128)(2,1)} %rest_4_.1) | copy-start | bytes 786436
  28.9 2.9 %copy-start.1 = (bf16[1,3,512,512]{3,2,1,0:T(8,128)(2,1)S(1)}, bf16[1,3,512,512]{3,2,1,0:T(8,128)(2,1)}, u32[]{:S(2)}) copy-start(bf16[1,3,512,512]{3,2,1,0:T(8,128)(2,1)} %w.5) | copy-start | bytes 4718596
  29.6 25.1 %copy-start.7 = (f32[1,3,64,512]{3,2,1,0:T(8,128)S(1)}, f32[1,3,64,512]{3,2,1,0:T(8,128)}, u32[]{:S(2)}) copy-start(f32[1,3,64,512]{3,2,1,0:T(8,128)} %momentum.1) | copy-start | bytes 1179652
  34.6 42.2 %copy-start.4 = (bf16[512,512]{1,0:T(8,128)(2,1)S(1)}, bf16[512,512]{1,0:T(8,128)(2,1)}, u32[]{:S(2)}) copy-start(bf16[512,512]{1,0:T(8,128)(2,1)} %k.3) | copy-start | bytes 1572868
  34.6 42.2 %copy-start.5 = (bf16[512,512]{1,0:T(8,128)(2,1)S(1)}, bf16[512,512]{1,0:T(8,128)(2,1)}, u32[]{:S(2)}) copy-start(bf16[512,512]{1,0:T(8,128)(2,1)} %q.3) | copy-start | bytes 1572868
  34.6 16.1 %collective-permute-start.6 = (bf16[768,512]{1,0:T(8,128)(2,1)S(1)}, bf16[768,512]{1,0:T(8,128)(2,1)S(1)}, u32[]{:S(2)}, u32[]{:S(2)}) collective-permute-start(bf16[768,512]{1,0:T(8,128)(2,1)S(1)} %crossing.1), channel_id=1, source_target_pairs={{0,4},{4,0},{8,12},{12,8},{16,20},{20,16},{24,28},{28,24},{1,5},{5... | collective-permute-start | bytes 2359304 | tf_op jit(solution)/shard_map/ppermute | solution.py:41
  35.0 10.6 %collective-permute-start.9 = (bf16[3,64,512]{2,1,0:T(8,128)(2,1)S(1)}, bf16[3,64,512]{2,1,0:T(8,128)(2,1)S(1)}, u32[]{:S(2)}, u32[]{:S(2)}) collective-permute-start(bf16[3,64,512]{2,1,0:T(8,128)(2,1)S(1)} %get-tuple-element.29), channel_id=1, source_target_pairs={{0,24},{4,28},{8,16},{12,20},{16,8},{20,12},{24,0},{28,4},{1,25},{... | collective-permute-start | bytes 589832 | tf_op jit(solution)/shard_map/ppermute | solution.py:41
  39.7 11.0 %collective-permute-start.7 = (bf16[3,64,512]{2,1,0:T(8,128)(2,1)S(1)}, bf16[3,64,512]{2,1,0:T(8,128)(2,1)S(1)}, u32[]{:S(2)}, u32[]{:S(2)}) collective-permute-start(bf16[3,64,512]{2,1,0:T(8,128)(2,1)S(1)} %get-tuple-element.25), channel_id=1, source_target_pairs={{0,8},{4,12},{8,0},{12,4},{16,24},{20,28},{24,16},{28,20},{1,9},{5... | collective-permute-start | bytes 589832 | tf_op jit(solution)/shard_map/ppermute | solution.py:41
  39.7 15.0 %collective-permute-start.8 = (bf16[3,64,512]{2,1,0:T(8,128)(2,1)S(1)}, bf16[3,64,512]{2,1,0:T(8,128)(2,1)S(1)}, u32[]{:S(2)}, u32[]{:S(2)}) collective-permute-start(bf16[3,64,512]{2,1,0:T(8,128)(2,1)S(1)} %get-tuple-element.28), channel_id=1, source_target_pairs={{0,16},{4,20},{8,24},{12,28},{16,0},{20,4},{24,8},{28,12},{1,17},{... | collective-permute-start | bytes 589832 | tf_op jit(solution)/shard_map/ppermute | solution.py:41
  56.1 10.0 %collective-permute-start.10 = (bf16[3,64,512]{2,1,0:T(8,128)(2,1)S(1)}, bf16[3,64,512]{2,1,0:T(8,128)(2,1)S(1)}, u32[]{:S(2)}, u32[]{:S(2)}) collective-permute-start(bf16[3,64,512]{2,1,0:T(8,128)(2,1)S(1)} %get-tuple-element.31.rest_0_), channel_id=1, source_target_pairs={{0,8},{4,12},{8,0},{12,4},{16,24},{20,28},{24,16},{28,20},{1,9},{5... | collective-permute-start | bytes 589832 | tf_op jit(solution)/shard_map/ppermute | solution.py:41
  56.2 10.0 %collective-permute-start.11 = (bf16[3,64,512]{2,1,0:T(8,128)(2,1)S(1)}, bf16[3,64,512]{2,1,0:T(8,128)(2,1)S(1)}, u32[]{:S(2)}, u32[]{:S(2)}) collective-permute-start(bf16[3,64,512]{2,1,0:T(8,128)(2,1)S(1)} %get-tuple-element.31.rest_0_), channel_id=1, source_target_pairs={{0,4},{4,0},{8,12},{12,8},{16,20},{20,16},{24,28},{28,24},{1,5},{5... | collective-permute-start | bytes 589832 | tf_op jit(solution)/shard_map/ppermute | solution.py:41
  56.6 16.1 %collective-permute-start.12 = (bf16[3,64,512]{2,1,0:T(8,128)(2,1)S(1)}, bf16[3,64,512]{2,1,0:T(8,128)(2,1)S(1)}, u32[]{:S(2)}, u32[]{:S(2)}) collective-permute-start(bf16[3,64,512]{2,1,0:T(8,128)(2,1)S(1)} %get-tuple-element.31.rest_0_), channel_id=1, source_target_pairs={{0,16},{4,20},{8,24},{12,28},{16,0},{20,4},{24,8},{28,12},{1,17},{... | collective-permute-start | bytes 589832 | tf_op jit(solution)/shard_map/ppermute | solution.py:41
  60.2 14.6 %collective-permute-start.13 = (bf16[3,64,512]{2,1,0:T(8,128)(2,1)S(1)}, bf16[3,64,512]{2,1,0:T(8,128)(2,1)S(1)}, u32[]{:S(2)}, u32[]{:S(2)}) collective-permute-start(bf16[3,64,512]{2,1,0:T(8,128)(2,1)S(1)} %get-tuple-element.31.rest_0_), channel_id=1, source_target_pairs={{0,24},{4,28},{8,16},{12,20},{16,8},{20,12},{24,0},{28,4},{1,25},{... | collective-permute-start | bytes 589832 | tf_op jit(solution)/shard_map/ppermute | solution.py:41
  66.1 14.8 %collective-permute-start.17 = (bf16[256,512]{1,0:T(8,128)(2,1)S(1)}, bf16[256,512]{1,0:T(8,128)(2,1)S(1)}, u32[]{:S(2)}, u32[]{:S(2)}) collective-permute-start(bf16[256,512]{1,0:T(8,128)(2,1)S(1)} %collective-permute-done.1.rest_5_), channel_id=1, source_target_pairs={{0,4},{4,0},{8,12},{12,8},{16,20},{20,16},{24,28},{28,24},{1,5},{5... | collective-permute-start | bytes 786440 | tf_op jit(solution)/shard_map/ppermute | solution.py:41
  72.7 8.4 %collective-permute-start.18 = (bf16[256,512]{1,0:T(8,128)(2,1)S(1)}, bf16[256,512]{1,0:T(8,128)(2,1)S(1)}, u32[]{:S(2)}, u32[]{:S(2)}) collective-permute-start(bf16[256,512]{1,0:T(8,128)(2,1)S(1)} %collective-permute-done.2.rest_6_), channel_id=1, source_target_pairs={{0,8},{4,12},{8,24},{12,28},{24,16},{28,20},{16,0},{20,4},{1,9},{5... | collective-permute-start | bytes 786440 | tf_op jit(solution)/shard_map/ppermute | solution.py:316
  73.0 6.1 %collective-permute-start.14 = (bf16[3,64,512]{2,1,0:T(8,128)(2,1)S(1)}, bf16[3,64,512]{2,1,0:T(8,128)(2,1)S(1)}, u32[]{:S(2)}, u32[]{:S(2)}) collective-permute-start(bf16[3,64,512]{2,1,0:T(8,128)(2,1)S(1)} %collective-permute-done.10.rest_1_), channel_id=1, source_target_pairs={{0,4},{4,0},{8,12},{12,8},{16,20},{20,16},{24,28},{28,24},{1,5},{5... | collective-permute-start | bytes 589832 | tf_op jit(solution)/shard_map/ppermute | solution.py:41
  74.7 6.2 %collective-permute-start.16 = (bf16[3,64,512]{2,1,0:T(8,128)(2,1)S(1)}, bf16[3,64,512]{2,1,0:T(8,128)(2,1)S(1)}, u32[]{:S(2)}, u32[]{:S(2)}) collective-permute-start(bf16[3,64,512]{2,1,0:T(8,128)(2,1)S(1)} %collective-permute-done.13.rest_3_), channel_id=1, source_target_pairs={{0,4},{4,0},{8,12},{12,8},{16,20},{20,16},{24,28},{28,24},{1,5},{5... | collective-permute-start | bytes 589832 | tf_op jit(solution)/shard_map/ppermute | solution.py:41
  75.0 8.1 %collective-permute-start.15 = (bf16[3,64,512]{2,1,0:T(8,128)(2,1)S(1)}, bf16[3,64,512]{2,1,0:T(8,128)(2,1)S(1)}, u32[]{:S(2)}, u32[]{:S(2)}) collective-permute-start(bf16[3,64,512]{2,1,0:T(8,128)(2,1)S(1)} %collective-permute-done.12.rest_2_), channel_id=1, source_target_pairs={{0,4},{4,0},{8,12},{12,8},{16,20},{20,16},{24,28},{28,24},{1,5},{5... | collective-permute-start | bytes 589832 | tf_op jit(solution)/shard_map/ppermute | solution.py:41
  84.7 11.5 %collective-permute-start.19 = (bf16[512,512]{1,0:T(8,128)(2,1)S(1)}, bf16[512,512]{1,0:T(8,128)(2,1)S(1)}, u32[]{:S(2)}, u32[]{:S(2)}) collective-permute-start(bf16[512,512]{1,0:T(8,128)(2,1)S(1)} %apply_fast.1.rest_0_), channel_id=1, source_target_pairs={{0,2},{1,3},{2,0},{3,1},{4,6},{5,7},{6,4},{7,5},{8,10},{9,11},{10,... | collective-permute-start | bytes 1572872 | tf_op jit(solution)/shard_map/ppermute | solution.py:41
  86.3 7.2 %collective-permute-start.20 = (bf16[256,512]{1,0:T(8,128)(2,1)S(1)}, bf16[256,512]{1,0:T(8,128)(2,1)S(1)}, u32[]{:S(2)}, u32[]{:S(2)}) collective-permute-start(bf16[256,512]{1,0:T(8,128)(2,1)S(1)} %collective-permute-done.2.rest_6_), channel_id=1, source_target_pairs={{0,4},{4,0},{8,12},{12,8},{16,20},{20,16},{24,28},{28,24},{1,5},{5... | collective-permute-start | bytes 786440 | tf_op jit(solution)/shard_map/ppermute | solution.py:41
  87.9 8.3 %collective-permute-start.21 = (bf16[256,512]{1,0:T(8,128)(2,1)S(1)}, bf16[256,512]{1,0:T(8,128)(2,1)S(1)}, u32[]{:S(2)}, u32[]{:S(2)}) collective-permute-start(bf16[256,512]{1,0:T(8,128)(2,1)S(1)} %collective-permute-done.18.rest_7_), channel_id=1, source_target_pairs={{0,4},{4,0},{8,12},{12,8},{16,20},{20,16},{24,28},{28,24},{1,5},{5... | collective-permute-start | bytes 786440 | tf_op jit(solution)/shard_map/ppermute | solution.py:41
  88.3 7.9 %collective-permute-start.22 = (bf16[512,512]{1,0:T(8,128)(2,1)S(1)}, bf16[512,512]{1,0:T(8,128)(2,1)S(1)}, u32[]{:S(2)}, u32[]{:S(2)}) collective-permute-start(bf16[512,512]{1,0:T(8,128)(2,1)S(1)} %apply_fast.1.rest_0_), channel_id=1, source_target_pairs={{0,1},{1,0},{2,3},{3,2},{4,5},{5,4},{6,7},{7,6},{8,9},{9,8},{10,11... | collective-permute-start | bytes 1572872 | tf_op jit(solution)/shard_map/ppermute | solution.py:41
  96.2 1.9 %collective-permute-start.23 = (bf16[512,512]{1,0:T(8,128)(2,1)S(1)}, bf16[512,512]{1,0:T(8,128)(2,1)S(1)}, u32[]{:S(2)}, u32[]{:S(2)}) collective-permute-start(bf16[512,512]{1,0:T(8,128)(2,1)S(1)} %collective-permute-done.19.rest_1_), channel_id=1, source_target_pairs={{0,1},{1,0},{2,3},{3,2},{4,5},{5,4},{6,7},{7,6},{8,9},{9,8},{10,11... | collective-permute-start | bytes 1572872 | tf_op jit(solution)/shard_map/ppermute | solution.py:41

commit v5 on v4

--- a/solution.py
+++ b/solution.py
@@ -215,13 +215,12 @@
 
 
 def renew_kernel(place, w, momentum, mine, *rest):
-    pieces, (moment, renewed) = rest[:-2], rest[-2:]
+    pieces, renewed = rest[:-1], rest[-1]
     own = mine.shape[1]
     total = mine[...]
     for piece in pieces:
         total = total + piece[...].astype(jnp.float32)
     new = MOMENTUM_DECAY * momentum[0] + total
-    moment[0] = new
     rows = pl.ds(pl.multiple_of(place[2] * own, own), own)
     for i in range(w.shape[1]):
         base = w[0, i, rows, :].astype(jnp.float32)
@@ -231,12 +230,9 @@
 def renew(place, w, momentum, mine, pieces):
     return pl.pallas_call(
         renew_kernel,
-        out_shape=[
-            jax.ShapeDtypeStruct(momentum.shape, jnp.float32),
-            jax.ShapeDtypeStruct(mine.shape, jnp.bfloat16),
-        ],
+        out_shape=jax.ShapeDtypeStruct(mine.shape, jnp.bfloat16),
         in_specs=[pl.BlockSpec(memory_space=pltpu.SMEM)] + [whole_spec()] * (3 + len(pieces)),
-        out_specs=[whole_spec()] * 2,
+        out_specs=whole_spec(),
         compiler_params=params(12),
         cost_estimate=BRIEF,
         name="renew",
@@ -271,36 +267,61 @@
     )(place, q, attended, *units)
 
 
-def project_kernel(tags, rows_in, place, *rest):
-    blocks, units = rest[: len(tags)], rest[len(tags) : -2]
-    mixed, full = rest[-2:]
-    for at, unit in enumerate(units):
+def most_kernel(tags, last, rows_in, offsets, place, *rest):
+    blocks, units = rest[: len(tags)], rest[len(tags) : -3]
+    partial, last_rows, full = rest[-3:]
+    for at, (unit, first) in enumerate(offsets):
         rows = pl.ds(pl.multiple_of(place[ORIGINS + at] * rows_in, rows_in), rows_in)
-        full[rows, :] = unit[unit.shape[0] - rows_in :, :]
+        full[rows, :] = units[unit][first : first + rows_in, :]
     width = blocks[0].shape[1]
     value = None
     for block, tag in zip(blocks, tags):
         rows = pl.ds(pl.multiple_of((place[3] ^ tag) * width, width), width)
         part = matmul(block[...], full[rows, :])
         value = part if value is None else value + part
-    mixed[...] = value.astype(mixed.dtype)
-
-
-def project(place, blocks, tags, near, far, rows_in):
-    tokens = blocks[0].shape[0]
+    partial[...] = value
+    rows = pl.ds(pl.multiple_of((place[3] ^ last) * width, width), width)
+    last_rows[...] = full[rows, :]
+
+
+def project_most(place, blocks, tags, last, near, far, rows_in):
+    tokens, width = blocks[0].shape
     units = near + far
-    depth, width = rows_in * len(units), units[0].shape[1]
-    return pl.pallas_call(
-        functools.partial(project_kernel, tags, rows_in),
-        out_shape=jax.ShapeDtypeStruct((tokens, width), jnp.bfloat16),
+    offsets = [(i, 0) for i in range(len(near))]
+    for i, unit in enumerate(far, len(near)):
+        firsts = range(0, unit.shape[0], rows_in)
+        offsets += [(i, first) for first in (firsts if i > len(near) else firsts[-1:])]
+    columns = near[0].shape[1]
+    return pl.pallas_call(
+        functools.partial(most_kernel, tags, last, rows_in, offsets),
+        out_shape=[
+            jax.ShapeDtypeStruct((tokens, columns), jnp.float32),
+            jax.ShapeDtypeStruct((width, columns), jnp.bfloat16),
+        ],
         in_specs=[pl.BlockSpec(memory_space=pltpu.SMEM)]
         + [whole_spec()] * (len(units) + len(blocks)),
-        out_specs=whole_spec(),
-        scratch_shapes=[pltpu.VMEM((depth, width), jnp.bfloat16)],
-        compiler_params=params(12),
-        cost_estimate=BRIEF,
-        name="project",
+        out_specs=[whole_spec()] * 2,
+        scratch_shapes=[pltpu.VMEM((rows_in * len(offsets), columns), jnp.bfloat16)],
+        compiler_params=params(12),
+        cost_estimate=BRIEF,
+        name="project_most",
     )(place, *blocks, *units)
+
+
+def last_kernel(partial, block, rows, mixed):
+    mixed[...] = (partial[...] + matmul(block[...], rows[...])).astype(mixed.dtype)
+
+
+def project_last(partial, block, rows):
+    return pl.pallas_call(
+        last_kernel,
+        out_shape=jax.ShapeDtypeStruct(partial.shape, jnp.bfloat16),
+        in_specs=[whole_spec()] * 3,
+        out_specs=whole_spec(),
+        compiler_params=params(12),
+        cost_estimate=BRIEF,
+        name="project_last",
+    )(partial, block, rows)
 
 
 def ring_order(outer):
@@ -360,7 +381,7 @@
     ranks = lax.axis_size("seq")
     heads = lax.axis_size("head")
     own_rows = momentum.shape[2]
-    if own_rows % 16 or ranks != 8 or heads % 2 or tok_rows != WINDOW:
+    if own_rows % 16 or ranks != 8 or heads != 4 or tok_rows != WINDOW:
         return plain(queries, keys, values, rates, fast, momentum, out_proj)
     outer = ranks // 2
     grad_scale = 1.0 / math.sqrt(tok_rows * ranks)
@@ -387,35 +408,39 @@
     pieces = [swap(summed[step], "seq", step * 2) for step in range(1, outer)]
     crossed = swap(after(across, summed[1]), "seq", 1)
     pieces[2] = after(pieces[2], crossed)
-    moment, renewed = renew(place, fast, momentum, summed[0], pieces)
+    renewed = renew(place, fast, momentum, summed[0], pieces)
 
     near = [renewed]
     for step in range(1, outer):
         near.append(swap(renewed, "seq", step * 2))
     far = [swap(renewed, "seq", 1)]
+    wide_far = [crossed, swap(after(wide[1], renewed), "seq", 1)]
     near[1] = after(near[1], far[0])
     far += [swap(unit, "seq", 1) for unit in near[1:]]
     attended = window_attention(
         place, queries, keys, values, pair_keys, up_keys, after(crossed, near[1])
     )
-    far[1] = after(far[1], attended)
-    wide_far = [crossed, swap(after(wide[1], near[1]), "seq", 1)]
-    wide.append(ring_step(after(wide[2], near[1], near[2]), outer))
-    far[-1] = after(far[-1], wide_far[1], wide[3])
-    wide_far += [swap(after(unit, far[1]), "seq", 1) for unit in wide[2:]]
+    wide.append(ring_step(after(wide[2], far[1], near[2], near[3], wide_far[1]), outer))
+    rest = jnp.concatenate(wide[2:])
+    far[-1] = after(far[-1], attended, rest)
+    wide_far.append(swap(after(rest, far[1]), "seq", 1))
+
+    total = after(summed[0], near[1])
+    for piece in pieces:
+        total = total + piece.astype(jnp.float32)
+    moment = MOMENTUM_DECAY * momentum + total[None]
+
     combined = apply_fast(place, queries, attended, near + far)
 
-    blocks = [(combined, 0)]
-    mask = heads // 2
-    while mask:
-        moved = [(swap(block, "head", mask), tag ^ mask) for block, tag in blocks]
-        if mask > 1:
-            moved = [(after(block, *wide_far[2:]), tag) for block, tag in moved]
-        blocks = blocks + moved
-        mask //= 2
-    mixed = project(
-        place, [b for b, _ in blocks], [t for _, t in blocks], wide, wide_far, out_proj.shape[0]
-    )
+    crossed_x = swap(combined, "head", 2)
+    other_core = swap(combined, "head", 1)
+    crossed_x = after(crossed_x, wide_far[2])
+    last = swap(crossed_x, "head", 3 ^ 2)
+    held = [out_proj] + wide[1:]
+    partial, rows = project_most(
+        place, [combined, other_core, crossed_x], [0, 1, 2], 3, held, wide_far, out_proj.shape[0]
+    )
+    mixed = project_last(partial, last, rows)
     return (mixed, moment)
 
 

time: 102 us -> 104 us (1.020)
  waiting for transfers between devices: 51.4 us -> 55.1 us
  starting transfers between devices: 29.3 us -> 27.9 us
    ppermute x3, waiting for transfers between devices: 7.02 us -> 12.4 us  [ring_step(): return lax.ppermute(unit, 'seq', pairs)]
    ppermute x19 -> x18, waiting for transfers between devices: 42.2 us -> 40.6 us  [swap(): return lax.ppermute(array, axis, [(i, i ^ mask) for i in range(devices)])]
    ppermute x19 -> x18, starting transfers between devices: 21 us -> 19.9 us  [swap(): return lax.ppermute(array, axis, [(i, i ^ mask) for i in range(devices)])]
    pallas_call x2 -> x3, Pallas kernels: 4.16 us -> 3.72 us  [the longest x1 1.66 us: project_most(): pl.pallas_call(functools.partial(most_kernel, tags, last, rows_in, offset...]
    unnamed x16 -> x17, local copies, waits for them, and re-layouts: 2.48 us -> 2.5 us
  transfers between devices with their start and end apart: 24 -> 23, of which waited for: 15 -> 14; matrix products, arithmetic and copies ran while one was open for 3% -> 3% of each run, Pallas kernels for 6% -> 7%
where the time goes in v5:
time: 104 us
  waiting for transfers between devices  55.1 us (53%)
  starting transfers between devices  27.9 us (27%)
  Pallas kernels  13.9 us (13%)
  local copies, waits for them, and re-layouts  3.21 us (3%)
  other arithmetic  2.78 us (3%)
    ppermute x18, waiting for transfers between devices, swap(): return lax.ppermute(array, axis, [(i, i ^ mask) for i in range(devices)])  40.6 us
    ppermute x18, starting transfers between devices, swap(): return lax.ppermute(array, axis, [(i, i ^ mask) for i in range(devices)])  19.9 us
    ppermute x3, waiting for transfers between devices, ring_step(): return lax.ppermute(unit, 'seq', pairs)  12.4 us
    ppermute x3, starting transfers between devices, ring_step(): return lax.ppermute(unit, 'seq', pairs)  4.02 us
    ppermute x1, starting transfers between devices, shards(): lax.ppermute(up_keys, 'seq', [(s, s + 2) for s in range(0, ranks - 2, 2)])  3.32 us
    pallas_call x1, Pallas kernels, both_gradients(): pl.pallas_call(functools.partial(both_kernel, outer), out_shape=[jax.Shap...  2.83 us
    pallas_call x1, Pallas kernels, own_gradients(): pl.pallas_call(functools.partial(own_kernel, outer), out_shape=jax.ShapeD...  2.77 us
    unnamed x17, local copies, waits for them, and re-layouts  2.5 us
  transfers between devices with their start and end apart: 23, of which 14 were waited for; matrix products, arithmetic and copies ran while one was open for 3% of the time, Pallas kernels for 7%

profile of v5, /device:TPU:0, one launch (start us, length us, event | category | flops | bytes accessed | tf_op | source)
XLA Modules:
  0.0 103.7 jit_solution(14213259085708967415)
XLA Ops:
  0.6 3.1 %collective-permute-start.1 = (bf16[256,512]{1,0:T(8,128)(2,1)}, bf16[256,512]{1,0:T(8,128)(2,1)S(1)}, u32[]{:S(2)}, u32[]{:S(2)}) collective-permute-start(bf16[256,512]{1,0:T(8,128)(2,1)} %rest_3_.1), channel_id=1, source_target_pairs={{0,8},{4,12},{8,24},{12,28},{24,16},{28,20},{16,0},{20,4},{1,9},{5... | collective-permute-start | bytes 786440 | tf_op jit(solution)/shard_map/ppermute | solution.py:337
  3.7 1.5 %collective-permute-start = (bf16[512,512]{1,0:T(8,128)(2,1)}, bf16[512,512]{1,0:T(8,128)(2,1)S(1)}, u32[]{:S(2)}, u32[]{:S(2)}) collective-permute-start(bf16[512,512]{1,0:T(8,128)(2,1)} %k.3), channel_id=1, source_target_pairs={{0,4},{4,0},{8,12},{12,8},{16,20},{20,16},{24,28},{28,24},{1,5},{5... | collective-permute-start | bytes 1572872 | tf_op jit(solution)/shard_map/ppermute | solution.py:41
  5.2 6.0 %collective-permute-done.1.rest_4_ = bf16[256,512]{1,0:T(8,128)(2,1)S(1)} collective-permute-done((bf16[256,512]{1,0:T(8,128)(2,1)}, bf16[256,512]{1,0:T(8,128)(2,1)S(1)}, u32[]{:S(2)}, u32[]{:S(2)}) %collective-permute-start.1) | collective-permute-done | bytes 262176 | tf_op jit(solution)/shard_map/ppermute | solution.py:337
  12.9 1.2 %multiply_convert_fusion.e = bf16[512,512]{1,0:T(8,128)(2,1)S(1)} fusion(bf16[512,512]{1,0:T(8,128)(2,1)} %v.1, f32[512]{0:T(512)S(1)} %bitcast.5), kind=kLoop, calls=%fused_computation | loop fusion | flops 786432 | bytes 1050624 | tf_op jit(solution)/shard_map/convert_element_type | solution.py:392
  14.1 1.6 %collective-permute-start.5 = (bf16[512,512]{1,0:T(8,128)(2,1)S(1)}, bf16[512,512]{1,0:T(8,128)(2,1)S(1)}, u32[]{:S(2)}, u32[]{:S(2)}) collective-permute-start(bf16[512,512]{1,0:T(8,128)(2,1)S(1)} %multiply_convert_fusion.e), channel_id=1, source_target_pairs={{0,4},{4,0},{8,12},{12,8},{16,20},{20,16},{24,28},{28,24},{1,5},{5... | collective-permute-start | bytes 1572872 | tf_op jit(solution)/shard_map/ppermute | solution.py:41
  16.3 3.3 %collective-permute-done.2.rest_5_ = bf16[256,512]{1,0:T(8,128)(2,1)S(1)} collective-permute-done((bf16[256,512]{1,0:T(8,128)(2,1)S(1)}, bf16[256,512]{1,0:T(8,128)(2,1)S(1)}, u32[]{:S(2)}, u32[]{:S(2)}) %collective-permute-start.2) | collective-permute-done | bytes 262176 | tf_op jit(solution)/shard_map/ppermute | solution.py:337
  19.6 3.3 %collective-permute-start.3 = (bf16[512,512]{1,0:T(8,128)(2,1)S(1)}, bf16[512,512]{1,0:T(8,128)(2,1)S(1)}, u32[]{:S(2)}, u32[]{:S(2)}) collective-permute-start(bf16[512,512]{1,0:T(8,128)(2,1)S(1)} %collective-permute-done.k.pair_k), channel_id=1, source_target_pairs={{0,8},{8,16},{16,24},{1,9},{9,17},{17,25},{2,10},{10,18},{18,26},{... | collective-permute-start | bytes 1572872 | tf_op jit(solution)/shard_map/ppermute | solution.py:402
  23.7 1.4 %copy-done = bf16[1,3,512,512]{3,2,1,0:T(8,128)(2,1)S(1)} copy-done((bf16[1,3,512,512]{3,2,1,0:T(8,128)(2,1)S(1)}, bf16[1,3,512,512]{3,2,1,0:T(8,128)(2,1)}, u32[]{:S(2)}) %copy-start) | copy-done | bytes 1572888
  25.1 1.0 %copy-done.3 = bf16[512,512]{1,0:T(8,128)(2,1)S(1)} copy-done((bf16[512,512]{1,0:T(8,128)(2,1)S(1)}, bf16[512,512]{1,0:T(8,128)(2,1)}, u32[]{:S(2)}) %copy-start.3) | copy-done | bytes 524312
  26.1 2.8 %own_gradients.1.acc = f32[4,3,64,512]{3,2,1,0:T(8,128)S(1)} custom-call(s32[12]{0:T(128)S(1)} %dynamic-slice_bitcast_fusion.place, bf16[512,512]{1,0:T(8,128)(2,1)S(1)} %copy-done.3, bf16[512,512]{1,0:T(8,128)(2,1)S(1)} %multiply_convert_fusion.e, bf16[1,3,512,512]{3,2,1,0:T(8,128)(2,1)S(1)} %copy-done), custom_call_target="tpu_custom_call" | custom-call | flops 1 | bytes 1 | tf_op jit(solution)/shard_map/own_gradients/pallas_call | solution.py:122
  29.6 2.2 %collective-permute-done.3.up_k = bf16[512,512]{1,0:T(8,128)(2,1)S(1)} collective-permute-done((bf16[512,512]{1,0:T(8,128)(2,1)S(1)}, bf16[512,512]{1,0:T(8,128)(2,1)S(1)}, u32[]{:S(2)}, u32[]{:S(2)}) %collective-permute-start.3) | collective-permute-done | bytes 524320 | tf_op jit(solution)/shard_map/ppermute | solution.py:402
  31.8 2.8 %both_gradients.1 = (f32[3,64,512]{2,1,0:T(8,128)S(1)}, bf16[3,64,512]{2,1,0:T(8,128)(2,1)S(1)}, bf16[3,64,512]{2,1,0:T(8,128)(2,1)S(1)}, bf16[3,64,512]{2,1,0:T(8,128)(2,1)S(1)}) custom-call(s32[12]{0:T(128)S(1)} %dynamic-slice_bitcast_fusion.place, bf16[512,512]{1,0:T(8,128)(2,1)S(1)} %collective-permute-done.k.pair_k, ...), custom_call_target="tpu_custom_call" | custom-call | flops 1 | bytes 1 | tf_op jit(solution)/shard_map/both_gradients/pallas_call | solution.py:137
  34.9 4.7 %collective-permute-start.9 = (bf16[3,64,512]{2,1,0:T(8,128)(2,1)S(1)}, bf16[3,64,512]{2,1,0:T(8,128)(2,1)S(1)}, u32[]{:S(2)}, u32[]{:S(2)}) collective-permute-start(bf16[3,64,512]{2,1,0:T(8,128)(2,1)S(1)} %get-tuple-element.28), channel_id=1, source_target_pairs={{0,24},{4,28},{8,16},{12,20},{16,8},{20,12},{24,0},{28,4},{1,25},{... | collective-permute-start | bytes 589832 | tf_op jit(solution)/shard_map/ppermute | solution.py:41
  40.3 5.2 %collective-permute-done.9.rest_2_ = bf16[3,64,512]{2,1,0:T(8,128)(2,1)S(1)} collective-permute-done((bf16[3,64,512]{2,1,0:T(8,128)(2,1)S(1)}, bf16[3,64,512]{2,1,0:T(8,128)(2,1)S(1)}, u32[]{:S(2)}, u32[]{:S(2)}) %collective-permute-start.9) | collective-permute-done | bytes 196640 | tf_op jit(solution)/shard_map/ppermute | solution.py:41
  45.6 5.1 %collective-permute-done.6.early_v.rest_7_ = bf16[768,512]{1,0:T(8,128)(2,1)S(1)} collective-permute-done((bf16[768,512]{1,0:T(8,128)(2,1)S(1)}, bf16[768,512]{1,0:T(8,128)(2,1)S(1)}, u32[]{:S(2)}, u32[]{:S(2)}) %collective-permute-start.6) | collective-permute-done | bytes 786464 | tf_op jit(solution)/shard_map/ppermute | solution.py:41
  50.7 4.0 %collective-permute-done.8.rest_1_ = bf16[3,64,512]{2,1,0:T(8,128)(2,1)S(1)} collective-permute-done((bf16[3,64,512]{2,1,0:T(8,128)(2,1)S(1)}, bf16[3,64,512]{2,1,0:T(8,128)(2,1)S(1)}, u32[]{:S(2)}, u32[]{:S(2)}) %collective-permute-start.8) | collective-permute-done | bytes 196640 | tf_op jit(solution)/shard_map/ppermute | solution.py:41
  55.9 1.7 %collective-permute-start.17 = (bf16[256,512]{1,0:T(8,128)(2,1)S(1)}, bf16[256,512]{1,0:T(8,128)(2,1)S(1)}, u32[]{:S(2)}, u32[]{:S(2)}) collective-permute-start(bf16[256,512]{1,0:T(8,128)(2,1)S(1)} %collective-permute-done.1.rest_4_), channel_id=1, source_target_pairs={{0,4},{4,0},{8,12},{12,8},{16,20},{20,16},{24,28},{28,24},{1,5},{5... | collective-permute-start | bytes 786440 | tf_op jit(solution)/shard_map/ppermute | solution.py:41
  57.6 2.7 %collective-permute-start.13 = (bf16[3,64,512]{2,1,0:T(8,128)(2,1)S(1)}, bf16[3,64,512]{2,1,0:T(8,128)(2,1)S(1)}, u32[]{:S(2)}, u32[]{:S(2)}) collective-permute-start(bf16[3,64,512]{2,1,0:T(8,128)(2,1)S(1)} %renew.1.rest_0_), channel_id=1, source_target_pairs={{0,24},{4,28},{8,16},{12,20},{16,8},{20,12},{24,0},{28,4},{1,25},{... | collective-permute-start | bytes 589832 | tf_op jit(solution)/shard_map/ppermute | solution.py:41
  61.1 2.3 %collective-permute-done.11.rest_4_ = bf16[3,64,512]{2,1,0:T(8,128)(2,1)S(1)} collective-permute-done((bf16[3,64,512]{2,1,0:T(8,128)(2,1)S(1)}, bf16[3,64,512]{2,1,0:T(8,128)(2,1)S(1)}, u32[]{:S(2)}, u32[]{:S(2)}) %collective-permute-start.11) | collective-permute-done | bytes 196640 | tf_op jit(solution)/shard_map/ppermute | solution.py:41
  63.7 1.0 collective-permute-start.14
  64.7 3.6 %collective-permute-done.13.rest_3_ = bf16[3,64,512]{2,1,0:T(8,128)(2,1)S(1)} collective-permute-done((bf16[3,64,512]{2,1,0:T(8,128)(2,1)S(1)}, bf16[3,64,512]{2,1,0:T(8,128)(2,1)S(1)}, u32[]{:S(2)}, u32[]{:S(2)}) %collective-permute-start.13) | collective-permute-done | bytes 196640 | tf_op jit(solution)/shard_map/ppermute | solution.py:41
  68.4 7.8 %collective-permute-done.12.rest_2_ = bf16[3,64,512]{2,1,0:T(8,128)(2,1)S(1)} collective-permute-done((bf16[3,64,512]{2,1,0:T(8,128)(2,1)S(1)}, bf16[3,64,512]{2,1,0:T(8,128)(2,1)S(1)}, u32[]{:S(2)}, u32[]{:S(2)}) %collective-permute-start.12) | collective-permute-done | bytes 196640 | tf_op jit(solution)/shard_map/ppermute | solution.py:41
  76.7 1.6 %collective-permute-start.15 = (bf16[3,64,512]{2,1,0:T(8,128)(2,1)S(1)}, bf16[3,64,512]{2,1,0:T(8,128)(2,1)S(1)}, u32[]{:S(2)}, u32[]{:S(2)}) collective-permute-start(bf16[3,64,512]{2,1,0:T(8,128)(2,1)S(1)} %collective-permute-done.12.rest_2_), channel_id=1, source_target_pairs={{0,4},{4,0},{8,12},{12,8},{16,20},{20,16},{24,28},{28,24},{1,5},{5... | collective-permute-start | bytes 589832 | tf_op jit(solution)/shard_map/ppermute | solution.py:41
  78.3 2.3 %window_attention.1.attended = f32[512,512]{1,0:T(8,128)S(1)} custom-call(s32[12]{0:T(128)S(1)} %dynamic-slice_bitcast_fusion.place, bf16[512,512]{1,0:T(8,128)(2,1)S(1)} %copy-done.5, bf16[512,512]{1,0:T(8,128)(2,1)S(1)} %copy-done.4, bf16[512,512]{1,0:T(8,128)(2,1)S(1)} %copy-done.2, bf16[512,512]{1,0:T(8,128)(2,1)S(1)} %collective-permute-done.k.pair_k, ...), custom_call_target="tpu_custom_call" | custom-call | flops 1 | bytes 1 | tf_op jit(solution)/shard_map/window_attention/pallas_call | solution.py:179
  80.6 3.1 %collective-permute-done.18.rest_6_ = bf16[256,512]{1,0:T(8,128)(2,1)S(1)} collective-permute-done((bf16[256,512]{1,0:T(8,128)(2,1)S(1)}, bf16[256,512]{1,0:T(8,128)(2,1)S(1)}, u32[]{:S(2)}, u32[]{:S(2)}) %collective-permute-start.18) | collective-permute-done | bytes 262176 | tf_op jit(solution)/shard_map/ppermute | solution.py:337
  83.7 1.9 %collective-permute-done.15.rest_6_ = bf16[3,64,512]{2,1,0:T(8,128)(2,1)S(1)} collective-permute-done((bf16[3,64,512]{2,1,0:T(8,128)(2,1)S(1)}, bf16[3,64,512]{2,1,0:T(8,128)(2,1)S(1)}, u32[]{:S(2)}, u32[]{:S(2)}) %collective-permute-start.15) | collective-permute-done | bytes 196640 | tf_op jit(solution)/shard_map/ppermute | solution.py:41
  85.7 1.7 %apply_fast.1.rest_0_ = bf16[512,512]{1,0:T(8,128)(2,1)S(1)} custom-call(s32[12]{0:T(128)S(1)} %dynamic-slice_bitcast_fusion.place, bf16[512,512]{1,0:T(8,128)(2,1)S(1)} %copy-done.5, f32[512,512]{1,0:T(8,128)S(1)} %window_attention.1.attended, bf16[3,64,512]{2,1,0:T(8,128)(2,1)S(1)} %renew.1.rest_0_, ...), custom_call_target="tpu_custom_call" | custom-call | flops 1 | bytes 1 | tf_op jit(solution)/shard_map/apply_fast/pallas_call | solution.py:258
  87.4 1.6 %collective-permute-start.20 = (bf16[512,512]{1,0:T(8,128)(2,1)S(1)}, bf16[512,512]{1,0:T(8,128)(2,1)S(1)}, u32[]{:S(2)}, u32[]{:S(2)}) collective-permute-start(bf16[512,512]{1,0:T(8,128)(2,1)S(1)} %apply_fast.1.rest_0_), channel_id=1, source_target_pairs={{0,2},{1,3},{2,0},{3,1},{4,6},{5,7},{6,4},{7,5},{8,10},{9,11},{10,... | collective-permute-start | bytes 1572872 | tf_op jit(solution)/shard_map/ppermute | solution.py:41
  89.7 9.0 %collective-permute-done.20.rest_2_ = bf16[512,512]{1,0:T(8,128)(2,1)S(1)} collective-permute-done((bf16[512,512]{1,0:T(8,128)(2,1)S(1)}, bf16[512,512]{1,0:T(8,128)(2,1)S(1)}, u32[]{:S(2)}, u32[]{:S(2)}) %collective-permute-start.20) | collective-permute-done | bytes 524320 | tf_op jit(solution)/shard_map/ppermute | solution.py:41
  98.7 1.2 %collective-permute-done.21.rest_9_ = bf16[512,512]{1,0:T(8,128)(2,1)S(1)} collective-permute-done((bf16[512,512]{1,0:T(8,128)(2,1)S(1)}, bf16[512,512]{1,0:T(8,128)(2,1)S(1)}, u32[]{:S(2)}, u32[]{:S(2)}) %collective-permute-start.21) | collective-permute-done | bytes 524320 | tf_op jit(solution)/shard_map/ppermute | solution.py:41
  100.9 1.7 %project_most.1 = (f32[512,512]{1,0:T(8,128)S(1)}, bf16[512,512]{1,0:T(8,128)(2,1)S(1)}) custom-call(s32[12]{0:T(128)S(1)} %dynamic-slice_bitcast_fusion.place, bf16[512,512]{1,0:T(8,128)(2,1)S(1)} %apply_fast.1.rest_0_, bf16[512,512]{1,0:T(8,128)(2,1)S(1)} %collective-permute-done.19.rest_1_, bf16[512,512]{1,0:T(8,128)(2,1)S(1)} %collective-permute-done.20.rest_2_, ...), custom_call_target="tpu_custom_call" | custom-call | flops 1 | bytes 1 | tf_op jit(solution)/shard_map/project_most/pallas_call | solution.py:295
  102.5 1.2 %project_last.1 = bf16[512,512]{1,0:T(8,128)(2,1)} custom-call(f32[512,512]{1,0:T(8,128)S(1)} %get-tuple-element.37.partial, bf16[512,512]{1,0:T(8,128)(2,1)S(1)} %collective-permute-done.22.block, bf16[512,512]{1,0:T(8,128)(2,1)S(1)} %get-tuple-element.38.rows), custom_call_target="tpu_custom_call" | custom-call | flops 1 | bytes 1 | tf_op jit(solution)/shard_map/project_last/pallas_call | solution.py:316
  (44 shorter events, 9.2 us)
Async XLA Ops:
  0.6 10.6 %collective-permute-start.1 = (bf16[256,512]{1,0:T(8,128)(2,1)}, bf16[256,512]{1,0:T(8,128)(2,1)S(1)}, u32[]{:S(2)}, u32[]{:S(2)}) collective-permute-start(bf16[256,512]{1,0:T(8,128)(2,1)} %rest_3_.1), channel_id=1, source_target_pairs={{0,8},{4,12},{8,24},{12,28},{24,16},{28,20},{16,0},{20,4},{1,9},{5... | collective-permute-start | bytes 786440 | tf_op jit(solution)/shard_map/ppermute | solution.py:337
  3.7 15.9 %collective-permute-start = (bf16[512,512]{1,0:T(8,128)(2,1)}, bf16[512,512]{1,0:T(8,128)(2,1)S(1)}, u32[]{:S(2)}, u32[]{:S(2)}) collective-permute-start(bf16[512,512]{1,0:T(8,128)(2,1)} %k.3), channel_id=1, source_target_pairs={{0,4},{4,0},{8,12},{12,8},{16,20},{20,16},{24,28},{28,24},{1,5},{5... | collective-permute-start | bytes 1572872 | tf_op jit(solution)/shard_map/ppermute | solution.py:41
  11.2 8.4 %collective-permute-start.2 = (bf16[256,512]{1,0:T(8,128)(2,1)S(1)}, bf16[256,512]{1,0:T(8,128)(2,1)S(1)}, u32[]{:S(2)}, u32[]{:S(2)}) collective-permute-start(bf16[256,512]{1,0:T(8,128)(2,1)S(1)} %collective-permute-done.1.rest_4_), channel_id=1, source_target_pairs={{0,8},{4,12},{8,24},{12,28},{24,16},{28,20},{16,0},{20,4},{1,9},{5... | collective-permute-start | bytes 786440 | tf_op jit(solution)/shard_map/ppermute | solution.py:337
  14.1 15.5 %collective-permute-start.5 = (bf16[512,512]{1,0:T(8,128)(2,1)S(1)}, bf16[512,512]{1,0:T(8,128)(2,1)S(1)}, u32[]{:S(2)}, u32[]{:S(2)}) collective-permute-start(bf16[512,512]{1,0:T(8,128)(2,1)S(1)} %multiply_convert_fusion.e), channel_id=1, source_target_pairs={{0,4},{4,0},{8,12},{12,8},{16,20},{20,16},{24,28},{28,24},{1,5},{5... | collective-permute-start | bytes 1572872 | tf_op jit(solution)/shard_map/ppermute | solution.py:41
  15.7 13.3 %collective-permute-start.4 = (bf16[512,512]{1,0:T(8,128)(2,1)}, bf16[512,512]{1,0:T(8,128)(2,1)S(1)}, u32[]{:S(2)}, u32[]{:S(2)}) collective-permute-start(bf16[512,512]{1,0:T(8,128)(2,1)} %v.1), channel_id=1, source_target_pairs={{4,12},{12,20},{20,28},{5,13},{13,21},{21,29},{6,14},{14,22},{22,3... | collective-permute-start | bytes 1572872 | tf_op jit(solution)/shard_map/ppermute | solution.py:400
  19.6 12.1 %collective-permute-start.3 = (bf16[512,512]{1,0:T(8,128)(2,1)S(1)}, bf16[512,512]{1,0:T(8,128)(2,1)S(1)}, u32[]{:S(2)}, u32[]{:S(2)}) collective-permute-start(bf16[512,512]{1,0:T(8,128)(2,1)S(1)} %collective-permute-done.k.pair_k), channel_id=1, source_target_pairs={{0,8},{8,16},{16,24},{1,9},{9,17},{17,25},{2,10},{10,18},{18,26},{... | collective-permute-start | bytes 1572872 | tf_op jit(solution)/shard_map/ppermute | solution.py:402
  23.7 1.4 %copy-start = (bf16[1,3,512,512]{3,2,1,0:T(8,128)(2,1)S(1)}, bf16[1,3,512,512]{3,2,1,0:T(8,128)(2,1)}, u32[]{:S(2)}) copy-start(bf16[1,3,512,512]{3,2,1,0:T(8,128)(2,1)} %w.5) | copy-start | bytes 4718596
  25.1 1.0 %copy-start.3 = (bf16[512,512]{1,0:T(8,128)(2,1)S(1)}, bf16[512,512]{1,0:T(8,128)(2,1)}, u32[]{:S(2)}) copy-start(bf16[512,512]{1,0:T(8,128)(2,1)} %k.3) | copy-start | bytes 1572868
  26.1 2.8 %copy-start.2 = (bf16[512,512]{1,0:T(8,128)(2,1)S(1)}, bf16[512,512]{1,0:T(8,128)(2,1)}, u32[]{:S(2)}) copy-start(bf16[512,512]{1,0:T(8,128)(2,1)} %v.1) | copy-start | bytes 1572868
  26.1 2.8 %copy-start.7 = (bf16[256,512]{1,0:T(8,128)(2,1)S(1)}, bf16[256,512]{1,0:T(8,128)(2,1)}, u32[]{:S(2)}) copy-start(bf16[256,512]{1,0:T(8,128)(2,1)} %rest_3_.1) | copy-start | bytes 786436
  28.9 2.9 %copy-start.1 = (bf16[1,3,512,512]{3,2,1,0:T(8,128)(2,1)S(1)}, bf16[1,3,512,512]{3,2,1,0:T(8,128)(2,1)}, u32[]{:S(2)}) copy-start(bf16[1,3,512,512]{3,2,1,0:T(8,128)(2,1)} %w.5) | copy-start | bytes 4718596
  29.6 25.1 %copy-start.6 = (f32[1,3,64,512]{3,2,1,0:T(8,128)S(1)}, f32[1,3,64,512]{3,2,1,0:T(8,128)}, u32[]{:S(2)}) copy-start(f32[1,3,64,512]{3,2,1,0:T(8,128)} %momentum.1) | copy-start | bytes 1179652
  34.6 16.1 %collective-permute-start.6 = (bf16[768,512]{1,0:T(8,128)(2,1)S(1)}, bf16[768,512]{1,0:T(8,128)(2,1)S(1)}, u32[]{:S(2)}, u32[]{:S(2)}) collective-permute-start(bf16[768,512]{1,0:T(8,128)(2,1)S(1)} %crossing.1), channel_id=1, source_target_pairs={{0,4},{4,0},{8,12},{12,8},{16,20},{20,16},{24,28},{28,24},{1,5},{5... | collective-permute-start | bytes 2359304 | tf_op jit(solution)/shard_map/ppermute | solution.py:41
  34.9 10.6 %collective-permute-start.9 = (bf16[3,64,512]{2,1,0:T(8,128)(2,1)S(1)}, bf16[3,64,512]{2,1,0:T(8,128)(2,1)S(1)}, u32[]{:S(2)}, u32[]{:S(2)}) collective-permute-start(bf16[3,64,512]{2,1,0:T(8,128)(2,1)S(1)} %get-tuple-element.28), channel_id=1, source_target_pairs={{0,24},{4,28},{8,16},{12,20},{16,8},{20,12},{24,0},{28,4},{1,25},{... | collective-permute-start | bytes 589832 | tf_op jit(solution)/shard_map/ppermute | solution.py:41
  39.7 15.0 %collective-permute-start.8 = (bf16[3,64,512]{2,1,0:T(8,128)(2,1)S(1)}, bf16[3,64,512]{2,1,0:T(8,128)(2,1)S(1)}, u32[]{:S(2)}, u32[]{:S(2)}) collective-permute-start(bf16[3,64,512]{2,1,0:T(8,128)(2,1)S(1)} %get-tuple-element.27), channel_id=1, source_target_pairs={{0,16},{4,20},{8,24},{12,28},{16,0},{20,4},{24,8},{28,12},{1,17},{... | collective-permute-start | bytes 589832 | tf_op jit(solution)/shard_map/ppermute | solution.py:41
  39.7 15.0 %collective-permute-start.7 = (bf16[3,64,512]{2,1,0:T(8,128)(2,1)S(1)}, bf16[3,64,512]{2,1,0:T(8,128)(2,1)S(1)}, u32[]{:S(2)}, u32[]{:S(2)}) collective-permute-start(bf16[3,64,512]{2,1,0:T(8,128)(2,1)S(1)} %get-tuple-element.24), channel_id=1, source_target_pairs={{0,8},{4,12},{8,0},{12,4},{16,24},{20,28},{24,16},{28,20},{1,9},{5... | collective-permute-start | bytes 589832 | tf_op jit(solution)/shard_map/ppermute | solution.py:41
  54.7 23.7 %copy-start.4 = (bf16[512,512]{1,0:T(8,128)(2,1)S(1)}, bf16[512,512]{1,0:T(8,128)(2,1)}, u32[]{:S(2)}) copy-start(bf16[512,512]{1,0:T(8,128)(2,1)} %k.3) | copy-start | bytes 1572868
  54.7 23.7 %copy-start.5 = (bf16[512,512]{1,0:T(8,128)(2,1)S(1)}, bf16[512,512]{1,0:T(8,128)(2,1)}, u32[]{:S(2)}) copy-start(bf16[512,512]{1,0:T(8,128)(2,1)} %q.3) | copy-start | bytes 1572868
  55.5 7.9 %collective-permute-start.11 = (bf16[3,64,512]{2,1,0:T(8,128)(2,1)S(1)}, bf16[3,64,512]{2,1,0:T(8,128)(2,1)S(1)}, u32[]{:S(2)}, u32[]{:S(2)}) collective-permute-start(bf16[3,64,512]{2,1,0:T(8,128)(2,1)S(1)} %renew.1.rest_0_), channel_id=1, source_target_pairs={{0,4},{4,0},{8,12},{12,8},{16,20},{20,16},{24,28},{28,24},{1,5},{5... | collective-permute-start | bytes 589832 | tf_op jit(solution)/shard_map/ppermute | solution.py:41
  55.9 7.8 %collective-permute-start.10 = (bf16[3,64,512]{2,1,0:T(8,128)(2,1)S(1)}, bf16[3,64,512]{2,1,0:T(8,128)(2,1)S(1)}, u32[]{:S(2)}, u32[]{:S(2)}) collective-permute-start(bf16[3,64,512]{2,1,0:T(8,128)(2,1)S(1)} %renew.1.rest_0_), channel_id=1, source_target_pairs={{0,8},{4,12},{8,0},{12,4},{16,24},{20,28},{24,16},{28,20},{1,9},{5... | collective-permute-start | bytes 589832 | tf_op jit(solution)/shard_map/ppermute | solution.py:41
  55.9 20.2 %collective-permute-start.17 = (bf16[256,512]{1,0:T(8,128)(2,1)S(1)}, bf16[256,512]{1,0:T(8,128)(2,1)S(1)}, u32[]{:S(2)}, u32[]{:S(2)}) collective-permute-start(bf16[256,512]{1,0:T(8,128)(2,1)S(1)} %collective-permute-done.1.rest_4_), channel_id=1, source_target_pairs={{0,4},{4,0},{8,12},{12,8},{16,20},{20,16},{24,28},{28,24},{1,5},{5... | collective-permute-start | bytes 786440 | tf_op jit(solution)/shard_map/ppermute | solution.py:41
  57.6 10.8 %collective-permute-start.13 = (bf16[3,64,512]{2,1,0:T(8,128)(2,1)S(1)}, bf16[3,64,512]{2,1,0:T(8,128)(2,1)S(1)}, u32[]{:S(2)}, u32[]{:S(2)}) collective-permute-start(bf16[3,64,512]{2,1,0:T(8,128)(2,1)S(1)} %renew.1.rest_0_), channel_id=1, source_target_pairs={{0,24},{4,28},{8,16},{12,20},{16,8},{20,12},{24,0},{28,4},{1,25},{... | collective-permute-start | bytes 589832 | tf_op jit(solution)/shard_map/ppermute | solution.py:41
  60.3 15.9 %collective-permute-start.12 = (bf16[3,64,512]{2,1,0:T(8,128)(2,1)S(1)}, bf16[3,64,512]{2,1,0:T(8,128)(2,1)S(1)}, u32[]{:S(2)}, u32[]{:S(2)}) collective-permute-start(bf16[3,64,512]{2,1,0:T(8,128)(2,1)S(1)} %renew.1.rest_0_), channel_id=1, source_target_pairs={{0,16},{4,20},{8,24},{12,28},{16,0},{20,4},{24,8},{28,12},{1,17},{... | collective-permute-start | bytes 589832 | tf_op jit(solution)/shard_map/ppermute | solution.py:41
  63.7 12.5 %collective-permute-start.14 = (bf16[3,64,512]{2,1,0:T(8,128)(2,1)S(1)}, bf16[3,64,512]{2,1,0:T(8,128)(2,1)S(1)}, u32[]{:S(2)}, u32[]{:S(2)}) collective-permute-start(bf16[3,64,512]{2,1,0:T(8,128)(2,1)S(1)} %collective-permute-done.10.rest_1_), channel_id=1, source_target_pairs={{0,4},{4,0},{8,12},{12,8},{16,20},{20,16},{24,28},{28,24},{1,5},{5... | collective-permute-start | bytes 589832 | tf_op jit(solution)/shard_map/ppermute | solution.py:41
  76.2 7.5 %collective-permute-start.18 = (bf16[256,512]{1,0:T(8,128)(2,1)S(1)}, bf16[256,512]{1,0:T(8,128)(2,1)S(1)}, u32[]{:S(2)}, u32[]{:S(2)}) collective-permute-start(bf16[256,512]{1,0:T(8,128)(2,1)S(1)} %collective-permute-done.2.rest_5_), channel_id=1, source_target_pairs={{0,8},{4,12},{8,24},{12,28},{24,16},{28,20},{16,0},{20,4},{1,9},{5... | collective-permute-start | bytes 786440 | tf_op jit(solution)/shard_map/ppermute | solution.py:337
  76.2 7.5 %collective-permute-start.16 = (bf16[3,64,512]{2,1,0:T(8,128)(2,1)S(1)}, bf16[3,64,512]{2,1,0:T(8,128)(2,1)S(1)}, u32[]{:S(2)}, u32[]{:S(2)}) collective-permute-start(bf16[3,64,512]{2,1,0:T(8,128)(2,1)S(1)} %collective-permute-done.13.rest_3_), channel_id=1, source_target_pairs={{0,4},{4,0},{8,12},{12,8},{16,20},{20,16},{24,28},{28,24},{1,5},{5... | collective-permute-start | bytes 589832 | tf_op jit(solution)/shard_map/ppermute | solution.py:41
  76.7 9.0 %collective-permute-start.15 = (bf16[3,64,512]{2,1,0:T(8,128)(2,1)S(1)}, bf16[3,64,512]{2,1,0:T(8,128)(2,1)S(1)}, u32[]{:S(2)}, u32[]{:S(2)}) collective-permute-start(bf16[3,64,512]{2,1,0:T(8,128)(2,1)S(1)} %collective-permute-done.12.rest_2_), channel_id=1, source_target_pairs={{0,4},{4,0},{8,12},{12,8},{16,20},{20,16},{24,28},{28,24},{1,5},{5... | collective-permute-start | bytes 589832 | tf_op jit(solution)/shard_map/ppermute | solution.py:41
  87.4 11.4 %collective-permute-start.20 = (bf16[512,512]{1,0:T(8,128)(2,1)S(1)}, bf16[512,512]{1,0:T(8,128)(2,1)S(1)}, u32[]{:S(2)}, u32[]{:S(2)}) collective-permute-start(bf16[512,512]{1,0:T(8,128)(2,1)S(1)} %apply_fast.1.rest_0_), channel_id=1, source_target_pairs={{0,2},{1,3},{2,0},{3,1},{4,6},{5,7},{6,4},{7,5},{8,10},{9,11},{10,... | collective-permute-start | bytes 1572872 | tf_op jit(solution)/shard_map/ppermute | solution.py:41
  88.9 11.0 %collective-permute-start.21 = (bf16[512,512]{1,0:T(8,128)(2,1)S(1)}, bf16[512,512]{1,0:T(8,128)(2,1)S(1)}, u32[]{:S(2)}, u32[]{:S(2)}) collective-permute-start(bf16[512,512]{1,0:T(8,128)(2,1)S(1)} %constant_dynamic-update-slice_fusion), channel_id=1, source_target_pairs={{0,4},{4,0},{8,12},{12,8},{16,20},{20,16},{24,28},{28,24},{1,5},{5... | collective-permute-start | bytes 1572872 | tf_op jit(solution)/shard_map/ppermute | solution.py:41
  89.7 11.2 %collective-permute-start.19 = (bf16[512,512]{1,0:T(8,128)(2,1)S(1)}, bf16[512,512]{1,0:T(8,128)(2,1)S(1)}, u32[]{:S(2)}, u32[]{:S(2)}) collective-permute-start(bf16[512,512]{1,0:T(8,128)(2,1)S(1)} %apply_fast.1.rest_0_), channel_id=1, source_target_pairs={{0,1},{1,0},{2,3},{3,2},{4,5},{5,4},{6,7},{7,6},{8,9},{9,8},{10,11... | collective-permute-start | bytes 1572872 | tf_op jit(solution)/shard_map/ppermute | solution.py:41
  100.0 2.6 %collective-permute-start.22 = (bf16[512,512]{1,0:T(8,128)(2,1)S(1)}, bf16[512,512]{1,0:T(8,128)(2,1)S(1)}, u32[]{:S(2)}, u32[]{:S(2)}) collective-permute-start(bf16[512,512]{1,0:T(8,128)(2,1)S(1)} %collective-permute-done.20.rest_2_), channel_id=1, source_target_pairs={{0,1},{1,0},{2,3},{3,2},{4,5},{5,4},{6,7},{7,6},{8,9},{9,8},{10,11... | collective-permute-start | bytes 1572872 | tf_op jit(solution)/shard_map/ppermute | solution.py:41

commit v6 on v5

--- a/solution.py
+++ b/solution.py
@@ -414,21 +414,22 @@
     for step in range(1, outer):
         near.append(swap(renewed, "seq", step * 2))
     far = [swap(renewed, "seq", 1)]
-    wide_far = [crossed, swap(after(wide[1], renewed), "seq", 1)]
+    wide_far = [crossed, swap(after(wide[1], near[1]), "seq", 1)]
     near[1] = after(near[1], far[0])
     far += [swap(unit, "seq", 1) for unit in near[1:]]
     attended = window_attention(
         place, queries, keys, values, pair_keys, up_keys, after(crossed, near[1])
     )
-    wide.append(ring_step(after(wide[2], far[1], near[2], near[3], wide_far[1]), outer))
+    wide.append(ring_step(after(wide[2], far[1], near[2], near[3]), outer))
     rest = jnp.concatenate(wide[2:])
-    far[-1] = after(far[-1], attended, rest)
-    wide_far.append(swap(after(rest, far[1]), "seq", 1))
 
     total = after(summed[0], near[1])
     for piece in pieces:
         total = total + piece.astype(jnp.float32)
     moment = MOMENTUM_DECAY * momentum + total[None]
+
+    far[-1] = after(far[-1], attended, rest, wide_far[1], moment)
+    wide_far.append(swap(after(rest, far[1]), "seq", 1))
 
     combined = apply_fast(place, queries, attended, near + far)
 

time: 104 us -> 102 us (0.981)
    ppermute x18, waiting for transfers between devices: 40.6 us -> 38.1 us  [swap(): return lax.ppermute(array, axis, [(i, i ^ mask) for i in range(devices)])]
    ppermute x3, waiting for transfers between devices: 12.4 us -> 13.8 us  [ring_step(): return lax.ppermute(unit, 'seq', pairs)]
where the time goes in v6:
time: 102 us
  waiting for transfers between devices  54.1 us (53%)
  starting transfers between devices  27.1 us (27%)
  Pallas kernels  13.9 us (14%)
  local copies, waits for them, and re-layouts  3.22 us (3%)
  other arithmetic  2.78 us (3%)
    ppermute x18, waiting for transfers between devices, swap(): return lax.ppermute(array, axis, [(i, i ^ mask) for i in range(devices)])  38.1 us
    ppermute x18, starting transfers between devices, swap(): return lax.ppermute(array, axis, [(i, i ^ mask) for i in range(devices)])  19 us
    ppermute x3, waiting for transfers between devices, ring_step(): return lax.ppermute(unit, 'seq', pairs)  13.8 us
    ppermute x3, starting transfers between devices, ring_step(): return lax.ppermute(unit, 'seq', pairs)  4.02 us
    ppermute x1, starting transfers between devices, shards(): lax.ppermute(up_keys, 'seq', [(s, s + 2) for s in range(0, ranks - 2, 2)])  3.32 us
    pallas_call x1, Pallas kernels, both_gradients(): pl.pallas_call(functools.partial(both_kernel, outer), out_shape=[jax.Shap...  2.83 us
    pallas_call x1, Pallas kernels, own_gradients(): pl.pallas_call(functools.partial(own_kernel, outer), out_shape=jax.ShapeD...  2.77 us
    unnamed x17, local copies, waits for them, and re-layouts  2.5 us
  transfers between devices with their start and end apart: 23, of which 14 were waited for; matrix products, arithmetic and copies ran while one was open for 3% of the time, Pallas kernels for 7%

profile of v6, /device:TPU:0, one launch (start us, length us, event | category | flops | bytes accessed | tf_op | source)
XLA Modules:
  0.0 101.9 jit_solution(12839017585693693932)
XLA Ops:
  0.6 3.1 %collective-permute-start.1 = (bf16[256,512]{1,0:T(8,128)(2,1)}, bf16[256,512]{1,0:T(8,128)(2,1)S(1)}, u32[]{:S(2)}, u32[]{:S(2)}) collective-permute-start(bf16[256,512]{1,0:T(8,128)(2,1)} %rest_3_.1), channel_id=1, source_target_pairs={{0,8},{4,12},{8,24},{12,28},{24,16},{28,20},{16,0},{20,4},{1,9},{5... | collective-permute-start | bytes 786440 | tf_op jit(solution)/shard_map/ppermute | solution.py:337
  3.7 1.5 %collective-permute-start = (bf16[512,512]{1,0:T(8,128)(2,1)}, bf16[512,512]{1,0:T(8,128)(2,1)S(1)}, u32[]{:S(2)}, u32[]{:S(2)}) collective-permute-start(bf16[512,512]{1,0:T(8,128)(2,1)} %k.3), channel_id=1, source_target_pairs={{0,4},{4,0},{8,12},{12,8},{16,20},{20,16},{24,28},{28,24},{1,5},{5... | collective-permute-start | bytes 1572872 | tf_op jit(solution)/shard_map/ppermute | solution.py:41
  5.2 6.0 %collective-permute-done.1.rest_4_ = bf16[256,512]{1,0:T(8,128)(2,1)S(1)} collective-permute-done((bf16[256,512]{1,0:T(8,128)(2,1)}, bf16[256,512]{1,0:T(8,128)(2,1)S(1)}, u32[]{:S(2)}, u32[]{:S(2)}) %collective-permute-start.1) | collective-permute-done | bytes 262176 | tf_op jit(solution)/shard_map/ppermute | solution.py:337
  11.2 0.9 collective-permute-start.2
  12.9 1.2 %multiply_convert_fusion.e = bf16[512,512]{1,0:T(8,128)(2,1)S(1)} fusion(bf16[512,512]{1,0:T(8,128)(2,1)} %v.1, f32[512]{0:T(512)S(1)} %bitcast.5), kind=kLoop, calls=%fused_computation | loop fusion | flops 786432 | bytes 1050624 | tf_op jit(solution)/shard_map/convert_element_type | solution.py:392
  14.1 1.6 %collective-permute-start.5 = (bf16[512,512]{1,0:T(8,128)(2,1)S(1)}, bf16[512,512]{1,0:T(8,128)(2,1)S(1)}, u32[]{:S(2)}, u32[]{:S(2)}) collective-permute-start(bf16[512,512]{1,0:T(8,128)(2,1)S(1)} %multiply_convert_fusion.e), channel_id=1, source_target_pairs={{0,4},{4,0},{8,12},{12,8},{16,20},{20,16},{24,28},{28,24},{1,5},{5... | collective-permute-start | bytes 1572872 | tf_op jit(solution)/shard_map/ppermute | solution.py:41
  16.3 3.3 %collective-permute-done.2.rest_5_ = bf16[256,512]{1,0:T(8,128)(2,1)S(1)} collective-permute-done((bf16[256,512]{1,0:T(8,128)(2,1)S(1)}, bf16[256,512]{1,0:T(8,128)(2,1)S(1)}, u32[]{:S(2)}, u32[]{:S(2)}) %collective-permute-start.2) | collective-permute-done | bytes 262176 | tf_op jit(solution)/shard_map/ppermute | solution.py:337
  19.6 3.3 %collective-permute-start.3 = (bf16[512,512]{1,0:T(8,128)(2,1)S(1)}, bf16[512,512]{1,0:T(8,128)(2,1)S(1)}, u32[]{:S(2)}, u32[]{:S(2)}) collective-permute-start(bf16[512,512]{1,0:T(8,128)(2,1)S(1)} %collective-permute-done.k.pair_k), channel_id=1, source_target_pairs={{0,8},{8,16},{16,24},{1,9},{9,17},{17,25},{2,10},{10,18},{18,26},{... | collective-permute-start | bytes 1572872 | tf_op jit(solution)/shard_map/ppermute | solution.py:402
  23.7 1.4 %copy-done = bf16[1,3,512,512]{3,2,1,0:T(8,128)(2,1)S(1)} copy-done((bf16[1,3,512,512]{3,2,1,0:T(8,128)(2,1)S(1)}, bf16[1,3,512,512]{3,2,1,0:T(8,128)(2,1)}, u32[]{:S(2)}) %copy-start) | copy-done | bytes 1572888
  25.1 1.0 %copy-done.3 = bf16[512,512]{1,0:T(8,128)(2,1)S(1)} copy-done((bf16[512,512]{1,0:T(8,128)(2,1)S(1)}, bf16[512,512]{1,0:T(8,128)(2,1)}, u32[]{:S(2)}) %copy-start.3) | copy-done | bytes 524312
  26.1 2.8 %own_gradients.1.acc = f32[4,3,64,512]{3,2,1,0:T(8,128)S(1)} custom-call(s32[12]{0:T(128)S(1)} %dynamic-slice_bitcast_fusion.place, bf16[512,512]{1,0:T(8,128)(2,1)S(1)} %copy-done.3, bf16[512,512]{1,0:T(8,128)(2,1)S(1)} %multiply_convert_fusion.e, bf16[1,3,512,512]{3,2,1,0:T(8,128)(2,1)S(1)} %copy-done), custom_call_target="tpu_custom_call" | custom-call | flops 1 | bytes 1 | tf_op jit(solution)/shard_map/own_gradients/pallas_call | solution.py:122
  29.6 2.2 %collective-permute-done.3.up_k = bf16[512,512]{1,0:T(8,128)(2,1)S(1)} collective-permute-done((bf16[512,512]{1,0:T(8,128)(2,1)S(1)}, bf16[512,512]{1,0:T(8,128)(2,1)S(1)}, u32[]{:S(2)}, u32[]{:S(2)}) %collective-permute-start.3) | collective-permute-done | bytes 524320 | tf_op jit(solution)/shard_map/ppermute | solution.py:402
  31.8 2.8 %both_gradients.1 = (f32[3,64,512]{2,1,0:T(8,128)S(1)}, bf16[3,64,512]{2,1,0:T(8,128)(2,1)S(1)}, bf16[3,64,512]{2,1,0:T(8,128)(2,1)S(1)}, bf16[3,64,512]{2,1,0:T(8,128)(2,1)S(1)}) custom-call(s32[12]{0:T(128)S(1)} %dynamic-slice_bitcast_fusion.place, bf16[512,512]{1,0:T(8,128)(2,1)S(1)} %collective-permute-done.k.pair_k, ...), custom_call_target="tpu_custom_call" | custom-call | flops 1 | bytes 1 | tf_op jit(solution)/shard_map/both_gradients/pallas_call | solution.py:137
  34.9 4.7 %collective-permute-start.9 = (bf16[3,64,512]{2,1,0:T(8,128)(2,1)S(1)}, bf16[3,64,512]{2,1,0:T(8,128)(2,1)S(1)}, u32[]{:S(2)}, u32[]{:S(2)}) collective-permute-start(bf16[3,64,512]{2,1,0:T(8,128)(2,1)S(1)} %get-tuple-element.28), channel_id=1, source_target_pairs={{0,24},{4,28},{8,16},{12,20},{16,8},{20,12},{24,0},{28,4},{1,25},{... | collective-permute-start | bytes 589832 | tf_op jit(solution)/shard_map/ppermute | solution.py:41
  40.3 5.2 %collective-permute-done.9.rest_2_ = bf16[3,64,512]{2,1,0:T(8,128)(2,1)S(1)} collective-permute-done((bf16[3,64,512]{2,1,0:T(8,128)(2,1)S(1)}, bf16[3,64,512]{2,1,0:T(8,128)(2,1)S(1)}, u32[]{:S(2)}, u32[]{:S(2)}) %collective-permute-start.9) | collective-permute-done | bytes 196640 | tf_op jit(solution)/shard_map/ppermute | solution.py:41
  45.6 5.1 %collective-permute-done.6.early_v.rest_7_ = bf16[768,512]{1,0:T(8,128)(2,1)S(1)} collective-permute-done((bf16[768,512]{1,0:T(8,128)(2,1)S(1)}, bf16[768,512]{1,0:T(8,128)(2,1)S(1)}, u32[]{:S(2)}, u32[]{:S(2)}) %collective-permute-start.6) | collective-permute-done | bytes 786464 | tf_op jit(solution)/shard_map/ppermute | solution.py:41
  50.7 4.0 %collective-permute-done.8.rest_1_ = bf16[3,64,512]{2,1,0:T(8,128)(2,1)S(1)} collective-permute-done((bf16[3,64,512]{2,1,0:T(8,128)(2,1)S(1)}, bf16[3,64,512]{2,1,0:T(8,128)(2,1)S(1)}, u32[]{:S(2)}, u32[]{:S(2)}) %collective-permute-start.8) | collective-permute-done | bytes 196640 | tf_op jit(solution)/shard_map/ppermute | solution.py:41
  55.9 3.1 %collective-permute-start.13 = (bf16[3,64,512]{2,1,0:T(8,128)(2,1)S(1)}, bf16[3,64,512]{2,1,0:T(8,128)(2,1)S(1)}, u32[]{:S(2)}, u32[]{:S(2)}) collective-permute-start(bf16[3,64,512]{2,1,0:T(8,128)(2,1)S(1)} %renew.1.rest_0_), channel_id=1, source_target_pairs={{0,24},{4,28},{8,16},{12,20},{16,8},{20,12},{24,0},{28,4},{1,25},{... | collective-permute-start | bytes 589832 | tf_op jit(solution)/shard_map/ppermute | solution.py:41
  59.6 1.6 %collective-permute-done.11.rest_4_ = bf16[3,64,512]{2,1,0:T(8,128)(2,1)S(1)} collective-permute-done((bf16[3,64,512]{2,1,0:T(8,128)(2,1)S(1)}, bf16[3,64,512]{2,1,0:T(8,128)(2,1)S(1)}, u32[]{:S(2)}, u32[]{:S(2)}) %collective-permute-start.11) | collective-permute-done | bytes 196640 | tf_op jit(solution)/shard_map/ppermute | solution.py:41
  61.3 3.3 %collective-permute-done.10.rest_1_ = bf16[3,64,512]{2,1,0:T(8,128)(2,1)S(1)} collective-permute-done((bf16[3,64,512]{2,1,0:T(8,128)(2,1)S(1)}, bf16[3,64,512]{2,1,0:T(8,128)(2,1)S(1)}, u32[]{:S(2)}, u32[]{:S(2)}) %collective-permute-start.10) | collective-permute-done | bytes 196640 | tf_op jit(solution)/shard_map/ppermute | solution.py:41
  64.8 1.9 %collective-permute-start.18 = (bf16[256,512]{1,0:T(8,128)(2,1)S(1)}, bf16[256,512]{1,0:T(8,128)(2,1)S(1)}, u32[]{:S(2)}, u32[]{:S(2)}) collective-permute-start(bf16[256,512]{1,0:T(8,128)(2,1)S(1)} %collective-permute-done.1.rest_4_), channel_id=1, source_target_pairs={{0,4},{4,0},{8,12},{12,8},{16,20},{20,16},{24,28},{28,24},{1,5},{5... | collective-permute-start | bytes 786440 | tf_op jit(solution)/shard_map/ppermute | solution.py:41
  66.7 1.6 %collective-permute-done.13.rest_3_ = bf16[3,64,512]{2,1,0:T(8,128)(2,1)S(1)} collective-permute-done((bf16[3,64,512]{2,1,0:T(8,128)(2,1)S(1)}, bf16[3,64,512]{2,1,0:T(8,128)(2,1)S(1)}, u32[]{:S(2)}, u32[]{:S(2)}) %collective-permute-start.13) | collective-permute-done | bytes 196640 | tf_op jit(solution)/shard_map/ppermute | solution.py:41
  68.9 6.0 %collective-permute-done.12.rest_2_ = bf16[3,64,512]{2,1,0:T(8,128)(2,1)S(1)} collective-permute-done((bf16[3,64,512]{2,1,0:T(8,128)(2,1)S(1)}, bf16[3,64,512]{2,1,0:T(8,128)(2,1)S(1)}, u32[]{:S(2)}, u32[]{:S(2)}) %collective-permute-start.12) | collective-permute-done | bytes 196640 | tf_op jit(solution)/shard_map/ppermute | solution.py:41
  74.9 1.6 %collective-permute-start.15 = (bf16[3,64,512]{2,1,0:T(8,128)(2,1)S(1)}, bf16[3,64,512]{2,1,0:T(8,128)(2,1)S(1)}, u32[]{:S(2)}, u32[]{:S(2)}) collective-permute-start(bf16[3,64,512]{2,1,0:T(8,128)(2,1)S(1)} %collective-permute-done.12.rest_2_), channel_id=1, source_target_pairs={{0,4},{4,0},{8,12},{12,8},{16,20},{20,16},{24,28},{28,24},{1,5},{5... | collective-permute-start | bytes 589832 | tf_op jit(solution)/shard_map/ppermute | solution.py:41
  77.4 2.3 %window_attention.1.attended = f32[512,512]{1,0:T(8,128)S(1)} custom-call(s32[12]{0:T(128)S(1)} %dynamic-slice_bitcast_fusion.place, bf16[512,512]{1,0:T(8,128)(2,1)S(1)} %copy-done.5, bf16[512,512]{1,0:T(8,128)(2,1)S(1)} %copy-done.4, bf16[512,512]{1,0:T(8,128)(2,1)S(1)} %copy-done.2, bf16[512,512]{1,0:T(8,128)(2,1)S(1)} %collective-permute-done.k.pair_k, ...), custom_call_target="tpu_custom_call" | custom-call | flops 1 | bytes 1 | tf_op jit(solution)/shard_map/window_attention/pallas_call | solution.py:179
  79.7 4.5 %collective-permute-done.17.rest_6_ = bf16[256,512]{1,0:T(8,128)(2,1)S(1)} collective-permute-done((bf16[256,512]{1,0:T(8,128)(2,1)S(1)}, bf16[256,512]{1,0:T(8,128)(2,1)S(1)}, u32[]{:S(2)}, u32[]{:S(2)}) %collective-permute-start.17) | collective-permute-done | bytes 262176 | tf_op jit(solution)/shard_map/ppermute | solution.py:337
  84.3 1.7 %apply_fast.1.rest_0_ = bf16[512,512]{1,0:T(8,128)(2,1)S(1)} custom-call(s32[12]{0:T(128)S(1)} %dynamic-slice_bitcast_fusion.place, bf16[512,512]{1,0:T(8,128)(2,1)S(1)} %copy-done.5, f32[512,512]{1,0:T(8,128)S(1)} %window_attention.1.attended, bf16[3,64,512]{2,1,0:T(8,128)(2,1)S(1)} %renew.1.rest_0_, ...), custom_call_target="tpu_custom_call" | custom-call | flops 1 | bytes 1 | tf_op jit(solution)/shard_map/apply_fast/pallas_call | solution.py:258
  85.9 1.6 %collective-permute-start.20 = (bf16[512,512]{1,0:T(8,128)(2,1)S(1)}, bf16[512,512]{1,0:T(8,128)(2,1)S(1)}, u32[]{:S(2)}, u32[]{:S(2)}) collective-permute-start(bf16[512,512]{1,0:T(8,128)(2,1)S(1)} %apply_fast.1.rest_0_), channel_id=1, source_target_pairs={{0,2},{1,3},{2,0},{3,1},{4,6},{5,7},{6,4},{7,5},{8,10},{9,11},{10,... | collective-permute-start | bytes 1572872 | tf_op jit(solution)/shard_map/ppermute | solution.py:41
  87.8 9.7 %collective-permute-done.20.rest_2_ = bf16[512,512]{1,0:T(8,128)(2,1)S(1)} collective-permute-done((bf16[512,512]{1,0:T(8,128)(2,1)S(1)}, bf16[512,512]{1,0:T(8,128)(2,1)S(1)}, u32[]{:S(2)}, u32[]{:S(2)}) %collective-permute-start.20) | collective-permute-done | bytes 524320 | tf_op jit(solution)/shard_map/ppermute | solution.py:41
  97.5 1.2 %collective-permute-done.21.rest_9_ = bf16[512,512]{1,0:T(8,128)(2,1)S(1)} collective-permute-done((bf16[512,512]{1,0:T(8,128)(2,1)S(1)}, bf16[512,512]{1,0:T(8,128)(2,1)S(1)}, u32[]{:S(2)}, u32[]{:S(2)}) %collective-permute-start.21) | collective-permute-done | bytes 524320 | tf_op jit(solution)/shard_map/ppermute | solution.py:41
  98.8 1.7 %project_most.1 = (f32[512,512]{1,0:T(8,128)S(1)}, bf16[512,512]{1,0:T(8,128)(2,1)S(1)}) custom-call(s32[12]{0:T(128)S(1)} %dynamic-slice_bitcast_fusion.place, bf16[512,512]{1,0:T(8,128)(2,1)S(1)} %apply_fast.1.rest_0_, bf16[512,512]{1,0:T(8,128)(2,1)S(1)} %collective-permute-done.19.rest_1_, bf16[512,512]{1,0:T(8,128)(2,1)S(1)} %collective-permute-done.20.rest_2_, ...), custom_call_target="tpu_custom_call" | custom-call | flops 1 | bytes 1 | tf_op jit(solution)/shard_map/project_most/pallas_call | solution.py:295
  100.7 1.2 %project_last.1 = bf16[512,512]{1,0:T(8,128)(2,1)} custom-call(f32[512,512]{1,0:T(8,128)S(1)} %get-tuple-element.38.partial, bf16[512,512]{1,0:T(8,128)(2,1)S(1)} %collective-permute-done.22.block, bf16[512,512]{1,0:T(8,128)(2,1)S(1)} %get-tuple-element.39.rows), custom_call_target="tpu_custom_call" | custom-call | flops 1 | bytes 1 | tf_op jit(solution)/shard_map/project_last/pallas_call | solution.py:316
  (44 shorter events, 7.8 us)
Async XLA Ops:
  0.6 10.6 %collective-permute-start.1 = (bf16[256,512]{1,0:T(8,128)(2,1)}, bf16[256,512]{1,0:T(8,128)(2,1)S(1)}, u32[]{:S(2)}, u32[]{:S(2)}) collective-permute-start(bf16[256,512]{1,0:T(8,128)(2,1)} %rest_3_.1), channel_id=1, source_target_pairs={{0,8},{4,12},{8,24},{12,28},{24,16},{28,20},{16,0},{20,4},{1,9},{5... | collective-permute-start | bytes 786440 | tf_op jit(solution)/shard_map/ppermute | solution.py:337
  3.7 15.9 %collective-permute-start = (bf16[512,512]{1,0:T(8,128)(2,1)}, bf16[512,512]{1,0:T(8,128)(2,1)S(1)}, u32[]{:S(2)}, u32[]{:S(2)}) collective-permute-start(bf16[512,512]{1,0:T(8,128)(2,1)} %k.3), channel_id=1, source_target_pairs={{0,4},{4,0},{8,12},{12,8},{16,20},{20,16},{24,28},{28,24},{1,5},{5... | collective-permute-start | bytes 1572872 | tf_op jit(solution)/shard_map/ppermute | solution.py:41
  11.2 8.4 %collective-permute-start.2 = (bf16[256,512]{1,0:T(8,128)(2,1)S(1)}, bf16[256,512]{1,0:T(8,128)(2,1)S(1)}, u32[]{:S(2)}, u32[]{:S(2)}) collective-permute-start(bf16[256,512]{1,0:T(8,128)(2,1)S(1)} %collective-permute-done.1.rest_4_), channel_id=1, source_target_pairs={{0,8},{4,12},{8,24},{12,28},{24,16},{28,20},{16,0},{20,4},{1,9},{5... | collective-permute-start | bytes 786440 | tf_op jit(solution)/shard_map/ppermute | solution.py:337
  14.1 15.5 %collective-permute-start.5 = (bf16[512,512]{1,0:T(8,128)(2,1)S(1)}, bf16[512,512]{1,0:T(8,128)(2,1)S(1)}, u32[]{:S(2)}, u32[]{:S(2)}) collective-permute-start(bf16[512,512]{1,0:T(8,128)(2,1)S(1)} %multiply_convert_fusion.e), channel_id=1, source_target_pairs={{0,4},{4,0},{8,12},{12,8},{16,20},{20,16},{24,28},{28,24},{1,5},{5... | collective-permute-start | bytes 1572872 | tf_op jit(solution)/shard_map/ppermute | solution.py:41
  15.7 13.3 %collective-permute-start.4 = (bf16[512,512]{1,0:T(8,128)(2,1)}, bf16[512,512]{1,0:T(8,128)(2,1)S(1)}, u32[]{:S(2)}, u32[]{:S(2)}) collective-permute-start(bf16[512,512]{1,0:T(8,128)(2,1)} %v.1), channel_id=1, source_target_pairs={{4,12},{12,20},{20,28},{5,13},{13,21},{21,29},{6,14},{14,22},{22,3... | collective-permute-start | bytes 1572872 | tf_op jit(solution)/shard_map/ppermute | solution.py:400
  19.6 12.1 %collective-permute-start.3 = (bf16[512,512]{1,0:T(8,128)(2,1)S(1)}, bf16[512,512]{1,0:T(8,128)(2,1)S(1)}, u32[]{:S(2)}, u32[]{:S(2)}) collective-permute-start(bf16[512,512]{1,0:T(8,128)(2,1)S(1)} %collective-permute-done.k.pair_k), channel_id=1, source_target_pairs={{0,8},{8,16},{16,24},{1,9},{9,17},{17,25},{2,10},{10,18},{18,26},{... | collective-permute-start | bytes 1572872 | tf_op jit(solution)/shard_map/ppermute | solution.py:402
  23.7 1.4 %copy-start = (bf16[1,3,512,512]{3,2,1,0:T(8,128)(2,1)S(1)}, bf16[1,3,512,512]{3,2,1,0:T(8,128)(2,1)}, u32[]{:S(2)}) copy-start(bf16[1,3,512,512]{3,2,1,0:T(8,128)(2,1)} %w.5) | copy-start | bytes 4718596
  25.1 1.0 %copy-start.3 = (bf16[512,512]{1,0:T(8,128)(2,1)S(1)}, bf16[512,512]{1,0:T(8,128)(2,1)}, u32[]{:S(2)}) copy-start(bf16[512,512]{1,0:T(8,128)(2,1)} %k.3) | copy-start | bytes 1572868
  26.1 2.8 %copy-start.2 = (bf16[512,512]{1,0:T(8,128)(2,1)S(1)}, bf16[512,512]{1,0:T(8,128)(2,1)}, u32[]{:S(2)}) copy-start(bf16[512,512]{1,0:T(8,128)(2,1)} %v.1) | copy-start | bytes 1572868
  26.1 2.8 %copy-start.7 = (bf16[256,512]{1,0:T(8,128)(2,1)S(1)}, bf16[256,512]{1,0:T(8,128)(2,1)}, u32[]{:S(2)}) copy-start(bf16[256,512]{1,0:T(8,128)(2,1)} %rest_3_.1) | copy-start | bytes 786436
  28.9 2.9 %copy-start.1 = (bf16[1,3,512,512]{3,2,1,0:T(8,128)(2,1)S(1)}, bf16[1,3,512,512]{3,2,1,0:T(8,128)(2,1)}, u32[]{:S(2)}) copy-start(bf16[1,3,512,512]{3,2,1,0:T(8,128)(2,1)} %w.5) | copy-start | bytes 4718596
  29.6 25.1 %copy-start.6 = (f32[1,3,64,512]{3,2,1,0:T(8,128)S(1)}, f32[1,3,64,512]{3,2,1,0:T(8,128)}, u32[]{:S(2)}) copy-start(f32[1,3,64,512]{3,2,1,0:T(8,128)} %momentum.1) | copy-start | bytes 1179652
  34.6 16.1 %collective-permute-start.6 = (bf16[768,512]{1,0:T(8,128)(2,1)S(1)}, bf16[768,512]{1,0:T(8,128)(2,1)S(1)}, u32[]{:S(2)}, u32[]{:S(2)}) collective-permute-start(bf16[768,512]{1,0:T(8,128)(2,1)S(1)} %crossing.1), channel_id=1, source_target_pairs={{0,4},{4,0},{8,12},{12,8},{16,20},{20,16},{24,28},{28,24},{1,5},{5... | collective-permute-start | bytes 2359304 | tf_op jit(solution)/shard_map/ppermute | solution.py:41
  34.9 10.6 %collective-permute-start.9 = (bf16[3,64,512]{2,1,0:T(8,128)(2,1)S(1)}, bf16[3,64,512]{2,1,0:T(8,128)(2,1)S(1)}, u32[]{:S(2)}, u32[]{:S(2)}) collective-permute-start(bf16[3,64,512]{2,1,0:T(8,128)(2,1)S(1)} %get-tuple-element.28), channel_id=1, source_target_pairs={{0,24},{4,28},{8,16},{12,20},{16,8},{20,12},{24,0},{28,4},{1,25},{... | collective-permute-start | bytes 589832 | tf_op jit(solution)/shard_map/ppermute | solution.py:41
  39.7 15.0 %collective-permute-start.8 = (bf16[3,64,512]{2,1,0:T(8,128)(2,1)S(1)}, bf16[3,64,512]{2,1,0:T(8,128)(2,1)S(1)}, u32[]{:S(2)}, u32[]{:S(2)}) collective-permute-start(bf16[3,64,512]{2,1,0:T(8,128)(2,1)S(1)} %get-tuple-element.27), channel_id=1, source_target_pairs={{0,16},{4,20},{8,24},{12,28},{16,0},{20,4},{24,8},{28,12},{1,17},{... | collective-permute-start | bytes 589832 | tf_op jit(solution)/shard_map/ppermute | solution.py:41
  39.7 15.0 %collective-permute-start.7 = (bf16[3,64,512]{2,1,0:T(8,128)(2,1)S(1)}, bf16[3,64,512]{2,1,0:T(8,128)(2,1)S(1)}, u32[]{:S(2)}, u32[]{:S(2)}) collective-permute-start(bf16[3,64,512]{2,1,0:T(8,128)(2,1)S(1)} %get-tuple-element.24), channel_id=1, source_target_pairs={{0,8},{4,12},{8,0},{12,4},{16,24},{20,28},{24,16},{28,20},{1,9},{5... | collective-permute-start | bytes 589832 | tf_op jit(solution)/shard_map/ppermute | solution.py:41
  55.5 21.9 %copy-start.4 = (bf16[512,512]{1,0:T(8,128)(2,1)S(1)}, bf16[512,512]{1,0:T(8,128)(2,1)}, u32[]{:S(2)}) copy-start(bf16[512,512]{1,0:T(8,128)(2,1)} %k.3) | copy-start | bytes 1572868
  55.5 21.9 %copy-start.5 = (bf16[512,512]{1,0:T(8,128)(2,1)S(1)}, bf16[512,512]{1,0:T(8,128)(2,1)}, u32[]{:S(2)}) copy-start(bf16[512,512]{1,0:T(8,128)(2,1)} %q.3) | copy-start | bytes 1572868
  55.5 5.7 %collective-permute-start.11 = (bf16[3,64,512]{2,1,0:T(8,128)(2,1)S(1)}, bf16[3,64,512]{2,1,0:T(8,128)(2,1)S(1)}, u32[]{:S(2)}, u32[]{:S(2)}) collective-permute-start(bf16[3,64,512]{2,1,0:T(8,128)(2,1)S(1)} %renew.1.rest_0_), channel_id=1, source_target_pairs={{0,4},{4,0},{8,12},{12,8},{16,20},{20,16},{24,28},{28,24},{1,5},{5... | collective-permute-start | bytes 589832 | tf_op jit(solution)/shard_map/ppermute | solution.py:41
  55.9 8.6 %collective-permute-start.10 = (bf16[3,64,512]{2,1,0:T(8,128)(2,1)S(1)}, bf16[3,64,512]{2,1,0:T(8,128)(2,1)S(1)}, u32[]{:S(2)}, u32[]{:S(2)}) collective-permute-start(bf16[3,64,512]{2,1,0:T(8,128)(2,1)S(1)} %renew.1.rest_0_), channel_id=1, source_target_pairs={{0,8},{4,12},{8,0},{12,4},{16,24},{20,28},{24,16},{28,20},{1,9},{5... | collective-permute-start | bytes 589832 | tf_op jit(solution)/shard_map/ppermute | solution.py:41
  55.9 12.3 %collective-permute-start.13 = (bf16[3,64,512]{2,1,0:T(8,128)(2,1)S(1)}, bf16[3,64,512]{2,1,0:T(8,128)(2,1)S(1)}, u32[]{:S(2)}, u32[]{:S(2)}) collective-permute-start(bf16[3,64,512]{2,1,0:T(8,128)(2,1)S(1)} %renew.1.rest_0_), channel_id=1, source_target_pairs={{0,24},{4,28},{8,16},{12,20},{16,8},{20,12},{24,0},{28,4},{1,25},{... | collective-permute-start | bytes 589832 | tf_op jit(solution)/shard_map/ppermute | solution.py:41
  59.1 15.8 %collective-permute-start.12 = (bf16[3,64,512]{2,1,0:T(8,128)(2,1)S(1)}, bf16[3,64,512]{2,1,0:T(8,128)(2,1)S(1)}, u32[]{:S(2)}, u32[]{:S(2)}) collective-permute-start(bf16[3,64,512]{2,1,0:T(8,128)(2,1)S(1)} %renew.1.rest_0_), channel_id=1, source_target_pairs={{0,16},{4,20},{8,24},{12,28},{16,0},{20,4},{24,8},{28,12},{1,17},{... | collective-permute-start | bytes 589832 | tf_op jit(solution)/shard_map/ppermute | solution.py:41
  64.6 11.9 %collective-permute-start.14 = (bf16[3,64,512]{2,1,0:T(8,128)(2,1)S(1)}, bf16[3,64,512]{2,1,0:T(8,128)(2,1)S(1)}, u32[]{:S(2)}, u32[]{:S(2)}) collective-permute-start(bf16[3,64,512]{2,1,0:T(8,128)(2,1)S(1)} %collective-permute-done.10.rest_1_), channel_id=1, source_target_pairs={{0,4},{4,0},{8,12},{12,8},{16,20},{20,16},{24,28},{28,24},{1,5},{5... | collective-permute-start | bytes 589832 | tf_op jit(solution)/shard_map/ppermute | solution.py:41
  64.8 19.5 %collective-permute-start.18 = (bf16[256,512]{1,0:T(8,128)(2,1)S(1)}, bf16[256,512]{1,0:T(8,128)(2,1)S(1)}, u32[]{:S(2)}, u32[]{:S(2)}) collective-permute-start(bf16[256,512]{1,0:T(8,128)(2,1)S(1)} %collective-permute-done.1.rest_4_), channel_id=1, source_target_pairs={{0,4},{4,0},{8,12},{12,8},{16,20},{20,16},{24,28},{28,24},{1,5},{5... | collective-permute-start | bytes 786440 | tf_op jit(solution)/shard_map/ppermute | solution.py:41
  68.3 15.9 %collective-permute-start.16 = (bf16[3,64,512]{2,1,0:T(8,128)(2,1)S(1)}, bf16[3,64,512]{2,1,0:T(8,128)(2,1)S(1)}, u32[]{:S(2)}, u32[]{:S(2)}) collective-permute-start(bf16[3,64,512]{2,1,0:T(8,128)(2,1)S(1)} %collective-permute-done.13.rest_3_), channel_id=1, source_target_pairs={{0,4},{4,0},{8,12},{12,8},{16,20},{20,16},{24,28},{28,24},{1,5},{5... | collective-permute-start | bytes 589832 | tf_op jit(solution)/shard_map/ppermute | solution.py:41
  74.9 9.4 %collective-permute-start.15 = (bf16[3,64,512]{2,1,0:T(8,128)(2,1)S(1)}, bf16[3,64,512]{2,1,0:T(8,128)(2,1)S(1)}, u32[]{:S(2)}, u32[]{:S(2)}) collective-permute-start(bf16[3,64,512]{2,1,0:T(8,128)(2,1)S(1)} %collective-permute-done.12.rest_2_), channel_id=1, source_target_pairs={{0,4},{4,0},{8,12},{12,8},{16,20},{20,16},{24,28},{28,24},{1,5},{5... | collective-permute-start | bytes 589832 | tf_op jit(solution)/shard_map/ppermute | solution.py:41
  76.5 7.7 %collective-permute-start.17 = (bf16[256,512]{1,0:T(8,128)(2,1)S(1)}, bf16[256,512]{1,0:T(8,128)(2,1)S(1)}, u32[]{:S(2)}, u32[]{:S(2)}) collective-permute-start(bf16[256,512]{1,0:T(8,128)(2,1)S(1)} %collective-permute-done.2.rest_5_), channel_id=1, source_target_pairs={{0,8},{4,12},{8,24},{12,28},{24,16},{28,20},{16,0},{20,4},{1,9},{5... | collective-permute-start | bytes 786440 | tf_op jit(solution)/shard_map/ppermute | solution.py:337
  85.9 11.6 %collective-permute-start.20 = (bf16[512,512]{1,0:T(8,128)(2,1)S(1)}, bf16[512,512]{1,0:T(8,128)(2,1)S(1)}, u32[]{:S(2)}, u32[]{:S(2)}) collective-permute-start(bf16[512,512]{1,0:T(8,128)(2,1)S(1)} %apply_fast.1.rest_0_), channel_id=1, source_target_pairs={{0,2},{1,3},{2,0},{3,1},{4,6},{5,7},{6,4},{7,5},{8,10},{9,11},{10,... | collective-permute-start | bytes 1572872 | tf_op jit(solution)/shard_map/ppermute | solution.py:41
  87.5 11.3 %collective-permute-start.21 = (bf16[512,512]{1,0:T(8,128)(2,1)S(1)}, bf16[512,512]{1,0:T(8,128)(2,1)S(1)}, u32[]{:S(2)}, u32[]{:S(2)}) collective-permute-start(bf16[512,512]{1,0:T(8,128)(2,1)S(1)} %constant_dynamic-update-slice_fusion), channel_id=1, source_target_pairs={{0,4},{4,0},{8,12},{12,8},{16,20},{20,16},{24,28},{28,24},{1,5},{5... | collective-permute-start | bytes 1572872 | tf_op jit(solution)/shard_map/ppermute | solution.py:41
  87.8 11.0 %collective-permute-start.19 = (bf16[512,512]{1,0:T(8,128)(2,1)S(1)}, bf16[512,512]{1,0:T(8,128)(2,1)S(1)}, u32[]{:S(2)}, u32[]{:S(2)}) collective-permute-start(bf16[512,512]{1,0:T(8,128)(2,1)S(1)} %apply_fast.1.rest_0_), channel_id=1, source_target_pairs={{0,1},{1,0},{2,3},{3,2},{4,5},{5,4},{6,7},{7,6},{8,9},{9,8},{10,11... | collective-permute-start | bytes 1572872 | tf_op jit(solution)/shard_map/ppermute | solution.py:41
  98.8 1.9 %collective-permute-start.22 = (bf16[512,512]{1,0:T(8,128)(2,1)S(1)}, bf16[512,512]{1,0:T(8,128)(2,1)S(1)}, u32[]{:S(2)}, u32[]{:S(2)}) collective-permute-start(bf16[512,512]{1,0:T(8,128)(2,1)S(1)} %collective-permute-done.20.rest_2_), channel_id=1, source_target_pairs={{0,1},{1,0},{2,3},{3,2},{4,5},{5,4},{6,7},{7,6},{8,9},{9,8},{10,11... | collective-permute-start | bytes 1572872 | tf_op jit(solution)/shard_map/ppermute | solution.py:41

commit v7 on v6

--- a/solution.py
+++ b/solution.py
@@ -289,8 +289,7 @@
     units = near + far
     offsets = [(i, 0) for i in range(len(near))]
     for i, unit in enumerate(far, len(near)):
-        firsts = range(0, unit.shape[0], rows_in)
-        offsets += [(i, first) for first in (firsts if i > len(near) else firsts[-1:])]
+        offsets.append((i, unit.shape[0] - rows_in))
     columns = near[0].shape[1]
     return pl.pallas_call(
         functools.partial(most_kernel, tags, last, rows_in, offsets),
@@ -421,21 +420,20 @@
         place, queries, keys, values, pair_keys, up_keys, after(crossed, near[1])
     )
     wide.append(ring_step(after(wide[2], far[1], near[2], near[3]), outer))
-    rest = jnp.concatenate(wide[2:])
 
     total = after(summed[0], near[1])
     for piece in pieces:
         total = total + piece.astype(jnp.float32)
     moment = MOMENTUM_DECAY * momentum + total[None]
 
-    far[-1] = after(far[-1], attended, rest, wide_far[1], moment)
-    wide_far.append(swap(after(rest, far[1]), "seq", 1))
+    far[-1] = after(far[-1], attended, wide_far[1], moment)
+    wide_far += [swap(after(wide[2], far[1]), "seq", 1), swap(wide[3], "seq", 1)]
 
     combined = apply_fast(place, queries, attended, near + far)
 
     crossed_x = swap(combined, "head", 2)
     other_core = swap(combined, "head", 1)
-    crossed_x = after(crossed_x, wide_far[2])
+    crossed_x = after(crossed_x, *wide_far[2:])
     last = swap(crossed_x, "head", 3 ^ 2)
     held = [out_proj] + wide[1:]
     partial, rows = project_most(

time: 102 us -> 98.5 us (0.966)
  waiting for transfers between devices: 54.1 us -> 47.4 us
  starting transfers between devices: 27.1 us -> 30.2 us
    ppermute x18 -> x19, waiting for transfers between devices: 38.1 us -> 34.3 us  [swap(): return lax.ppermute(array, axis, [(i, i ^ mask) for i in range(devices)])]
    ppermute x18 -> x19, starting transfers between devices: 19 us -> 22.1 us  [swap(): return lax.ppermute(array, axis, [(i, i ^ mask) for i in range(devices)])]
    ppermute x3, waiting for transfers between devices: 13.8 us -> 10.9 us  [ring_step(): return lax.ppermute(unit, 'seq', pairs)]
    unnamed x17 -> x16, local copies, waits for them, and re-layouts: 2.5 us -> 2.48 us
  transfers between devices with their start and end apart: 23 -> 24, of which waited for: 14 -> 14; matrix products, arithmetic and copies ran while one was open for 3% -> 4% of each run, Pallas kernels for 7% -> 9%
where the time goes in v7:
time: 98.5 us; the launch traced here: 98.2 us
  waiting for transfers between devices  47.4 us (48%)
  starting transfers between devices  30.2 us (31%)
  Pallas kernels  13.9 us (14%)
  local copies, waits for them, and re-layouts  3.17 us (3%)
  other arithmetic  2.79 us (3%)
    ppermute x19, waiting for transfers between devices, swap(): return lax.ppermute(array, axis, [(i, i ^ mask) for i in range(devices)])  34.3 us
    ppermute x19, starting transfers between devices, swap(): return lax.ppermute(array, axis, [(i, i ^ mask) for i in range(devices)])  22.1 us
    ppermute x3, waiting for transfers between devices, ring_step(): return lax.ppermute(unit, 'seq', pairs)  10.9 us
    ppermute x3, starting transfers between devices, ring_step(): return lax.ppermute(unit, 'seq', pairs)  4.02 us
    ppermute x1, starting transfers between devices, shards(): lax.ppermute(up_keys, 'seq', [(s, s + 2) for s in range(0, ranks - 2, 2)])  3.32 us
    pallas_call x1, Pallas kernels, both_gradients(): pl.pallas_call(functools.partial(both_kernel, outer), out_shape=[jax.Shap...  2.83 us
    pallas_call x1, Pallas kernels, own_gradients(): pl.pallas_call(functools.partial(own_kernel, outer), out_shape=jax.ShapeD...  2.77 us
    unnamed x16, local copies, waits for them, and re-layouts  2.48 us
  transfers between devices with their start and end apart: 24, of which 14 were waited for; matrix products, arithmetic and copies ran while one was open for 4% of the time, Pallas kernels for 9%

profile of v7, /device:TPU:0, one launch (start us, length us, event | category | flops | bytes accessed | tf_op | source)
XLA Modules:
  0.0 98.2 jit_solution(2702493992675101376)
XLA Ops:
  0.6 3.1 %collective-permute-start.1 = (bf16[256,512]{1,0:T(8,128)(2,1)}, bf16[256,512]{1,0:T(8,128)(2,1)S(1)}, u32[]{:S(2)}, u32[]{:S(2)}) collective-permute-start(bf16[256,512]{1,0:T(8,128)(2,1)} %rest_3_.1), channel_id=1, source_target_pairs={{0,8},{4,12},{8,24},{12,28},{24,16},{28,20},{16,0},{20,4},{1,9},{5... | collective-permute-start | bytes 786440 | tf_op jit(solution)/shard_map/ppermute | solution.py:336
  3.7 1.5 %collective-permute-start = (bf16[512,512]{1,0:T(8,128)(2,1)}, bf16[512,512]{1,0:T(8,128)(2,1)S(1)}, u32[]{:S(2)}, u32[]{:S(2)}) collective-permute-start(bf16[512,512]{1,0:T(8,128)(2,1)} %k.3), channel_id=1, source_target_pairs={{0,4},{4,0},{8,12},{12,8},{16,20},{20,16},{24,28},{28,24},{1,5},{5... | collective-permute-start | bytes 1572872 | tf_op jit(solution)/shard_map/ppermute | solution.py:41
  5.2 6.0 %collective-permute-done.1.rest_4_ = bf16[256,512]{1,0:T(8,128)(2,1)S(1)} collective-permute-done((bf16[256,512]{1,0:T(8,128)(2,1)}, bf16[256,512]{1,0:T(8,128)(2,1)S(1)}, u32[]{:S(2)}, u32[]{:S(2)}) %collective-permute-start.1) | collective-permute-done | bytes 262176 | tf_op jit(solution)/shard_map/ppermute | solution.py:336
  12.9 1.2 %multiply_convert_fusion.e = bf16[512,512]{1,0:T(8,128)(2,1)S(1)} fusion(bf16[512,512]{1,0:T(8,128)(2,1)} %v.1, f32[512]{0:T(512)S(1)} %bitcast.5), kind=kLoop, calls=%fused_computation | loop fusion | flops 786432 | bytes 1050624 | tf_op jit(solution)/shard_map/convert_element_type | solution.py:391
  14.1 1.6 %collective-permute-start.5 = (bf16[512,512]{1,0:T(8,128)(2,1)S(1)}, bf16[512,512]{1,0:T(8,128)(2,1)S(1)}, u32[]{:S(2)}, u32[]{:S(2)}) collective-permute-start(bf16[512,512]{1,0:T(8,128)(2,1)S(1)} %multiply_convert_fusion.e), channel_id=1, source_target_pairs={{0,4},{4,0},{8,12},{12,8},{16,20},{20,16},{24,28},{28,24},{1,5},{5... | collective-permute-start | bytes 1572872 | tf_op jit(solution)/shard_map/ppermute | solution.py:41
  16.3 3.3 %collective-permute-done.2.rest_5_ = bf16[256,512]{1,0:T(8,128)(2,1)S(1)} collective-permute-done((bf16[256,512]{1,0:T(8,128)(2,1)S(1)}, bf16[256,512]{1,0:T(8,128)(2,1)S(1)}, u32[]{:S(2)}, u32[]{:S(2)}) %collective-permute-start.2) | collective-permute-done | bytes 262176 | tf_op jit(solution)/shard_map/ppermute | solution.py:336
  19.6 3.3 %collective-permute-start.3 = (bf16[512,512]{1,0:T(8,128)(2,1)S(1)}, bf16[512,512]{1,0:T(8,128)(2,1)S(1)}, u32[]{:S(2)}, u32[]{:S(2)}) collective-permute-start(bf16[512,512]{1,0:T(8,128)(2,1)S(1)} %collective-permute-done.k.pair_k), channel_id=1, source_target_pairs={{0,8},{8,16},{16,24},{1,9},{9,17},{17,25},{2,10},{10,18},{18,26},{... | collective-permute-start | bytes 1572872 | tf_op jit(solution)/shard_map/ppermute | solution.py:401
  23.7 1.4 %copy-done = bf16[1,3,512,512]{3,2,1,0:T(8,128)(2,1)S(1)} copy-done((bf16[1,3,512,512]{3,2,1,0:T(8,128)(2,1)S(1)}, bf16[1,3,512,512]{3,2,1,0:T(8,128)(2,1)}, u32[]{:S(2)}) %copy-start) | copy-done | bytes 1572888
  25.1 1.0 %copy-done.3 = bf16[512,512]{1,0:T(8,128)(2,1)S(1)} copy-done((bf16[512,512]{1,0:T(8,128)(2,1)S(1)}, bf16[512,512]{1,0:T(8,128)(2,1)}, u32[]{:S(2)}) %copy-start.3) | copy-done | bytes 524312
  26.1 2.8 %own_gradients.1.acc = f32[4,3,64,512]{3,2,1,0:T(8,128)S(1)} custom-call(s32[12]{0:T(128)S(1)} %dynamic-slice_bitcast_fusion.place, bf16[512,512]{1,0:T(8,128)(2,1)S(1)} %copy-done.3, bf16[512,512]{1,0:T(8,128)(2,1)S(1)} %multiply_convert_fusion.e, bf16[1,3,512,512]{3,2,1,0:T(8,128)(2,1)S(1)} %copy-done), custom_call_target="tpu_custom_call" | custom-call | flops 1 | bytes 1 | tf_op jit(solution)/shard_map/own_gradients/pallas_call | solution.py:122
  29.6 2.2 %collective-permute-done.3.up_k = bf16[512,512]{1,0:T(8,128)(2,1)S(1)} collective-permute-done((bf16[512,512]{1,0:T(8,128)(2,1)S(1)}, bf16[512,512]{1,0:T(8,128)(2,1)S(1)}, u32[]{:S(2)}, u32[]{:S(2)}) %collective-permute-start.3) | collective-permute-done | bytes 524320 | tf_op jit(solution)/shard_map/ppermute | solution.py:401
  31.8 2.8 %both_gradients.1 = (f32[3,64,512]{2,1,0:T(8,128)S(1)}, bf16[3,64,512]{2,1,0:T(8,128)(2,1)S(1)}, bf16[3,64,512]{2,1,0:T(8,128)(2,1)S(1)}, bf16[3,64,512]{2,1,0:T(8,128)(2,1)S(1)}) custom-call(s32[12]{0:T(128)S(1)} %dynamic-slice_bitcast_fusion.place, bf16[512,512]{1,0:T(8,128)(2,1)S(1)} %collective-permute-done.k.pair_k, ...), custom_call_target="tpu_custom_call" | custom-call | flops 1 | bytes 1 | tf_op jit(solution)/shard_map/both_gradients/pallas_call | solution.py:137
  34.9 4.7 %collective-permute-start.9 = (bf16[3,64,512]{2,1,0:T(8,128)(2,1)S(1)}, bf16[3,64,512]{2,1,0:T(8,128)(2,1)S(1)}, u32[]{:S(2)}, u32[]{:S(2)}) collective-permute-start(bf16[3,64,512]{2,1,0:T(8,128)(2,1)S(1)} %get-tuple-element.28), channel_id=1, source_target_pairs={{0,24},{4,28},{8,16},{12,20},{16,8},{20,12},{24,0},{28,4},{1,25},{... | collective-permute-start | bytes 589832 | tf_op jit(solution)/shard_map/ppermute | solution.py:41
  40.3 5.2 %collective-permute-done.9.rest_2_ = bf16[3,64,512]{2,1,0:T(8,128)(2,1)S(1)} collective-permute-done((bf16[3,64,512]{2,1,0:T(8,128)(2,1)S(1)}, bf16[3,64,512]{2,1,0:T(8,128)(2,1)S(1)}, u32[]{:S(2)}, u32[]{:S(2)}) %collective-permute-start.9) | collective-permute-done | bytes 196640 | tf_op jit(solution)/shard_map/ppermute | solution.py:41
  45.5 5.2 %collective-permute-done.6.early_v.rest_7_ = bf16[768,512]{1,0:T(8,128)(2,1)S(1)} collective-permute-done((bf16[768,512]{1,0:T(8,128)(2,1)S(1)}, bf16[768,512]{1,0:T(8,128)(2,1)S(1)}, u32[]{:S(2)}, u32[]{:S(2)}) %collective-permute-start.6) | collective-permute-done | bytes 786464 | tf_op jit(solution)/shard_map/ppermute | solution.py:41
  50.7 3.9 %collective-permute-done.8.rest_1_ = bf16[3,64,512]{2,1,0:T(8,128)(2,1)S(1)} collective-permute-done((bf16[3,64,512]{2,1,0:T(8,128)(2,1)S(1)}, bf16[3,64,512]{2,1,0:T(8,128)(2,1)S(1)}, u32[]{:S(2)}, u32[]{:S(2)}) %collective-permute-start.8) | collective-permute-done | bytes 196640 | tf_op jit(solution)/shard_map/ppermute | solution.py:41
  56.0 3.1 %collective-permute-start.13 = (bf16[3,64,512]{2,1,0:T(8,128)(2,1)S(1)}, bf16[3,64,512]{2,1,0:T(8,128)(2,1)S(1)}, u32[]{:S(2)}, u32[]{:S(2)}) collective-permute-start(bf16[3,64,512]{2,1,0:T(8,128)(2,1)S(1)} %renew.1.rest_0_), channel_id=1, source_target_pairs={{0,24},{4,28},{8,16},{12,20},{16,8},{20,12},{24,0},{28,4},{1,25},{... | collective-permute-start | bytes 589832 | tf_op jit(solution)/shard_map/ppermute | solution.py:41
  59.6 3.4 %collective-permute-done.10.rest_1_ = bf16[3,64,512]{2,1,0:T(8,128)(2,1)S(1)} collective-permute-done((bf16[3,64,512]{2,1,0:T(8,128)(2,1)S(1)}, bf16[3,64,512]{2,1,0:T(8,128)(2,1)S(1)}, u32[]{:S(2)}, u32[]{:S(2)}) %collective-permute-start.10) | collective-permute-done | bytes 196640 | tf_op jit(solution)/shard_map/ppermute | solution.py:41
  63.2 1.8 %collective-permute-start.17 = (bf16[256,512]{1,0:T(8,128)(2,1)S(1)}, bf16[256,512]{1,0:T(8,128)(2,1)S(1)}, u32[]{:S(2)}, u32[]{:S(2)}) collective-permute-start(bf16[256,512]{1,0:T(8,128)(2,1)S(1)} %collective-permute-done.1.rest_4_), channel_id=1, source_target_pairs={{0,4},{4,0},{8,12},{12,8},{16,20},{20,16},{24,28},{28,24},{1,5},{5... | collective-permute-start | bytes 786440 | tf_op jit(solution)/shard_map/ppermute | solution.py:41
  65.0 2.1 %collective-permute-done.13.rest_3_ = bf16[3,64,512]{2,1,0:T(8,128)(2,1)S(1)} collective-permute-done((bf16[3,64,512]{2,1,0:T(8,128)(2,1)S(1)}, bf16[3,64,512]{2,1,0:T(8,128)(2,1)S(1)}, u32[]{:S(2)}, u32[]{:S(2)}) %collective-permute-start.13) | collective-permute-done | bytes 196640 | tf_op jit(solution)/shard_map/ppermute | solution.py:41
  67.1 1.6 %collective-permute-start.16 = (bf16[3,64,512]{2,1,0:T(8,128)(2,1)S(1)}, bf16[3,64,512]{2,1,0:T(8,128)(2,1)S(1)}, u32[]{:S(2)}, u32[]{:S(2)}) collective-permute-start(bf16[3,64,512]{2,1,0:T(8,128)(2,1)S(1)} %collective-permute-done.13.rest_3_), channel_id=1, source_target_pairs={{0,4},{4,0},{8,12},{12,8},{16,20},{20,16},{24,28},{28,24},{1,5},{5... | collective-permute-start | bytes 589832 | tf_op jit(solution)/shard_map/ppermute | solution.py:41
  68.7 6.2 %collective-permute-done.12.rest_2_ = bf16[3,64,512]{2,1,0:T(8,128)(2,1)S(1)} collective-permute-done((bf16[3,64,512]{2,1,0:T(8,128)(2,1)S(1)}, bf16[3,64,512]{2,1,0:T(8,128)(2,1)S(1)}, u32[]{:S(2)}, u32[]{:S(2)}) %collective-permute-start.12) | collective-permute-done | bytes 196640 | tf_op jit(solution)/shard_map/ppermute | solution.py:41
  74.9 1.6 %collective-permute-start.15 = (bf16[3,64,512]{2,1,0:T(8,128)(2,1)S(1)}, bf16[3,64,512]{2,1,0:T(8,128)(2,1)S(1)}, u32[]{:S(2)}, u32[]{:S(2)}) collective-permute-start(bf16[3,64,512]{2,1,0:T(8,128)(2,1)S(1)} %collective-permute-done.12.rest_2_), channel_id=1, source_target_pairs={{0,4},{4,0},{8,12},{12,8},{16,20},{20,16},{24,28},{28,24},{1,5},{5... | collective-permute-start | bytes 589832 | tf_op jit(solution)/shard_map/ppermute | solution.py:41
  76.5 2.3 %window_attention.1.attended = f32[512,512]{1,0:T(8,128)S(1)} custom-call(s32[12]{0:T(128)S(1)} %dynamic-slice_bitcast_fusion.place, bf16[512,512]{1,0:T(8,128)(2,1)S(1)} %copy-done.5, bf16[512,512]{1,0:T(8,128)(2,1)S(1)} %copy-done.4, bf16[512,512]{1,0:T(8,128)(2,1)S(1)} %copy-done.2, bf16[512,512]{1,0:T(8,128)(2,1)S(1)} %collective-permute-done.k.pair_k, ...), custom_call_target="tpu_custom_call" | custom-call | flops 1 | bytes 1 | tf_op jit(solution)/shard_map/window_attention/pallas_call | solution.py:179
  80.6 1.7 %apply_fast.1.rest_0_ = bf16[512,512]{1,0:T(8,128)(2,1)S(1)} custom-call(s32[12]{0:T(128)S(1)} %dynamic-slice_bitcast_fusion.place, bf16[512,512]{1,0:T(8,128)(2,1)S(1)} %copy-done.5, f32[512,512]{1,0:T(8,128)S(1)} %window_attention.1.attended, bf16[3,64,512]{2,1,0:T(8,128)(2,1)S(1)} %renew.1.rest_0_, ...), custom_call_target="tpu_custom_call" | custom-call | flops 1 | bytes 1 | tf_op jit(solution)/shard_map/apply_fast/pallas_call | solution.py:258
  82.2 1.5 %collective-permute-start.19 = (bf16[512,512]{1,0:T(8,128)(2,1)S(1)}, bf16[512,512]{1,0:T(8,128)(2,1)S(1)}, u32[]{:S(2)}, u32[]{:S(2)}) collective-permute-start(bf16[512,512]{1,0:T(8,128)(2,1)S(1)} %apply_fast.1.rest_0_), channel_id=1, source_target_pairs={{0,2},{1,3},{2,0},{3,1},{4,6},{5,7},{6,4},{7,5},{8,10},{9,11},{10,... | collective-permute-start | bytes 1572872 | tf_op jit(solution)/shard_map/ppermute | solution.py:41
  83.8 1.6 %collective-permute-start.20 = (bf16[256,512]{1,0:T(8,128)(2,1)S(1)}, bf16[256,512]{1,0:T(8,128)(2,1)S(1)}, u32[]{:S(2)}, u32[]{:S(2)}) collective-permute-start(bf16[256,512]{1,0:T(8,128)(2,1)S(1)} %collective-permute-done.2.rest_5_), channel_id=1, source_target_pairs={{0,4},{4,0},{8,12},{12,8},{16,20},{20,16},{24,28},{28,24},{1,5},{5... | collective-permute-start | bytes 786440 | tf_op jit(solution)/shard_map/ppermute | solution.py:41
  85.4 1.6 %collective-permute-done.21.rest_6_ = bf16[256,512]{1,0:T(8,128)(2,1)S(1)} collective-permute-done((bf16[256,512]{1,0:T(8,128)(2,1)S(1)}, bf16[256,512]{1,0:T(8,128)(2,1)S(1)}, u32[]{:S(2)}, u32[]{:S(2)}) %collective-permute-start.21) | collective-permute-done | bytes 262176 | tf_op jit(solution)/shard_map/ppermute | solution.py:336
  87.8 4.4 %collective-permute-done.20.rest_9_ = bf16[256,512]{1,0:T(8,128)(2,1)S(1)} collective-permute-done((bf16[256,512]{1,0:T(8,128)(2,1)S(1)}, bf16[256,512]{1,0:T(8,128)(2,1)S(1)}, u32[]{:S(2)}, u32[]{:S(2)}) %collective-permute-start.20) | collective-permute-done | bytes 262176 | tf_op jit(solution)/shard_map/ppermute | solution.py:41
  92.2 2.8 %collective-permute-done.22.rest_10_ = bf16[256,512]{1,0:T(8,128)(2,1)S(1)} collective-permute-done((bf16[256,512]{1,0:T(8,128)(2,1)S(1)}, bf16[256,512]{1,0:T(8,128)(2,1)S(1)}, u32[]{:S(2)}, u32[]{:S(2)}) %collective-permute-start.22) | collective-permute-done | bytes 262176 | tf_op jit(solution)/shard_map/ppermute | solution.py:41
  95.0 1.7 %project_most.1 = (f32[512,512]{1,0:T(8,128)S(1)}, bf16[512,512]{1,0:T(8,128)(2,1)S(1)}) custom-call(s32[12]{0:T(128)S(1)} %dynamic-slice_bitcast_fusion.place, bf16[512,512]{1,0:T(8,128)(2,1)S(1)} %apply_fast.1.rest_0_, bf16[512,512]{1,0:T(8,128)(2,1)S(1)} %collective-permute-done.18.rest_1_, bf16[512,512]{1,0:T(8,128)(2,1)S(1)} %collective-permute-done.19.rest_2_, ...), custom_call_target="tpu_custom_call" | custom-call | flops 1 | bytes 1 | tf_op jit(solution)/shard_map/project_most/pallas_call | solution.py:294
  97.0 1.2 %project_last.1 = bf16[512,512]{1,0:T(8,128)(2,1)} custom-call(f32[512,512]{1,0:T(8,128)S(1)} %get-tuple-element.38.partial, bf16[512,512]{1,0:T(8,128)(2,1)S(1)} %collective-permute-done.23.block, bf16[512,512]{1,0:T(8,128)(2,1)S(1)} %get-tuple-element.39.rows), custom_call_target="tpu_custom_call" | custom-call | flops 1 | bytes 1 | tf_op jit(solution)/shard_map/project_last/pallas_call | solution.py:315
  (44 shorter events, 9.7 us)
Async XLA Ops:
  0.6 10.6 %collective-permute-start.1 = (bf16[256,512]{1,0:T(8,128)(2,1)}, bf16[256,512]{1,0:T(8,128)(2,1)S(1)}, u32[]{:S(2)}, u32[]{:S(2)}) collective-permute-start(bf16[256,512]{1,0:T(8,128)(2,1)} %rest_3_.1), channel_id=1, source_target_pairs={{0,8},{4,12},{8,24},{12,28},{24,16},{28,20},{16,0},{20,4},{1,9},{5... | collective-permute-start | bytes 786440 | tf_op jit(solution)/shard_map/ppermute | solution.py:336
  3.7 15.9 %collective-permute-start = (bf16[512,512]{1,0:T(8,128)(2,1)}, bf16[512,512]{1,0:T(8,128)(2,1)S(1)}, u32[]{:S(2)}, u32[]{:S(2)}) collective-permute-start(bf16[512,512]{1,0:T(8,128)(2,1)} %k.3), channel_id=1, source_target_pairs={{0,4},{4,0},{8,12},{12,8},{16,20},{20,16},{24,28},{28,24},{1,5},{5... | collective-permute-start | bytes 1572872 | tf_op jit(solution)/shard_map/ppermute | solution.py:41
  11.2 8.4 %collective-permute-start.2 = (bf16[256,512]{1,0:T(8,128)(2,1)S(1)}, bf16[256,512]{1,0:T(8,128)(2,1)S(1)}, u32[]{:S(2)}, u32[]{:S(2)}) collective-permute-start(bf16[256,512]{1,0:T(8,128)(2,1)S(1)} %collective-permute-done.1.rest_4_), channel_id=1, source_target_pairs={{0,8},{4,12},{8,24},{12,28},{24,16},{28,20},{16,0},{20,4},{1,9},{5... | collective-permute-start | bytes 786440 | tf_op jit(solution)/shard_map/ppermute | solution.py:336
  14.1 15.5 %collective-permute-start.5 = (bf16[512,512]{1,0:T(8,128)(2,1)S(1)}, bf16[512,512]{1,0:T(8,128)(2,1)S(1)}, u32[]{:S(2)}, u32[]{:S(2)}) collective-permute-start(bf16[512,512]{1,0:T(8,128)(2,1)S(1)} %multiply_convert_fusion.e), channel_id=1, source_target_pairs={{0,4},{4,0},{8,12},{12,8},{16,20},{20,16},{24,28},{28,24},{1,5},{5... | collective-permute-start | bytes 1572872 | tf_op jit(solution)/shard_map/ppermute | solution.py:41
  15.7 13.3 %collective-permute-start.4 = (bf16[512,512]{1,0:T(8,128)(2,1)}, bf16[512,512]{1,0:T(8,128)(2,1)S(1)}, u32[]{:S(2)}, u32[]{:S(2)}) collective-permute-start(bf16[512,512]{1,0:T(8,128)(2,1)} %v.1), channel_id=1, source_target_pairs={{4,12},{12,20},{20,28},{5,13},{13,21},{21,29},{6,14},{14,22},{22,3... | collective-permute-start | bytes 1572872 | tf_op jit(solution)/shard_map/ppermute | solution.py:399
  19.6 12.1 %collective-permute-start.3 = (bf16[512,512]{1,0:T(8,128)(2,1)S(1)}, bf16[512,512]{1,0:T(8,128)(2,1)S(1)}, u32[]{:S(2)}, u32[]{:S(2)}) collective-permute-start(bf16[512,512]{1,0:T(8,128)(2,1)S(1)} %collective-permute-done.k.pair_k), channel_id=1, source_target_pairs={{0,8},{8,16},{16,24},{1,9},{9,17},{17,25},{2,10},{10,18},{18,26},{... | collective-permute-start | bytes 1572872 | tf_op jit(solution)/shard_map/ppermute | solution.py:401
  23.7 1.4 %copy-start = (bf16[1,3,512,512]{3,2,1,0:T(8,128)(2,1)S(1)}, bf16[1,3,512,512]{3,2,1,0:T(8,128)(2,1)}, u32[]{:S(2)}) copy-start(bf16[1,3,512,512]{3,2,1,0:T(8,128)(2,1)} %w.5) | copy-start | bytes 4718596
  25.1 1.0 %copy-start.3 = (bf16[512,512]{1,0:T(8,128)(2,1)S(1)}, bf16[512,512]{1,0:T(8,128)(2,1)}, u32[]{:S(2)}) copy-start(bf16[512,512]{1,0:T(8,128)(2,1)} %k.3) | copy-start | bytes 1572868
  26.1 2.8 %copy-start.2 = (bf16[512,512]{1,0:T(8,128)(2,1)S(1)}, bf16[512,512]{1,0:T(8,128)(2,1)}, u32[]{:S(2)}) copy-start(bf16[512,512]{1,0:T(8,128)(2,1)} %v.1) | copy-start | bytes 1572868
  26.1 2.8 %copy-start.7 = (bf16[256,512]{1,0:T(8,128)(2,1)S(1)}, bf16[256,512]{1,0:T(8,128)(2,1)}, u32[]{:S(2)}) copy-start(bf16[256,512]{1,0:T(8,128)(2,1)} %rest_3_.1) | copy-start | bytes 786436
  28.9 2.9 %copy-start.1 = (bf16[1,3,512,512]{3,2,1,0:T(8,128)(2,1)S(1)}, bf16[1,3,512,512]{3,2,1,0:T(8,128)(2,1)}, u32[]{:S(2)}) copy-start(bf16[1,3,512,512]{3,2,1,0:T(8,128)(2,1)} %w.5) | copy-start | bytes 4718596
  29.6 25.1 %copy-start.6 = (f32[1,3,64,512]{3,2,1,0:T(8,128)S(1)}, f32[1,3,64,512]{3,2,1,0:T(8,128)}, u32[]{:S(2)}) copy-start(f32[1,3,64,512]{3,2,1,0:T(8,128)} %momentum.1) | copy-start | bytes 1179652
  34.6 16.1 %collective-permute-start.6 = (bf16[768,512]{1,0:T(8,128)(2,1)S(1)}, bf16[768,512]{1,0:T(8,128)(2,1)S(1)}, u32[]{:S(2)}, u32[]{:S(2)}) collective-permute-start(bf16[768,512]{1,0:T(8,128)(2,1)S(1)} %crossing.1), channel_id=1, source_target_pairs={{0,4},{4,0},{8,12},{12,8},{16,20},{20,16},{24,28},{28,24},{1,5},{5... | collective-permute-start | bytes 2359304 | tf_op jit(solution)/shard_map/ppermute | solution.py:41
  34.9 10.6 %collective-permute-start.9 = (bf16[3,64,512]{2,1,0:T(8,128)(2,1)S(1)}, bf16[3,64,512]{2,1,0:T(8,128)(2,1)S(1)}, u32[]{:S(2)}, u32[]{:S(2)}) collective-permute-start(bf16[3,64,512]{2,1,0:T(8,128)(2,1)S(1)} %get-tuple-element.28), channel_id=1, source_target_pairs={{0,24},{4,28},{8,16},{12,20},{16,8},{20,12},{24,0},{28,4},{1,25},{... | collective-permute-start | bytes 589832 | tf_op jit(solution)/shard_map/ppermute | solution.py:41
  39.7 11.0 %collective-permute-start.7 = (bf16[3,64,512]{2,1,0:T(8,128)(2,1)S(1)}, bf16[3,64,512]{2,1,0:T(8,128)(2,1)S(1)}, u32[]{:S(2)}, u32[]{:S(2)}) collective-permute-start(bf16[3,64,512]{2,1,0:T(8,128)(2,1)S(1)} %get-tuple-element.24), channel_id=1, source_target_pairs={{0,8},{4,12},{8,0},{12,4},{16,24},{20,28},{24,16},{28,20},{1,9},{5... | collective-permute-start | bytes 589832 | tf_op jit(solution)/shard_map/ppermute | solution.py:41
  39.7 15.0 %collective-permute-start.8 = (bf16[3,64,512]{2,1,0:T(8,128)(2,1)S(1)}, bf16[3,64,512]{2,1,0:T(8,128)(2,1)S(1)}, u32[]{:S(2)}, u32[]{:S(2)}) collective-permute-start(bf16[3,64,512]{2,1,0:T(8,128)(2,1)S(1)} %get-tuple-element.27), channel_id=1, source_target_pairs={{0,16},{4,20},{8,24},{12,28},{16,0},{20,4},{24,8},{28,12},{1,17},{... | collective-permute-start | bytes 589832 | tf_op jit(solution)/shard_map/ppermute | solution.py:41
  54.7 21.8 %copy-start.4 = (bf16[512,512]{1,0:T(8,128)(2,1)S(1)}, bf16[512,512]{1,0:T(8,128)(2,1)}, u32[]{:S(2)}) copy-start(bf16[512,512]{1,0:T(8,128)(2,1)} %k.3) | copy-start | bytes 1572868
  54.7 21.8 %copy-start.5 = (bf16[512,512]{1,0:T(8,128)(2,1)S(1)}, bf16[512,512]{1,0:T(8,128)(2,1)}, u32[]{:S(2)}) copy-start(bf16[512,512]{1,0:T(8,128)(2,1)} %q.3) | copy-start | bytes 1572868
  55.5 7.5 %collective-permute-start.10 = (bf16[3,64,512]{2,1,0:T(8,128)(2,1)S(1)}, bf16[3,64,512]{2,1,0:T(8,128)(2,1)S(1)}, u32[]{:S(2)}, u32[]{:S(2)}) collective-permute-start(bf16[3,64,512]{2,1,0:T(8,128)(2,1)S(1)} %renew.1.rest_0_), channel_id=1, source_target_pairs={{0,8},{4,12},{8,0},{12,4},{16,24},{20,28},{24,16},{28,20},{1,9},{5... | collective-permute-start | bytes 589832 | tf_op jit(solution)/shard_map/ppermute | solution.py:41
  55.6 7.4 %collective-permute-start.11 = (bf16[3,64,512]{2,1,0:T(8,128)(2,1)S(1)}, bf16[3,64,512]{2,1,0:T(8,128)(2,1)S(1)}, u32[]{:S(2)}, u32[]{:S(2)}) collective-permute-start(bf16[3,64,512]{2,1,0:T(8,128)(2,1)S(1)} %renew.1.rest_0_), channel_id=1, source_target_pairs={{0,4},{4,0},{8,12},{12,8},{16,20},{20,16},{24,28},{28,24},{1,5},{5... | collective-permute-start | bytes 589832 | tf_op jit(solution)/shard_map/ppermute | solution.py:41
  56.0 11.1 %collective-permute-start.13 = (bf16[3,64,512]{2,1,0:T(8,128)(2,1)S(1)}, bf16[3,64,512]{2,1,0:T(8,128)(2,1)S(1)}, u32[]{:S(2)}, u32[]{:S(2)}) collective-permute-start(bf16[3,64,512]{2,1,0:T(8,128)(2,1)S(1)} %renew.1.rest_0_), channel_id=1, source_target_pairs={{0,24},{4,28},{8,16},{12,20},{16,8},{20,12},{24,0},{28,4},{1,25},{... | collective-permute-start | bytes 589832 | tf_op jit(solution)/shard_map/ppermute | solution.py:41
  59.1 15.8 %collective-permute-start.12 = (bf16[3,64,512]{2,1,0:T(8,128)(2,1)S(1)}, bf16[3,64,512]{2,1,0:T(8,128)(2,1)S(1)}, u32[]{:S(2)}, u32[]{:S(2)}) collective-permute-start(bf16[3,64,512]{2,1,0:T(8,128)(2,1)S(1)} %renew.1.rest_0_), channel_id=1, source_target_pairs={{0,16},{4,20},{8,24},{12,28},{16,0},{20,4},{24,8},{28,12},{1,17},{... | collective-permute-start | bytes 589832 | tf_op jit(solution)/shard_map/ppermute | solution.py:41
  63.0 16.7 %collective-permute-start.14 = (bf16[3,64,512]{2,1,0:T(8,128)(2,1)S(1)}, bf16[3,64,512]{2,1,0:T(8,128)(2,1)S(1)}, u32[]{:S(2)}, u32[]{:S(2)}) collective-permute-start(bf16[3,64,512]{2,1,0:T(8,128)(2,1)S(1)} %collective-permute-done.10.rest_1_), channel_id=1, source_target_pairs={{0,4},{4,0},{8,12},{12,8},{16,20},{20,16},{24,28},{28,24},{1,5},{5... | collective-permute-start | bytes 589832 | tf_op jit(solution)/shard_map/ppermute | solution.py:41
  63.2 16.4 %collective-permute-start.17 = (bf16[256,512]{1,0:T(8,128)(2,1)S(1)}, bf16[256,512]{1,0:T(8,128)(2,1)S(1)}, u32[]{:S(2)}, u32[]{:S(2)}) collective-permute-start(bf16[256,512]{1,0:T(8,128)(2,1)S(1)} %collective-permute-done.1.rest_4_), channel_id=1, source_target_pairs={{0,4},{4,0},{8,12},{12,8},{16,20},{20,16},{24,28},{28,24},{1,5},{5... | collective-permute-start | bytes 786440 | tf_op jit(solution)/shard_map/ppermute | solution.py:41
  67.1 12.5 %collective-permute-start.16 = (bf16[3,64,512]{2,1,0:T(8,128)(2,1)S(1)}, bf16[3,64,512]{2,1,0:T(8,128)(2,1)S(1)}, u32[]{:S(2)}, u32[]{:S(2)}) collective-permute-start(bf16[3,64,512]{2,1,0:T(8,128)(2,1)S(1)} %collective-permute-done.13.rest_3_), channel_id=1, source_target_pairs={{0,4},{4,0},{8,12},{12,8},{16,20},{20,16},{24,28},{28,24},{1,5},{5... | collective-permute-start | bytes 589832 | tf_op jit(solution)/shard_map/ppermute | solution.py:41
  74.9 5.7 %collective-permute-start.15 = (bf16[3,64,512]{2,1,0:T(8,128)(2,1)S(1)}, bf16[3,64,512]{2,1,0:T(8,128)(2,1)S(1)}, u32[]{:S(2)}, u32[]{:S(2)}) collective-permute-start(bf16[3,64,512]{2,1,0:T(8,128)(2,1)S(1)} %collective-permute-done.12.rest_2_), channel_id=1, source_target_pairs={{0,4},{4,0},{8,12},{12,8},{16,20},{20,16},{24,28},{28,24},{1,5},{5... | collective-permute-start | bytes 589832 | tf_op jit(solution)/shard_map/ppermute | solution.py:41
  79.7 7.3 %collective-permute-start.21 = (bf16[256,512]{1,0:T(8,128)(2,1)S(1)}, bf16[256,512]{1,0:T(8,128)(2,1)S(1)}, u32[]{:S(2)}, u32[]{:S(2)}) collective-permute-start(bf16[256,512]{1,0:T(8,128)(2,1)S(1)} %collective-permute-done.2.rest_5_), channel_id=1, source_target_pairs={{0,8},{4,12},{8,24},{12,28},{24,16},{28,20},{16,0},{20,4},{1,9},{5... | collective-permute-start | bytes 786440 | tf_op jit(solution)/shard_map/ppermute | solution.py:336
  82.2 12.8 %collective-permute-start.19 = (bf16[512,512]{1,0:T(8,128)(2,1)S(1)}, bf16[512,512]{1,0:T(8,128)(2,1)S(1)}, u32[]{:S(2)}, u32[]{:S(2)}) collective-permute-start(bf16[512,512]{1,0:T(8,128)(2,1)S(1)} %apply_fast.1.rest_0_), channel_id=1, source_target_pairs={{0,2},{1,3},{2,0},{3,1},{4,6},{5,7},{6,4},{7,5},{8,10},{9,11},{10,... | collective-permute-start | bytes 1572872 | tf_op jit(solution)/shard_map/ppermute | solution.py:41
  83.8 8.4 %collective-permute-start.20 = (bf16[256,512]{1,0:T(8,128)(2,1)S(1)}, bf16[256,512]{1,0:T(8,128)(2,1)S(1)}, u32[]{:S(2)}, u32[]{:S(2)}) collective-permute-start(bf16[256,512]{1,0:T(8,128)(2,1)S(1)} %collective-permute-done.2.rest_5_), channel_id=1, source_target_pairs={{0,4},{4,0},{8,12},{12,8},{16,20},{20,16},{24,28},{28,24},{1,5},{5... | collective-permute-start | bytes 786440 | tf_op jit(solution)/shard_map/ppermute | solution.py:41
  86.9 8.1 %collective-permute-start.22 = (bf16[256,512]{1,0:T(8,128)(2,1)S(1)}, bf16[256,512]{1,0:T(8,128)(2,1)S(1)}, u32[]{:S(2)}, u32[]{:S(2)}) collective-permute-start(bf16[256,512]{1,0:T(8,128)(2,1)S(1)} %collective-permute-done.21.rest_6_), channel_id=1, source_target_pairs={{0,4},{4,0},{8,12},{12,8},{16,20},{20,16},{24,28},{28,24},{1,5},{5... | collective-permute-start | bytes 786440 | tf_op jit(solution)/shard_map/ppermute | solution.py:41
  87.8 7.2 %collective-permute-start.18 = (bf16[512,512]{1,0:T(8,128)(2,1)S(1)}, bf16[512,512]{1,0:T(8,128)(2,1)S(1)}, u32[]{:S(2)}, u32[]{:S(2)}) collective-permute-start(bf16[512,512]{1,0:T(8,128)(2,1)S(1)} %apply_fast.1.rest_0_), channel_id=1, source_target_pairs={{0,1},{1,0},{2,3},{3,2},{4,5},{5,4},{6,7},{7,6},{8,9},{9,8},{10,11... | collective-permute-start | bytes 1572872 | tf_op jit(solution)/shard_map/ppermute | solution.py:41
  95.0 1.9 %collective-permute-start.23 = (bf16[512,512]{1,0:T(8,128)(2,1)S(1)}, bf16[512,512]{1,0:T(8,128)(2,1)S(1)}, u32[]{:S(2)}, u32[]{:S(2)}) collective-permute-start(bf16[512,512]{1,0:T(8,128)(2,1)S(1)} %collective-permute-done.19.rest_2_), channel_id=1, source_target_pairs={{0,1},{1,0},{2,3},{3,2},{4,5},{5,4},{6,7},{7,6},{8,9},{9,8},{10,11... | collective-permute-start | bytes 1572872 | tf_op jit(solution)/shard_map/ppermute | solution.py:41

commit v8 on v7

--- a/solution.py
+++ b/solution.py
@@ -417,17 +417,18 @@
     near[1] = after(near[1], far[0])
     far += [swap(unit, "seq", 1) for unit in near[1:]]
     attended = window_attention(
-        place, queries, keys, values, pair_keys, up_keys, after(crossed, near[1])
+        place, queries, keys, values, pair_keys, up_keys, after(crossed, far[1])
     )
     wide.append(ring_step(after(wide[2], far[1], near[2], near[3]), outer))
 
-    total = after(summed[0], near[1])
+    total = after(summed[0], far[1])
     for piece in pieces:
         total = total + piece.astype(jnp.float32)
     moment = MOMENTUM_DECAY * momentum + total[None]
 
     far[-1] = after(far[-1], attended, wide_far[1], moment)
-    wide_far += [swap(after(wide[2], far[1]), "seq", 1), swap(wide[3], "seq", 1)]
+    wide_far.append(swap(after(wide[2], far[1]), "seq", 1))
+    wide_far.append(swap(after(wide[3], wide_far[2]), "seq", 1))
 
     combined = apply_fast(place, queries, attended, near + far)
 

time: 98.5 us -> 99.7 us (1.012)
  starting transfers between devices: 30.2 us -> 33.7 us
  waiting for transfers between devices: 47.4 us -> 45.1 us
    ppermute x3, starting transfers between devices: 4.02 us -> 7.41 us  [ring_step(): return lax.ppermute(unit, 'seq', pairs)]
    ppermute x3, waiting for transfers between devices: 10.9 us -> 9.3 us  [ring_step(): return lax.ppermute(unit, 'seq', pairs)]
  transfers between devices with their start and end apart: 24 -> 24, of which waited for: 14 -> 15; matrix products, arithmetic and copies ran while one was open for 4% -> 4% of each run, Pallas kernels for 9% -> 9%
where the time goes in v8:
time: 99.7 us; the launch traced here: 99.4 us
  waiting for transfers between devices  45.1 us (45%)
  starting transfers between devices  33.7 us (34%)
  Pallas kernels  13.9 us (14%)
  local copies, waits for them, and re-layouts  3.17 us (3%)
  other arithmetic  2.79 us (3%)
    ppermute x19, waiting for transfers between devices, swap(): return lax.ppermute(array, axis, [(i, i ^ mask) for i in range(devices)])  33.6 us
    ppermute x19, starting transfers between devices, swap(): return lax.ppermute(array, axis, [(i, i ^ mask) for i in range(devices)])  22.3 us
    ppermute x3, waiting for transfers between devices, ring_step(): return lax.ppermute(unit, 'seq', pairs)  9.3 us
    ppermute x3, starting transfers between devices, ring_step(): return lax.ppermute(unit, 'seq', pairs)  7.41 us
    ppermute x1, starting transfers between devices, shards(): lax.ppermute(up_keys, 'seq', [(s, s + 2) for s in range(0, ranks - 2, 2)])  3.32 us
    pallas_call x1, Pallas kernels, both_gradients(): pl.pallas_call(functools.partial(both_kernel, outer), out_shape=[jax.Shap...  2.83 us
    pallas_call x1, Pallas kernels, own_gradients(): pl.pallas_call(functools.partial(own_kernel, outer), out_shape=jax.ShapeD...  2.77 us
    unnamed x16, local copies, waits for them, and re-layouts  2.48 us
  transfers between devices with their start and end apart: 24, of which 15 were waited for; matrix products, arithmetic and copies ran while one was open for 4% of the time, Pallas kernels for 9%

profile of v8, /device:TPU:0, one launch (start us, length us, event | category | flops | bytes accessed | tf_op | source)
XLA Modules:
  0.0 99.4 jit_solution(1856671535810081704)
XLA Ops:
  0.6 3.1 %collective-permute-start.1 = (bf16[256,512]{1,0:T(8,128)(2,1)}, bf16[256,512]{1,0:T(8,128)(2,1)S(1)}, u32[]{:S(2)}, u32[]{:S(2)}) collective-permute-start(bf16[256,512]{1,0:T(8,128)(2,1)} %rest_3_.1), channel_id=1, source_target_pairs={{0,8},{4,12},{8,24},{12,28},{24,16},{28,20},{16,0},{20,4},{1,9},{5... | collective-permute-start | bytes 786440 | tf_op jit(solution)/shard_map/ppermute | solution.py:336
  3.7 1.5 %collective-permute-start = (bf16[512,512]{1,0:T(8,128)(2,1)}, bf16[512,512]{1,0:T(8,128)(2,1)S(1)}, u32[]{:S(2)}, u32[]{:S(2)}) collective-permute-start(bf16[512,512]{1,0:T(8,128)(2,1)} %k.3), channel_id=1, source_target_pairs={{0,4},{4,0},{8,12},{12,8},{16,20},{20,16},{24,28},{28,24},{1,5},{5... | collective-permute-start | bytes 1572872 | tf_op jit(solution)/shard_map/ppermute | solution.py:41
  5.2 6.0 %collective-permute-done.1.rest_4_ = bf16[256,512]{1,0:T(8,128)(2,1)S(1)} collective-permute-done((bf16[256,512]{1,0:T(8,128)(2,1)}, bf16[256,512]{1,0:T(8,128)(2,1)S(1)}, u32[]{:S(2)}, u32[]{:S(2)}) %collective-permute-start.1) | collective-permute-done | bytes 262176 | tf_op jit(solution)/shard_map/ppermute | solution.py:336
  12.9 1.2 %multiply_convert_fusion.e = bf16[512,512]{1,0:T(8,128)(2,1)S(1)} fusion(bf16[512,512]{1,0:T(8,128)(2,1)} %v.1, f32[512]{0:T(512)S(1)} %bitcast.5), kind=kLoop, calls=%fused_computation | loop fusion | flops 786432 | bytes 1050624 | tf_op jit(solution)/shard_map/convert_element_type | solution.py:391
  14.1 1.6 %collective-permute-start.5 = (bf16[512,512]{1,0:T(8,128)(2,1)S(1)}, bf16[512,512]{1,0:T(8,128)(2,1)S(1)}, u32[]{:S(2)}, u32[]{:S(2)}) collective-permute-start(bf16[512,512]{1,0:T(8,128)(2,1)S(1)} %multiply_convert_fusion.e), channel_id=1, source_target_pairs={{0,4},{4,0},{8,12},{12,8},{16,20},{20,16},{24,28},{28,24},{1,5},{5... | collective-permute-start | bytes 1572872 | tf_op jit(solution)/shard_map/ppermute | solution.py:41
  16.3 3.3 %collective-permute-done.2.rest_5_ = bf16[256,512]{1,0:T(8,128)(2,1)S(1)} collective-permute-done((bf16[256,512]{1,0:T(8,128)(2,1)S(1)}, bf16[256,512]{1,0:T(8,128)(2,1)S(1)}, u32[]{:S(2)}, u32[]{:S(2)}) %collective-permute-start.2) | collective-permute-done | bytes 262176 | tf_op jit(solution)/shard_map/ppermute | solution.py:336
  19.6 3.3 %collective-permute-start.3 = (bf16[512,512]{1,0:T(8,128)(2,1)S(1)}, bf16[512,512]{1,0:T(8,128)(2,1)S(1)}, u32[]{:S(2)}, u32[]{:S(2)}) collective-permute-start(bf16[512,512]{1,0:T(8,128)(2,1)S(1)} %collective-permute-done.k.pair_k), channel_id=1, source_target_pairs={{0,8},{8,16},{16,24},{1,9},{9,17},{17,25},{2,10},{10,18},{18,26},{... | collective-permute-start | bytes 1572872 | tf_op jit(solution)/shard_map/ppermute | solution.py:401
  23.7 1.4 %copy-done = bf16[1,3,512,512]{3,2,1,0:T(8,128)(2,1)S(1)} copy-done((bf16[1,3,512,512]{3,2,1,0:T(8,128)(2,1)S(1)}, bf16[1,3,512,512]{3,2,1,0:T(8,128)(2,1)}, u32[]{:S(2)}) %copy-start) | copy-done | bytes 1572888
  26.1 2.8 %own_gradients.1.acc = f32[4,3,64,512]{3,2,1,0:T(8,128)S(1)} custom-call(s32[12]{0:T(128)S(1)} %dynamic-slice_bitcast_fusion.place, bf16[512,512]{1,0:T(8,128)(2,1)S(1)} %copy-done.3, bf16[512,512]{1,0:T(8,128)(2,1)S(1)} %multiply_convert_fusion.e, bf16[1,3,512,512]{3,2,1,0:T(8,128)(2,1)S(1)} %copy-done), custom_call_target="tpu_custom_call" | custom-call | flops 1 | bytes 1 | tf_op jit(solution)/shard_map/own_gradients/pallas_call | solution.py:122
  29.6 2.2 %collective-permute-done.3.up_k = bf16[512,512]{1,0:T(8,128)(2,1)S(1)} collective-permute-done((bf16[512,512]{1,0:T(8,128)(2,1)S(1)}, bf16[512,512]{1,0:T(8,128)(2,1)S(1)}, u32[]{:S(2)}, u32[]{:S(2)}) %collective-permute-start.3) | collective-permute-done | bytes 524320 | tf_op jit(solution)/shard_map/ppermute | solution.py:401
  31.8 2.8 %both_gradients.1 = (f32[3,64,512]{2,1,0:T(8,128)S(1)}, bf16[3,64,512]{2,1,0:T(8,128)(2,1)S(1)}, bf16[3,64,512]{2,1,0:T(8,128)(2,1)S(1)}, bf16[3,64,512]{2,1,0:T(8,128)(2,1)S(1)}) custom-call(s32[12]{0:T(128)S(1)} %dynamic-slice_bitcast_fusion.place, bf16[512,512]{1,0:T(8,128)(2,1)S(1)} %collective-permute-done.k.pair_k, ...), custom_call_target="tpu_custom_call" | custom-call | flops 1 | bytes 1 | tf_op jit(solution)/shard_map/both_gradients/pallas_call | solution.py:137
  34.9 4.7 %collective-permute-start.9 = (bf16[3,64,512]{2,1,0:T(8,128)(2,1)S(1)}, bf16[3,64,512]{2,1,0:T(8,128)(2,1)S(1)}, u32[]{:S(2)}, u32[]{:S(2)}) collective-permute-start(bf16[3,64,512]{2,1,0:T(8,128)(2,1)S(1)} %get-tuple-element.29), channel_id=1, source_target_pairs={{0,24},{4,28},{8,16},{12,20},{16,8},{20,12},{24,0},{28,4},{1,25},{... | collective-permute-start | bytes 589832 | tf_op jit(solution)/shard_map/ppermute | solution.py:41
  40.3 5.2 %collective-permute-done.9.rest_2_ = bf16[3,64,512]{2,1,0:T(8,128)(2,1)S(1)} collective-permute-done((bf16[3,64,512]{2,1,0:T(8,128)(2,1)S(1)}, bf16[3,64,512]{2,1,0:T(8,128)(2,1)S(1)}, u32[]{:S(2)}, u32[]{:S(2)}) %collective-permute-start.9) | collective-permute-done | bytes 196640 | tf_op jit(solution)/shard_map/ppermute | solution.py:41
  45.5 5.2 %collective-permute-done.6.early_v.rest_7_ = bf16[768,512]{1,0:T(8,128)(2,1)S(1)} collective-permute-done((bf16[768,512]{1,0:T(8,128)(2,1)S(1)}, bf16[768,512]{1,0:T(8,128)(2,1)S(1)}, u32[]{:S(2)}, u32[]{:S(2)}) %collective-permute-start.6) | collective-permute-done | bytes 786464 | tf_op jit(solution)/shard_map/ppermute | solution.py:41
  50.7 3.9 %collective-permute-done.8.rest_1_ = bf16[3,64,512]{2,1,0:T(8,128)(2,1)S(1)} collective-permute-done((bf16[3,64,512]{2,1,0:T(8,128)(2,1)S(1)}, bf16[3,64,512]{2,1,0:T(8,128)(2,1)S(1)}, u32[]{:S(2)}, u32[]{:S(2)}) %collective-permute-start.8) | collective-permute-done | bytes 196640 | tf_op jit(solution)/shard_map/ppermute | solution.py:41
  56.0 3.6 %collective-permute-start.13 = (bf16[3,64,512]{2,1,0:T(8,128)(2,1)S(1)}, bf16[3,64,512]{2,1,0:T(8,128)(2,1)S(1)}, u32[]{:S(2)}, u32[]{:S(2)}) collective-permute-start(bf16[3,64,512]{2,1,0:T(8,128)(2,1)S(1)} %renew.1.rest_0_), channel_id=1, source_target_pairs={{0,16},{4,20},{8,24},{12,28},{16,0},{20,4},{24,8},{28,12},{1,17},{... | collective-permute-start | bytes 589832 | tf_op jit(solution)/shard_map/ppermute | solution.py:41
  60.3 5.3 %collective-permute-done.10.rest_1_ = bf16[3,64,512]{2,1,0:T(8,128)(2,1)S(1)} collective-permute-done((bf16[3,64,512]{2,1,0:T(8,128)(2,1)S(1)}, bf16[3,64,512]{2,1,0:T(8,128)(2,1)S(1)}, u32[]{:S(2)}, u32[]{:S(2)}) %collective-permute-start.10) | collective-permute-done | bytes 196640 | tf_op jit(solution)/shard_map/ppermute | solution.py:41
  65.6 2.0 %collective-permute-start.17 = (bf16[256,512]{1,0:T(8,128)(2,1)S(1)}, bf16[256,512]{1,0:T(8,128)(2,1)S(1)}, u32[]{:S(2)}, u32[]{:S(2)}) collective-permute-start(bf16[256,512]{1,0:T(8,128)(2,1)S(1)} %collective-permute-done.1.rest_4_), channel_id=1, source_target_pairs={{0,4},{4,0},{8,12},{12,8},{16,20},{20,16},{24,28},{28,24},{1,5},{5... | collective-permute-start | bytes 786440 | tf_op jit(solution)/shard_map/ppermute | solution.py:41
  67.7 1.7 %collective-permute-done.14.rest_3_ = bf16[3,64,512]{2,1,0:T(8,128)(2,1)S(1)} collective-permute-done((bf16[3,64,512]{2,1,0:T(8,128)(2,1)S(1)}, bf16[3,64,512]{2,1,0:T(8,128)(2,1)S(1)}, u32[]{:S(2)}, u32[]{:S(2)}) %collective-permute-start.14) | collective-permute-done | bytes 196640 | tf_op jit(solution)/shard_map/ppermute | solution.py:41
  69.3 1.7 %collective-permute-start.16 = (bf16[3,64,512]{2,1,0:T(8,128)(2,1)S(1)}, bf16[3,64,512]{2,1,0:T(8,128)(2,1)S(1)}, u32[]{:S(2)}, u32[]{:S(2)}) collective-permute-start(bf16[3,64,512]{2,1,0:T(8,128)(2,1)S(1)} %collective-permute-done.14.rest_3_), channel_id=1, source_target_pairs={{0,4},{4,0},{8,12},{12,8},{16,20},{20,16},{24,28},{28,24},{1,5},{5... | collective-permute-start | bytes 589832 | tf_op jit(solution)/shard_map/ppermute | solution.py:41
  71.0 1.1 %collective-permute-done.13.rest_2_ = bf16[3,64,512]{2,1,0:T(8,128)(2,1)S(1)} collective-permute-done((bf16[3,64,512]{2,1,0:T(8,128)(2,1)S(1)}, bf16[3,64,512]{2,1,0:T(8,128)(2,1)S(1)}, u32[]{:S(2)}, u32[]{:S(2)}) %collective-permute-start.13) | collective-permute-done | bytes 196640 | tf_op jit(solution)/shard_map/ppermute | solution.py:41
  72.1 2.0 %collective-permute-start.15 = (bf16[3,64,512]{2,1,0:T(8,128)(2,1)S(1)}, bf16[3,64,512]{2,1,0:T(8,128)(2,1)S(1)}, u32[]{:S(2)}, u32[]{:S(2)}) collective-permute-start(bf16[3,64,512]{2,1,0:T(8,128)(2,1)S(1)} %collective-permute-done.13.rest_2_), channel_id=1, source_target_pairs={{0,4},{4,0},{8,12},{12,8},{16,20},{20,16},{24,28},{28,24},{1,5},{5... | collective-permute-start | bytes 589832 | tf_op jit(solution)/shard_map/ppermute | solution.py:41
  74.1 3.4 %collective-permute-start.21 = (bf16[256,512]{1,0:T(8,128)(2,1)S(1)}, bf16[256,512]{1,0:T(8,128)(2,1)S(1)}, u32[]{:S(2)}, u32[]{:S(2)}) collective-permute-start(bf16[256,512]{1,0:T(8,128)(2,1)S(1)} %collective-permute-done.2.rest_5_), channel_id=1, source_target_pairs={{0,8},{4,12},{8,24},{12,28},{24,16},{28,20},{16,0},{20,4},{1,9},{5... | collective-permute-start | bytes 786440 | tf_op jit(solution)/shard_map/ppermute | solution.py:336
  77.5 1.3 %collective-permute-start.20 = (bf16[256,512]{1,0:T(8,128)(2,1)S(1)}, bf16[256,512]{1,0:T(8,128)(2,1)S(1)}, u32[]{:S(2)}, u32[]{:S(2)}) collective-permute-start(bf16[256,512]{1,0:T(8,128)(2,1)S(1)} %collective-permute-done.2.rest_5_), channel_id=1, source_target_pairs={{0,4},{4,0},{8,12},{12,8},{16,20},{20,16},{24,28},{28,24},{1,5},{5... | collective-permute-start | bytes 786440 | tf_op jit(solution)/shard_map/ppermute | solution.py:41
  78.9 2.3 %window_attention.1.attended = f32[512,512]{1,0:T(8,128)S(1)} custom-call(s32[12]{0:T(128)S(1)} %dynamic-slice_bitcast_fusion.place, bf16[512,512]{1,0:T(8,128)(2,1)S(1)} %copy-done.5, bf16[512,512]{1,0:T(8,128)(2,1)S(1)} %copy-done.4, bf16[512,512]{1,0:T(8,128)(2,1)S(1)} %copy-done.2, bf16[512,512]{1,0:T(8,128)(2,1)S(1)} %collective-permute-done.k.pair_k, ...), custom_call_target="tpu_custom_call" | custom-call | flops 1 | bytes 1 | tf_op jit(solution)/shard_map/window_attention/pallas_call | solution.py:179
  82.8 2.6 %collective-permute-done.15.rest_6_ = bf16[3,64,512]{2,1,0:T(8,128)(2,1)S(1)} collective-permute-done((bf16[3,64,512]{2,1,0:T(8,128)(2,1)S(1)}, bf16[3,64,512]{2,1,0:T(8,128)(2,1)S(1)}, u32[]{:S(2)}, u32[]{:S(2)}) %collective-permute-start.15) | collective-permute-done | bytes 196640 | tf_op jit(solution)/shard_map/ppermute | solution.py:41
  85.3 1.7 %apply_fast.1.rest_0_ = bf16[512,512]{1,0:T(8,128)(2,1)S(1)} custom-call(s32[12]{0:T(128)S(1)} %dynamic-slice_bitcast_fusion.place, bf16[512,512]{1,0:T(8,128)(2,1)S(1)} %copy-done.5, f32[512,512]{1,0:T(8,128)S(1)} %window_attention.1.attended, bf16[3,64,512]{2,1,0:T(8,128)(2,1)S(1)} %renew.1.rest_0_, ...), custom_call_target="tpu_custom_call" | custom-call | flops 1 | bytes 1 | tf_op jit(solution)/shard_map/apply_fast/pallas_call | solution.py:258
  87.0 1.6 %collective-permute-start.19 = (bf16[512,512]{1,0:T(8,128)(2,1)S(1)}, bf16[512,512]{1,0:T(8,128)(2,1)S(1)}, u32[]{:S(2)}, u32[]{:S(2)}) collective-permute-start(bf16[512,512]{1,0:T(8,128)(2,1)S(1)} %apply_fast.1.rest_0_), channel_id=1, source_target_pairs={{0,2},{1,3},{2,0},{3,1},{4,6},{5,7},{6,4},{7,5},{8,10},{9,11},{10,... | collective-permute-start | bytes 1572872 | tf_op jit(solution)/shard_map/ppermute | solution.py:41
  88.6 1.3 %collective-permute-done.20.rest_9_ = bf16[256,512]{1,0:T(8,128)(2,1)S(1)} collective-permute-done((bf16[256,512]{1,0:T(8,128)(2,1)S(1)}, bf16[256,512]{1,0:T(8,128)(2,1)S(1)}, u32[]{:S(2)}, u32[]{:S(2)}) %collective-permute-start.20) | collective-permute-done | bytes 262176 | tf_op jit(solution)/shard_map/ppermute | solution.py:41
  89.8 6.4 %collective-permute-done.22.rest_10_ = bf16[256,512]{1,0:T(8,128)(2,1)S(1)} collective-permute-done((bf16[256,512]{1,0:T(8,128)(2,1)S(1)}, bf16[256,512]{1,0:T(8,128)(2,1)S(1)}, u32[]{:S(2)}, u32[]{:S(2)}) %collective-permute-start.22) | collective-permute-done | bytes 262176 | tf_op jit(solution)/shard_map/ppermute | solution.py:41
  96.3 1.7 %project_most.1 = (f32[512,512]{1,0:T(8,128)S(1)}, bf16[512,512]{1,0:T(8,128)(2,1)S(1)}) custom-call(s32[12]{0:T(128)S(1)} %dynamic-slice_bitcast_fusion.place, bf16[512,512]{1,0:T(8,128)(2,1)S(1)} %apply_fast.1.rest_0_, bf16[512,512]{1,0:T(8,128)(2,1)S(1)} %collective-permute-done.18.rest_1_, bf16[512,512]{1,0:T(8,128)(2,1)S(1)} %collective-permute-done.19.rest_2_, ...), custom_call_target="tpu_custom_call" | custom-call | flops 1 | bytes 1 | tf_op jit(solution)/shard_map/project_most/pallas_call | solution.py:294
  98.2 1.2 %project_last.1 = bf16[512,512]{1,0:T(8,128)(2,1)} custom-call(f32[512,512]{1,0:T(8,128)S(1)} %get-tuple-element.40.partial, bf16[512,512]{1,0:T(8,128)(2,1)S(1)} %collective-permute-done.23.block, bf16[512,512]{1,0:T(8,128)(2,1)S(1)} %get-tuple-element.41.rows), custom_call_target="tpu_custom_call" | custom-call | flops 1 | bytes 1 | tf_op jit(solution)/shard_map/project_last/pallas_call | solution.py:315
  (44 shorter events, 9.7 us)
Async XLA Ops:
  0.6 10.6 %collective-permute-start.1 = (bf16[256,512]{1,0:T(8,128)(2,1)}, bf16[256,512]{1,0:T(8,128)(2,1)S(1)}, u32[]{:S(2)}, u32[]{:S(2)}) collective-permute-start(bf16[256,512]{1,0:T(8,128)(2,1)} %rest_3_.1), channel_id=1, source_target_pairs={{0,8},{4,12},{8,24},{12,28},{24,16},{28,20},{16,0},{20,4},{1,9},{5... | collective-permute-start | bytes 786440 | tf_op jit(solution)/shard_map/ppermute | solution.py:336
  3.7 15.9 %collective-permute-start = (bf16[512,512]{1,0:T(8,128)(2,1)}, bf16[512,512]{1,0:T(8,128)(2,1)S(1)}, u32[]{:S(2)}, u32[]{:S(2)}) collective-permute-start(bf16[512,512]{1,0:T(8,128)(2,1)} %k.3), channel_id=1, source_target_pairs={{0,4},{4,0},{8,12},{12,8},{16,20},{20,16},{24,28},{28,24},{1,5},{5... | collective-permute-start | bytes 1572872 | tf_op jit(solution)/shard_map/ppermute | solution.py:41
  11.2 8.4 %collective-permute-start.2 = (bf16[256,512]{1,0:T(8,128)(2,1)S(1)}, bf16[256,512]{1,0:T(8,128)(2,1)S(1)}, u32[]{:S(2)}, u32[]{:S(2)}) collective-permute-start(bf16[256,512]{1,0:T(8,128)(2,1)S(1)} %collective-permute-done.1.rest_4_), channel_id=1, source_target_pairs={{0,8},{4,12},{8,24},{12,28},{24,16},{28,20},{16,0},{20,4},{1,9},{5... | collective-permute-start | bytes 786440 | tf_op jit(solution)/shard_map/ppermute | solution.py:336
  14.1 15.5 %collective-permute-start.5 = (bf16[512,512]{1,0:T(8,128)(2,1)S(1)}, bf16[512,512]{1,0:T(8,128)(2,1)S(1)}, u32[]{:S(2)}, u32[]{:S(2)}) collective-permute-start(bf16[512,512]{1,0:T(8,128)(2,1)S(1)} %multiply_convert_fusion.e), channel_id=1, source_target_pairs={{0,4},{4,0},{8,12},{12,8},{16,20},{20,16},{24,28},{28,24},{1,5},{5... | collective-permute-start | bytes 1572872 | tf_op jit(solution)/shard_map/ppermute | solution.py:41
  15.7 13.3 %collective-permute-start.4 = (bf16[512,512]{1,0:T(8,128)(2,1)}, bf16[512,512]{1,0:T(8,128)(2,1)S(1)}, u32[]{:S(2)}, u32[]{:S(2)}) collective-permute-start(bf16[512,512]{1,0:T(8,128)(2,1)} %v.1), channel_id=1, source_target_pairs={{4,12},{12,20},{20,28},{5,13},{13,21},{21,29},{6,14},{14,22},{22,3... | collective-permute-start | bytes 1572872 | tf_op jit(solution)/shard_map/ppermute | solution.py:399
  19.6 12.1 %collective-permute-start.3 = (bf16[512,512]{1,0:T(8,128)(2,1)S(1)}, bf16[512,512]{1,0:T(8,128)(2,1)S(1)}, u32[]{:S(2)}, u32[]{:S(2)}) collective-permute-start(bf16[512,512]{1,0:T(8,128)(2,1)S(1)} %collective-permute-done.k.pair_k), channel_id=1, source_target_pairs={{0,8},{8,16},{16,24},{1,9},{9,17},{17,25},{2,10},{10,18},{18,26},{... | collective-permute-start | bytes 1572872 | tf_op jit(solution)/shard_map/ppermute | solution.py:401
  23.7 1.4 %copy-start = (bf16[1,3,512,512]{3,2,1,0:T(8,128)(2,1)S(1)}, bf16[1,3,512,512]{3,2,1,0:T(8,128)(2,1)}, u32[]{:S(2)}) copy-start(bf16[1,3,512,512]{3,2,1,0:T(8,128)(2,1)} %w.5) | copy-start | bytes 4718596
  25.1 1.0 %copy-start.3 = (bf16[512,512]{1,0:T(8,128)(2,1)S(1)}, bf16[512,512]{1,0:T(8,128)(2,1)}, u32[]{:S(2)}) copy-start(bf16[512,512]{1,0:T(8,128)(2,1)} %k.3) | copy-start | bytes 1572868
  26.1 2.8 %copy-start.2 = (bf16[512,512]{1,0:T(8,128)(2,1)S(1)}, bf16[512,512]{1,0:T(8,128)(2,1)}, u32[]{:S(2)}) copy-start(bf16[512,512]{1,0:T(8,128)(2,1)} %v.1) | copy-start | bytes 1572868
  26.1 2.8 %copy-start.7 = (bf16[256,512]{1,0:T(8,128)(2,1)S(1)}, bf16[256,512]{1,0:T(8,128)(2,1)}, u32[]{:S(2)}) copy-start(bf16[256,512]{1,0:T(8,128)(2,1)} %rest_3_.1) | copy-start | bytes 786436
  28.9 2.9 %copy-start.1 = (bf16[1,3,512,512]{3,2,1,0:T(8,128)(2,1)S(1)}, bf16[1,3,512,512]{3,2,1,0:T(8,128)(2,1)}, u32[]{:S(2)}) copy-start(bf16[1,3,512,512]{3,2,1,0:T(8,128)(2,1)} %w.5) | copy-start | bytes 4718596
  29.6 25.1 %copy-start.6 = (f32[1,3,64,512]{3,2,1,0:T(8,128)S(1)}, f32[1,3,64,512]{3,2,1,0:T(8,128)}, u32[]{:S(2)}) copy-start(f32[1,3,64,512]{3,2,1,0:T(8,128)} %momentum.1) | copy-start | bytes 1179652
  34.6 16.1 %collective-permute-start.6 = (bf16[768,512]{1,0:T(8,128)(2,1)S(1)}, bf16[768,512]{1,0:T(8,128)(2,1)S(1)}, u32[]{:S(2)}, u32[]{:S(2)}) collective-permute-start(bf16[768,512]{1,0:T(8,128)(2,1)S(1)} %crossing.1), channel_id=1, source_target_pairs={{0,4},{4,0},{8,12},{12,8},{16,20},{20,16},{24,28},{28,24},{1,5},{5... | collective-permute-start | bytes 2359304 | tf_op jit(solution)/shard_map/ppermute | solution.py:41
  34.9 10.6 %collective-permute-start.9 = (bf16[3,64,512]{2,1,0:T(8,128)(2,1)S(1)}, bf16[3,64,512]{2,1,0:T(8,128)(2,1)S(1)}, u32[]{:S(2)}, u32[]{:S(2)}) collective-permute-start(bf16[3,64,512]{2,1,0:T(8,128)(2,1)S(1)} %get-tuple-element.29), channel_id=1, source_target_pairs={{0,24},{4,28},{8,16},{12,20},{16,8},{20,12},{24,0},{28,4},{1,25},{... | collective-permute-start | bytes 589832 | tf_op jit(solution)/shard_map/ppermute | solution.py:41
  39.7 11.0 %collective-permute-start.7 = (bf16[3,64,512]{2,1,0:T(8,128)(2,1)S(1)}, bf16[3,64,512]{2,1,0:T(8,128)(2,1)S(1)}, u32[]{:S(2)}, u32[]{:S(2)}) collective-permute-start(bf16[3,64,512]{2,1,0:T(8,128)(2,1)S(1)} %get-tuple-element.25), channel_id=1, source_target_pairs={{0,8},{4,12},{8,0},{12,4},{16,24},{20,28},{24,16},{28,20},{1,9},{5... | collective-permute-start | bytes 589832 | tf_op jit(solution)/shard_map/ppermute | solution.py:41
  39.7 15.0 %collective-permute-start.8 = (bf16[3,64,512]{2,1,0:T(8,128)(2,1)S(1)}, bf16[3,64,512]{2,1,0:T(8,128)(2,1)S(1)}, u32[]{:S(2)}, u32[]{:S(2)}) collective-permute-start(bf16[3,64,512]{2,1,0:T(8,128)(2,1)S(1)} %get-tuple-element.28), channel_id=1, source_target_pairs={{0,16},{4,20},{8,24},{12,28},{16,0},{20,4},{24,8},{28,12},{1,17},{... | collective-permute-start | bytes 589832 | tf_op jit(solution)/shard_map/ppermute | solution.py:41
  54.7 24.2 %copy-start.4 = (bf16[512,512]{1,0:T(8,128)(2,1)S(1)}, bf16[512,512]{1,0:T(8,128)(2,1)}, u32[]{:S(2)}) copy-start(bf16[512,512]{1,0:T(8,128)(2,1)} %k.3) | copy-start | bytes 1572868
  54.7 24.2 %copy-start.5 = (bf16[512,512]{1,0:T(8,128)(2,1)S(1)}, bf16[512,512]{1,0:T(8,128)(2,1)}, u32[]{:S(2)}) copy-start(bf16[512,512]{1,0:T(8,128)(2,1)} %q.3) | copy-start | bytes 1572868
  55.5 10.1 %collective-permute-start.10 = (bf16[3,64,512]{2,1,0:T(8,128)(2,1)S(1)}, bf16[3,64,512]{2,1,0:T(8,128)(2,1)S(1)}, u32[]{:S(2)}, u32[]{:S(2)}) collective-permute-start(bf16[3,64,512]{2,1,0:T(8,128)(2,1)S(1)} %renew.1.rest_0_), channel_id=1, source_target_pairs={{0,8},{4,12},{8,0},{12,4},{16,24},{20,28},{24,16},{28,20},{1,9},{5... | collective-permute-start | bytes 589832 | tf_op jit(solution)/shard_map/ppermute | solution.py:41
  55.6 10.0 %collective-permute-start.11 = (bf16[3,64,512]{2,1,0:T(8,128)(2,1)S(1)}, bf16[3,64,512]{2,1,0:T(8,128)(2,1)S(1)}, u32[]{:S(2)}, u32[]{:S(2)}) collective-permute-start(bf16[3,64,512]{2,1,0:T(8,128)(2,1)S(1)} %renew.1.rest_0_), channel_id=1, source_target_pairs={{0,4},{4,0},{8,12},{12,8},{16,20},{20,16},{24,28},{28,24},{1,5},{5... | collective-permute-start | bytes 589832 | tf_op jit(solution)/shard_map/ppermute | solution.py:41
  56.0 16.1 %collective-permute-start.13 = (bf16[3,64,512]{2,1,0:T(8,128)(2,1)S(1)}, bf16[3,64,512]{2,1,0:T(8,128)(2,1)S(1)}, u32[]{:S(2)}, u32[]{:S(2)}) collective-permute-start(bf16[3,64,512]{2,1,0:T(8,128)(2,1)S(1)} %renew.1.rest_0_), channel_id=1, source_target_pairs={{0,16},{4,20},{8,24},{12,28},{16,0},{20,4},{24,8},{28,12},{1,17},{... | collective-permute-start | bytes 589832 | tf_op jit(solution)/shard_map/ppermute | solution.py:41
  59.6 9.7 %collective-permute-start.14 = (bf16[3,64,512]{2,1,0:T(8,128)(2,1)S(1)}, bf16[3,64,512]{2,1,0:T(8,128)(2,1)S(1)}, u32[]{:S(2)}, u32[]{:S(2)}) collective-permute-start(bf16[3,64,512]{2,1,0:T(8,128)(2,1)S(1)} %renew.1.rest_0_), channel_id=1, source_target_pairs={{0,24},{4,28},{8,16},{12,20},{16,8},{20,12},{24,0},{28,4},{1,25},{... | collective-permute-start | bytes 589832 | tf_op jit(solution)/shard_map/ppermute | solution.py:41
  65.6 8.5 %collective-permute-start.12 = (bf16[3,64,512]{2,1,0:T(8,128)(2,1)S(1)}, bf16[3,64,512]{2,1,0:T(8,128)(2,1)S(1)}, u32[]{:S(2)}, u32[]{:S(2)}) collective-permute-start(bf16[3,64,512]{2,1,0:T(8,128)(2,1)S(1)} %collective-permute-done.10.rest_1_), channel_id=1, source_target_pairs={{0,4},{4,0},{8,12},{12,8},{16,20},{20,16},{24,28},{28,24},{1,5},{5... | collective-permute-start | bytes 589832 | tf_op jit(solution)/shard_map/ppermute | solution.py:41
  65.6 17.1 %collective-permute-start.17 = (bf16[256,512]{1,0:T(8,128)(2,1)S(1)}, bf16[256,512]{1,0:T(8,128)(2,1)S(1)}, u32[]{:S(2)}, u32[]{:S(2)}) collective-permute-start(bf16[256,512]{1,0:T(8,128)(2,1)S(1)} %collective-permute-done.1.rest_4_), channel_id=1, source_target_pairs={{0,4},{4,0},{8,12},{12,8},{16,20},{20,16},{24,28},{28,24},{1,5},{5... | collective-permute-start | bytes 786440 | tf_op jit(solution)/shard_map/ppermute | solution.py:41
  69.3 13.4 %collective-permute-start.16 = (bf16[3,64,512]{2,1,0:T(8,128)(2,1)S(1)}, bf16[3,64,512]{2,1,0:T(8,128)(2,1)S(1)}, u32[]{:S(2)}, u32[]{:S(2)}) collective-permute-start(bf16[3,64,512]{2,1,0:T(8,128)(2,1)S(1)} %collective-permute-done.14.rest_3_), channel_id=1, source_target_pairs={{0,4},{4,0},{8,12},{12,8},{16,20},{20,16},{24,28},{28,24},{1,5},{5... | collective-permute-start | bytes 589832 | tf_op jit(solution)/shard_map/ppermute | solution.py:41
  72.1 13.2 %collective-permute-start.15 = (bf16[3,64,512]{2,1,0:T(8,128)(2,1)S(1)}, bf16[3,64,512]{2,1,0:T(8,128)(2,1)S(1)}, u32[]{:S(2)}, u32[]{:S(2)}) collective-permute-start(bf16[3,64,512]{2,1,0:T(8,128)(2,1)S(1)} %collective-permute-done.13.rest_2_), channel_id=1, source_target_pairs={{0,4},{4,0},{8,12},{12,8},{16,20},{20,16},{24,28},{28,24},{1,5},{5... | collective-permute-start | bytes 589832 | tf_op jit(solution)/shard_map/ppermute | solution.py:41
  74.1 14.4 %collective-permute-start.21 = (bf16[256,512]{1,0:T(8,128)(2,1)S(1)}, bf16[256,512]{1,0:T(8,128)(2,1)S(1)}, u32[]{:S(2)}, u32[]{:S(2)}) collective-permute-start(bf16[256,512]{1,0:T(8,128)(2,1)S(1)} %collective-permute-done.2.rest_5_), channel_id=1, source_target_pairs={{0,8},{4,12},{8,24},{12,28},{24,16},{28,20},{16,0},{20,4},{1,9},{5... | collective-permute-start | bytes 786440 | tf_op jit(solution)/shard_map/ppermute | solution.py:336
  77.5 12.3 %collective-permute-start.20 = (bf16[256,512]{1,0:T(8,128)(2,1)S(1)}, bf16[256,512]{1,0:T(8,128)(2,1)S(1)}, u32[]{:S(2)}, u32[]{:S(2)}) collective-permute-start(bf16[256,512]{1,0:T(8,128)(2,1)S(1)} %collective-permute-done.2.rest_5_), channel_id=1, source_target_pairs={{0,4},{4,0},{8,12},{12,8},{16,20},{20,16},{24,28},{28,24},{1,5},{5... | collective-permute-start | bytes 786440 | tf_op jit(solution)/shard_map/ppermute | solution.py:41
  87.0 9.2 %collective-permute-start.19 = (bf16[512,512]{1,0:T(8,128)(2,1)S(1)}, bf16[512,512]{1,0:T(8,128)(2,1)S(1)}, u32[]{:S(2)}, u32[]{:S(2)}) collective-permute-start(bf16[512,512]{1,0:T(8,128)(2,1)S(1)} %apply_fast.1.rest_0_), channel_id=1, source_target_pairs={{0,2},{1,3},{2,0},{3,1},{4,6},{5,7},{6,4},{7,5},{8,10},{9,11},{10,... | collective-permute-start | bytes 1572872 | tf_op jit(solution)/shard_map/ppermute | solution.py:41
  89.8 6.4 %collective-permute-start.22 = (bf16[256,512]{1,0:T(8,128)(2,1)S(1)}, bf16[256,512]{1,0:T(8,128)(2,1)S(1)}, u32[]{:S(2)}, u32[]{:S(2)}) collective-permute-start(bf16[256,512]{1,0:T(8,128)(2,1)S(1)} %collective-permute-done.21.rest_6_), channel_id=1, source_target_pairs={{0,4},{4,0},{8,12},{12,8},{16,20},{20,16},{24,28},{28,24},{1,5},{5... | collective-permute-start | bytes 786440 | tf_op jit(solution)/shard_map/ppermute | solution.py:41
  89.8 6.4 %collective-permute-start.18 = (bf16[512,512]{1,0:T(8,128)(2,1)S(1)}, bf16[512,512]{1,0:T(8,128)(2,1)S(1)}, u32[]{:S(2)}, u32[]{:S(2)}) collective-permute-start(bf16[512,512]{1,0:T(8,128)(2,1)S(1)} %apply_fast.1.rest_0_), channel_id=1, source_target_pairs={{0,1},{1,0},{2,3},{3,2},{4,5},{5,4},{6,7},{7,6},{8,9},{9,8},{10,11... | collective-permute-start | bytes 1572872 | tf_op jit(solution)/shard_map/ppermute | solution.py:41
  96.3 1.9 %collective-permute-start.23 = (bf16[512,512]{1,0:T(8,128)(2,1)S(1)}, bf16[512,512]{1,0:T(8,128)(2,1)S(1)}, u32[]{:S(2)}, u32[]{:S(2)}) collective-permute-start(bf16[512,512]{1,0:T(8,128)(2,1)S(1)} %collective-permute-done.19.rest_2_), channel_id=1, source_target_pairs={{0,1},{1,0},{2,3},{3,2},{4,5},{5,4},{6,7},{7,6},{8,9},{9,8},{10,11... | collective-permute-start | bytes 1572872 | tf_op jit(solution)/shard_map/ppermute | solution.py:41

commit v9 on v7

--- a/solution.py
+++ b/solution.py
@@ -187,8 +187,9 @@
     )(place, q, k, v, *early)
 
 
-def crossing_kernel(place, even, odd, rows, out):
-    tokens = even.shape[0]
+def crossing_kernel(place, even, odd, *rest):
+    units, out = rest[:-1], rest[-1]
+    tokens, rows_in = even.shape[0], units[0].shape[0]
 
     @pl.when(place[0] == 0)
     def _():
@@ -198,20 +199,21 @@
     def _():
         out[:tokens] = odd[...]
 
-    out[tokens:] = rows[...]
-
-
-def crossing(place, even, odd, rows):
-    shape = (even.shape[0] + rows.shape[0], even.shape[1])
+    for i, unit in enumerate(units):
+        out[tokens + i * rows_in : tokens + (i + 1) * rows_in] = unit[...]
+
+
+def crossing(place, even, odd, units):
+    shape = (even.shape[0] + sum(unit.shape[0] for unit in units), even.shape[1])
     return pl.pallas_call(
         crossing_kernel,
         out_shape=jax.ShapeDtypeStruct(shape, even.dtype),
-        in_specs=[pl.BlockSpec(memory_space=pltpu.SMEM)] + [whole_spec()] * 3,
+        in_specs=[pl.BlockSpec(memory_space=pltpu.SMEM)] + [whole_spec()] * (2 + len(units)),
         out_specs=whole_spec(),
         compiler_params=params(12),
         cost_estimate=BRIEF,
         name="crossing",
-    )(place, even, odd, rows)
+    )(place, even, odd, *units)
 
 
 def renew_kernel(place, w, momentum, mine, *rest):
@@ -289,7 +291,8 @@
     units = near + far
     offsets = [(i, 0) for i in range(len(near))]
     for i, unit in enumerate(far, len(near)):
-        offsets.append((i, unit.shape[0] - rows_in))
+        firsts = [tokens, tokens + rows_in] if i == len(near) else [0]
+        offsets += [(i, first) for first in firsts]
     columns = near[0].shape[1]
     return pl.pallas_call(
         functools.partial(most_kernel, tags, last, rows_in, offsets),
@@ -401,7 +404,7 @@
     up_keys = lax.ppermute(up_keys, "seq", [(s, s + 2) for s in range(0, ranks - 2, 2)])
 
     acc = own_gradients(place, keys, errors, fast, outer)
-    across = crossing(place, values, up_values, wide[0])
+    across = crossing(place, values, up_values, wide[:2])
     pair_errors = after(pair_errors, up_keys, across)
     summed = both_gradients(place, pair_keys, pair_errors, fast, acc, outer)
     pieces = [swap(summed[step], "seq", step * 2) for step in range(1, outer)]
@@ -413,7 +416,7 @@
     for step in range(1, outer):
         near.append(swap(renewed, "seq", step * 2))
     far = [swap(renewed, "seq", 1)]
-    wide_far = [crossed, swap(after(wide[1], near[1]), "seq", 1)]
+    wide_far = [crossed, swap(after(wide[2], near[1]), "seq", 1)]
     near[1] = after(near[1], far[0])
     far += [swap(unit, "seq", 1) for unit in near[1:]]
     attended = window_attention(
@@ -427,13 +430,13 @@
     moment = MOMENTUM_DECAY * momentum + total[None]
 
     far[-1] = after(far[-1], attended, wide_far[1], moment)
-    wide_far += [swap(after(wide[2], far[1]), "seq", 1), swap(wide[3], "seq", 1)]
+    wide_far.append(swap(wide[3], "seq", 1))
 
     combined = apply_fast(place, queries, attended, near + far)
 
     crossed_x = swap(combined, "head", 2)
     other_core = swap(combined, "head", 1)
-    crossed_x = after(crossed_x, *wide_far[2:])
+    crossed_x = after(crossed_x, wide_far[2])
     last = swap(crossed_x, "head", 3 ^ 2)
     held = [out_proj] + wide[1:]
     partial, rows = project_most(

time: 98.5 us -> 103 us (1.046)
  starting transfers between devices: 30.2 us -> 33.5 us
    ppermute x19 -> x18, starting transfers between devices: 22.1 us -> 25.5 us  [swap(): return lax.ppermute(array, axis, [(i, i ^ mask) for i in range(devices)])]
    ppermute x19 -> x18, waiting for transfers between devices: 34.3 us -> 34.5 us  [swap(): return lax.ppermute(array, axis, [(i, i ^ mask) for i in range(devices)])]
  transfers between devices with their start and end apart: 24 -> 23, of which waited for: 14 -> 13; matrix products, arithmetic and copies ran while one was open for 4% -> 3% of each run, Pallas kernels for 9% -> 9%
where the time goes in v9:
time: 103 us; the launch traced here: 102 us
  waiting for transfers between devices  48.3 us (47%)
  starting transfers between devices  33.5 us (33%)
  Pallas kernels  13.9 us (13%)
  local copies, waits for them, and re-layouts  3.18 us (3%)
  other arithmetic  2.79 us (3%)
    ppermute x18, waiting for transfers between devices, swap(): return lax.ppermute(array, axis, [(i, i ^ mask) for i in range(devices)])  34.5 us
    ppermute x18, starting transfers between devices, swap(): return lax.ppermute(array, axis, [(i, i ^ mask) for i in range(devices)])  25.5 us
    ppermute x3, waiting for transfers between devices, ring_step(): return lax.ppermute(unit, 'seq', pairs)  11.6 us
    ppermute x3, starting transfers between devices, ring_step(): return lax.ppermute(unit, 'seq', pairs)  4.02 us
    ppermute x1, starting transfers between devices, shards(): lax.ppermute(up_keys, 'seq', [(s, s + 2) for s in range(0, ranks - 2, 2)])  3.32 us
    pallas_call x1, Pallas kernels, both_gradients(): pl.pallas_call(functools.partial(both_kernel, outer), out_shape=[jax.Shap...  2.83 us
    pallas_call x1, Pallas kernels, own_gradients(): pl.pallas_call(functools.partial(own_kernel, outer), out_shape=jax.ShapeD...  2.77 us
    unnamed x16, local copies, waits for them, and re-layouts  2.48 us
  transfers between devices with their start and end apart: 23, of which 13 were waited for; matrix products, arithmetic and copies ran while one was open for 3% of the time, Pallas kernels for 9%

profile of v9, /device:TPU:0, one launch (start us, length us, event | category | flops | bytes accessed | tf_op | source)
XLA Modules:
  0.0 102.5 jit_solution(5270078421833997086)
XLA Ops:
  0.6 3.1 %collective-permute-start.1 = (bf16[256,512]{1,0:T(8,128)(2,1)}, bf16[256,512]{1,0:T(8,128)(2,1)S(1)}, u32[]{:S(2)}, u32[]{:S(2)}) collective-permute-start(bf16[256,512]{1,0:T(8,128)(2,1)} %rest_3_.1), channel_id=1, source_target_pairs={{0,8},{4,12},{8,24},{12,28},{24,16},{28,20},{16,0},{20,4},{1,9},{5... | collective-permute-start | bytes 786440 | tf_op jit(solution)/shard_map/ppermute | solution.py:339
  3.7 1.5 %collective-permute-start = (bf16[512,512]{1,0:T(8,128)(2,1)}, bf16[512,512]{1,0:T(8,128)(2,1)S(1)}, u32[]{:S(2)}, u32[]{:S(2)}) collective-permute-start(bf16[512,512]{1,0:T(8,128)(2,1)} %k.3), channel_id=1, source_target_pairs={{0,4},{4,0},{8,12},{12,8},{16,20},{20,16},{24,28},{28,24},{1,5},{5... | collective-permute-start | bytes 1572872 | tf_op jit(solution)/shard_map/ppermute | solution.py:41
  5.2 6.0 %collective-permute-done.1.rest_1_.rest_4_ = bf16[256,512]{1,0:T(8,128)(2,1)S(1)} collective-permute-done((bf16[256,512]{1,0:T(8,128)(2,1)}, bf16[256,512]{1,0:T(8,128)(2,1)S(1)}, u32[]{:S(2)}, u32[]{:S(2)}) %collective-permute-start.1) | collective-permute-done | bytes 262176 | tf_op jit(solution)/shard_map/ppermute | solution.py:339
  12.9 1.2 %multiply_convert_fusion.e = bf16[512,512]{1,0:T(8,128)(2,1)S(1)} fusion(bf16[512,512]{1,0:T(8,128)(2,1)} %v.1, f32[512]{0:T(512)S(1)} %bitcast.5), kind=kLoop, calls=%fused_computation | loop fusion | flops 786432 | bytes 1050624 | tf_op jit(solution)/shard_map/convert_element_type | solution.py:394
  14.1 1.6 %collective-permute-start.5 = (bf16[512,512]{1,0:T(8,128)(2,1)S(1)}, bf16[512,512]{1,0:T(8,128)(2,1)S(1)}, u32[]{:S(2)}, u32[]{:S(2)}) collective-permute-start(bf16[512,512]{1,0:T(8,128)(2,1)S(1)} %multiply_convert_fusion.e), channel_id=1, source_target_pairs={{0,4},{4,0},{8,12},{12,8},{16,20},{20,16},{24,28},{28,24},{1,5},{5... | collective-permute-start | bytes 1572872 | tf_op jit(solution)/shard_map/ppermute | solution.py:41
  16.3 3.3 %collective-permute-done.2.rest_5_ = bf16[256,512]{1,0:T(8,128)(2,1)S(1)} collective-permute-done((bf16[256,512]{1,0:T(8,128)(2,1)S(1)}, bf16[256,512]{1,0:T(8,128)(2,1)S(1)}, u32[]{:S(2)}, u32[]{:S(2)}) %collective-permute-start.2) | collective-permute-done | bytes 262176 | tf_op jit(solution)/shard_map/ppermute | solution.py:339
  19.6 3.3 %collective-permute-start.3 = (bf16[512,512]{1,0:T(8,128)(2,1)S(1)}, bf16[512,512]{1,0:T(8,128)(2,1)S(1)}, u32[]{:S(2)}, u32[]{:S(2)}) collective-permute-start(bf16[512,512]{1,0:T(8,128)(2,1)S(1)} %collective-permute-done.k.pair_k), channel_id=1, source_target_pairs={{0,8},{8,16},{16,24},{1,9},{9,17},{17,25},{2,10},{10,18},{18,26},{... | collective-permute-start | bytes 1572872 | tf_op jit(solution)/shard_map/ppermute | solution.py:404
  23.7 1.4 %copy-done = bf16[1,3,512,512]{3,2,1,0:T(8,128)(2,1)S(1)} copy-done((bf16[1,3,512,512]{3,2,1,0:T(8,128)(2,1)S(1)}, bf16[1,3,512,512]{3,2,1,0:T(8,128)(2,1)}, u32[]{:S(2)}) %copy-start) | copy-done | bytes 1572888
  25.1 1.0 %copy-done.3 = bf16[512,512]{1,0:T(8,128)(2,1)S(1)} copy-done((bf16[512,512]{1,0:T(8,128)(2,1)S(1)}, bf16[512,512]{1,0:T(8,128)(2,1)}, u32[]{:S(2)}) %copy-start.3) | copy-done | bytes 524312
  26.1 2.8 %own_gradients.1.acc = f32[4,3,64,512]{3,2,1,0:T(8,128)S(1)} custom-call(s32[12]{0:T(128)S(1)} %dynamic-slice_bitcast_fusion.place, bf16[512,512]{1,0:T(8,128)(2,1)S(1)} %copy-done.3, bf16[512,512]{1,0:T(8,128)(2,1)S(1)} %multiply_convert_fusion.e, bf16[1,3,512,512]{3,2,1,0:T(8,128)(2,1)S(1)} %copy-done), custom_call_target="tpu_custom_call" | custom-call | flops 1 | bytes 1 | tf_op jit(solution)/shard_map/own_gradients/pallas_call | solution.py:122
  29.6 2.2 %collective-permute-done.3.up_k = bf16[512,512]{1,0:T(8,128)(2,1)S(1)} collective-permute-done((bf16[512,512]{1,0:T(8,128)(2,1)S(1)}, bf16[512,512]{1,0:T(8,128)(2,1)S(1)}, u32[]{:S(2)}, u32[]{:S(2)}) %collective-permute-start.3) | collective-permute-done | bytes 524320 | tf_op jit(solution)/shard_map/ppermute | solution.py:404
  31.8 2.8 %both_gradients.1 = (f32[3,64,512]{2,1,0:T(8,128)S(1)}, bf16[3,64,512]{2,1,0:T(8,128)(2,1)S(1)}, bf16[3,64,512]{2,1,0:T(8,128)(2,1)S(1)}, bf16[3,64,512]{2,1,0:T(8,128)(2,1)S(1)}) custom-call(s32[12]{0:T(128)S(1)} %dynamic-slice_bitcast_fusion.place, bf16[512,512]{1,0:T(8,128)(2,1)S(1)} %collective-permute-done.k.pair_k, ...), custom_call_target="tpu_custom_call" | custom-call | flops 1 | bytes 1 | tf_op jit(solution)/shard_map/both_gradients/pallas_call | solution.py:137
  35.0 4.7 %collective-permute-start.9 = (bf16[3,64,512]{2,1,0:T(8,128)(2,1)S(1)}, bf16[3,64,512]{2,1,0:T(8,128)(2,1)S(1)}, u32[]{:S(2)}, u32[]{:S(2)}) collective-permute-start(bf16[3,64,512]{2,1,0:T(8,128)(2,1)S(1)} %get-tuple-element.27), channel_id=1, source_target_pairs={{0,24},{4,28},{8,16},{12,20},{16,8},{20,12},{24,0},{28,4},{1,25},{... | collective-permute-start | bytes 589832 | tf_op jit(solution)/shard_map/ppermute | solution.py:41
  40.3 5.2 %collective-permute-done.9.rest_2_ = bf16[3,64,512]{2,1,0:T(8,128)(2,1)S(1)} collective-permute-done((bf16[3,64,512]{2,1,0:T(8,128)(2,1)S(1)}, bf16[3,64,512]{2,1,0:T(8,128)(2,1)S(1)}, u32[]{:S(2)}, u32[]{:S(2)}) %collective-permute-start.9) | collective-permute-done | bytes 196640 | tf_op jit(solution)/shard_map/ppermute | solution.py:41
  45.5 10.8 %collective-permute-done.6.early_v.rest_7_ = bf16[1024,512]{1,0:T(8,128)(2,1)S(1)} collective-permute-done((bf16[1024,512]{1,0:T(8,128)(2,1)S(1)}, bf16[1024,512]{1,0:T(8,128)(2,1)S(1)}, u32[]{:S(2)}, u32[]{:S(2)}) %collective-permute-start.6) | collective-permute-done | bytes 1048608 | tf_op jit(solution)/shard_map/ppermute | solution.py:41
  57.2 2.5 %collective-permute-start.10 = (bf16[3,64,512]{2,1,0:T(8,128)(2,1)S(1)}, bf16[3,64,512]{2,1,0:T(8,128)(2,1)S(1)}, u32[]{:S(2)}, u32[]{:S(2)}) collective-permute-start(bf16[3,64,512]{2,1,0:T(8,128)(2,1)S(1)} %renew.1.rest_0_), channel_id=1, source_target_pairs={{0,8},{4,12},{8,0},{12,4},{16,24},{20,28},{24,16},{28,20},{1,9},{5... | collective-permute-start | bytes 589832 | tf_op jit(solution)/shard_map/ppermute | solution.py:41
  59.7 1.7 %collective-permute-start.11 = (bf16[3,64,512]{2,1,0:T(8,128)(2,1)S(1)}, bf16[3,64,512]{2,1,0:T(8,128)(2,1)S(1)}, u32[]{:S(2)}, u32[]{:S(2)}) collective-permute-start(bf16[3,64,512]{2,1,0:T(8,128)(2,1)S(1)} %renew.1.rest_0_), channel_id=1, source_target_pairs={{0,4},{4,0},{8,12},{12,8},{16,20},{20,16},{24,28},{28,24},{1,5},{5... | collective-permute-start | bytes 589832 | tf_op jit(solution)/shard_map/ppermute | solution.py:41
  61.5 3.3 %collective-permute-start.13 = (bf16[3,64,512]{2,1,0:T(8,128)(2,1)S(1)}, bf16[3,64,512]{2,1,0:T(8,128)(2,1)S(1)}, u32[]{:S(2)}, u32[]{:S(2)}) collective-permute-start(bf16[3,64,512]{2,1,0:T(8,128)(2,1)S(1)} %renew.1.rest_0_), channel_id=1, source_target_pairs={{0,24},{4,28},{8,16},{12,20},{16,8},{20,12},{24,0},{28,4},{1,25},{... | collective-permute-start | bytes 589832 | tf_op jit(solution)/shard_map/ppermute | solution.py:41
  66.0 2.5 %collective-permute-start.14 = (bf16[3,64,512]{2,1,0:T(8,128)(2,1)S(1)}, bf16[3,64,512]{2,1,0:T(8,128)(2,1)S(1)}, u32[]{:S(2)}, u32[]{:S(2)}) collective-permute-start(bf16[3,64,512]{2,1,0:T(8,128)(2,1)S(1)} %collective-permute-done.10.rest_1_), channel_id=1, source_target_pairs={{0,4},{4,0},{8,12},{12,8},{16,20},{20,16},{24,28},{28,24},{1,5},{5... | collective-permute-start | bytes 589832 | tf_op jit(solution)/shard_map/ppermute | solution.py:41
  68.6 3.4 %collective-permute-done.13.rest_3_ = bf16[3,64,512]{2,1,0:T(8,128)(2,1)S(1)} collective-permute-done((bf16[3,64,512]{2,1,0:T(8,128)(2,1)S(1)}, bf16[3,64,512]{2,1,0:T(8,128)(2,1)S(1)}, u32[]{:S(2)}, u32[]{:S(2)}) %collective-permute-start.13) | collective-permute-done | bytes 196640 | tf_op jit(solution)/shard_map/ppermute | solution.py:41
  72.0 2.3 %collective-permute-start.16 = (bf16[3,64,512]{2,1,0:T(8,128)(2,1)S(1)}, bf16[3,64,512]{2,1,0:T(8,128)(2,1)S(1)}, u32[]{:S(2)}, u32[]{:S(2)}) collective-permute-start(bf16[3,64,512]{2,1,0:T(8,128)(2,1)S(1)} %collective-permute-done.13.rest_3_), channel_id=1, source_target_pairs={{0,4},{4,0},{8,12},{12,8},{16,20},{20,16},{24,28},{28,24},{1,5},{5... | collective-permute-start | bytes 589832 | tf_op jit(solution)/shard_map/ppermute | solution.py:41
  74.2 6.1 %collective-permute-done.12.rest_2_ = bf16[3,64,512]{2,1,0:T(8,128)(2,1)S(1)} collective-permute-done((bf16[3,64,512]{2,1,0:T(8,128)(2,1)S(1)}, bf16[3,64,512]{2,1,0:T(8,128)(2,1)S(1)}, u32[]{:S(2)}, u32[]{:S(2)}) %collective-permute-start.12) | collective-permute-done | bytes 196640 | tf_op jit(solution)/shard_map/ppermute | solution.py:41
  80.8 2.3 %window_attention.1.attended = f32[512,512]{1,0:T(8,128)S(1)} custom-call(s32[12]{0:T(128)S(1)} %dynamic-slice_bitcast_fusion.place, bf16[512,512]{1,0:T(8,128)(2,1)S(1)} %copy-done.5, bf16[512,512]{1,0:T(8,128)(2,1)S(1)} %copy-done.4, bf16[512,512]{1,0:T(8,128)(2,1)S(1)} %copy-done.2, bf16[512,512]{1,0:T(8,128)(2,1)S(1)} %collective-permute-done.k.pair_k, ...), custom_call_target="tpu_custom_call" | custom-call | flops 1 | bytes 1 | tf_op jit(solution)/shard_map/window_attention/pallas_call | solution.py:179
  84.1 2.0 %collective-permute-done.15.rest_6_ = bf16[3,64,512]{2,1,0:T(8,128)(2,1)S(1)} collective-permute-done((bf16[3,64,512]{2,1,0:T(8,128)(2,1)S(1)}, bf16[3,64,512]{2,1,0:T(8,128)(2,1)S(1)}, u32[]{:S(2)}, u32[]{:S(2)}) %collective-permute-start.15) | collective-permute-done | bytes 196640 | tf_op jit(solution)/shard_map/ppermute | solution.py:41
  86.1 1.7 %apply_fast.1.rest_0_ = bf16[512,512]{1,0:T(8,128)(2,1)S(1)} custom-call(s32[12]{0:T(128)S(1)} %dynamic-slice_bitcast_fusion.place, bf16[512,512]{1,0:T(8,128)(2,1)S(1)} %copy-done.5, f32[512,512]{1,0:T(8,128)S(1)} %window_attention.1.attended, bf16[3,64,512]{2,1,0:T(8,128)(2,1)S(1)} %renew.1.rest_0_, ...), custom_call_target="tpu_custom_call" | custom-call | flops 1 | bytes 1 | tf_op jit(solution)/shard_map/apply_fast/pallas_call | solution.py:260
  87.7 1.6 %collective-permute-start.19 = (bf16[512,512]{1,0:T(8,128)(2,1)S(1)}, bf16[512,512]{1,0:T(8,128)(2,1)S(1)}, u32[]{:S(2)}, u32[]{:S(2)}) collective-permute-start(bf16[512,512]{1,0:T(8,128)(2,1)S(1)} %apply_fast.1.rest_0_), channel_id=1, source_target_pairs={{0,2},{1,3},{2,0},{3,1},{4,6},{5,7},{6,4},{7,5},{8,10},{9,11},{10,... | collective-permute-start | bytes 1572872 | tf_op jit(solution)/shard_map/ppermute | solution.py:41
  89.3 2.3 %collective-permute-done.20.rest_6_ = bf16[256,512]{1,0:T(8,128)(2,1)S(1)} collective-permute-done((bf16[256,512]{1,0:T(8,128)(2,1)S(1)}, bf16[256,512]{1,0:T(8,128)(2,1)S(1)}, u32[]{:S(2)}, u32[]{:S(2)}) %collective-permute-start.20) | collective-permute-done | bytes 262176 | tf_op jit(solution)/shard_map/ppermute | solution.py:339
  91.6 1.8 %collective-permute-start.21 = (bf16[256,512]{1,0:T(8,128)(2,1)S(1)}, bf16[256,512]{1,0:T(8,128)(2,1)S(1)}, u32[]{:S(2)}, u32[]{:S(2)}) collective-permute-start(bf16[256,512]{1,0:T(8,128)(2,1)S(1)} %collective-permute-done.20.rest_6_), channel_id=1, source_target_pairs={{0,4},{4,0},{8,12},{12,8},{16,20},{20,16},{24,28},{28,24},{1,5},{5... | collective-permute-start | bytes 786440 | tf_op jit(solution)/shard_map/ppermute | solution.py:41
  93.3 4.6 %collective-permute-done.21.rest_9_ = bf16[256,512]{1,0:T(8,128)(2,1)S(1)} collective-permute-done((bf16[256,512]{1,0:T(8,128)(2,1)S(1)}, bf16[256,512]{1,0:T(8,128)(2,1)S(1)}, u32[]{:S(2)}, u32[]{:S(2)}) %collective-permute-start.21) | collective-permute-done | bytes 262176 | tf_op jit(solution)/shard_map/ppermute | solution.py:41
  97.9 1.4 %collective-permute-done.19.rest_2_ = bf16[512,512]{1,0:T(8,128)(2,1)S(1)} collective-permute-done((bf16[512,512]{1,0:T(8,128)(2,1)S(1)}, bf16[512,512]{1,0:T(8,128)(2,1)S(1)}, u32[]{:S(2)}, u32[]{:S(2)}) %collective-permute-start.19) | collective-permute-done | bytes 524320 | tf_op jit(solution)/shard_map/ppermute | solution.py:41
  99.3 1.7 %project_most.1 = (f32[512,512]{1,0:T(8,128)S(1)}, bf16[512,512]{1,0:T(8,128)(2,1)S(1)}) custom-call(s32[12]{0:T(128)S(1)} %dynamic-slice_bitcast_fusion.place, bf16[512,512]{1,0:T(8,128)(2,1)S(1)} %apply_fast.1.rest_0_, bf16[512,512]{1,0:T(8,128)(2,1)S(1)} %collective-permute-done.18.rest_1_, bf16[512,512]{1,0:T(8,128)(2,1)S(1)} %collective-permute-done.19.rest_2_, ...), custom_call_target="tpu_custom_call" | custom-call | flops 1 | bytes 1 | tf_op jit(solution)/shard_map/project_most/pallas_call | solution.py:297
  101.2 1.2 %project_last.1 = bf16[512,512]{1,0:T(8,128)(2,1)} custom-call(f32[512,512]{1,0:T(8,128)S(1)} %get-tuple-element.36.partial, bf16[512,512]{1,0:T(8,128)(2,1)S(1)} %collective-permute-done.22.block, bf16[512,512]{1,0:T(8,128)(2,1)S(1)} %get-tuple-element.37.rows), custom_call_target="tpu_custom_call" | custom-call | flops 1 | bytes 1 | tf_op jit(solution)/shard_map/project_last/pallas_call | solution.py:318
  (42 shorter events, 8.5 us)
Async XLA Ops:
  0.6 10.6 %collective-permute-start.1 = (bf16[256,512]{1,0:T(8,128)(2,1)}, bf16[256,512]{1,0:T(8,128)(2,1)S(1)}, u32[]{:S(2)}, u32[]{:S(2)}) collective-permute-start(bf16[256,512]{1,0:T(8,128)(2,1)} %rest_3_.1), channel_id=1, source_target_pairs={{0,8},{4,12},{8,24},{12,28},{24,16},{28,20},{16,0},{20,4},{1,9},{5... | collective-permute-start | bytes 786440 | tf_op jit(solution)/shard_map/ppermute | solution.py:339
  3.7 15.9 %collective-permute-start = (bf16[512,512]{1,0:T(8,128)(2,1)}, bf16[512,512]{1,0:T(8,128)(2,1)S(1)}, u32[]{:S(2)}, u32[]{:S(2)}) collective-permute-start(bf16[512,512]{1,0:T(8,128)(2,1)} %k.3), channel_id=1, source_target_pairs={{0,4},{4,0},{8,12},{12,8},{16,20},{20,16},{24,28},{28,24},{1,5},{5... | collective-permute-start | bytes 1572872 | tf_op jit(solution)/shard_map/ppermute | solution.py:41
  11.2 8.4 %collective-permute-start.2 = (bf16[256,512]{1,0:T(8,128)(2,1)S(1)}, bf16[256,512]{1,0:T(8,128)(2,1)S(1)}, u32[]{:S(2)}, u32[]{:S(2)}) collective-permute-start(bf16[256,512]{1,0:T(8,128)(2,1)S(1)} %collective-permute-done.1.rest_1_.rest_4_), channel_id=1, source_target_pairs={{0,8},{4,12},{8,24},{12,28},{24,16},{28,20},{16,0},{20,4},{1,9},{5... | collective-permute-start | bytes 786440 | tf_op jit(solution)/shard_map/ppermute | solution.py:339
  14.1 15.5 %collective-permute-start.5 = (bf16[512,512]{1,0:T(8,128)(2,1)S(1)}, bf16[512,512]{1,0:T(8,128)(2,1)S(1)}, u32[]{:S(2)}, u32[]{:S(2)}) collective-permute-start(bf16[512,512]{1,0:T(8,128)(2,1)S(1)} %multiply_convert_fusion.e), channel_id=1, source_target_pairs={{0,4},{4,0},{8,12},{12,8},{16,20},{20,16},{24,28},{28,24},{1,5},{5... | collective-permute-start | bytes 1572872 | tf_op jit(solution)/shard_map/ppermute | solution.py:41
  15.7 13.3 %collective-permute-start.4 = (bf16[512,512]{1,0:T(8,128)(2,1)}, bf16[512,512]{1,0:T(8,128)(2,1)S(1)}, u32[]{:S(2)}, u32[]{:S(2)}) collective-permute-start(bf16[512,512]{1,0:T(8,128)(2,1)} %v.1), channel_id=1, source_target_pairs={{4,12},{12,20},{20,28},{5,13},{13,21},{21,29},{6,14},{14,22},{22,3... | collective-permute-start | bytes 1572872 | tf_op jit(solution)/shard_map/ppermute | solution.py:402
  19.6 12.1 %collective-permute-start.3 = (bf16[512,512]{1,0:T(8,128)(2,1)S(1)}, bf16[512,512]{1,0:T(8,128)(2,1)S(1)}, u32[]{:S(2)}, u32[]{:S(2)}) collective-permute-start(bf16[512,512]{1,0:T(8,128)(2,1)S(1)} %collective-permute-done.k.pair_k), channel_id=1, source_target_pairs={{0,8},{8,16},{16,24},{1,9},{9,17},{17,25},{2,10},{10,18},{18,26},{... | collective-permute-start | bytes 1572872 | tf_op jit(solution)/shard_map/ppermute | solution.py:404
  23.7 1.4 %copy-start = (bf16[1,3,512,512]{3,2,1,0:T(8,128)(2,1)S(1)}, bf16[1,3,512,512]{3,2,1,0:T(8,128)(2,1)}, u32[]{:S(2)}) copy-start(bf16[1,3,512,512]{3,2,1,0:T(8,128)(2,1)} %w.5) | copy-start | bytes 4718596
  25.1 1.0 %copy-start.3 = (bf16[512,512]{1,0:T(8,128)(2,1)S(1)}, bf16[512,512]{1,0:T(8,128)(2,1)}, u32[]{:S(2)}) copy-start(bf16[512,512]{1,0:T(8,128)(2,1)} %k.3) | copy-start | bytes 1572868
  26.1 2.8 %copy-start.2 = (bf16[512,512]{1,0:T(8,128)(2,1)S(1)}, bf16[512,512]{1,0:T(8,128)(2,1)}, u32[]{:S(2)}) copy-start(bf16[512,512]{1,0:T(8,128)(2,1)} %v.1) | copy-start | bytes 1572868
  26.1 2.8 %copy-start.7 = (bf16[256,512]{1,0:T(8,128)(2,1)S(1)}, bf16[256,512]{1,0:T(8,128)(2,1)}, u32[]{:S(2)}) copy-start(bf16[256,512]{1,0:T(8,128)(2,1)} %rest_3_.1) | copy-start | bytes 786436
  28.9 2.9 %copy-start.1 = (bf16[1,3,512,512]{3,2,1,0:T(8,128)(2,1)S(1)}, bf16[1,3,512,512]{3,2,1,0:T(8,128)(2,1)}, u32[]{:S(2)}) copy-start(bf16[1,3,512,512]{3,2,1,0:T(8,128)(2,1)} %w.5) | copy-start | bytes 4718596
  29.6 26.8 %copy-start.6 = (f32[1,3,64,512]{3,2,1,0:T(8,128)S(1)}, f32[1,3,64,512]{3,2,1,0:T(8,128)}, u32[]{:S(2)}) copy-start(f32[1,3,64,512]{3,2,1,0:T(8,128)} %momentum.1) | copy-start | bytes 1179652
  34.6 21.7 %collective-permute-start.6 = (bf16[1024,512]{1,0:T(8,128)(2,1)S(1)}, bf16[1024,512]{1,0:T(8,128)(2,1)S(1)}, u32[]{:S(2)}, u32[]{:S(2)}) collective-permute-start(bf16[1024,512]{1,0:T(8,128)(2,1)S(1)} %crossing.1), channel_id=1, source_target_pairs={{0,4},{4,0},{8,12},{12,8},{16,20},{20,16},{24,28},{28,24},{1,5},{5... | collective-permute-start | bytes 3145736 | tf_op jit(solution)/shard_map/ppermute | solution.py:41
  35.0 10.5 %collective-permute-start.9 = (bf16[3,64,512]{2,1,0:T(8,128)(2,1)S(1)}, bf16[3,64,512]{2,1,0:T(8,128)(2,1)S(1)}, u32[]{:S(2)}, u32[]{:S(2)}) collective-permute-start(bf16[3,64,512]{2,1,0:T(8,128)(2,1)S(1)} %get-tuple-element.27), channel_id=1, source_target_pairs={{0,24},{4,28},{8,16},{12,20},{16,8},{20,12},{24,0},{28,4},{1,25},{... | collective-permute-start | bytes 589832 | tf_op jit(solution)/shard_map/ppermute | solution.py:41
  39.7 16.6 %collective-permute-start.7 = (bf16[3,64,512]{2,1,0:T(8,128)(2,1)S(1)}, bf16[3,64,512]{2,1,0:T(8,128)(2,1)S(1)}, u32[]{:S(2)}, u32[]{:S(2)}) collective-permute-start(bf16[3,64,512]{2,1,0:T(8,128)(2,1)S(1)} %get-tuple-element.23), channel_id=1, source_target_pairs={{0,8},{4,12},{8,0},{12,4},{16,24},{20,28},{24,16},{28,20},{1,9},{5... | collective-permute-start | bytes 589832 | tf_op jit(solution)/shard_map/ppermute | solution.py:41
  39.7 16.6 %collective-permute-start.8 = (bf16[3,64,512]{2,1,0:T(8,128)(2,1)S(1)}, bf16[3,64,512]{2,1,0:T(8,128)(2,1)S(1)}, u32[]{:S(2)}, u32[]{:S(2)}) collective-permute-start(bf16[3,64,512]{2,1,0:T(8,128)(2,1)S(1)} %get-tuple-element.26), channel_id=1, source_target_pairs={{0,16},{4,20},{8,24},{12,28},{16,0},{20,4},{24,8},{28,12},{1,17},{... | collective-permute-start | bytes 589832 | tf_op jit(solution)/shard_map/ppermute | solution.py:41
  56.3 24.5 %copy-start.4 = (bf16[512,512]{1,0:T(8,128)(2,1)S(1)}, bf16[512,512]{1,0:T(8,128)(2,1)}, u32[]{:S(2)}) copy-start(bf16[512,512]{1,0:T(8,128)(2,1)} %k.3) | copy-start | bytes 1572868
  56.3 24.5 %copy-start.5 = (bf16[512,512]{1,0:T(8,128)(2,1)S(1)}, bf16[512,512]{1,0:T(8,128)(2,1)}, u32[]{:S(2)}) copy-start(bf16[512,512]{1,0:T(8,128)(2,1)} %q.3) | copy-start | bytes 1572868
  57.2 8.1 %collective-permute-start.10 = (bf16[3,64,512]{2,1,0:T(8,128)(2,1)S(1)}, bf16[3,64,512]{2,1,0:T(8,128)(2,1)S(1)}, u32[]{:S(2)}, u32[]{:S(2)}) collective-permute-start(bf16[3,64,512]{2,1,0:T(8,128)(2,1)S(1)} %renew.1.rest_0_), channel_id=1, source_target_pairs={{0,8},{4,12},{8,0},{12,4},{16,24},{20,28},{24,16},{28,20},{1,9},{5... | collective-permute-start | bytes 589832 | tf_op jit(solution)/shard_map/ppermute | solution.py:41
  59.7 6.3 %collective-permute-start.11 = (bf16[3,64,512]{2,1,0:T(8,128)(2,1)S(1)}, bf16[3,64,512]{2,1,0:T(8,128)(2,1)S(1)}, u32[]{:S(2)}, u32[]{:S(2)}) collective-permute-start(bf16[3,64,512]{2,1,0:T(8,128)(2,1)S(1)} %renew.1.rest_0_), channel_id=1, source_target_pairs={{0,4},{4,0},{8,12},{12,8},{16,20},{20,16},{24,28},{28,24},{1,5},{5... | collective-permute-start | bytes 589832 | tf_op jit(solution)/shard_map/ppermute | solution.py:41
  61.5 10.5 %collective-permute-start.13 = (bf16[3,64,512]{2,1,0:T(8,128)(2,1)S(1)}, bf16[3,64,512]{2,1,0:T(8,128)(2,1)S(1)}, u32[]{:S(2)}, u32[]{:S(2)}) collective-permute-start(bf16[3,64,512]{2,1,0:T(8,128)(2,1)S(1)} %renew.1.rest_0_), channel_id=1, source_target_pairs={{0,24},{4,28},{8,16},{12,20},{16,8},{20,12},{24,0},{28,4},{1,25},{... | collective-permute-start | bytes 589832 | tf_op jit(solution)/shard_map/ppermute | solution.py:41
  64.8 15.6 %collective-permute-start.12 = (bf16[3,64,512]{2,1,0:T(8,128)(2,1)S(1)}, bf16[3,64,512]{2,1,0:T(8,128)(2,1)S(1)}, u32[]{:S(2)}, u32[]{:S(2)}) collective-permute-start(bf16[3,64,512]{2,1,0:T(8,128)(2,1)S(1)} %renew.1.rest_0_), channel_id=1, source_target_pairs={{0,16},{4,20},{8,24},{12,28},{16,0},{20,4},{24,8},{28,12},{1,17},{... | collective-permute-start | bytes 589832 | tf_op jit(solution)/shard_map/ppermute | solution.py:41
  66.0 18.0 %collective-permute-start.14 = (bf16[3,64,512]{2,1,0:T(8,128)(2,1)S(1)}, bf16[3,64,512]{2,1,0:T(8,128)(2,1)S(1)}, u32[]{:S(2)}, u32[]{:S(2)}) collective-permute-start(bf16[3,64,512]{2,1,0:T(8,128)(2,1)S(1)} %collective-permute-done.10.rest_1_), channel_id=1, source_target_pairs={{0,4},{4,0},{8,12},{12,8},{16,20},{20,16},{24,28},{28,24},{1,5},{5... | collective-permute-start | bytes 589832 | tf_op jit(solution)/shard_map/ppermute | solution.py:41
  68.5 15.5 %collective-permute-start.17 = (bf16[256,512]{1,0:T(8,128)(2,1)S(1)}, bf16[256,512]{1,0:T(8,128)(2,1)S(1)}, u32[]{:S(2)}, u32[]{:S(2)}) collective-permute-start(bf16[256,512]{1,0:T(8,128)(2,1)S(1)} %collective-permute-done.2.rest_5_), channel_id=1, source_target_pairs={{0,4},{4,0},{8,12},{12,8},{16,20},{20,16},{24,28},{28,24},{1,5},{5... | collective-permute-start | bytes 786440 | tf_op jit(solution)/shard_map/ppermute | solution.py:41
  72.0 12.1 %collective-permute-start.16 = (bf16[3,64,512]{2,1,0:T(8,128)(2,1)S(1)}, bf16[3,64,512]{2,1,0:T(8,128)(2,1)S(1)}, u32[]{:S(2)}, u32[]{:S(2)}) collective-permute-start(bf16[3,64,512]{2,1,0:T(8,128)(2,1)S(1)} %collective-permute-done.13.rest_3_), channel_id=1, source_target_pairs={{0,4},{4,0},{8,12},{12,8},{16,20},{20,16},{24,28},{28,24},{1,5},{5... | collective-permute-start | bytes 589832 | tf_op jit(solution)/shard_map/ppermute | solution.py:41
  80.3 5.7 %collective-permute-start.15 = (bf16[3,64,512]{2,1,0:T(8,128)(2,1)S(1)}, bf16[3,64,512]{2,1,0:T(8,128)(2,1)S(1)}, u32[]{:S(2)}, u32[]{:S(2)}) collective-permute-start(bf16[3,64,512]{2,1,0:T(8,128)(2,1)S(1)} %collective-permute-done.12.rest_2_), channel_id=1, source_target_pairs={{0,4},{4,0},{8,12},{12,8},{16,20},{20,16},{24,28},{28,24},{1,5},{5... | collective-permute-start | bytes 589832 | tf_op jit(solution)/shard_map/ppermute | solution.py:41
  84.0 7.5 %collective-permute-start.20 = (bf16[256,512]{1,0:T(8,128)(2,1)S(1)}, bf16[256,512]{1,0:T(8,128)(2,1)S(1)}, u32[]{:S(2)}, u32[]{:S(2)}) collective-permute-start(bf16[256,512]{1,0:T(8,128)(2,1)S(1)} %collective-permute-done.2.rest_5_), channel_id=1, source_target_pairs={{0,8},{4,12},{8,24},{12,28},{24,16},{28,20},{16,0},{20,4},{1,9},{5... | collective-permute-start | bytes 786440 | tf_op jit(solution)/shard_map/ppermute | solution.py:339
  87.7 11.6 %collective-permute-start.19 = (bf16[512,512]{1,0:T(8,128)(2,1)S(1)}, bf16[512,512]{1,0:T(8,128)(2,1)S(1)}, u32[]{:S(2)}, u32[]{:S(2)}) collective-permute-start(bf16[512,512]{1,0:T(8,128)(2,1)S(1)} %apply_fast.1.rest_0_), channel_id=1, source_target_pairs={{0,2},{1,3},{2,0},{3,1},{4,6},{5,7},{6,4},{7,5},{8,10},{9,11},{10,... | collective-permute-start | bytes 1572872 | tf_op jit(solution)/shard_map/ppermute | solution.py:41
  91.6 6.4 %collective-permute-start.21 = (bf16[256,512]{1,0:T(8,128)(2,1)S(1)}, bf16[256,512]{1,0:T(8,128)(2,1)S(1)}, u32[]{:S(2)}, u32[]{:S(2)}) collective-permute-start(bf16[256,512]{1,0:T(8,128)(2,1)S(1)} %collective-permute-done.20.rest_6_), channel_id=1, source_target_pairs={{0,4},{4,0},{8,12},{12,8},{16,20},{20,16},{24,28},{28,24},{1,5},{5... | collective-permute-start | bytes 786440 | tf_op jit(solution)/shard_map/ppermute | solution.py:41
  93.3 6.0 %collective-permute-start.18 = (bf16[512,512]{1,0:T(8,128)(2,1)S(1)}, bf16[512,512]{1,0:T(8,128)(2,1)S(1)}, u32[]{:S(2)}, u32[]{:S(2)}) collective-permute-start(bf16[512,512]{1,0:T(8,128)(2,1)S(1)} %apply_fast.1.rest_0_), channel_id=1, source_target_pairs={{0,1},{1,0},{2,3},{3,2},{4,5},{5,4},{6,7},{7,6},{8,9},{9,8},{10,11... | collective-permute-start | bytes 1572872 | tf_op jit(solution)/shard_map/ppermute | solution.py:41
  99.3 1.9 %collective-permute-start.22 = (bf16[512,512]{1,0:T(8,128)(2,1)S(1)}, bf16[512,512]{1,0:T(8,128)(2,1)S(1)}, u32[]{:S(2)}, u32[]{:S(2)}) collective-permute-start(bf16[512,512]{1,0:T(8,128)(2,1)S(1)} %collective-permute-done.19.rest_2_), channel_id=1, source_target_pairs={{0,1},{1,0},{2,3},{3,2},{4,5},{5,4},{6,7},{7,6},{8,9},{9,8},{10,11... | collective-permute-start | bytes 1572872 | tf_op jit(solution)/shard_map/ppermute | solution.py:41

commit v10 on v7

--- a/solution.py
+++ b/solution.py
@@ -49,102 +49,124 @@
     return pl.BlockSpec(memory_space=pltpu.VMEM)
 
 
-def gradient_rows(outer, side, k, e, w, eye, hg_s, hu_s, err_s, dg_s, du_s):
-    tokens, hidden = k.shape
-    own = hidden // (2 * outer)
-    hg = times_transposed(w[0], k)
-    hu = times_transposed(w[1], k)
-    hg_s[...] = hg
-    hu_s[...] = hu
-    gated = (hg * jax.nn.sigmoid(hg) * hu).astype(jnp.bfloat16)
-    err_s[...] = times_transposed(eye, e).astype(jnp.bfloat16)
-    down_t = times_transposed(eye, w[2]).astype(jnp.bfloat16)
-    back = matmul(down_t, err_s[...])
-    dg_s[2] = back
-    errors = []
-    for z in range(outer):
-        rows = pl.ds(pl.multiple_of((2 * z + side) * own, own), own)
-        to = pl.ds(z * own, own)
-        g, u, b = hg_s[rows], hu_s[rows], dg_s[2, rows]
-        s = jax.nn.sigmoid(g)
-        du_s[0, to] = (b * u * s * (1.0 + g * (1.0 - s))).astype(jnp.bfloat16)
-        du_s[1, to] = (b * g * s).astype(jnp.bfloat16)
-        du_s[2, to] = err_s[rows]
-    return (
-        matmul(du_s[0], k),
-        matmul(du_s[1], k),
-        times_transposed(du_s[2], gated),
-    )
-
-
 def identity(size):
     rows = lax.broadcasted_iota(jnp.int32, (size, size), 0)
     columns = lax.broadcasted_iota(jnp.int32, (size, size), 1)
     return jnp.where(rows == columns, 1.0, 0.0).astype(jnp.bfloat16)
 
 
-def own_kernel(outer, place, k, e, w, acc, *scratch):
-    eye = identity(e.shape[1])
-    parts = gradient_rows(outer, place[0], k[...], e[...], w[0], eye, *scratch)
-    own = acc.shape[2]
+def parity_rows(place, z, own):
+    return pl.ds(pl.multiple_of((2 * z + place[0]) * own, own), own)
+
+
+def keys_kernel(outer, place, k, w, gated, gate, up, down, hg_s, hu_s, down_s):
+    own = gate.shape[0] // outer
+    hg = times_transposed(w[0, 0], k[...])
+    hu = times_transposed(w[0, 1], k[...])
+    hg_s[...] = hg
+    hu_s[...] = hu
+    gated[...] = (hg * jax.nn.sigmoid(hg) * hu).astype(jnp.bfloat16)
+    down_s[...] = times_transposed(identity(w.shape[3]), w[0, 2]).astype(jnp.bfloat16)
+    for z in range(outer):
+        rows, to = parity_rows(place, z, own), pl.ds(z * own, own)
+        g, u = hg_s[rows], hu_s[rows]
+        s = jax.nn.sigmoid(g)
+        gate[to] = u * s * (1.0 + g * (1.0 - s))
+        up[to] = g * s
+        down[to] = down_s[rows]
+
+
+def keys_part(place, k, w, outer):
+    tokens, hidden = k.shape
+    half = jax.ShapeDtypeStruct((hidden // 2, tokens), jnp.float32)
+    return pl.pallas_call(
+        functools.partial(keys_kernel, outer),
+        out_shape=[
+            jax.ShapeDtypeStruct((hidden, tokens), jnp.bfloat16),
+            half,
+            half,
+            jax.ShapeDtypeStruct((hidden // 2, hidden), jnp.bfloat16),
+        ],
+        in_specs=[pl.BlockSpec(memory_space=pltpu.SMEM)] + [whole_spec()] * 2,
+        out_specs=[whole_spec()] * 4,
+        scratch_shapes=[
+            pltpu.VMEM((hidden, tokens), jnp.float32),
+            pltpu.VMEM((hidden, tokens), jnp.float32),
+            pltpu.VMEM((hidden, hidden), jnp.bfloat16),
+        ],
+        compiler_params=params(12),
+        cost_estimate=BRIEF,
+        name="keys_part",
+    )(place, k, w)
+
+
+def gradient_rows(outer, place, k, e, gated, gate, up, down, err_s, er_s):
+    own = gate.shape[0] // outer
+    err_s[...] = times_transposed(identity(e.shape[1]), e[...]).astype(jnp.bfloat16)
+    for z in range(outer):
+        er_s[pl.ds(z * own, own)] = err_s[parity_rows(place, z, own)]
+    back = matmul(down[...], err_s[...])
+    return (
+        matmul((back * gate[...]).astype(jnp.bfloat16), k[...]),
+        matmul((back * up[...]).astype(jnp.bfloat16), k[...]),
+        times_transposed(er_s[...], gated[...]),
+    )
+
+
+def own_kernel(outer, place, k, e, gated, gate, up, down, acc, *scratch):
+    parts = gradient_rows(outer, place, k, e, gated, gate, up, down, *scratch)
     for i, part in enumerate(parts):
-        acc[:, i] = part.reshape(outer, own, part.shape[1])
-
-
-def both_kernel(outer, place, k, e, w, acc, mine, *rest):
-    sent, scratch = rest[: outer - 1], rest[outer - 1 :]
-    eye = identity(e.shape[1])
-    parts = gradient_rows(outer, place[0], k[...], e[...], w[0], eye, *scratch)
-    own = acc.shape[2]
-    total = scratch[1]
+        acc[i] = part
+
+
+def both_kernel(outer, place, k, e, gated, gate, up, down, acc, mine, *rest):
+    sent, (total, *scratch) = rest[: outer - 1], rest[outer - 1 :]
+    parts = gradient_rows(outer, place, k, e, gated, gate, up, down, *scratch)
+    own = mine.shape[1]
     for i, part in enumerate(parts):
-        total[pl.ds(0, outer * own), :] = part + acc[:, i].reshape(outer * own, part.shape[1])
-        mine[i] = total[pl.ds(pl.multiple_of(place[1] * own, own), own), :]
+        total[i] = part + acc[i]
+        mine[i] = total[i, pl.ds(pl.multiple_of(place[1] * own, own), own), :]
         for step in range(1, outer):
             other = place[1] ^ step
-            block = total[pl.ds(pl.multiple_of(other * own, own), own), :]
+            block = total[i, pl.ds(pl.multiple_of(other * own, own), own), :]
             sent[step - 1][i] = block.astype(jnp.bfloat16)
 
 
 def gradient_scratch(tokens, hidden):
     return [
-        pltpu.VMEM((hidden, tokens), jnp.float32),
-        pltpu.VMEM((hidden, tokens), jnp.float32),
         pltpu.VMEM((hidden, tokens), jnp.bfloat16),
-        pltpu.VMEM((3, hidden, tokens), jnp.float32),
-        pltpu.VMEM((3, hidden // 2, tokens), jnp.bfloat16),
+        pltpu.VMEM((hidden // 2, tokens), jnp.bfloat16),
     ]
 
 
-def own_gradients(place, k, e, w, outer):
+def own_gradients(place, k, e, factors, outer):
     tokens, hidden = k.shape
-    own = hidden // (2 * outer)
     return pl.pallas_call(
         functools.partial(own_kernel, outer),
-        out_shape=jax.ShapeDtypeStruct((outer, 3, own, hidden), jnp.float32),
-        in_specs=[pl.BlockSpec(memory_space=pltpu.SMEM)] + [whole_spec()] * 3,
+        out_shape=jax.ShapeDtypeStruct((3, hidden // 2, hidden), jnp.float32),
+        in_specs=[pl.BlockSpec(memory_space=pltpu.SMEM)] + [whole_spec()] * 6,
         out_specs=whole_spec(),
         scratch_shapes=gradient_scratch(tokens, hidden),
         compiler_params=params(12),
         cost_estimate=BRIEF,
         name="own_gradients",
-    )(place, k, e, w)
-
-
-def both_gradients(place, k, e, w, acc, outer):
+    )(place, k, e, *factors)
+
+
+def both_gradients(place, k, e, factors, acc, outer):
     tokens, hidden = k.shape
     own = hidden // (2 * outer)
     return pl.pallas_call(
         functools.partial(both_kernel, outer),
         out_shape=[jax.ShapeDtypeStruct((3, own, hidden), jnp.float32)]
         + [jax.ShapeDtypeStruct((3, own, hidden), jnp.bfloat16)] * (outer - 1),
-        in_specs=[pl.BlockSpec(memory_space=pltpu.SMEM)] + [whole_spec()] * 4,
+        in_specs=[pl.BlockSpec(memory_space=pltpu.SMEM)] + [whole_spec()] * 7,
         out_specs=[whole_spec()] * outer,
-        scratch_shapes=gradient_scratch(tokens, hidden),
+        scratch_shapes=[pltpu.VMEM(acc.shape, jnp.float32)] + gradient_scratch(tokens, hidden),
         compiler_params=params(12),
         cost_estimate=BRIEF,
         name="both_gradients",
-    )(place, k, e, w, acc)
+    )(place, k, e, *factors, acc)
 
 
 def attend_kernel(blocks, place, q, k, v, pair_k, up_k, early_v, out):
@@ -391,19 +413,20 @@
     errors = (-grad_scale * rates * values.astype(jnp.float32)).astype(jnp.bfloat16)
     pair_errors = swap(errors, "seq", 1)
 
-    wide = [out_proj]
-    for _ in range(2):
-        wide.append(ring_step(wide[-1], outer))
+    wide = [out_proj, ring_step(out_proj, outer)]
+    own_factors = keys_part(place, keys, fast, outer)
+    wide.append(ring_step(after(wide[1], own_factors[0]), outer))
 
     up_values = after(values, wide[1])
     up_values = lax.ppermute(up_values, "seq", [(s, s + 2) for s in range(1, ranks - 2, 2)])
     up_keys = after(pair_keys, wide[2])
     up_keys = lax.ppermute(up_keys, "seq", [(s, s + 2) for s in range(0, ranks - 2, 2)])
 
-    acc = own_gradients(place, keys, errors, fast, outer)
+    acc = own_gradients(place, keys, errors, own_factors, outer)
+    pair_factors = keys_part(place, pair_keys, fast, outer)
     across = crossing(place, values, up_values, wide[0])
     pair_errors = after(pair_errors, up_keys, across)
-    summed = both_gradients(place, pair_keys, pair_errors, fast, acc, outer)
+    summed = both_gradients(place, pair_keys, pair_errors, pair_factors, acc, outer)
     pieces = [swap(summed[step], "seq", step * 2) for step in range(1, outer)]
     crossed = swap(after(across, summed[1]), "seq", 1)
     pieces[2] = after(pieces[2], crossed)

time: 98.5 us -> 99.3 us (level)
  other arithmetic: 2.79 us -> 1.07 us
  Pallas kernels: 13.9 us -> 15.3 us
  waiting for transfers between devices: 47.4 us -> 48.7 us
    pallas_call x0 -> x2, Pallas kernels: none -> 3.49 us  [keys_part(): pl.pallas_call(functools.partial(keys_kernel, outer), out_shape=[jax.Shap...]
    ppermute x19, waiting for transfers between devices: 34.3 us -> 37.3 us  [swap(): return lax.ppermute(array, axis, [(i, i ^ mask) for i in range(devices)])]
    ppermute x3, waiting for transfers between devices: 10.9 us -> 8.1 us  [ring_step(): return lax.ppermute(unit, 'seq', pairs)]
    ppermute x1, waiting for transfers between devices: 2.19 us -> 3.31 us  [shards(): lax.ppermute(up_keys, 'seq', [(s, s + 2) for s in range(0, ranks - 2, 2)])]
    pallas_call x1, Pallas kernels: 2.83 us -> 1.77 us  [both_gradients(): pl.pallas_call(functools.partial(both_kernel, outer), out_shape=[jax.Shap...]
    pallas_call x1, Pallas kernels: 2.77 us -> 1.72 us  [own_gradients(): pl.pallas_call(functools.partial(own_kernel, outer), out_shape=jax.ShapeD...]
    convert_element_type x1, other arithmetic: 1.2 us -> 0.16 us  [shards(): (-grad_scale * rates * values.astype(jnp.float32)).astype(jnp.bfloat16)]
    ppermute x19, starting transfers between devices: 22.1 us -> 21.1 us  [swap(): return lax.ppermute(array, axis, [(i, i ^ mask) for i in range(devices)])]
  transfers between devices with their start and end apart: 24 -> 24, of which waited for: 14 -> 15; matrix products, arithmetic and copies ran while one was open for 4% -> 2% of each run, Pallas kernels for 9% -> 12%
where the time goes in v10:
time: 99.3 us; the launch traced here: 99.1 us
  waiting for transfers between devices  48.7 us (49%)
  starting transfers between devices  30.1 us (30%)
  Pallas kernels  15.3 us (15%)
  local copies, waits for them, and re-layouts  3.17 us (3%)
  other arithmetic  1.07 us (1%)
    ppermute x19, waiting for transfers between devices, swap(): return lax.ppermute(array, axis, [(i, i ^ mask) for i in range(devices)])  37.3 us
    ppermute x19, starting transfers between devices, swap(): return lax.ppermute(array, axis, [(i, i ^ mask) for i in range(devices)])  21.1 us
    ppermute x3, waiting for transfers between devices, ring_step(): return lax.ppermute(unit, 'seq', pairs)  8.1 us
    ppermute x3, starting transfers between devices, ring_step(): return lax.ppermute(unit, 'seq', pairs)  4.63 us
    ppermute x1, starting transfers between devices, shards(): lax.ppermute(up_keys, 'seq', [(s, s + 2) for s in range(0, ranks - 2, 2)])  3.65 us
    pallas_call x2, Pallas kernels, keys_part(): pl.pallas_call(functools.partial(keys_kernel, outer), out_shape=[jax.Shap...  3.49 us
    ppermute x1, waiting for transfers between devices, shards(): lax.ppermute(up_keys, 'seq', [(s, s + 2) for s in range(0, ranks - 2, 2)])  3.31 us
    unnamed x18, local copies, waits for them, and re-layouts  2.48 us
  transfers between devices with their start and end apart: 24, of which 15 were waited for; matrix products, arithmetic and copies ran while one was open for 2% of the time, Pallas kernels for 12%

profile of v10, /device:TPU:0, one launch (start us, length us, event | category | flops | bytes accessed | tf_op | source)
XLA Modules:
  0.0 99.1 jit_solution(18312554822341755956)
XLA Ops:
  0.6 3.1 %collective-permute-start.1 = (bf16[256,512]{1,0:T(8,128)(2,1)}, bf16[256,512]{1,0:T(8,128)(2,1)S(1)}, u32[]{:S(2)}, u32[]{:S(2)}) collective-permute-start(bf16[256,512]{1,0:T(8,128)(2,1)} %rest_3_.1), channel_id=1, source_target_pairs={{0,8},{4,12},{8,24},{12,28},{24,16},{28,20},{16,0},{20,4},{1,9},{5... | collective-permute-start | bytes 786440 | tf_op jit(solution)/shard_map/ppermute | solution.py:358
  3.7 1.5 %collective-permute-start = (bf16[512,512]{1,0:T(8,128)(2,1)}, bf16[512,512]{1,0:T(8,128)(2,1)S(1)}, u32[]{:S(2)}, u32[]{:S(2)}) collective-permute-start(bf16[512,512]{1,0:T(8,128)(2,1)} %k.5), channel_id=1, source_target_pairs={{0,4},{4,0},{8,12},{12,8},{16,20},{20,16},{24,28},{28,24},{1,5},{5... | collective-permute-start | bytes 1572872 | tf_op jit(solution)/shard_map/ppermute | solution.py:41
  5.9 1.4 %copy-done = bf16[1,3,512,512]{3,2,1,0:T(8,128)(2,1)S(1)} copy-done((bf16[1,3,512,512]{3,2,1,0:T(8,128)(2,1)S(1)}, bf16[1,3,512,512]{3,2,1,0:T(8,128)(2,1)}, u32[]{:S(2)}) %copy-start) | copy-done | bytes 1572888
  8.4 1.7 %keys_part.2 = (bf16[512,512]{1,0:T(8,128)(2,1)S(1)}, f32[256,512]{1,0:T(8,128)S(1)}, f32[256,512]{1,0:T(8,128)S(1)}, bf16[256,512]{1,0:T(8,128)(2,1)S(1)}) custom-call(s32[12]{0:T(128)S(1)} %dynamic-slice_bitcast_fusion.place, bf16[512,512]{1,0:T(8,128)(2,1)S(1)} %copy-done.2, bf16[1,3,512,512]{3,2,1,0:T(8,128)(2,1)S(1)} %copy-done), custom_call_target="tpu_custom_call" | custom-call | flops 1 | bytes 1 | tf_op jit(solution)/shard_map/keys_part/pallas_call | solution.py:82
  10.1 1.1 %collective-permute-done.1.rest_4_ = bf16[256,512]{1,0:T(8,128)(2,1)S(1)} collective-permute-done((bf16[256,512]{1,0:T(8,128)(2,1)}, bf16[256,512]{1,0:T(8,128)(2,1)S(1)}, u32[]{:S(2)}, u32[]{:S(2)}) %collective-permute-start.1) | collective-permute-done | bytes 262176 | tf_op jit(solution)/shard_map/ppermute | solution.py:358
  11.2 1.5 %collective-permute-start.2 = (bf16[256,512]{1,0:T(8,128)(2,1)S(1)}, bf16[256,512]{1,0:T(8,128)(2,1)S(1)}, u32[]{:S(2)}, u32[]{:S(2)}) collective-permute-start(bf16[256,512]{1,0:T(8,128)(2,1)S(1)} %collective-permute-done.1.rest_4_), channel_id=1, source_target_pairs={{0,8},{4,12},{8,24},{12,28},{24,16},{28,20},{16,0},{20,4},{1,9},{5... | collective-permute-start | bytes 786440 | tf_op jit(solution)/shard_map/ppermute | solution.py:358
  14.6 5.0 %collective-permute-done.2.rest_5_ = bf16[256,512]{1,0:T(8,128)(2,1)S(1)} collective-permute-done((bf16[256,512]{1,0:T(8,128)(2,1)S(1)}, bf16[256,512]{1,0:T(8,128)(2,1)S(1)}, u32[]{:S(2)}, u32[]{:S(2)}) %collective-permute-start.2) | collective-permute-done | bytes 262176 | tf_op jit(solution)/shard_map/ppermute | solution.py:358
  19.6 3.6 %collective-permute-start.3 = (bf16[512,512]{1,0:T(8,128)(2,1)S(1)}, bf16[512,512]{1,0:T(8,128)(2,1)S(1)}, u32[]{:S(2)}, u32[]{:S(2)}) collective-permute-start(bf16[512,512]{1,0:T(8,128)(2,1)S(1)} %collective-permute-done.k.pair_k), channel_id=1, source_target_pairs={{0,8},{8,16},{16,24},{1,9},{9,17},{17,25},{2,10},{10,18},{18,26},{... | collective-permute-start | bytes 1572872 | tf_op jit(solution)/shard_map/ppermute | solution.py:423
  23.3 1.7 %own_gradients.1.acc = f32[3,256,512]{2,1,0:T(8,128)S(1)} custom-call(s32[12]{0:T(128)S(1)} %dynamic-slice_bitcast_fusion.place, bf16[512,512]{1,0:T(8,128)(2,1)S(1)} %copy-done.3, bf16[512,512]{1,0:T(8,128)(2,1)S(1)} %multiply_convert_fusion.e, bf16[512,512]{1,0:T(8,128)(2,1)S(1)} %get-tuple-element.30.gated, f32[256,512]{1,0:T(8,128)S(1)} %get-tuple-element.39.gate, ...), custom_call_target="tpu_custom_call" | custom-call | flops 1 | bytes 1 | tf_op jit(solution)/shard_map/own_gradients/pallas_call | solution.py:144
  25.1 1.7 %keys_part.3 = (bf16[512,512]{1,0:T(8,128)(2,1)S(1)}, f32[256,512]{1,0:T(8,128)S(1)}, f32[256,512]{1,0:T(8,128)S(1)}, bf16[256,512]{1,0:T(8,128)(2,1)S(1)}) custom-call(s32[12]{0:T(128)S(1)} %dynamic-slice_bitcast_fusion.place, bf16[512,512]{1,0:T(8,128)(2,1)S(1)} %collective-permute-done.k.pair_k, bf16[1,3,512,512]{3,2,1,0:T(8,128)(2,1)S(1)} %copy-done.1), custom_call_target="tpu_custom_call" | custom-call | flops 1 | bytes 1 | tf_op jit(solution)/shard_map/keys_part/pallas_call | solution.py:82
  28.5 3.3 %collective-permute-done.3.up_k = bf16[512,512]{1,0:T(8,128)(2,1)S(1)} collective-permute-done((bf16[512,512]{1,0:T(8,128)(2,1)S(1)}, bf16[512,512]{1,0:T(8,128)(2,1)S(1)}, u32[]{:S(2)}, u32[]{:S(2)}) %collective-permute-start.3) | collective-permute-done | bytes 524320 | tf_op jit(solution)/shard_map/ppermute | solution.py:423
  31.9 1.8 %both_gradients.1 = (f32[3,64,512]{2,1,0:T(8,128)S(1)}, bf16[3,64,512]{2,1,0:T(8,128)(2,1)S(1)}, bf16[3,64,512]{2,1,0:T(8,128)(2,1)S(1)}, bf16[3,64,512]{2,1,0:T(8,128)(2,1)S(1)}) custom-call(s32[12]{0:T(128)S(1)} %dynamic-slice_bitcast_fusion.place, bf16[512,512]{1,0:T(8,128)(2,1)S(1)} %collective-permute-done.k.pair_k, ...), custom_call_target="tpu_custom_call" | custom-call | flops 1 | bytes 1 | tf_op jit(solution)/shard_map/both_gradients/pallas_call | solution.py:159
  33.7 5.0 %collective-permute-start.9 = (bf16[3,64,512]{2,1,0:T(8,128)(2,1)S(1)}, bf16[3,64,512]{2,1,0:T(8,128)(2,1)S(1)}, u32[]{:S(2)}, u32[]{:S(2)}) collective-permute-start(bf16[3,64,512]{2,1,0:T(8,128)(2,1)S(1)} %get-tuple-element.46), channel_id=1, source_target_pairs={{0,24},{4,28},{8,16},{12,20},{16,8},{20,12},{24,0},{28,4},{1,25},{... | collective-permute-start | bytes 589832 | tf_op jit(solution)/shard_map/ppermute | solution.py:41
  39.3 5.2 %collective-permute-done.9.rest_2_ = bf16[3,64,512]{2,1,0:T(8,128)(2,1)S(1)} collective-permute-done((bf16[3,64,512]{2,1,0:T(8,128)(2,1)S(1)}, bf16[3,64,512]{2,1,0:T(8,128)(2,1)S(1)}, u32[]{:S(2)}, u32[]{:S(2)}) %collective-permute-start.9) | collective-permute-done | bytes 196640 | tf_op jit(solution)/shard_map/ppermute | solution.py:41
  44.5 5.0 %collective-permute-done.6.early_v.rest_7_ = bf16[768,512]{1,0:T(8,128)(2,1)S(1)} collective-permute-done((bf16[768,512]{1,0:T(8,128)(2,1)S(1)}, bf16[768,512]{1,0:T(8,128)(2,1)S(1)}, u32[]{:S(2)}, u32[]{:S(2)}) %collective-permute-start.6) | collective-permute-done | bytes 786464 | tf_op jit(solution)/shard_map/ppermute | solution.py:41
  49.5 4.2 %collective-permute-done.8.rest_1_ = bf16[3,64,512]{2,1,0:T(8,128)(2,1)S(1)} collective-permute-done((bf16[3,64,512]{2,1,0:T(8,128)(2,1)S(1)}, bf16[3,64,512]{2,1,0:T(8,128)(2,1)S(1)}, u32[]{:S(2)}, u32[]{:S(2)}) %collective-permute-start.8) | collective-permute-done | bytes 196640 | tf_op jit(solution)/shard_map/ppermute | solution.py:41
  55.6 3.1 %collective-permute-start.13 = (bf16[3,64,512]{2,1,0:T(8,128)(2,1)S(1)}, bf16[3,64,512]{2,1,0:T(8,128)(2,1)S(1)}, u32[]{:S(2)}, u32[]{:S(2)}) collective-permute-start(bf16[3,64,512]{2,1,0:T(8,128)(2,1)S(1)} %renew.1.rest_0_), channel_id=1, source_target_pairs={{0,24},{4,28},{8,16},{12,20},{16,8},{20,12},{24,0},{28,4},{1,25},{... | collective-permute-start | bytes 589832 | tf_op jit(solution)/shard_map/ppermute | solution.py:41
  59.2 3.0 %collective-permute-done.10.rest_1_ = bf16[3,64,512]{2,1,0:T(8,128)(2,1)S(1)} collective-permute-done((bf16[3,64,512]{2,1,0:T(8,128)(2,1)S(1)}, bf16[3,64,512]{2,1,0:T(8,128)(2,1)S(1)}, u32[]{:S(2)}, u32[]{:S(2)}) %collective-permute-start.10) | collective-permute-done | bytes 196640 | tf_op jit(solution)/shard_map/ppermute | solution.py:41
  62.2 2.0 %collective-permute-start.17 = (bf16[256,512]{1,0:T(8,128)(2,1)S(1)}, bf16[256,512]{1,0:T(8,128)(2,1)S(1)}, u32[]{:S(2)}, u32[]{:S(2)}) collective-permute-start(bf16[256,512]{1,0:T(8,128)(2,1)S(1)} %collective-permute-done.1.rest_4_), channel_id=1, source_target_pairs={{0,4},{4,0},{8,12},{12,8},{16,20},{20,16},{24,28},{28,24},{1,5},{5... | collective-permute-start | bytes 786440 | tf_op jit(solution)/shard_map/ppermute | solution.py:41
  64.2 2.2 %collective-permute-done.13.rest_3_ = bf16[3,64,512]{2,1,0:T(8,128)(2,1)S(1)} collective-permute-done((bf16[3,64,512]{2,1,0:T(8,128)(2,1)S(1)}, bf16[3,64,512]{2,1,0:T(8,128)(2,1)S(1)}, u32[]{:S(2)}, u32[]{:S(2)}) %collective-permute-start.13) | collective-permute-done | bytes 196640 | tf_op jit(solution)/shard_map/ppermute | solution.py:41
  66.4 2.2 %collective-permute-start.16 = (bf16[3,64,512]{2,1,0:T(8,128)(2,1)S(1)}, bf16[3,64,512]{2,1,0:T(8,128)(2,1)S(1)}, u32[]{:S(2)}, u32[]{:S(2)}) collective-permute-start(bf16[3,64,512]{2,1,0:T(8,128)(2,1)S(1)} %collective-permute-done.13.rest_3_), channel_id=1, source_target_pairs={{0,4},{4,0},{8,12},{12,8},{16,20},{20,16},{24,28},{28,24},{1,5},{5... | collective-permute-start | bytes 589832 | tf_op jit(solution)/shard_map/ppermute | solution.py:41
  68.6 6.2 %collective-permute-done.12.rest_2_ = bf16[3,64,512]{2,1,0:T(8,128)(2,1)S(1)} collective-permute-done((bf16[3,64,512]{2,1,0:T(8,128)(2,1)S(1)}, bf16[3,64,512]{2,1,0:T(8,128)(2,1)S(1)}, u32[]{:S(2)}, u32[]{:S(2)}) %collective-permute-start.12) | collective-permute-done | bytes 196640 | tf_op jit(solution)/shard_map/ppermute | solution.py:41
  75.4 2.3 %window_attention.1.attended = f32[512,512]{1,0:T(8,128)S(1)} custom-call(s32[12]{0:T(128)S(1)} %dynamic-slice_bitcast_fusion.place, bf16[512,512]{1,0:T(8,128)(2,1)S(1)} %copy-done.5, bf16[512,512]{1,0:T(8,128)(2,1)S(1)} %copy-done.3, bf16[512,512]{1,0:T(8,128)(2,1)S(1)} %copy-done.4, bf16[512,512]{1,0:T(8,128)(2,1)S(1)} %collective-permute-done.k.pair_k, ...), custom_call_target="tpu_custom_call" | custom-call | flops 1 | bytes 1 | tf_op jit(solution)/shard_map/window_attention/pallas_call | solution.py:201
  78.6 2.3 %collective-permute-done.15.rest_6_ = bf16[3,64,512]{2,1,0:T(8,128)(2,1)S(1)} collective-permute-done((bf16[3,64,512]{2,1,0:T(8,128)(2,1)S(1)}, bf16[3,64,512]{2,1,0:T(8,128)(2,1)S(1)}, u32[]{:S(2)}, u32[]{:S(2)}) %collective-permute-start.15) | collective-permute-done | bytes 196640 | tf_op jit(solution)/shard_map/ppermute | solution.py:41
  80.8 1.7 %apply_fast.1.rest_0_ = bf16[512,512]{1,0:T(8,128)(2,1)S(1)} custom-call(s32[12]{0:T(128)S(1)} %dynamic-slice_bitcast_fusion.place, bf16[512,512]{1,0:T(8,128)(2,1)S(1)} %copy-done.5, f32[512,512]{1,0:T(8,128)S(1)} %window_attention.1.attended, bf16[3,64,512]{2,1,0:T(8,128)(2,1)S(1)} %renew.1.rest_0_, ...), custom_call_target="tpu_custom_call" | custom-call | flops 1 | bytes 1 | tf_op jit(solution)/shard_map/apply_fast/pallas_call | solution.py:280
  82.5 1.6 %collective-permute-start.19 = (bf16[512,512]{1,0:T(8,128)(2,1)S(1)}, bf16[512,512]{1,0:T(8,128)(2,1)S(1)}, u32[]{:S(2)}, u32[]{:S(2)}) collective-permute-start(bf16[512,512]{1,0:T(8,128)(2,1)S(1)} %apply_fast.1.rest_0_), channel_id=1, source_target_pairs={{0,2},{1,3},{2,0},{3,1},{4,6},{5,7},{6,4},{7,5},{8,10},{9,11},{10,... | collective-permute-start | bytes 1572872 | tf_op jit(solution)/shard_map/ppermute | solution.py:41
  84.4 2.0 %collective-permute-done.21.rest_6_ = bf16[256,512]{1,0:T(8,128)(2,1)S(1)} collective-permute-done((bf16[256,512]{1,0:T(8,128)(2,1)S(1)}, bf16[256,512]{1,0:T(8,128)(2,1)S(1)}, u32[]{:S(2)}, u32[]{:S(2)}) %collective-permute-start.21) | collective-permute-done | bytes 262176 | tf_op jit(solution)/shard_map/ppermute | solution.py:358
  86.4 1.8 %collective-permute-start.22 = (bf16[256,512]{1,0:T(8,128)(2,1)S(1)}, bf16[256,512]{1,0:T(8,128)(2,1)S(1)}, u32[]{:S(2)}, u32[]{:S(2)}) collective-permute-start(bf16[256,512]{1,0:T(8,128)(2,1)S(1)} %collective-permute-done.21.rest_6_), channel_id=1, source_target_pairs={{0,4},{4,0},{8,12},{12,8},{16,20},{20,16},{24,28},{28,24},{1,5},{5... | collective-permute-start | bytes 786440 | tf_op jit(solution)/shard_map/ppermute | solution.py:41
  88.1 5.0 %collective-permute-done.20.rest_9_ = bf16[256,512]{1,0:T(8,128)(2,1)S(1)} collective-permute-done((bf16[256,512]{1,0:T(8,128)(2,1)S(1)}, bf16[256,512]{1,0:T(8,128)(2,1)S(1)}, u32[]{:S(2)}, u32[]{:S(2)}) %collective-permute-start.20) | collective-permute-done | bytes 262176 | tf_op jit(solution)/shard_map/ppermute | solution.py:41
  93.1 2.8 %collective-permute-done.22.rest_10_ = bf16[256,512]{1,0:T(8,128)(2,1)S(1)} collective-permute-done((bf16[256,512]{1,0:T(8,128)(2,1)S(1)}, bf16[256,512]{1,0:T(8,128)(2,1)S(1)}, u32[]{:S(2)}, u32[]{:S(2)}) %collective-permute-start.22) | collective-permute-done | bytes 262176 | tf_op jit(solution)/shard_map/ppermute | solution.py:41
  95.9 1.7 %project_most.1 = (f32[512,512]{1,0:T(8,128)S(1)}, bf16[512,512]{1,0:T(8,128)(2,1)S(1)}) custom-call(s32[12]{0:T(128)S(1)} %dynamic-slice_bitcast_fusion.place, bf16[512,512]{1,0:T(8,128)(2,1)S(1)} %apply_fast.1.rest_0_, bf16[512,512]{1,0:T(8,128)(2,1)S(1)} %collective-permute-done.18.rest_1_, bf16[512,512]{1,0:T(8,128)(2,1)S(1)} %collective-permute-done.19.rest_2_, ...), custom_call_target="tpu_custom_call" | custom-call | flops 1 | bytes 1 | tf_op jit(solution)/shard_map/project_most/pallas_call | solution.py:316
  97.8 1.2 %project_last.1 = bf16[512,512]{1,0:T(8,128)(2,1)} custom-call(f32[512,512]{1,0:T(8,128)S(1)} %get-tuple-element.56.partial, bf16[512,512]{1,0:T(8,128)(2,1)S(1)} %collective-permute-done.23.block, bf16[512,512]{1,0:T(8,128)(2,1)S(1)} %get-tuple-element.57.rows), custom_call_target="tpu_custom_call" | custom-call | flops 1 | bytes 1 | tf_op jit(solution)/shard_map/project_last/pallas_call | solution.py:337
  (48 shorter events, 10.3 us)
Async XLA Ops:
  0.6 12.2 %copy-start.8 = (f32[512,1]{0,1:T(1,128)S(1)}, f32[512,1]{0,1:T(1,128)}, u32[]{:S(2)}) copy-start(f32[512,1]{0,1:T(1,128)} %param.11) | copy-start | bytes 6148
  0.6 10.6 %collective-permute-start.1 = (bf16[256,512]{1,0:T(8,128)(2,1)}, bf16[256,512]{1,0:T(8,128)(2,1)S(1)}, u32[]{:S(2)}, u32[]{:S(2)}) collective-permute-start(bf16[256,512]{1,0:T(8,128)(2,1)} %rest_3_.1), channel_id=1, source_target_pairs={{0,8},{4,12},{8,24},{12,28},{24,16},{28,20},{16,0},{20,4},{1,9},{5... | collective-permute-start | bytes 786440 | tf_op jit(solution)/shard_map/ppermute | solution.py:358
  3.7 15.9 %collective-permute-start = (bf16[512,512]{1,0:T(8,128)(2,1)}, bf16[512,512]{1,0:T(8,128)(2,1)S(1)}, u32[]{:S(2)}, u32[]{:S(2)}) collective-permute-start(bf16[512,512]{1,0:T(8,128)(2,1)} %k.5), channel_id=1, source_target_pairs={{0,4},{4,0},{8,12},{12,8},{16,20},{20,16},{24,28},{28,24},{1,5},{5... | collective-permute-start | bytes 1572872 | tf_op jit(solution)/shard_map/ppermute | solution.py:41
  5.9 1.4 %copy-start = (bf16[1,3,512,512]{3,2,1,0:T(8,128)(2,1)S(1)}, bf16[1,3,512,512]{3,2,1,0:T(8,128)(2,1)}, u32[]{:S(2)}) copy-start(bf16[1,3,512,512]{3,2,1,0:T(8,128)(2,1)} %w.5) | copy-start | bytes 4718596
  8.4 4.4 %copy-start.4 = (bf16[512,512]{1,0:T(8,128)(2,1)S(1)}, bf16[512,512]{1,0:T(8,128)(2,1)}, u32[]{:S(2)}) copy-start(bf16[512,512]{1,0:T(8,128)(2,1)} %v.1) | copy-start | bytes 1572868
  8.4 14.9 %copy-start.3 = (bf16[512,512]{1,0:T(8,128)(2,1)S(1)}, bf16[512,512]{1,0:T(8,128)(2,1)}, u32[]{:S(2)}) copy-start(bf16[512,512]{1,0:T(8,128)(2,1)} %k.5) | copy-start | bytes 1572868
  11.2 8.4 %collective-permute-start.2 = (bf16[256,512]{1,0:T(8,128)(2,1)S(1)}, bf16[256,512]{1,0:T(8,128)(2,1)S(1)}, u32[]{:S(2)}, u32[]{:S(2)}) collective-permute-start(bf16[256,512]{1,0:T(8,128)(2,1)S(1)} %collective-permute-done.1.rest_4_), channel_id=1, source_target_pairs={{0,8},{4,12},{8,24},{12,28},{24,16},{28,20},{16,0},{20,4},{1,9},{5... | collective-permute-start | bytes 786440 | tf_op jit(solution)/shard_map/ppermute | solution.py:358
  13.0 15.6 %collective-permute-start.5 = (bf16[512,512]{1,0:T(8,128)(2,1)S(1)}, bf16[512,512]{1,0:T(8,128)(2,1)S(1)}, u32[]{:S(2)}, u32[]{:S(2)}) collective-permute-start(bf16[512,512]{1,0:T(8,128)(2,1)S(1)} %multiply_convert_fusion.e), channel_id=1, source_target_pairs={{0,4},{4,0},{8,12},{12,8},{16,20},{20,16},{24,28},{28,24},{1,5},{5... | collective-permute-start | bytes 1572872 | tf_op jit(solution)/shard_map/ppermute | solution.py:41
  14.0 12.9 %collective-permute-start.4 = (bf16[512,512]{1,0:T(8,128)(2,1)S(1)}, bf16[512,512]{1,0:T(8,128)(2,1)S(1)}, u32[]{:S(2)}, u32[]{:S(2)}) collective-permute-start(bf16[512,512]{1,0:T(8,128)(2,1)S(1)} %copy-done.4), channel_id=1, source_target_pairs={{4,12},{12,20},{20,28},{5,13},{13,21},{21,29},{6,14},{14,22},{22,3... | collective-permute-start | bytes 1572872 | tf_op jit(solution)/shard_map/ppermute | solution.py:421
  19.6 12.2 %collective-permute-start.3 = (bf16[512,512]{1,0:T(8,128)(2,1)S(1)}, bf16[512,512]{1,0:T(8,128)(2,1)S(1)}, u32[]{:S(2)}, u32[]{:S(2)}) collective-permute-start(bf16[512,512]{1,0:T(8,128)(2,1)S(1)} %collective-permute-done.k.pair_k), channel_id=1, source_target_pairs={{0,8},{8,16},{16,24},{1,9},{9,17},{17,25},{2,10},{10,18},{18,26},{... | collective-permute-start | bytes 1572872 | tf_op jit(solution)/shard_map/ppermute | solution.py:423
  23.3 1.7 %copy-start.1 = (bf16[1,3,512,512]{3,2,1,0:T(8,128)(2,1)S(1)}, bf16[1,3,512,512]{3,2,1,0:T(8,128)(2,1)}, u32[]{:S(2)}) copy-start(bf16[1,3,512,512]{3,2,1,0:T(8,128)(2,1)} %w.5) | copy-start | bytes 4718596
  25.1 1.8 %copy-start.7 = (bf16[256,512]{1,0:T(8,128)(2,1)S(1)}, bf16[256,512]{1,0:T(8,128)(2,1)}, u32[]{:S(2)}) copy-start(bf16[256,512]{1,0:T(8,128)(2,1)} %rest_3_.1) | copy-start | bytes 786436
  31.9 21.9 %copy-start.6 = (f32[1,3,64,512]{3,2,1,0:T(8,128)S(1)}, f32[1,3,64,512]{3,2,1,0:T(8,128)}, u32[]{:S(2)}) copy-start(f32[1,3,64,512]{3,2,1,0:T(8,128)} %momentum.1) | copy-start | bytes 1179652
  33.6 15.9 %collective-permute-start.6 = (bf16[768,512]{1,0:T(8,128)(2,1)S(1)}, bf16[768,512]{1,0:T(8,128)(2,1)S(1)}, u32[]{:S(2)}, u32[]{:S(2)}) collective-permute-start(bf16[768,512]{1,0:T(8,128)(2,1)S(1)} %crossing.1), channel_id=1, source_target_pairs={{0,4},{4,0},{8,12},{12,8},{16,20},{20,16},{24,28},{28,24},{1,5},{5... | collective-permute-start | bytes 2359304 | tf_op jit(solution)/shard_map/ppermute | solution.py:41
  33.7 10.8 %collective-permute-start.9 = (bf16[3,64,512]{2,1,0:T(8,128)(2,1)S(1)}, bf16[3,64,512]{2,1,0:T(8,128)(2,1)S(1)}, u32[]{:S(2)}, u32[]{:S(2)}) collective-permute-start(bf16[3,64,512]{2,1,0:T(8,128)(2,1)S(1)} %get-tuple-element.46), channel_id=1, source_target_pairs={{0,24},{4,28},{8,16},{12,20},{16,8},{20,12},{24,0},{28,4},{1,25},{... | collective-permute-start | bytes 589832 | tf_op jit(solution)/shard_map/ppermute | solution.py:41
  38.7 10.8 %collective-permute-start.7 = (bf16[3,64,512]{2,1,0:T(8,128)(2,1)S(1)}, bf16[3,64,512]{2,1,0:T(8,128)(2,1)S(1)}, u32[]{:S(2)}, u32[]{:S(2)}) collective-permute-start(bf16[3,64,512]{2,1,0:T(8,128)(2,1)S(1)} %get-tuple-element.42), channel_id=1, source_target_pairs={{0,8},{4,12},{8,0},{12,4},{16,24},{20,28},{24,16},{28,20},{1,9},{5... | collective-permute-start | bytes 589832 | tf_op jit(solution)/shard_map/ppermute | solution.py:41
  38.7 15.0 %collective-permute-start.8 = (bf16[3,64,512]{2,1,0:T(8,128)(2,1)S(1)}, bf16[3,64,512]{2,1,0:T(8,128)(2,1)S(1)}, u32[]{:S(2)}, u32[]{:S(2)}) collective-permute-start(bf16[3,64,512]{2,1,0:T(8,128)(2,1)S(1)} %get-tuple-element.45), channel_id=1, source_target_pairs={{0,16},{4,20},{8,24},{12,28},{16,0},{20,4},{24,8},{28,12},{1,17},{... | collective-permute-start | bytes 589832 | tf_op jit(solution)/shard_map/ppermute | solution.py:41
  53.7 21.6 %copy-start.5 = (bf16[512,512]{1,0:T(8,128)(2,1)S(1)}, bf16[512,512]{1,0:T(8,128)(2,1)}, u32[]{:S(2)}) copy-start(bf16[512,512]{1,0:T(8,128)(2,1)} %q.3) | copy-start | bytes 1572868
  54.6 7.6 %collective-permute-start.10 = (bf16[3,64,512]{2,1,0:T(8,128)(2,1)S(1)}, bf16[3,64,512]{2,1,0:T(8,128)(2,1)S(1)}, u32[]{:S(2)}, u32[]{:S(2)}) collective-permute-start(bf16[3,64,512]{2,1,0:T(8,128)(2,1)S(1)} %renew.1.rest_0_), channel_id=1, source_target_pairs={{0,8},{4,12},{8,0},{12,4},{16,24},{20,28},{24,16},{28,20},{1,9},{5... | collective-permute-start | bytes 589832 | tf_op jit(solution)/shard_map/ppermute | solution.py:41
  54.7 7.5 %collective-permute-start.11 = (bf16[3,64,512]{2,1,0:T(8,128)(2,1)S(1)}, bf16[3,64,512]{2,1,0:T(8,128)(2,1)S(1)}, u32[]{:S(2)}, u32[]{:S(2)}) collective-permute-start(bf16[3,64,512]{2,1,0:T(8,128)(2,1)S(1)} %renew.1.rest_0_), channel_id=1, source_target_pairs={{0,4},{4,0},{8,12},{12,8},{16,20},{20,16},{24,28},{28,24},{1,5},{5... | collective-permute-start | bytes 589832 | tf_op jit(solution)/shard_map/ppermute | solution.py:41
  55.6 10.9 %collective-permute-start.13 = (bf16[3,64,512]{2,1,0:T(8,128)(2,1)S(1)}, bf16[3,64,512]{2,1,0:T(8,128)(2,1)S(1)}, u32[]{:S(2)}, u32[]{:S(2)}) collective-permute-start(bf16[3,64,512]{2,1,0:T(8,128)(2,1)S(1)} %renew.1.rest_0_), channel_id=1, source_target_pairs={{0,24},{4,28},{8,16},{12,20},{16,8},{20,12},{24,0},{28,4},{1,25},{... | collective-permute-start | bytes 589832 | tf_op jit(solution)/shard_map/ppermute | solution.py:41
  58.7 16.1 %collective-permute-start.12 = (bf16[3,64,512]{2,1,0:T(8,128)(2,1)S(1)}, bf16[3,64,512]{2,1,0:T(8,128)(2,1)S(1)}, u32[]{:S(2)}, u32[]{:S(2)}) collective-permute-start(bf16[3,64,512]{2,1,0:T(8,128)(2,1)S(1)} %renew.1.rest_0_), channel_id=1, source_target_pairs={{0,16},{4,20},{8,24},{12,28},{16,0},{20,4},{24,8},{28,12},{1,17},{... | collective-permute-start | bytes 589832 | tf_op jit(solution)/shard_map/ppermute | solution.py:41
  62.2 16.4 %collective-permute-start.14 = (bf16[3,64,512]{2,1,0:T(8,128)(2,1)S(1)}, bf16[3,64,512]{2,1,0:T(8,128)(2,1)S(1)}, u32[]{:S(2)}, u32[]{:S(2)}) collective-permute-start(bf16[3,64,512]{2,1,0:T(8,128)(2,1)S(1)} %collective-permute-done.10.rest_1_), channel_id=1, source_target_pairs={{0,4},{4,0},{8,12},{12,8},{16,20},{20,16},{24,28},{28,24},{1,5},{5... | collective-permute-start | bytes 589832 | tf_op jit(solution)/shard_map/ppermute | solution.py:41
  62.2 16.4 %collective-permute-start.17 = (bf16[256,512]{1,0:T(8,128)(2,1)S(1)}, bf16[256,512]{1,0:T(8,128)(2,1)S(1)}, u32[]{:S(2)}, u32[]{:S(2)}) collective-permute-start(bf16[256,512]{1,0:T(8,128)(2,1)S(1)} %collective-permute-done.1.rest_4_), channel_id=1, source_target_pairs={{0,4},{4,0},{8,12},{12,8},{16,20},{20,16},{24,28},{28,24},{1,5},{5... | collective-permute-start | bytes 786440 | tf_op jit(solution)/shard_map/ppermute | solution.py:41
  66.4 12.1 %collective-permute-start.16 = (bf16[3,64,512]{2,1,0:T(8,128)(2,1)S(1)}, bf16[3,64,512]{2,1,0:T(8,128)(2,1)S(1)}, u32[]{:S(2)}, u32[]{:S(2)}) collective-permute-start(bf16[3,64,512]{2,1,0:T(8,128)(2,1)S(1)} %collective-permute-done.13.rest_3_), channel_id=1, source_target_pairs={{0,4},{4,0},{8,12},{12,8},{16,20},{20,16},{24,28},{28,24},{1,5},{5... | collective-permute-start | bytes 589832 | tf_op jit(solution)/shard_map/ppermute | solution.py:41
  74.8 6.0 %collective-permute-start.15 = (bf16[3,64,512]{2,1,0:T(8,128)(2,1)S(1)}, bf16[3,64,512]{2,1,0:T(8,128)(2,1)S(1)}, u32[]{:S(2)}, u32[]{:S(2)}) collective-permute-start(bf16[3,64,512]{2,1,0:T(8,128)(2,1)S(1)} %collective-permute-done.12.rest_2_), channel_id=1, source_target_pairs={{0,4},{4,0},{8,12},{12,8},{16,20},{20,16},{24,28},{28,24},{1,5},{5... | collective-permute-start | bytes 589832 | tf_op jit(solution)/shard_map/ppermute | solution.py:41
  78.6 7.8 %collective-permute-start.21 = (bf16[256,512]{1,0:T(8,128)(2,1)S(1)}, bf16[256,512]{1,0:T(8,128)(2,1)S(1)}, u32[]{:S(2)}, u32[]{:S(2)}) collective-permute-start(bf16[256,512]{1,0:T(8,128)(2,1)S(1)} %collective-permute-done.2.rest_5_), channel_id=1, source_target_pairs={{0,8},{4,12},{8,24},{12,28},{24,16},{28,20},{16,0},{20,4},{1,9},{5... | collective-permute-start | bytes 786440 | tf_op jit(solution)/shard_map/ppermute | solution.py:358
  82.5 13.4 %collective-permute-start.19 = (bf16[512,512]{1,0:T(8,128)(2,1)S(1)}, bf16[512,512]{1,0:T(8,128)(2,1)S(1)}, u32[]{:S(2)}, u32[]{:S(2)}) collective-permute-start(bf16[512,512]{1,0:T(8,128)(2,1)S(1)} %apply_fast.1.rest_0_), channel_id=1, source_target_pairs={{0,2},{1,3},{2,0},{3,1},{4,6},{5,7},{6,4},{7,5},{8,10},{9,11},{10,... | collective-permute-start | bytes 1572872 | tf_op jit(solution)/shard_map/ppermute | solution.py:41
  84.1 9.0 %collective-permute-start.20 = (bf16[256,512]{1,0:T(8,128)(2,1)S(1)}, bf16[256,512]{1,0:T(8,128)(2,1)S(1)}, u32[]{:S(2)}, u32[]{:S(2)}) collective-permute-start(bf16[256,512]{1,0:T(8,128)(2,1)S(1)} %collective-permute-done.2.rest_5_), channel_id=1, source_target_pairs={{0,4},{4,0},{8,12},{12,8},{16,20},{20,16},{24,28},{28,24},{1,5},{5... | collective-permute-start | bytes 786440 | tf_op jit(solution)/shard_map/ppermute | solution.py:41
  86.4 9.6 %collective-permute-start.22 = (bf16[256,512]{1,0:T(8,128)(2,1)S(1)}, bf16[256,512]{1,0:T(8,128)(2,1)S(1)}, u32[]{:S(2)}, u32[]{:S(2)}) collective-permute-start(bf16[256,512]{1,0:T(8,128)(2,1)S(1)} %collective-permute-done.21.rest_6_), channel_id=1, source_target_pairs={{0,4},{4,0},{8,12},{12,8},{16,20},{20,16},{24,28},{28,24},{1,5},{5... | collective-permute-start | bytes 786440 | tf_op jit(solution)/shard_map/ppermute | solution.py:41
  88.1 7.8 %collective-permute-start.18 = (bf16[512,512]{1,0:T(8,128)(2,1)S(1)}, bf16[512,512]{1,0:T(8,128)(2,1)S(1)}, u32[]{:S(2)}, u32[]{:S(2)}) collective-permute-start(bf16[512,512]{1,0:T(8,128)(2,1)S(1)} %apply_fast.1.rest_0_), channel_id=1, source_target_pairs={{0,1},{1,0},{2,3},{3,2},{4,5},{5,4},{6,7},{7,6},{8,9},{9,8},{10,11... | collective-permute-start | bytes 1572872 | tf_op jit(solution)/shard_map/ppermute | solution.py:41
  95.9 1.9 %collective-permute-start.23 = (bf16[512,512]{1,0:T(8,128)(2,1)S(1)}, bf16[512,512]{1,0:T(8,128)(2,1)S(1)}, u32[]{:S(2)}, u32[]{:S(2)}) collective-permute-start(bf16[512,512]{1,0:T(8,128)(2,1)S(1)} %collective-permute-done.19.rest_2_), channel_id=1, source_target_pairs={{0,1},{1,0},{2,3},{3,2},{4,5},{5,4},{6,7},{7,6},{8,9},{9,8},{10,11... | collective-permute-start | bytes 1572872 | tf_op jit(solution)/shard_map/ppermute | solution.py:41
  (1 other events, 1.0 us)

commit v11 on v10

--- a/solution.py
+++ b/solution.py
@@ -449,8 +449,10 @@
         total = total + piece.astype(jnp.float32)
     moment = MOMENTUM_DECAY * momentum + total[None]
 
+    forwarded = far[-1]
     far[-1] = after(far[-1], attended, wide_far[1], moment)
-    wide_far += [swap(after(wide[2], far[1]), "seq", 1), swap(wide[3], "seq", 1)]
+    wide_far.append(swap(after(wide[2], forwarded), "seq", 1))
+    wide_far.append(swap(after(wide[3], wide_far[2]), "seq", 1))
 
     combined = apply_fast(place, queries, attended, near + far)
 

time: 99.3 us -> 98.1 us (0.988)
  waiting for transfers between devices: 48.7 us -> 46.3 us
  starting transfers between devices: 30.1 us -> 31.3 us
    ppermute x19, waiting for transfers between devices: 37.3 us -> 35.4 us  [swap(): return lax.ppermute(array, axis, [(i, i ^ mask) for i in range(devices)])]
    ppermute x19, starting transfers between devices: 21.1 us -> 22.3 us  [swap(): return lax.ppermute(array, axis, [(i, i ^ mask) for i in range(devices)])]
  transfers between devices with their start and end apart: 24 -> 24, of which waited for: 15 -> 16; matrix products, arithmetic and copies ran while one was open for 2% -> 2% of each run, Pallas kernels for 12% -> 12%
where the time goes in v11:
time: 98.1 us; the launch traced here: 97.8 us
  waiting for transfers between devices  46.3 us (47%)
  starting transfers between devices  31.3 us (32%)
  Pallas kernels  15.3 us (16%)
  local copies, waits for them, and re-layouts  3.17 us (3%)
  other arithmetic  1.07 us (1%)
    ppermute x19, waiting for transfers between devices, swap(): return lax.ppermute(array, axis, [(i, i ^ mask) for i in range(devices)])  35.4 us
    ppermute x19, starting transfers between devices, swap(): return lax.ppermute(array, axis, [(i, i ^ mask) for i in range(devices)])  22.3 us
    ppermute x3, waiting for transfers between devices, ring_step(): return lax.ppermute(unit, 'seq', pairs)  7.53 us
    ppermute x3, starting transfers between devices, ring_step(): return lax.ppermute(unit, 'seq', pairs)  4.63 us
    ppermute x1, starting transfers between devices, shards(): lax.ppermute(up_keys, 'seq', [(s, s + 2) for s in range(0, ranks - 2, 2)])  3.65 us
    pallas_call x2, Pallas kernels, keys_part(): pl.pallas_call(functools.partial(keys_kernel, outer), out_shape=[jax.Shap...  3.49 us
    ppermute x1, waiting for transfers between devices, shards(): lax.ppermute(up_keys, 'seq', [(s, s + 2) for s in range(0, ranks - 2, 2)])  3.31 us
    unnamed x18, local copies, waits for them, and re-layouts  2.48 us
  transfers between devices with their start and end apart: 24, of which 16 were waited for; matrix products, arithmetic and copies ran while one was open for 2% of the time, Pallas kernels for 12%

profile of v11, /device:TPU:0, one launch (start us, length us, event | category | flops | bytes accessed | tf_op | source)
XLA Modules:
  0.0 97.8 jit_solution(1337747518511726357)
XLA Ops:
  0.6 3.1 %collective-permute-start.1 = (bf16[256,512]{1,0:T(8,128)(2,1)}, bf16[256,512]{1,0:T(8,128)(2,1)S(1)}, u32[]{:S(2)}, u32[]{:S(2)}) collective-permute-start(bf16[256,512]{1,0:T(8,128)(2,1)} %rest_3_.1), channel_id=1, source_target_pairs={{0,8},{4,12},{8,24},{12,28},{24,16},{28,20},{16,0},{20,4},{1,9},{5... | collective-permute-start | bytes 786440 | tf_op jit(solution)/shard_map/ppermute | solution.py:358
  3.7 1.5 %collective-permute-start = (bf16[512,512]{1,0:T(8,128)(2,1)}, bf16[512,512]{1,0:T(8,128)(2,1)S(1)}, u32[]{:S(2)}, u32[]{:S(2)}) collective-permute-start(bf16[512,512]{1,0:T(8,128)(2,1)} %k.5), channel_id=1, source_target_pairs={{0,4},{4,0},{8,12},{12,8},{16,20},{20,16},{24,28},{28,24},{1,5},{5... | collective-permute-start | bytes 1572872 | tf_op jit(solution)/shard_map/ppermute | solution.py:41
  5.9 1.4 %copy-done = bf16[1,3,512,512]{3,2,1,0:T(8,128)(2,1)S(1)} copy-done((bf16[1,3,512,512]{3,2,1,0:T(8,128)(2,1)S(1)}, bf16[1,3,512,512]{3,2,1,0:T(8,128)(2,1)}, u32[]{:S(2)}) %copy-start) | copy-done | bytes 1572888
  8.4 1.7 %keys_part.2 = (bf16[512,512]{1,0:T(8,128)(2,1)S(1)}, f32[256,512]{1,0:T(8,128)S(1)}, f32[256,512]{1,0:T(8,128)S(1)}, bf16[256,512]{1,0:T(8,128)(2,1)S(1)}) custom-call(s32[12]{0:T(128)S(1)} %dynamic-slice_bitcast_fusion.place, bf16[512,512]{1,0:T(8,128)(2,1)S(1)} %copy-done.2, bf16[1,3,512,512]{3,2,1,0:T(8,128)(2,1)S(1)} %copy-done), custom_call_target="tpu_custom_call" | custom-call | flops 1 | bytes 1 | tf_op jit(solution)/shard_map/keys_part/pallas_call | solution.py:82
  11.2 1.5 %collective-permute-start.2 = (bf16[256,512]{1,0:T(8,128)(2,1)S(1)}, bf16[256,512]{1,0:T(8,128)(2,1)S(1)}, u32[]{:S(2)}, u32[]{:S(2)}) collective-permute-start(bf16[256,512]{1,0:T(8,128)(2,1)S(1)} %collective-permute-done.1.rest_4_), channel_id=1, source_target_pairs={{0,8},{4,12},{8,24},{12,28},{24,16},{28,20},{16,0},{20,4},{1,9},{5... | collective-permute-start | bytes 786440 | tf_op jit(solution)/shard_map/ppermute | solution.py:358
  14.6 5.0 %collective-permute-done.2.rest_5_ = bf16[256,512]{1,0:T(8,128)(2,1)S(1)} collective-permute-done((bf16[256,512]{1,0:T(8,128)(2,1)S(1)}, bf16[256,512]{1,0:T(8,128)(2,1)S(1)}, u32[]{:S(2)}, u32[]{:S(2)}) %collective-permute-start.2) | collective-permute-done | bytes 262176 | tf_op jit(solution)/shard_map/ppermute | solution.py:358
  19.6 3.6 %collective-permute-start.3 = (bf16[512,512]{1,0:T(8,128)(2,1)S(1)}, bf16[512,512]{1,0:T(8,128)(2,1)S(1)}, u32[]{:S(2)}, u32[]{:S(2)}) collective-permute-start(bf16[512,512]{1,0:T(8,128)(2,1)S(1)} %collective-permute-done.k.pair_k), channel_id=1, source_target_pairs={{0,8},{8,16},{16,24},{1,9},{9,17},{17,25},{2,10},{10,18},{18,26},{... | collective-permute-start | bytes 1572872 | tf_op jit(solution)/shard_map/ppermute | solution.py:423
  23.3 1.7 %own_gradients.1.acc = f32[3,256,512]{2,1,0:T(8,128)S(1)} custom-call(s32[12]{0:T(128)S(1)} %dynamic-slice_bitcast_fusion.place, bf16[512,512]{1,0:T(8,128)(2,1)S(1)} %copy-done.3, bf16[512,512]{1,0:T(8,128)(2,1)S(1)} %multiply_convert_fusion.e, bf16[512,512]{1,0:T(8,128)(2,1)S(1)} %get-tuple-element.31.gated, f32[256,512]{1,0:T(8,128)S(1)} %get-tuple-element.40.gate, ...), custom_call_target="tpu_custom_call" | custom-call | flops 1 | bytes 1 | tf_op jit(solution)/shard_map/own_gradients/pallas_call | solution.py:144
  25.1 1.7 %keys_part.3 = (bf16[512,512]{1,0:T(8,128)(2,1)S(1)}, f32[256,512]{1,0:T(8,128)S(1)}, f32[256,512]{1,0:T(8,128)S(1)}, bf16[256,512]{1,0:T(8,128)(2,1)S(1)}) custom-call(s32[12]{0:T(128)S(1)} %dynamic-slice_bitcast_fusion.place, bf16[512,512]{1,0:T(8,128)(2,1)S(1)} %collective-permute-done.k.pair_k, bf16[1,3,512,512]{3,2,1,0:T(8,128)(2,1)S(1)} %copy-done.1), custom_call_target="tpu_custom_call" | custom-call | flops 1 | bytes 1 | tf_op jit(solution)/shard_map/keys_part/pallas_call | solution.py:82
  28.5 3.3 %collective-permute-done.3.up_k = bf16[512,512]{1,0:T(8,128)(2,1)S(1)} collective-permute-done((bf16[512,512]{1,0:T(8,128)(2,1)S(1)}, bf16[512,512]{1,0:T(8,128)(2,1)S(1)}, u32[]{:S(2)}, u32[]{:S(2)}) %collective-permute-start.3) | collective-permute-done | bytes 524320 | tf_op jit(solution)/shard_map/ppermute | solution.py:423
  31.9 1.8 %both_gradients.1 = (f32[3,64,512]{2,1,0:T(8,128)S(1)}, bf16[3,64,512]{2,1,0:T(8,128)(2,1)S(1)}, bf16[3,64,512]{2,1,0:T(8,128)(2,1)S(1)}, bf16[3,64,512]{2,1,0:T(8,128)(2,1)S(1)}) custom-call(s32[12]{0:T(128)S(1)} %dynamic-slice_bitcast_fusion.place, bf16[512,512]{1,0:T(8,128)(2,1)S(1)} %collective-permute-done.k.pair_k, ...), custom_call_target="tpu_custom_call" | custom-call | flops 1 | bytes 1 | tf_op jit(solution)/shard_map/both_gradients/pallas_call | solution.py:159
  33.7 5.0 %collective-permute-start.9 = (bf16[3,64,512]{2,1,0:T(8,128)(2,1)S(1)}, bf16[3,64,512]{2,1,0:T(8,128)(2,1)S(1)}, u32[]{:S(2)}, u32[]{:S(2)}) collective-permute-start(bf16[3,64,512]{2,1,0:T(8,128)(2,1)S(1)} %get-tuple-element.47), channel_id=1, source_target_pairs={{0,24},{4,28},{8,16},{12,20},{16,8},{20,12},{24,0},{28,4},{1,25},{... | collective-permute-start | bytes 589832 | tf_op jit(solution)/shard_map/ppermute | solution.py:41
  39.3 5.2 %collective-permute-done.9.rest_2_ = bf16[3,64,512]{2,1,0:T(8,128)(2,1)S(1)} collective-permute-done((bf16[3,64,512]{2,1,0:T(8,128)(2,1)S(1)}, bf16[3,64,512]{2,1,0:T(8,128)(2,1)S(1)}, u32[]{:S(2)}, u32[]{:S(2)}) %collective-permute-start.9) | collective-permute-done | bytes 196640 | tf_op jit(solution)/shard_map/ppermute | solution.py:41
  44.5 5.0 %collective-permute-done.6.early_v.rest_7_ = bf16[768,512]{1,0:T(8,128)(2,1)S(1)} collective-permute-done((bf16[768,512]{1,0:T(8,128)(2,1)S(1)}, bf16[768,512]{1,0:T(8,128)(2,1)S(1)}, u32[]{:S(2)}, u32[]{:S(2)}) %collective-permute-start.6) | collective-permute-done | bytes 786464 | tf_op jit(solution)/shard_map/ppermute | solution.py:41
  49.5 4.2 %collective-permute-done.8.rest_1_ = bf16[3,64,512]{2,1,0:T(8,128)(2,1)S(1)} collective-permute-done((bf16[3,64,512]{2,1,0:T(8,128)(2,1)S(1)}, bf16[3,64,512]{2,1,0:T(8,128)(2,1)S(1)}, u32[]{:S(2)}, u32[]{:S(2)}) %collective-permute-start.8) | collective-permute-done | bytes 196640 | tf_op jit(solution)/shard_map/ppermute | solution.py:41
  55.6 3.1 %collective-permute-start.13 = (bf16[3,64,512]{2,1,0:T(8,128)(2,1)S(1)}, bf16[3,64,512]{2,1,0:T(8,128)(2,1)S(1)}, u32[]{:S(2)}, u32[]{:S(2)}) collective-permute-start(bf16[3,64,512]{2,1,0:T(8,128)(2,1)S(1)} %renew.1.rest_0_), channel_id=1, source_target_pairs={{0,24},{4,28},{8,16},{12,20},{16,8},{20,12},{24,0},{28,4},{1,25},{... | collective-permute-start | bytes 589832 | tf_op jit(solution)/shard_map/ppermute | solution.py:41
  59.2 3.0 %collective-permute-done.10.rest_1_ = bf16[3,64,512]{2,1,0:T(8,128)(2,1)S(1)} collective-permute-done((bf16[3,64,512]{2,1,0:T(8,128)(2,1)S(1)}, bf16[3,64,512]{2,1,0:T(8,128)(2,1)S(1)}, u32[]{:S(2)}, u32[]{:S(2)}) %collective-permute-start.10) | collective-permute-done | bytes 196640 | tf_op jit(solution)/shard_map/ppermute | solution.py:41
  62.2 2.0 %collective-permute-start.17 = (bf16[256,512]{1,0:T(8,128)(2,1)S(1)}, bf16[256,512]{1,0:T(8,128)(2,1)S(1)}, u32[]{:S(2)}, u32[]{:S(2)}) collective-permute-start(bf16[256,512]{1,0:T(8,128)(2,1)S(1)} %collective-permute-done.1.rest_4_), channel_id=1, source_target_pairs={{0,4},{4,0},{8,12},{12,8},{16,20},{20,16},{24,28},{28,24},{1,5},{5... | collective-permute-start | bytes 786440 | tf_op jit(solution)/shard_map/ppermute | solution.py:41
  64.2 2.2 %collective-permute-done.13.rest_3_ = bf16[3,64,512]{2,1,0:T(8,128)(2,1)S(1)} collective-permute-done((bf16[3,64,512]{2,1,0:T(8,128)(2,1)S(1)}, bf16[3,64,512]{2,1,0:T(8,128)(2,1)S(1)}, u32[]{:S(2)}, u32[]{:S(2)}) %collective-permute-start.13) | collective-permute-done | bytes 196640 | tf_op jit(solution)/shard_map/ppermute | solution.py:41
  66.4 2.2 %collective-permute-start.16 = (bf16[3,64,512]{2,1,0:T(8,128)(2,1)S(1)}, bf16[3,64,512]{2,1,0:T(8,128)(2,1)S(1)}, u32[]{:S(2)}, u32[]{:S(2)}) collective-permute-start(bf16[3,64,512]{2,1,0:T(8,128)(2,1)S(1)} %collective-permute-done.13.rest_3_), channel_id=1, source_target_pairs={{0,4},{4,0},{8,12},{12,8},{16,20},{20,16},{24,28},{28,24},{1,5},{5... | collective-permute-start | bytes 589832 | tf_op jit(solution)/shard_map/ppermute | solution.py:41
  68.6 6.2 %collective-permute-done.12.rest_2_ = bf16[3,64,512]{2,1,0:T(8,128)(2,1)S(1)} collective-permute-done((bf16[3,64,512]{2,1,0:T(8,128)(2,1)S(1)}, bf16[3,64,512]{2,1,0:T(8,128)(2,1)S(1)}, u32[]{:S(2)}, u32[]{:S(2)}) %collective-permute-start.12) | collective-permute-done | bytes 196640 | tf_op jit(solution)/shard_map/ppermute | solution.py:41
  75.4 2.3 %window_attention.1.attended = f32[512,512]{1,0:T(8,128)S(1)} custom-call(s32[12]{0:T(128)S(1)} %dynamic-slice_bitcast_fusion.place, bf16[512,512]{1,0:T(8,128)(2,1)S(1)} %copy-done.5, bf16[512,512]{1,0:T(8,128)(2,1)S(1)} %copy-done.3, bf16[512,512]{1,0:T(8,128)(2,1)S(1)} %copy-done.4, bf16[512,512]{1,0:T(8,128)(2,1)S(1)} %collective-permute-done.k.pair_k, ...), custom_call_target="tpu_custom_call" | custom-call | flops 1 | bytes 1 | tf_op jit(solution)/shard_map/window_attention/pallas_call | solution.py:201
  78.6 1.6 %collective-permute-start.20 = (bf16[256,512]{1,0:T(8,128)(2,1)S(1)}, bf16[256,512]{1,0:T(8,128)(2,1)S(1)}, u32[]{:S(2)}, u32[]{:S(2)}) collective-permute-start(bf16[256,512]{1,0:T(8,128)(2,1)S(1)} %collective-permute-done.2.rest_5_), channel_id=1, source_target_pairs={{0,4},{4,0},{8,12},{12,8},{16,20},{20,16},{24,28},{28,24},{1,5},{5... | collective-permute-start | bytes 786440 | tf_op jit(solution)/shard_map/ppermute | solution.py:41
  80.1 1.6 %collective-permute-done.15.rest_6_ = bf16[3,64,512]{2,1,0:T(8,128)(2,1)S(1)} collective-permute-done((bf16[3,64,512]{2,1,0:T(8,128)(2,1)S(1)}, bf16[3,64,512]{2,1,0:T(8,128)(2,1)S(1)}, u32[]{:S(2)}, u32[]{:S(2)}) %collective-permute-start.15) | collective-permute-done | bytes 196640 | tf_op jit(solution)/shard_map/ppermute | solution.py:41
  81.7 1.7 %apply_fast.1.rest_0_ = bf16[512,512]{1,0:T(8,128)(2,1)S(1)} custom-call(s32[12]{0:T(128)S(1)} %dynamic-slice_bitcast_fusion.place, bf16[512,512]{1,0:T(8,128)(2,1)S(1)} %copy-done.5, f32[512,512]{1,0:T(8,128)S(1)} %window_attention.1.attended, bf16[3,64,512]{2,1,0:T(8,128)(2,1)S(1)} %renew.1.rest_0_, ...), custom_call_target="tpu_custom_call" | custom-call | flops 1 | bytes 1 | tf_op jit(solution)/shard_map/apply_fast/pallas_call | solution.py:280
  83.4 1.6 %collective-permute-start.19 = (bf16[512,512]{1,0:T(8,128)(2,1)S(1)}, bf16[512,512]{1,0:T(8,128)(2,1)S(1)}, u32[]{:S(2)}, u32[]{:S(2)}) collective-permute-start(bf16[512,512]{1,0:T(8,128)(2,1)S(1)} %apply_fast.1.rest_0_), channel_id=1, source_target_pairs={{0,2},{1,3},{2,0},{3,1},{4,6},{5,7},{6,4},{7,5},{8,10},{9,11},{10,... | collective-permute-start | bytes 1572872 | tf_op jit(solution)/shard_map/ppermute | solution.py:41
  84.9 1.4 %collective-permute-done.21.rest_6_ = bf16[256,512]{1,0:T(8,128)(2,1)S(1)} collective-permute-done((bf16[256,512]{1,0:T(8,128)(2,1)S(1)}, bf16[256,512]{1,0:T(8,128)(2,1)S(1)}, u32[]{:S(2)}, u32[]{:S(2)}) %collective-permute-start.21) | collective-permute-done | bytes 262176 | tf_op jit(solution)/shard_map/ppermute | solution.py:358
  86.5 1.7 %collective-permute-start.22 = (bf16[256,512]{1,0:T(8,128)(2,1)S(1)}, bf16[256,512]{1,0:T(8,128)(2,1)S(1)}, u32[]{:S(2)}, u32[]{:S(2)}) collective-permute-start(bf16[256,512]{1,0:T(8,128)(2,1)S(1)} %collective-permute-done.21.rest_6_), channel_id=1, source_target_pairs={{0,4},{4,0},{8,12},{12,8},{16,20},{20,16},{24,28},{28,24},{1,5},{5... | collective-permute-start | bytes 786440 | tf_op jit(solution)/shard_map/ppermute | solution.py:41
  88.1 5.2 %collective-permute-done.22.rest_10_ = bf16[256,512]{1,0:T(8,128)(2,1)S(1)} collective-permute-done((bf16[256,512]{1,0:T(8,128)(2,1)S(1)}, bf16[256,512]{1,0:T(8,128)(2,1)S(1)}, u32[]{:S(2)}, u32[]{:S(2)}) %collective-permute-start.22) | collective-permute-done | bytes 262176 | tf_op jit(solution)/shard_map/ppermute | solution.py:41
  93.4 1.3 %collective-permute-done.19.rest_2_ = bf16[512,512]{1,0:T(8,128)(2,1)S(1)} collective-permute-done((bf16[512,512]{1,0:T(8,128)(2,1)S(1)}, bf16[512,512]{1,0:T(8,128)(2,1)S(1)}, u32[]{:S(2)}, u32[]{:S(2)}) %collective-permute-start.19) | collective-permute-done | bytes 524320 | tf_op jit(solution)/shard_map/ppermute | solution.py:41
  94.7 1.7 %project_most.1 = (f32[512,512]{1,0:T(8,128)S(1)}, bf16[512,512]{1,0:T(8,128)(2,1)S(1)}) custom-call(s32[12]{0:T(128)S(1)} %dynamic-slice_bitcast_fusion.place, bf16[512,512]{1,0:T(8,128)(2,1)S(1)} %apply_fast.1.rest_0_, bf16[512,512]{1,0:T(8,128)(2,1)S(1)} %collective-permute-done.18.rest_1_, bf16[512,512]{1,0:T(8,128)(2,1)S(1)} %collective-permute-done.19.rest_2_, ...), custom_call_target="tpu_custom_call" | custom-call | flops 1 | bytes 1 | tf_op jit(solution)/shard_map/project_most/pallas_call | solution.py:316
  96.6 1.2 %project_last.1 = bf16[512,512]{1,0:T(8,128)(2,1)} custom-call(f32[512,512]{1,0:T(8,128)S(1)} %get-tuple-element.58.partial, bf16[512,512]{1,0:T(8,128)(2,1)S(1)} %collective-permute-done.23.block, bf16[512,512]{1,0:T(8,128)(2,1)S(1)} %get-tuple-element.59.rows), custom_call_target="tpu_custom_call" | custom-call | flops 1 | bytes 1 | tf_op jit(solution)/shard_map/project_last/pallas_call | solution.py:337
  (48 shorter events, 11.2 us)
Async XLA Ops:
  0.6 12.2 %copy-start.8 = (f32[512,1]{0,1:T(1,128)S(1)}, f32[512,1]{0,1:T(1,128)}, u32[]{:S(2)}) copy-start(f32[512,1]{0,1:T(1,128)} %param.11) | copy-start | bytes 6148
  0.6 10.6 %collective-permute-start.1 = (bf16[256,512]{1,0:T(8,128)(2,1)}, bf16[256,512]{1,0:T(8,128)(2,1)S(1)}, u32[]{:S(2)}, u32[]{:S(2)}) collective-permute-start(bf16[256,512]{1,0:T(8,128)(2,1)} %rest_3_.1), channel_id=1, source_target_pairs={{0,8},{4,12},{8,24},{12,28},{24,16},{28,20},{16,0},{20,4},{1,9},{5... | collective-permute-start | bytes 786440 | tf_op jit(solution)/shard_map/ppermute | solution.py:358
  3.7 15.9 %collective-permute-start = (bf16[512,512]{1,0:T(8,128)(2,1)}, bf16[512,512]{1,0:T(8,128)(2,1)S(1)}, u32[]{:S(2)}, u32[]{:S(2)}) collective-permute-start(bf16[512,512]{1,0:T(8,128)(2,1)} %k.5), channel_id=1, source_target_pairs={{0,4},{4,0},{8,12},{12,8},{16,20},{20,16},{24,28},{28,24},{1,5},{5... | collective-permute-start | bytes 1572872 | tf_op jit(solution)/shard_map/ppermute | solution.py:41
  5.9 1.4 %copy-start = (bf16[1,3,512,512]{3,2,1,0:T(8,128)(2,1)S(1)}, bf16[1,3,512,512]{3,2,1,0:T(8,128)(2,1)}, u32[]{:S(2)}) copy-start(bf16[1,3,512,512]{3,2,1,0:T(8,128)(2,1)} %w.5) | copy-start | bytes 4718596
  8.4 4.4 %copy-start.4 = (bf16[512,512]{1,0:T(8,128)(2,1)S(1)}, bf16[512,512]{1,0:T(8,128)(2,1)}, u32[]{:S(2)}) copy-start(bf16[512,512]{1,0:T(8,128)(2,1)} %v.1) | copy-start | bytes 1572868
  8.4 14.9 %copy-start.3 = (bf16[512,512]{1,0:T(8,128)(2,1)S(1)}, bf16[512,512]{1,0:T(8,128)(2,1)}, u32[]{:S(2)}) copy-start(bf16[512,512]{1,0:T(8,128)(2,1)} %k.5) | copy-start | bytes 1572868
  11.2 8.4 %collective-permute-start.2 = (bf16[256,512]{1,0:T(8,128)(2,1)S(1)}, bf16[256,512]{1,0:T(8,128)(2,1)S(1)}, u32[]{:S(2)}, u32[]{:S(2)}) collective-permute-start(bf16[256,512]{1,0:T(8,128)(2,1)S(1)} %collective-permute-done.1.rest_4_), channel_id=1, source_target_pairs={{0,8},{4,12},{8,24},{12,28},{24,16},{28,20},{16,0},{20,4},{1,9},{5... | collective-permute-start | bytes 786440 | tf_op jit(solution)/shard_map/ppermute | solution.py:358
  13.0 15.6 %collective-permute-start.5 = (bf16[512,512]{1,0:T(8,128)(2,1)S(1)}, bf16[512,512]{1,0:T(8,128)(2,1)S(1)}, u32[]{:S(2)}, u32[]{:S(2)}) collective-permute-start(bf16[512,512]{1,0:T(8,128)(2,1)S(1)} %multiply_convert_fusion.e), channel_id=1, source_target_pairs={{0,4},{4,0},{8,12},{12,8},{16,20},{20,16},{24,28},{28,24},{1,5},{5... | collective-permute-start | bytes 1572872 | tf_op jit(solution)/shard_map/ppermute | solution.py:41
  14.0 12.9 %collective-permute-start.4 = (bf16[512,512]{1,0:T(8,128)(2,1)S(1)}, bf16[512,512]{1,0:T(8,128)(2,1)S(1)}, u32[]{:S(2)}, u32[]{:S(2)}) collective-permute-start(bf16[512,512]{1,0:T(8,128)(2,1)S(1)} %copy-done.4), channel_id=1, source_target_pairs={{4,12},{12,20},{20,28},{5,13},{13,21},{21,29},{6,14},{14,22},{22,3... | collective-permute-start | bytes 1572872 | tf_op jit(solution)/shard_map/ppermute | solution.py:421
  19.6 12.2 %collective-permute-start.3 = (bf16[512,512]{1,0:T(8,128)(2,1)S(1)}, bf16[512,512]{1,0:T(8,128)(2,1)S(1)}, u32[]{:S(2)}, u32[]{:S(2)}) collective-permute-start(bf16[512,512]{1,0:T(8,128)(2,1)S(1)} %collective-permute-done.k.pair_k), channel_id=1, source_target_pairs={{0,8},{8,16},{16,24},{1,9},{9,17},{17,25},{2,10},{10,18},{18,26},{... | collective-permute-start | bytes 1572872 | tf_op jit(solution)/shard_map/ppermute | solution.py:423
  23.3 1.7 %copy-start.1 = (bf16[1,3,512,512]{3,2,1,0:T(8,128)(2,1)S(1)}, bf16[1,3,512,512]{3,2,1,0:T(8,128)(2,1)}, u32[]{:S(2)}) copy-start(bf16[1,3,512,512]{3,2,1,0:T(8,128)(2,1)} %w.5) | copy-start | bytes 4718596
  25.1 1.8 %copy-start.7 = (bf16[256,512]{1,0:T(8,128)(2,1)S(1)}, bf16[256,512]{1,0:T(8,128)(2,1)}, u32[]{:S(2)}) copy-start(bf16[256,512]{1,0:T(8,128)(2,1)} %rest_3_.1) | copy-start | bytes 786436
  31.9 21.9 %copy-start.6 = (f32[1,3,64,512]{3,2,1,0:T(8,128)S(1)}, f32[1,3,64,512]{3,2,1,0:T(8,128)}, u32[]{:S(2)}) copy-start(f32[1,3,64,512]{3,2,1,0:T(8,128)} %momentum.1) | copy-start | bytes 1179652
  33.6 15.9 %collective-permute-start.6 = (bf16[768,512]{1,0:T(8,128)(2,1)S(1)}, bf16[768,512]{1,0:T(8,128)(2,1)S(1)}, u32[]{:S(2)}, u32[]{:S(2)}) collective-permute-start(bf16[768,512]{1,0:T(8,128)(2,1)S(1)} %crossing.1), channel_id=1, source_target_pairs={{0,4},{4,0},{8,12},{12,8},{16,20},{20,16},{24,28},{28,24},{1,5},{5... | collective-permute-start | bytes 2359304 | tf_op jit(solution)/shard_map/ppermute | solution.py:41
  33.7 10.8 %collective-permute-start.9 = (bf16[3,64,512]{2,1,0:T(8,128)(2,1)S(1)}, bf16[3,64,512]{2,1,0:T(8,128)(2,1)S(1)}, u32[]{:S(2)}, u32[]{:S(2)}) collective-permute-start(bf16[3,64,512]{2,1,0:T(8,128)(2,1)S(1)} %get-tuple-element.47), channel_id=1, source_target_pairs={{0,24},{4,28},{8,16},{12,20},{16,8},{20,12},{24,0},{28,4},{1,25},{... | collective-permute-start | bytes 589832 | tf_op jit(solution)/shard_map/ppermute | solution.py:41
  38.7 10.8 %collective-permute-start.7 = (bf16[3,64,512]{2,1,0:T(8,128)(2,1)S(1)}, bf16[3,64,512]{2,1,0:T(8,128)(2,1)S(1)}, u32[]{:S(2)}, u32[]{:S(2)}) collective-permute-start(bf16[3,64,512]{2,1,0:T(8,128)(2,1)S(1)} %get-tuple-element.43), channel_id=1, source_target_pairs={{0,8},{4,12},{8,0},{12,4},{16,24},{20,28},{24,16},{28,20},{1,9},{5... | collective-permute-start | bytes 589832 | tf_op jit(solution)/shard_map/ppermute | solution.py:41
  38.7 15.0 %collective-permute-start.8 = (bf16[3,64,512]{2,1,0:T(8,128)(2,1)S(1)}, bf16[3,64,512]{2,1,0:T(8,128)(2,1)S(1)}, u32[]{:S(2)}, u32[]{:S(2)}) collective-permute-start(bf16[3,64,512]{2,1,0:T(8,128)(2,1)S(1)} %get-tuple-element.46), channel_id=1, source_target_pairs={{0,16},{4,20},{8,24},{12,28},{16,0},{20,4},{24,8},{28,12},{1,17},{... | collective-permute-start | bytes 589832 | tf_op jit(solution)/shard_map/ppermute | solution.py:41
  53.7 21.6 %copy-start.5 = (bf16[512,512]{1,0:T(8,128)(2,1)S(1)}, bf16[512,512]{1,0:T(8,128)(2,1)}, u32[]{:S(2)}) copy-start(bf16[512,512]{1,0:T(8,128)(2,1)} %q.3) | copy-start | bytes 1572868
  54.6 7.6 %collective-permute-start.10 = (bf16[3,64,512]{2,1,0:T(8,128)(2,1)S(1)}, bf16[3,64,512]{2,1,0:T(8,128)(2,1)S(1)}, u32[]{:S(2)}, u32[]{:S(2)}) collective-permute-start(bf16[3,64,512]{2,1,0:T(8,128)(2,1)S(1)} %renew.1.rest_0_), channel_id=1, source_target_pairs={{0,8},{4,12},{8,0},{12,4},{16,24},{20,28},{24,16},{28,20},{1,9},{5... | collective-permute-start | bytes 589832 | tf_op jit(solution)/shard_map/ppermute | solution.py:41
  54.7 7.5 %collective-permute-start.11 = (bf16[3,64,512]{2,1,0:T(8,128)(2,1)S(1)}, bf16[3,64,512]{2,1,0:T(8,128)(2,1)S(1)}, u32[]{:S(2)}, u32[]{:S(2)}) collective-permute-start(bf16[3,64,512]{2,1,0:T(8,128)(2,1)S(1)} %renew.1.rest_0_), channel_id=1, source_target_pairs={{0,4},{4,0},{8,12},{12,8},{16,20},{20,16},{24,28},{28,24},{1,5},{5... | collective-permute-start | bytes 589832 | tf_op jit(solution)/shard_map/ppermute | solution.py:41
  55.6 10.9 %collective-permute-start.13 = (bf16[3,64,512]{2,1,0:T(8,128)(2,1)S(1)}, bf16[3,64,512]{2,1,0:T(8,128)(2,1)S(1)}, u32[]{:S(2)}, u32[]{:S(2)}) collective-permute-start(bf16[3,64,512]{2,1,0:T(8,128)(2,1)S(1)} %renew.1.rest_0_), channel_id=1, source_target_pairs={{0,24},{4,28},{8,16},{12,20},{16,8},{20,12},{24,0},{28,4},{1,25},{... | collective-permute-start | bytes 589832 | tf_op jit(solution)/shard_map/ppermute | solution.py:41
  58.7 16.1 %collective-permute-start.12 = (bf16[3,64,512]{2,1,0:T(8,128)(2,1)S(1)}, bf16[3,64,512]{2,1,0:T(8,128)(2,1)S(1)}, u32[]{:S(2)}, u32[]{:S(2)}) collective-permute-start(bf16[3,64,512]{2,1,0:T(8,128)(2,1)S(1)} %renew.1.rest_0_), channel_id=1, source_target_pairs={{0,16},{4,20},{8,24},{12,28},{16,0},{20,4},{24,8},{28,12},{1,17},{... | collective-permute-start | bytes 589832 | tf_op jit(solution)/shard_map/ppermute | solution.py:41
  62.2 16.4 %collective-permute-start.14 = (bf16[3,64,512]{2,1,0:T(8,128)(2,1)S(1)}, bf16[3,64,512]{2,1,0:T(8,128)(2,1)S(1)}, u32[]{:S(2)}, u32[]{:S(2)}) collective-permute-start(bf16[3,64,512]{2,1,0:T(8,128)(2,1)S(1)} %collective-permute-done.10.rest_1_), channel_id=1, source_target_pairs={{0,4},{4,0},{8,12},{12,8},{16,20},{20,16},{24,28},{28,24},{1,5},{5... | collective-permute-start | bytes 589832 | tf_op jit(solution)/shard_map/ppermute | solution.py:41
  62.2 17.9 %collective-permute-start.17 = (bf16[256,512]{1,0:T(8,128)(2,1)S(1)}, bf16[256,512]{1,0:T(8,128)(2,1)S(1)}, u32[]{:S(2)}, u32[]{:S(2)}) collective-permute-start(bf16[256,512]{1,0:T(8,128)(2,1)S(1)} %collective-permute-done.1.rest_4_), channel_id=1, source_target_pairs={{0,4},{4,0},{8,12},{12,8},{16,20},{20,16},{24,28},{28,24},{1,5},{5... | collective-permute-start | bytes 786440 | tf_op jit(solution)/shard_map/ppermute | solution.py:41
  66.4 12.1 %collective-permute-start.16 = (bf16[3,64,512]{2,1,0:T(8,128)(2,1)S(1)}, bf16[3,64,512]{2,1,0:T(8,128)(2,1)S(1)}, u32[]{:S(2)}, u32[]{:S(2)}) collective-permute-start(bf16[3,64,512]{2,1,0:T(8,128)(2,1)S(1)} %collective-permute-done.13.rest_3_), channel_id=1, source_target_pairs={{0,4},{4,0},{8,12},{12,8},{16,20},{20,16},{24,28},{28,24},{1,5},{5... | collective-permute-start | bytes 589832 | tf_op jit(solution)/shard_map/ppermute | solution.py:41
  74.8 6.9 %collective-permute-start.15 = (bf16[3,64,512]{2,1,0:T(8,128)(2,1)S(1)}, bf16[3,64,512]{2,1,0:T(8,128)(2,1)S(1)}, u32[]{:S(2)}, u32[]{:S(2)}) collective-permute-start(bf16[3,64,512]{2,1,0:T(8,128)(2,1)S(1)} %collective-permute-done.12.rest_2_), channel_id=1, source_target_pairs={{0,4},{4,0},{8,12},{12,8},{16,20},{20,16},{24,28},{28,24},{1,5},{5... | collective-permute-start | bytes 589832 | tf_op jit(solution)/shard_map/ppermute | solution.py:41
  78.6 7.8 %collective-permute-start.21 = (bf16[256,512]{1,0:T(8,128)(2,1)S(1)}, bf16[256,512]{1,0:T(8,128)(2,1)S(1)}, u32[]{:S(2)}, u32[]{:S(2)}) collective-permute-start(bf16[256,512]{1,0:T(8,128)(2,1)S(1)} %collective-permute-done.2.rest_5_), channel_id=1, source_target_pairs={{0,8},{4,12},{8,24},{12,28},{24,16},{28,20},{16,0},{20,4},{1,9},{5... | collective-permute-start | bytes 786440 | tf_op jit(solution)/shard_map/ppermute | solution.py:358
  78.6 7.9 %collective-permute-start.20 = (bf16[256,512]{1,0:T(8,128)(2,1)S(1)}, bf16[256,512]{1,0:T(8,128)(2,1)S(1)}, u32[]{:S(2)}, u32[]{:S(2)}) collective-permute-start(bf16[256,512]{1,0:T(8,128)(2,1)S(1)} %collective-permute-done.2.rest_5_), channel_id=1, source_target_pairs={{0,4},{4,0},{8,12},{12,8},{16,20},{20,16},{24,28},{28,24},{1,5},{5... | collective-permute-start | bytes 786440 | tf_op jit(solution)/shard_map/ppermute | solution.py:41
  83.4 11.3 %collective-permute-start.19 = (bf16[512,512]{1,0:T(8,128)(2,1)S(1)}, bf16[512,512]{1,0:T(8,128)(2,1)S(1)}, u32[]{:S(2)}, u32[]{:S(2)}) collective-permute-start(bf16[512,512]{1,0:T(8,128)(2,1)S(1)} %apply_fast.1.rest_0_), channel_id=1, source_target_pairs={{0,2},{1,3},{2,0},{3,1},{4,6},{5,7},{6,4},{7,5},{8,10},{9,11},{10,... | collective-permute-start | bytes 1572872 | tf_op jit(solution)/shard_map/ppermute | solution.py:41
  86.5 6.9 %collective-permute-start.22 = (bf16[256,512]{1,0:T(8,128)(2,1)S(1)}, bf16[256,512]{1,0:T(8,128)(2,1)S(1)}, u32[]{:S(2)}, u32[]{:S(2)}) collective-permute-start(bf16[256,512]{1,0:T(8,128)(2,1)S(1)} %collective-permute-done.21.rest_6_), channel_id=1, source_target_pairs={{0,4},{4,0},{8,12},{12,8},{16,20},{20,16},{24,28},{28,24},{1,5},{5... | collective-permute-start | bytes 786440 | tf_op jit(solution)/shard_map/ppermute | solution.py:41
  88.1 6.6 %collective-permute-start.18 = (bf16[512,512]{1,0:T(8,128)(2,1)S(1)}, bf16[512,512]{1,0:T(8,128)(2,1)S(1)}, u32[]{:S(2)}, u32[]{:S(2)}) collective-permute-start(bf16[512,512]{1,0:T(8,128)(2,1)S(1)} %apply_fast.1.rest_0_), channel_id=1, source_target_pairs={{0,1},{1,0},{2,3},{3,2},{4,5},{5,4},{6,7},{7,6},{8,9},{9,8},{10,11... | collective-permute-start | bytes 1572872 | tf_op jit(solution)/shard_map/ppermute | solution.py:41
  94.7 1.9 %collective-permute-start.23 = (bf16[512,512]{1,0:T(8,128)(2,1)S(1)}, bf16[512,512]{1,0:T(8,128)(2,1)S(1)}, u32[]{:S(2)}, u32[]{:S(2)}) collective-permute-start(bf16[512,512]{1,0:T(8,128)(2,1)S(1)} %collective-permute-done.19.rest_2_), channel_id=1, source_target_pairs={{0,1},{1,0},{2,3},{3,2},{4,5},{5,4},{6,7},{7,6},{8,9},{9,8},{10,11... | collective-permute-start | bytes 1572872 | tf_op jit(solution)/shard_map/ppermute | solution.py:41
  (1 other events, 1.0 us)

commit v12 on v11

--- a/solution.py
+++ b/solution.py
@@ -438,22 +438,22 @@
     far = [swap(renewed, "seq", 1)]
     wide_far = [crossed, swap(after(wide[1], near[1]), "seq", 1)]
     near[1] = after(near[1], far[0])
-    far += [swap(unit, "seq", 1) for unit in near[1:]]
     attended = window_attention(
         place, queries, keys, values, pair_keys, up_keys, after(crossed, near[1])
     )
-    wide.append(ring_step(after(wide[2], far[1], near[2], near[3]), outer))
 
     total = after(summed[0], near[1])
     for piece in pieces:
         total = total + piece.astype(jnp.float32)
     moment = MOMENTUM_DECAY * momentum + total[None]
 
+    near[3] = after(near[3], attended, moment)
+    far += [swap(unit, "seq", 1) for unit in near[1:]]
+    wide.append(ring_step(after(wide[2], far[1], near[2], near[3]), outer))
     forwarded = far[-1]
-    far[-1] = after(far[-1], attended, wide_far[1], moment)
+    far[-1] = after(far[-1], wide_far[1])
     wide_far.append(swap(after(wide[2], forwarded), "seq", 1))
     wide_far.append(swap(after(wide[3], wide_far[2]), "seq", 1))
-
     combined = apply_fast(place, queries, attended, near + far)
 
     crossed_x = swap(combined, "head", 2)

time: 98.1 us -> 98.1 us (level)
  starting transfers between devices: 31.3 us -> 28.9 us
  waiting for transfers between devices: 46.3 us -> 48.6 us
    ppermute x19, waiting for transfers between devices: 35.4 us -> 39.2 us  [swap(): return lax.ppermute(array, axis, [(i, i ^ mask) for i in range(devices)])]
    ppermute x19, starting transfers between devices: 22.3 us -> 19.9 us  [swap(): return lax.ppermute(array, axis, [(i, i ^ mask) for i in range(devices)])]
    ppermute x3, waiting for transfers between devices: 7.53 us -> 6.11 us  [ring_step(): return lax.ppermute(unit, 'seq', pairs)]
  transfers between devices with their start and end apart: 24 -> 24, of which waited for: 16 -> 14; matrix products, arithmetic and copies ran while one was open for 2% -> 2% of each run, Pallas kernels for 12% -> 12%
where the time goes in v12:
time: 98.1 us; the launch traced here: 97.8 us
  waiting for transfers between devices  48.6 us (50%)
  starting transfers between devices  28.9 us (29%)
  Pallas kernels  15.3 us (16%)
  local copies, waits for them, and re-layouts  3.17 us (3%)
  other arithmetic  1.07 us (1%)
    ppermute x19, waiting for transfers between devices, swap(): return lax.ppermute(array, axis, [(i, i ^ mask) for i in range(devices)])  39.2 us
    ppermute x19, starting transfers between devices, swap(): return lax.ppermute(array, axis, [(i, i ^ mask) for i in range(devices)])  19.9 us
    ppermute x3, waiting for transfers between devices, ring_step(): return lax.ppermute(unit, 'seq', pairs)  6.11 us
    ppermute x3, starting transfers between devices, ring_step(): return lax.ppermute(unit, 'seq', pairs)  4.63 us
    ppermute x1, starting transfers between devices, shards(): lax.ppermute(up_keys, 'seq', [(s, s + 2) for s in range(0, ranks - 2, 2)])  3.65 us
    pallas_call x2, Pallas kernels, keys_part(): pl.pallas_call(functools.partial(keys_kernel, outer), out_shape=[jax.Shap...  3.49 us
    ppermute x1, waiting for transfers between devices, shards(): lax.ppermute(up_keys, 'seq', [(s, s + 2) for s in range(0, ranks - 2, 2)])  3.31 us
    unnamed x18, local copies, waits for them, and re-layouts  2.48 us
  transfers between devices with their start and end apart: 24, of which 14 were waited for; matrix products, arithmetic and copies ran while one was open for 2% of the time, Pallas kernels for 12%

profile of v12, /device:TPU:0, one launch (start us, length us, event | category | flops | bytes accessed | tf_op | source)
XLA Modules:
  0.0 97.8 jit_solution(12720574845250660546)
XLA Ops:
  0.6 3.1 %collective-permute-start.1 = (bf16[256,512]{1,0:T(8,128)(2,1)}, bf16[256,512]{1,0:T(8,128)(2,1)S(1)}, u32[]{:S(2)}, u32[]{:S(2)}) collective-permute-start(bf16[256,512]{1,0:T(8,128)(2,1)} %rest_3_.1), channel_id=1, source_target_pairs={{0,8},{4,12},{8,24},{12,28},{24,16},{28,20},{16,0},{20,4},{1,9},{5... | collective-permute-start | bytes 786440 | tf_op jit(solution)/shard_map/ppermute | solution.py:358
  3.7 1.5 %collective-permute-start = (bf16[512,512]{1,0:T(8,128)(2,1)}, bf16[512,512]{1,0:T(8,128)(2,1)S(1)}, u32[]{:S(2)}, u32[]{:S(2)}) collective-permute-start(bf16[512,512]{1,0:T(8,128)(2,1)} %k.5), channel_id=1, source_target_pairs={{0,4},{4,0},{8,12},{12,8},{16,20},{20,16},{24,28},{28,24},{1,5},{5... | collective-permute-start | bytes 1572872 | tf_op jit(solution)/shard_map/ppermute | solution.py:41
  5.9 1.4 %copy-done = bf16[1,3,512,512]{3,2,1,0:T(8,128)(2,1)S(1)} copy-done((bf16[1,3,512,512]{3,2,1,0:T(8,128)(2,1)S(1)}, bf16[1,3,512,512]{3,2,1,0:T(8,128)(2,1)}, u32[]{:S(2)}) %copy-start) | copy-done | bytes 1572888
  7.3 1.0 %copy-done.2 = bf16[512,512]{1,0:T(8,128)(2,1)S(1)} copy-done((bf16[512,512]{1,0:T(8,128)(2,1)S(1)}, bf16[512,512]{1,0:T(8,128)(2,1)}, u32[]{:S(2)}) %copy-start.2) | copy-done | bytes 524312
  8.4 1.7 %keys_part.2 = (bf16[512,512]{1,0:T(8,128)(2,1)S(1)}, f32[256,512]{1,0:T(8,128)S(1)}, f32[256,512]{1,0:T(8,128)S(1)}, bf16[256,512]{1,0:T(8,128)(2,1)S(1)}) custom-call(s32[12]{0:T(128)S(1)} %dynamic-slice_bitcast_fusion.place, bf16[512,512]{1,0:T(8,128)(2,1)S(1)} %copy-done.2, bf16[1,3,512,512]{3,2,1,0:T(8,128)(2,1)S(1)} %copy-done), custom_call_target="tpu_custom_call" | custom-call | flops 1 | bytes 1 | tf_op jit(solution)/shard_map/keys_part/pallas_call | solution.py:82
  10.1 1.1 %collective-permute-done.1.rest_4_ = bf16[256,512]{1,0:T(8,128)(2,1)S(1)} collective-permute-done((bf16[256,512]{1,0:T(8,128)(2,1)}, bf16[256,512]{1,0:T(8,128)(2,1)S(1)}, u32[]{:S(2)}, u32[]{:S(2)}) %collective-permute-start.1) | collective-permute-done | bytes 262176 | tf_op jit(solution)/shard_map/ppermute | solution.py:358
  11.2 1.5 %collective-permute-start.2 = (bf16[256,512]{1,0:T(8,128)(2,1)S(1)}, bf16[256,512]{1,0:T(8,128)(2,1)S(1)}, u32[]{:S(2)}, u32[]{:S(2)}) collective-permute-start(bf16[256,512]{1,0:T(8,128)(2,1)S(1)} %collective-permute-done.1.rest_4_), channel_id=1, source_target_pairs={{0,8},{4,12},{8,24},{12,28},{24,16},{28,20},{16,0},{20,4},{1,9},{5... | collective-permute-start | bytes 786440 | tf_op jit(solution)/shard_map/ppermute | solution.py:358
  14.6 5.0 %collective-permute-done.2.rest_5_ = bf16[256,512]{1,0:T(8,128)(2,1)S(1)} collective-permute-done((bf16[256,512]{1,0:T(8,128)(2,1)S(1)}, bf16[256,512]{1,0:T(8,128)(2,1)S(1)}, u32[]{:S(2)}, u32[]{:S(2)}) %collective-permute-start.2) | collective-permute-done | bytes 262176 | tf_op jit(solution)/shard_map/ppermute | solution.py:358
  19.6 3.6 %collective-permute-start.3 = (bf16[512,512]{1,0:T(8,128)(2,1)S(1)}, bf16[512,512]{1,0:T(8,128)(2,1)S(1)}, u32[]{:S(2)}, u32[]{:S(2)}) collective-permute-start(bf16[512,512]{1,0:T(8,128)(2,1)S(1)} %collective-permute-done.k.pair_k), channel_id=1, source_target_pairs={{0,8},{8,16},{16,24},{1,9},{9,17},{17,25},{2,10},{10,18},{18,26},{... | collective-permute-start | bytes 1572872 | tf_op jit(solution)/shard_map/ppermute | solution.py:423
  23.3 1.7 %own_gradients.1.acc = f32[3,256,512]{2,1,0:T(8,128)S(1)} custom-call(s32[12]{0:T(128)S(1)} %dynamic-slice_bitcast_fusion.place, bf16[512,512]{1,0:T(8,128)(2,1)S(1)} %copy-done.3, bf16[512,512]{1,0:T(8,128)(2,1)S(1)} %multiply_convert_fusion.e, bf16[512,512]{1,0:T(8,128)(2,1)S(1)} %get-tuple-element.32.gated, f32[256,512]{1,0:T(8,128)S(1)} %get-tuple-element.41.gate, ...), custom_call_target="tpu_custom_call" | custom-call | flops 1 | bytes 1 | tf_op jit(solution)/shard_map/own_gradients/pallas_call | solution.py:144
  25.1 1.7 %keys_part.3 = (bf16[512,512]{1,0:T(8,128)(2,1)S(1)}, f32[256,512]{1,0:T(8,128)S(1)}, f32[256,512]{1,0:T(8,128)S(1)}, bf16[256,512]{1,0:T(8,128)(2,1)S(1)}) custom-call(s32[12]{0:T(128)S(1)} %dynamic-slice_bitcast_fusion.place, bf16[512,512]{1,0:T(8,128)(2,1)S(1)} %collective-permute-done.k.pair_k, bf16[1,3,512,512]{3,2,1,0:T(8,128)(2,1)S(1)} %copy-done.1), custom_call_target="tpu_custom_call" | custom-call | flops 1 | bytes 1 | tf_op jit(solution)/shard_map/keys_part/pallas_call | solution.py:82
  27.5 1.1 %collective-permute-done.5.e = bf16[512,512]{1,0:T(8,128)(2,1)S(1)} collective-permute-done((bf16[512,512]{1,0:T(8,128)(2,1)S(1)}, bf16[512,512]{1,0:T(8,128)(2,1)S(1)}, u32[]{:S(2)}, u32[]{:S(2)}) %collective-permute-start.5) | collective-permute-done | bytes 524320 | tf_op jit(solution)/shard_map/ppermute | solution.py:41
  28.5 3.3 %collective-permute-done.3.up_k = bf16[512,512]{1,0:T(8,128)(2,1)S(1)} collective-permute-done((bf16[512,512]{1,0:T(8,128)(2,1)S(1)}, bf16[512,512]{1,0:T(8,128)(2,1)S(1)}, u32[]{:S(2)}, u32[]{:S(2)}) %collective-permute-start.3) | collective-permute-done | bytes 524320 | tf_op jit(solution)/shard_map/ppermute | solution.py:423
  31.9 1.8 %both_gradients.1 = (f32[3,64,512]{2,1,0:T(8,128)S(1)}, bf16[3,64,512]{2,1,0:T(8,128)(2,1)S(1)}, bf16[3,64,512]{2,1,0:T(8,128)(2,1)S(1)}, bf16[3,64,512]{2,1,0:T(8,128)(2,1)S(1)}) custom-call(s32[12]{0:T(128)S(1)} %dynamic-slice_bitcast_fusion.place, bf16[512,512]{1,0:T(8,128)(2,1)S(1)} %collective-permute-done.k.pair_k, ...), custom_call_target="tpu_custom_call" | custom-call | flops 1 | bytes 1 | tf_op jit(solution)/shard_map/both_gradients/pallas_call | solution.py:159
  33.7 5.0 %collective-permute-start.9 = (bf16[3,64,512]{2,1,0:T(8,128)(2,1)S(1)}, bf16[3,64,512]{2,1,0:T(8,128)(2,1)S(1)}, u32[]{:S(2)}, u32[]{:S(2)}) collective-permute-start(bf16[3,64,512]{2,1,0:T(8,128)(2,1)S(1)} %get-tuple-element.48), channel_id=1, source_target_pairs={{0,24},{4,28},{8,16},{12,20},{16,8},{20,12},{24,0},{28,4},{1,25},{... | collective-permute-start | bytes 589832 | tf_op jit(solution)/shard_map/ppermute | solution.py:41
  39.3 5.2 %collective-permute-done.9.rest_2_ = bf16[3,64,512]{2,1,0:T(8,128)(2,1)S(1)} collective-permute-done((bf16[3,64,512]{2,1,0:T(8,128)(2,1)S(1)}, bf16[3,64,512]{2,1,0:T(8,128)(2,1)S(1)}, u32[]{:S(2)}, u32[]{:S(2)}) %collective-permute-start.9) | collective-permute-done | bytes 196640 | tf_op jit(solution)/shard_map/ppermute | solution.py:41
  44.5 5.0 %collective-permute-done.6.early_v.rest_7_ = bf16[768,512]{1,0:T(8,128)(2,1)S(1)} collective-permute-done((bf16[768,512]{1,0:T(8,128)(2,1)S(1)}, bf16[768,512]{1,0:T(8,128)(2,1)S(1)}, u32[]{:S(2)}, u32[]{:S(2)}) %collective-permute-start.6) | collective-permute-done | bytes 786464 | tf_op jit(solution)/shard_map/ppermute | solution.py:41
  49.5 4.2 %collective-permute-done.8.rest_1_ = bf16[3,64,512]{2,1,0:T(8,128)(2,1)S(1)} collective-permute-done((bf16[3,64,512]{2,1,0:T(8,128)(2,1)S(1)}, bf16[3,64,512]{2,1,0:T(8,128)(2,1)S(1)}, u32[]{:S(2)}, u32[]{:S(2)}) %collective-permute-start.8) | collective-permute-done | bytes 196640 | tf_op jit(solution)/shard_map/ppermute | solution.py:41
  55.6 3.1 %collective-permute-start.13 = (bf16[3,64,512]{2,1,0:T(8,128)(2,1)S(1)}, bf16[3,64,512]{2,1,0:T(8,128)(2,1)S(1)}, u32[]{:S(2)}, u32[]{:S(2)}) collective-permute-start(bf16[3,64,512]{2,1,0:T(8,128)(2,1)S(1)} %renew.1.rest_0_), channel_id=1, source_target_pairs={{0,24},{4,28},{8,16},{12,20},{16,8},{20,12},{24,0},{28,4},{1,25},{... | collective-permute-start | bytes 589832 | tf_op jit(solution)/shard_map/ppermute | solution.py:41
  59.2 3.0 %collective-permute-done.10.rest_1_ = bf16[3,64,512]{2,1,0:T(8,128)(2,1)S(1)} collective-permute-done((bf16[3,64,512]{2,1,0:T(8,128)(2,1)S(1)}, bf16[3,64,512]{2,1,0:T(8,128)(2,1)S(1)}, u32[]{:S(2)}, u32[]{:S(2)}) %collective-permute-start.10) | collective-permute-done | bytes 196640 | tf_op jit(solution)/shard_map/ppermute | solution.py:41
  62.2 2.0 %collective-permute-start.17 = (bf16[256,512]{1,0:T(8,128)(2,1)S(1)}, bf16[256,512]{1,0:T(8,128)(2,1)S(1)}, u32[]{:S(2)}, u32[]{:S(2)}) collective-permute-start(bf16[256,512]{1,0:T(8,128)(2,1)S(1)} %collective-permute-done.1.rest_4_), channel_id=1, source_target_pairs={{0,4},{4,0},{8,12},{12,8},{16,20},{20,16},{24,28},{28,24},{1,5},{5... | collective-permute-start | bytes 786440 | tf_op jit(solution)/shard_map/ppermute | solution.py:41
  65.1 2.3 %window_attention.1.attended = f32[512,512]{1,0:T(8,128)S(1)} custom-call(s32[12]{0:T(128)S(1)} %dynamic-slice_bitcast_fusion.place, bf16[512,512]{1,0:T(8,128)(2,1)S(1)} %copy-done.5, bf16[512,512]{1,0:T(8,128)(2,1)S(1)} %copy-done.3, bf16[512,512]{1,0:T(8,128)(2,1)S(1)} %copy-done.4, bf16[512,512]{1,0:T(8,128)(2,1)S(1)} %collective-permute-done.k.pair_k, ...), custom_call_target="tpu_custom_call" | custom-call | flops 1 | bytes 1 | tf_op jit(solution)/shard_map/window_attention/pallas_call | solution.py:201
  67.4 1.2 %collective-permute-start.16 = (bf16[3,64,512]{2,1,0:T(8,128)(2,1)S(1)}, bf16[3,64,512]{2,1,0:T(8,128)(2,1)S(1)}, u32[]{:S(2)}, u32[]{:S(2)}) collective-permute-start(bf16[3,64,512]{2,1,0:T(8,128)(2,1)S(1)} %collective-permute-done.13.rest_3_), channel_id=1, source_target_pairs={{0,4},{4,0},{8,12},{12,8},{16,20},{20,16},{24,28},{28,24},{1,5},{5... | collective-permute-start | bytes 589832 | tf_op jit(solution)/shard_map/ppermute | solution.py:41
  68.6 6.2 %collective-permute-done.12.rest_2_ = bf16[3,64,512]{2,1,0:T(8,128)(2,1)S(1)} collective-permute-done((bf16[3,64,512]{2,1,0:T(8,128)(2,1)S(1)}, bf16[3,64,512]{2,1,0:T(8,128)(2,1)S(1)}, u32[]{:S(2)}, u32[]{:S(2)}) %collective-permute-start.12) | collective-permute-done | bytes 196640 | tf_op jit(solution)/shard_map/ppermute | solution.py:41
  75.4 1.6 %collective-permute-start.20 = (bf16[256,512]{1,0:T(8,128)(2,1)S(1)}, bf16[256,512]{1,0:T(8,128)(2,1)S(1)}, u32[]{:S(2)}, u32[]{:S(2)}) collective-permute-start(bf16[256,512]{1,0:T(8,128)(2,1)S(1)} %collective-permute-done.2.rest_5_), channel_id=1, source_target_pairs={{0,4},{4,0},{8,12},{12,8},{16,20},{20,16},{24,28},{28,24},{1,5},{5... | collective-permute-start | bytes 786440 | tf_op jit(solution)/shard_map/ppermute | solution.py:41
  76.9 5.7 %collective-permute-done.15.rest_6_ = bf16[3,64,512]{2,1,0:T(8,128)(2,1)S(1)} collective-permute-done((bf16[3,64,512]{2,1,0:T(8,128)(2,1)S(1)}, bf16[3,64,512]{2,1,0:T(8,128)(2,1)S(1)}, u32[]{:S(2)}, u32[]{:S(2)}) %collective-permute-start.15) | collective-permute-done | bytes 196640 | tf_op jit(solution)/shard_map/ppermute | solution.py:41
  82.7 1.7 %apply_fast.1.rest_0_ = bf16[512,512]{1,0:T(8,128)(2,1)S(1)} custom-call(s32[12]{0:T(128)S(1)} %dynamic-slice_bitcast_fusion.place, bf16[512,512]{1,0:T(8,128)(2,1)S(1)} %copy-done.5, f32[512,512]{1,0:T(8,128)S(1)} %window_attention.1.attended, bf16[3,64,512]{2,1,0:T(8,128)(2,1)S(1)} %renew.1.rest_0_, ...), custom_call_target="tpu_custom_call" | custom-call | flops 1 | bytes 1 | tf_op jit(solution)/shard_map/apply_fast/pallas_call | solution.py:280
  84.3 1.6 %collective-permute-start.19 = (bf16[512,512]{1,0:T(8,128)(2,1)S(1)}, bf16[512,512]{1,0:T(8,128)(2,1)S(1)}, u32[]{:S(2)}, u32[]{:S(2)}) collective-permute-start(bf16[512,512]{1,0:T(8,128)(2,1)S(1)} %apply_fast.1.rest_0_), channel_id=1, source_target_pairs={{0,2},{1,3},{2,0},{3,1},{4,6},{5,7},{6,4},{7,5},{8,10},{9,11},{10,... | collective-permute-start | bytes 1572872 | tf_op jit(solution)/shard_map/ppermute | solution.py:41
  86.7 6.2 %collective-permute-done.22.rest_10_ = bf16[256,512]{1,0:T(8,128)(2,1)S(1)} collective-permute-done((bf16[256,512]{1,0:T(8,128)(2,1)S(1)}, bf16[256,512]{1,0:T(8,128)(2,1)S(1)}, u32[]{:S(2)}, u32[]{:S(2)}) %collective-permute-start.22) | collective-permute-done | bytes 262176 | tf_op jit(solution)/shard_map/ppermute | solution.py:41
  93.0 1.7 %collective-permute-done.19.rest_2_ = bf16[512,512]{1,0:T(8,128)(2,1)S(1)} collective-permute-done((bf16[512,512]{1,0:T(8,128)(2,1)S(1)}, bf16[512,512]{1,0:T(8,128)(2,1)S(1)}, u32[]{:S(2)}, u32[]{:S(2)}) %collective-permute-start.19) | collective-permute-done | bytes 524320 | tf_op jit(solution)/shard_map/ppermute | solution.py:41
  94.7 1.7 %project_most.1 = (f32[512,512]{1,0:T(8,128)S(1)}, bf16[512,512]{1,0:T(8,128)(2,1)S(1)}) custom-call(s32[12]{0:T(128)S(1)} %dynamic-slice_bitcast_fusion.place, bf16[512,512]{1,0:T(8,128)(2,1)S(1)} %apply_fast.1.rest_0_, bf16[512,512]{1,0:T(8,128)(2,1)S(1)} %collective-permute-done.18.rest_1_, bf16[512,512]{1,0:T(8,128)(2,1)S(1)} %collective-permute-done.19.rest_2_, ...), custom_call_target="tpu_custom_call" | custom-call | flops 1 | bytes 1 | tf_op jit(solution)/shard_map/project_most/pallas_call | solution.py:316
  96.6 1.2 %project_last.1 = bf16[512,512]{1,0:T(8,128)(2,1)} custom-call(f32[512,512]{1,0:T(8,128)S(1)} %get-tuple-element.60.partial, bf16[512,512]{1,0:T(8,128)(2,1)S(1)} %collective-permute-done.23.block, bf16[512,512]{1,0:T(8,128)(2,1)S(1)} %get-tuple-element.61.rows), custom_call_target="tpu_custom_call" | custom-call | flops 1 | bytes 1 | tf_op jit(solution)/shard_map/project_last/pallas_call | solution.py:337
  (48 shorter events, 8.8 us)
Async XLA Ops:
  0.6 12.2 %copy-start.8 = (f32[512,1]{0,1:T(1,128)S(1)}, f32[512,1]{0,1:T(1,128)}, u32[]{:S(2)}) copy-start(f32[512,1]{0,1:T(1,128)} %param.11) | copy-start | bytes 6148
  0.6 10.6 %collective-permute-start.1 = (bf16[256,512]{1,0:T(8,128)(2,1)}, bf16[256,512]{1,0:T(8,128)(2,1)S(1)}, u32[]{:S(2)}, u32[]{:S(2)}) collective-permute-start(bf16[256,512]{1,0:T(8,128)(2,1)} %rest_3_.1), channel_id=1, source_target_pairs={{0,8},{4,12},{8,24},{12,28},{24,16},{28,20},{16,0},{20,4},{1,9},{5... | collective-permute-start | bytes 786440 | tf_op jit(solution)/shard_map/ppermute | solution.py:358
  3.7 15.9 %collective-permute-start = (bf16[512,512]{1,0:T(8,128)(2,1)}, bf16[512,512]{1,0:T(8,128)(2,1)S(1)}, u32[]{:S(2)}, u32[]{:S(2)}) collective-permute-start(bf16[512,512]{1,0:T(8,128)(2,1)} %k.5), channel_id=1, source_target_pairs={{0,4},{4,0},{8,12},{12,8},{16,20},{20,16},{24,28},{28,24},{1,5},{5... | collective-permute-start | bytes 1572872 | tf_op jit(solution)/shard_map/ppermute | solution.py:41
  5.9 1.4 %copy-start = (bf16[1,3,512,512]{3,2,1,0:T(8,128)(2,1)S(1)}, bf16[1,3,512,512]{3,2,1,0:T(8,128)(2,1)}, u32[]{:S(2)}) copy-start(bf16[1,3,512,512]{3,2,1,0:T(8,128)(2,1)} %w.5) | copy-start | bytes 4718596
  8.4 4.4 %copy-start.4 = (bf16[512,512]{1,0:T(8,128)(2,1)S(1)}, bf16[512,512]{1,0:T(8,128)(2,1)}, u32[]{:S(2)}) copy-start(bf16[512,512]{1,0:T(8,128)(2,1)} %v.1) | copy-start | bytes 1572868
  8.4 14.9 %copy-start.3 = (bf16[512,512]{1,0:T(8,128)(2,1)S(1)}, bf16[512,512]{1,0:T(8,128)(2,1)}, u32[]{:S(2)}) copy-start(bf16[512,512]{1,0:T(8,128)(2,1)} %k.5) | copy-start | bytes 1572868
  11.2 8.4 %collective-permute-start.2 = (bf16[256,512]{1,0:T(8,128)(2,1)S(1)}, bf16[256,512]{1,0:T(8,128)(2,1)S(1)}, u32[]{:S(2)}, u32[]{:S(2)}) collective-permute-start(bf16[256,512]{1,0:T(8,128)(2,1)S(1)} %collective-permute-done.1.rest_4_), channel_id=1, source_target_pairs={{0,8},{4,12},{8,24},{12,28},{24,16},{28,20},{16,0},{20,4},{1,9},{5... | collective-permute-start | bytes 786440 | tf_op jit(solution)/shard_map/ppermute | solution.py:358
  13.0 15.6 %collective-permute-start.5 = (bf16[512,512]{1,0:T(8,128)(2,1)S(1)}, bf16[512,512]{1,0:T(8,128)(2,1)S(1)}, u32[]{:S(2)}, u32[]{:S(2)}) collective-permute-start(bf16[512,512]{1,0:T(8,128)(2,1)S(1)} %multiply_convert_fusion.e), channel_id=1, source_target_pairs={{0,4},{4,0},{8,12},{12,8},{16,20},{20,16},{24,28},{28,24},{1,5},{5... | collective-permute-start | bytes 1572872 | tf_op jit(solution)/shard_map/ppermute | solution.py:41
  14.0 12.9 %collective-permute-start.4 = (bf16[512,512]{1,0:T(8,128)(2,1)S(1)}, bf16[512,512]{1,0:T(8,128)(2,1)S(1)}, u32[]{:S(2)}, u32[]{:S(2)}) collective-permute-start(bf16[512,512]{1,0:T(8,128)(2,1)S(1)} %copy-done.4), channel_id=1, source_target_pairs={{4,12},{12,20},{20,28},{5,13},{13,21},{21,29},{6,14},{14,22},{22,3... | collective-permute-start | bytes 1572872 | tf_op jit(solution)/shard_map/ppermute | solution.py:421
  19.6 12.2 %collective-permute-start.3 = (bf16[512,512]{1,0:T(8,128)(2,1)S(1)}, bf16[512,512]{1,0:T(8,128)(2,1)S(1)}, u32[]{:S(2)}, u32[]{:S(2)}) collective-permute-start(bf16[512,512]{1,0:T(8,128)(2,1)S(1)} %collective-permute-done.k.pair_k), channel_id=1, source_target_pairs={{0,8},{8,16},{16,24},{1,9},{9,17},{17,25},{2,10},{10,18},{18,26},{... | collective-permute-start | bytes 1572872 | tf_op jit(solution)/shard_map/ppermute | solution.py:423
  23.3 1.7 %copy-start.1 = (bf16[1,3,512,512]{3,2,1,0:T(8,128)(2,1)S(1)}, bf16[1,3,512,512]{3,2,1,0:T(8,128)(2,1)}, u32[]{:S(2)}) copy-start(bf16[1,3,512,512]{3,2,1,0:T(8,128)(2,1)} %w.5) | copy-start | bytes 4718596
  25.1 1.8 %copy-start.7 = (bf16[256,512]{1,0:T(8,128)(2,1)S(1)}, bf16[256,512]{1,0:T(8,128)(2,1)}, u32[]{:S(2)}) copy-start(bf16[256,512]{1,0:T(8,128)(2,1)} %rest_3_.1) | copy-start | bytes 786436
  31.9 21.9 %copy-start.6 = (f32[1,3,64,512]{3,2,1,0:T(8,128)S(1)}, f32[1,3,64,512]{3,2,1,0:T(8,128)}, u32[]{:S(2)}) copy-start(f32[1,3,64,512]{3,2,1,0:T(8,128)} %momentum.1) | copy-start | bytes 1179652
  33.6 15.9 %collective-permute-start.6 = (bf16[768,512]{1,0:T(8,128)(2,1)S(1)}, bf16[768,512]{1,0:T(8,128)(2,1)S(1)}, u32[]{:S(2)}, u32[]{:S(2)}) collective-permute-start(bf16[768,512]{1,0:T(8,128)(2,1)S(1)} %crossing.1), channel_id=1, source_target_pairs={{0,4},{4,0},{8,12},{12,8},{16,20},{20,16},{24,28},{28,24},{1,5},{5... | collective-permute-start | bytes 2359304 | tf_op jit(solution)/shard_map/ppermute | solution.py:41
  33.7 10.8 %collective-permute-start.9 = (bf16[3,64,512]{2,1,0:T(8,128)(2,1)S(1)}, bf16[3,64,512]{2,1,0:T(8,128)(2,1)S(1)}, u32[]{:S(2)}, u32[]{:S(2)}) collective-permute-start(bf16[3,64,512]{2,1,0:T(8,128)(2,1)S(1)} %get-tuple-element.48), channel_id=1, source_target_pairs={{0,24},{4,28},{8,16},{12,20},{16,8},{20,12},{24,0},{28,4},{1,25},{... | collective-permute-start | bytes 589832 | tf_op jit(solution)/shard_map/ppermute | solution.py:41
  38.7 10.8 %collective-permute-start.7 = (bf16[3,64,512]{2,1,0:T(8,128)(2,1)S(1)}, bf16[3,64,512]{2,1,0:T(8,128)(2,1)S(1)}, u32[]{:S(2)}, u32[]{:S(2)}) collective-permute-start(bf16[3,64,512]{2,1,0:T(8,128)(2,1)S(1)} %get-tuple-element.44), channel_id=1, source_target_pairs={{0,8},{4,12},{8,0},{12,4},{16,24},{20,28},{24,16},{28,20},{1,9},{5... | collective-permute-start | bytes 589832 | tf_op jit(solution)/shard_map/ppermute | solution.py:41
  38.7 15.0 %collective-permute-start.8 = (bf16[3,64,512]{2,1,0:T(8,128)(2,1)S(1)}, bf16[3,64,512]{2,1,0:T(8,128)(2,1)S(1)}, u32[]{:S(2)}, u32[]{:S(2)}) collective-permute-start(bf16[3,64,512]{2,1,0:T(8,128)(2,1)S(1)} %get-tuple-element.47), channel_id=1, source_target_pairs={{0,16},{4,20},{8,24},{12,28},{16,0},{20,4},{24,8},{28,12},{1,17},{... | collective-permute-start | bytes 589832 | tf_op jit(solution)/shard_map/ppermute | solution.py:41
  54.6 10.5 %copy-start.5 = (bf16[512,512]{1,0:T(8,128)(2,1)S(1)}, bf16[512,512]{1,0:T(8,128)(2,1)}, u32[]{:S(2)}) copy-start(bf16[512,512]{1,0:T(8,128)(2,1)} %q.3) | copy-start | bytes 1572868
  54.6 7.6 %collective-permute-start.10 = (bf16[3,64,512]{2,1,0:T(8,128)(2,1)S(1)}, bf16[3,64,512]{2,1,0:T(8,128)(2,1)S(1)}, u32[]{:S(2)}, u32[]{:S(2)}) collective-permute-start(bf16[3,64,512]{2,1,0:T(8,128)(2,1)S(1)} %renew.1.rest_0_), channel_id=1, source_target_pairs={{0,8},{4,12},{8,0},{12,4},{16,24},{20,28},{24,16},{28,20},{1,9},{5... | collective-permute-start | bytes 589832 | tf_op jit(solution)/shard_map/ppermute | solution.py:41
  54.7 7.5 %collective-permute-start.11 = (bf16[3,64,512]{2,1,0:T(8,128)(2,1)S(1)}, bf16[3,64,512]{2,1,0:T(8,128)(2,1)S(1)}, u32[]{:S(2)}, u32[]{:S(2)}) collective-permute-start(bf16[3,64,512]{2,1,0:T(8,128)(2,1)S(1)} %renew.1.rest_0_), channel_id=1, source_target_pairs={{0,4},{4,0},{8,12},{12,8},{16,20},{20,16},{24,28},{28,24},{1,5},{5... | collective-permute-start | bytes 589832 | tf_op jit(solution)/shard_map/ppermute | solution.py:41
  55.6 11.8 %collective-permute-start.13 = (bf16[3,64,512]{2,1,0:T(8,128)(2,1)S(1)}, bf16[3,64,512]{2,1,0:T(8,128)(2,1)S(1)}, u32[]{:S(2)}, u32[]{:S(2)}) collective-permute-start(bf16[3,64,512]{2,1,0:T(8,128)(2,1)S(1)} %renew.1.rest_0_), channel_id=1, source_target_pairs={{0,24},{4,28},{8,16},{12,20},{16,8},{20,12},{24,0},{28,4},{1,25},{... | collective-permute-start | bytes 589832 | tf_op jit(solution)/shard_map/ppermute | solution.py:41
  58.7 16.1 %collective-permute-start.12 = (bf16[3,64,512]{2,1,0:T(8,128)(2,1)S(1)}, bf16[3,64,512]{2,1,0:T(8,128)(2,1)S(1)}, u32[]{:S(2)}, u32[]{:S(2)}) collective-permute-start(bf16[3,64,512]{2,1,0:T(8,128)(2,1)S(1)} %renew.1.rest_0_), channel_id=1, source_target_pairs={{0,16},{4,20},{8,24},{12,28},{16,0},{20,4},{24,8},{28,12},{1,17},{... | collective-permute-start | bytes 589832 | tf_op jit(solution)/shard_map/ppermute | solution.py:41
  62.2 13.2 %collective-permute-start.14 = (bf16[3,64,512]{2,1,0:T(8,128)(2,1)S(1)}, bf16[3,64,512]{2,1,0:T(8,128)(2,1)S(1)}, u32[]{:S(2)}, u32[]{:S(2)}) collective-permute-start(bf16[3,64,512]{2,1,0:T(8,128)(2,1)S(1)} %collective-permute-done.10.rest_1_), channel_id=1, source_target_pairs={{0,4},{4,0},{8,12},{12,8},{16,20},{20,16},{24,28},{28,24},{1,5},{5... | collective-permute-start | bytes 589832 | tf_op jit(solution)/shard_map/ppermute | solution.py:41
  62.2 14.7 %collective-permute-start.17 = (bf16[256,512]{1,0:T(8,128)(2,1)S(1)}, bf16[256,512]{1,0:T(8,128)(2,1)S(1)}, u32[]{:S(2)}, u32[]{:S(2)}) collective-permute-start(bf16[256,512]{1,0:T(8,128)(2,1)S(1)} %collective-permute-done.1.rest_4_), channel_id=1, source_target_pairs={{0,4},{4,0},{8,12},{12,8},{16,20},{20,16},{24,28},{28,24},{1,5},{5... | collective-permute-start | bytes 786440 | tf_op jit(solution)/shard_map/ppermute | solution.py:41
  67.4 7.9 %collective-permute-start.16 = (bf16[3,64,512]{2,1,0:T(8,128)(2,1)S(1)}, bf16[3,64,512]{2,1,0:T(8,128)(2,1)S(1)}, u32[]{:S(2)}, u32[]{:S(2)}) collective-permute-start(bf16[3,64,512]{2,1,0:T(8,128)(2,1)S(1)} %collective-permute-done.13.rest_3_), channel_id=1, source_target_pairs={{0,4},{4,0},{8,12},{12,8},{16,20},{20,16},{24,28},{28,24},{1,5},{5... | collective-permute-start | bytes 589832 | tf_op jit(solution)/shard_map/ppermute | solution.py:41
  74.8 7.8 %collective-permute-start.15 = (bf16[3,64,512]{2,1,0:T(8,128)(2,1)S(1)}, bf16[3,64,512]{2,1,0:T(8,128)(2,1)S(1)}, u32[]{:S(2)}, u32[]{:S(2)}) collective-permute-start(bf16[3,64,512]{2,1,0:T(8,128)(2,1)S(1)} %collective-permute-done.12.rest_2_), channel_id=1, source_target_pairs={{0,4},{4,0},{8,12},{12,8},{16,20},{20,16},{24,28},{28,24},{1,5},{5... | collective-permute-start | bytes 589832 | tf_op jit(solution)/shard_map/ppermute | solution.py:41
  75.4 10.5 %collective-permute-start.21 = (bf16[256,512]{1,0:T(8,128)(2,1)S(1)}, bf16[256,512]{1,0:T(8,128)(2,1)S(1)}, u32[]{:S(2)}, u32[]{:S(2)}) collective-permute-start(bf16[256,512]{1,0:T(8,128)(2,1)S(1)} %collective-permute-done.2.rest_5_), channel_id=1, source_target_pairs={{0,8},{4,12},{8,24},{12,28},{24,16},{28,20},{16,0},{20,4},{1,9},{5... | collective-permute-start | bytes 786440 | tf_op jit(solution)/shard_map/ppermute | solution.py:358
  75.4 11.1 %collective-permute-start.20 = (bf16[256,512]{1,0:T(8,128)(2,1)S(1)}, bf16[256,512]{1,0:T(8,128)(2,1)S(1)}, u32[]{:S(2)}, u32[]{:S(2)}) collective-permute-start(bf16[256,512]{1,0:T(8,128)(2,1)S(1)} %collective-permute-done.2.rest_5_), channel_id=1, source_target_pairs={{0,4},{4,0},{8,12},{12,8},{16,20},{20,16},{24,28},{28,24},{1,5},{5... | collective-permute-start | bytes 786440 | tf_op jit(solution)/shard_map/ppermute | solution.py:41
  84.3 10.4 %collective-permute-start.19 = (bf16[512,512]{1,0:T(8,128)(2,1)S(1)}, bf16[512,512]{1,0:T(8,128)(2,1)S(1)}, u32[]{:S(2)}, u32[]{:S(2)}) collective-permute-start(bf16[512,512]{1,0:T(8,128)(2,1)S(1)} %apply_fast.1.rest_0_), channel_id=1, source_target_pairs={{0,2},{1,3},{2,0},{3,1},{4,6},{5,7},{6,4},{7,5},{8,10},{9,11},{10,... | collective-permute-start | bytes 1572872 | tf_op jit(solution)/shard_map/ppermute | solution.py:41
  86.5 6.5 %collective-permute-start.22 = (bf16[256,512]{1,0:T(8,128)(2,1)S(1)}, bf16[256,512]{1,0:T(8,128)(2,1)S(1)}, u32[]{:S(2)}, u32[]{:S(2)}) collective-permute-start(bf16[256,512]{1,0:T(8,128)(2,1)S(1)} %collective-permute-done.21.rest_6_), channel_id=1, source_target_pairs={{0,4},{4,0},{8,12},{12,8},{16,20},{20,16},{24,28},{28,24},{1,5},{5... | collective-permute-start | bytes 786440 | tf_op jit(solution)/shard_map/ppermute | solution.py:41
  86.7 8.0 %collective-permute-start.18 = (bf16[512,512]{1,0:T(8,128)(2,1)S(1)}, bf16[512,512]{1,0:T(8,128)(2,1)S(1)}, u32[]{:S(2)}, u32[]{:S(2)}) collective-permute-start(bf16[512,512]{1,0:T(8,128)(2,1)S(1)} %apply_fast.1.rest_0_), channel_id=1, source_target_pairs={{0,1},{1,0},{2,3},{3,2},{4,5},{5,4},{6,7},{7,6},{8,9},{9,8},{10,11... | collective-permute-start | bytes 1572872 | tf_op jit(solution)/shard_map/ppermute | solution.py:41
  94.7 1.9 %collective-permute-start.23 = (bf16[512,512]{1,0:T(8,128)(2,1)S(1)}, bf16[512,512]{1,0:T(8,128)(2,1)S(1)}, u32[]{:S(2)}, u32[]{:S(2)}) collective-permute-start(bf16[512,512]{1,0:T(8,128)(2,1)S(1)} %collective-permute-done.19.rest_2_), channel_id=1, source_target_pairs={{0,1},{1,0},{2,3},{3,2},{4,5},{5,4},{6,7},{7,6},{8,9},{9,8},{10,11... | collective-permute-start | bytes 1572872 | tf_op jit(solution)/shard_map/ppermute | solution.py:41
  (1 other events, 1.0 us)

commit v13 on v12

--- a/solution.py
+++ b/solution.py
@@ -452,7 +452,7 @@
     wide.append(ring_step(after(wide[2], far[1], near[2], near[3]), outer))
     forwarded = far[-1]
     far[-1] = after(far[-1], wide_far[1])
-    wide_far.append(swap(after(wide[2], forwarded), "seq", 1))
+    wide_far.append(swap(after(wide[2], forwarded, far[2]), "seq", 1))
     wide_far.append(swap(after(wide[3], wide_far[2]), "seq", 1))
     combined = apply_fast(place, queries, attended, near + far)
 

time: 98.1 us -> 98.1 us (level)
  starting transfers between devices: 28.9 us -> 27.6 us
  waiting for transfers between devices: 48.6 us -> 49.9 us
    ppermute x19, waiting for transfers between devices: 39.2 us -> 40.5 us  [swap(): return lax.ppermute(array, axis, [(i, i ^ mask) for i in range(devices)])]
    ppermute x19, starting transfers between devices: 19.9 us -> 18.7 us  [swap(): return lax.ppermute(array, axis, [(i, i ^ mask) for i in range(devices)])]
where the time goes in v13:
time: 98.1 us; the launch traced here: 97.9 us
  waiting for transfers between devices  49.9 us (51%)
  starting transfers between devices  27.6 us (28%)
  Pallas kernels  15.3 us (16%)
  local copies, waits for them, and re-layouts  3.17 us (3%)
  other arithmetic  1.07 us (1%)
    ppermute x19, waiting for transfers between devices, swap(): return lax.ppermute(array, axis, [(i, i ^ mask) for i in range(devices)])  40.5 us
    ppermute x19, starting transfers between devices, swap(): return lax.ppermute(array, axis, [(i, i ^ mask) for i in range(devices)])  18.7 us
    ppermute x3, waiting for transfers between devices, ring_step(): return lax.ppermute(unit, 'seq', pairs)  6.11 us
    ppermute x3, starting transfers between devices, ring_step(): return lax.ppermute(unit, 'seq', pairs)  4.63 us
    ppermute x1, starting transfers between devices, shards(): lax.ppermute(up_keys, 'seq', [(s, s + 2) for s in range(0, ranks - 2, 2)])  3.65 us
    pallas_call x2, Pallas kernels, keys_part(): pl.pallas_call(functools.partial(keys_kernel, outer), out_shape=[jax.Shap...  3.49 us
    ppermute x1, waiting for transfers between devices, shards(): lax.ppermute(up_keys, 'seq', [(s, s + 2) for s in range(0, ranks - 2, 2)])  3.31 us
    unnamed x18, local copies, waits for them, and re-layouts  2.48 us
  transfers between devices with their start and end apart: 24, of which 14 were waited for; matrix products, arithmetic and copies ran while one was open for 2% of the time, Pallas kernels for 12%

profile of v13, /device:TPU:0, one launch (start us, length us, event | category | flops | bytes accessed | tf_op | source)
XLA Modules:
  0.0 97.9 jit_solution(5637176410225208616)
XLA Ops:
  0.6 3.1 %collective-permute-start.1 = (bf16[256,512]{1,0:T(8,128)(2,1)}, bf16[256,512]{1,0:T(8,128)(2,1)S(1)}, u32[]{:S(2)}, u32[]{:S(2)}) collective-permute-start(bf16[256,512]{1,0:T(8,128)(2,1)} %rest_3_.1), channel_id=1, source_target_pairs={{0,8},{4,12},{8,24},{12,28},{24,16},{28,20},{16,0},{20,4},{1,9},{5... | collective-permute-start | bytes 786440 | tf_op jit(solution)/shard_map/ppermute | solution.py:358
  3.7 1.5 %collective-permute-start = (bf16[512,512]{1,0:T(8,128)(2,1)}, bf16[512,512]{1,0:T(8,128)(2,1)S(1)}, u32[]{:S(2)}, u32[]{:S(2)}) collective-permute-start(bf16[512,512]{1,0:T(8,128)(2,1)} %k.5), channel_id=1, source_target_pairs={{0,4},{4,0},{8,12},{12,8},{16,20},{20,16},{24,28},{28,24},{1,5},{5... | collective-permute-start | bytes 1572872 | tf_op jit(solution)/shard_map/ppermute | solution.py:41
  5.9 1.4 %copy-done = bf16[1,3,512,512]{3,2,1,0:T(8,128)(2,1)S(1)} copy-done((bf16[1,3,512,512]{3,2,1,0:T(8,128)(2,1)S(1)}, bf16[1,3,512,512]{3,2,1,0:T(8,128)(2,1)}, u32[]{:S(2)}) %copy-start) | copy-done | bytes 1572888
  7.3 1.0 %copy-done.2 = bf16[512,512]{1,0:T(8,128)(2,1)S(1)} copy-done((bf16[512,512]{1,0:T(8,128)(2,1)S(1)}, bf16[512,512]{1,0:T(8,128)(2,1)}, u32[]{:S(2)}) %copy-start.2) | copy-done | bytes 524312
  8.4 1.7 %keys_part.2 = (bf16[512,512]{1,0:T(8,128)(2,1)S(1)}, f32[256,512]{1,0:T(8,128)S(1)}, f32[256,512]{1,0:T(8,128)S(1)}, bf16[256,512]{1,0:T(8,128)(2,1)S(1)}) custom-call(s32[12]{0:T(128)S(1)} %dynamic-slice_bitcast_fusion.place, bf16[512,512]{1,0:T(8,128)(2,1)S(1)} %copy-done.2, bf16[1,3,512,512]{3,2,1,0:T(8,128)(2,1)S(1)} %copy-done), custom_call_target="tpu_custom_call" | custom-call | flops 1 | bytes 1 | tf_op jit(solution)/shard_map/keys_part/pallas_call | solution.py:82
  10.1 1.1 %collective-permute-done.1.rest_4_ = bf16[256,512]{1,0:T(8,128)(2,1)S(1)} collective-permute-done((bf16[256,512]{1,0:T(8,128)(2,1)}, bf16[256,512]{1,0:T(8,128)(2,1)S(1)}, u32[]{:S(2)}, u32[]{:S(2)}) %collective-permute-start.1) | collective-permute-done | bytes 262176 | tf_op jit(solution)/shard_map/ppermute | solution.py:358
  11.2 1.5 %collective-permute-start.2 = (bf16[256,512]{1,0:T(8,128)(2,1)S(1)}, bf16[256,512]{1,0:T(8,128)(2,1)S(1)}, u32[]{:S(2)}, u32[]{:S(2)}) collective-permute-start(bf16[256,512]{1,0:T(8,128)(2,1)S(1)} %collective-permute-done.1.rest_4_), channel_id=1, source_target_pairs={{0,8},{4,12},{8,24},{12,28},{24,16},{28,20},{16,0},{20,4},{1,9},{5... | collective-permute-start | bytes 786440 | tf_op jit(solution)/shard_map/ppermute | solution.py:358
  14.6 5.0 %collective-permute-done.2.rest_5_ = bf16[256,512]{1,0:T(8,128)(2,1)S(1)} collective-permute-done((bf16[256,512]{1,0:T(8,128)(2,1)S(1)}, bf16[256,512]{1,0:T(8,128)(2,1)S(1)}, u32[]{:S(2)}, u32[]{:S(2)}) %collective-permute-start.2) | collective-permute-done | bytes 262176 | tf_op jit(solution)/shard_map/ppermute | solution.py:358
  19.6 3.6 %collective-permute-start.3 = (bf16[512,512]{1,0:T(8,128)(2,1)S(1)}, bf16[512,512]{1,0:T(8,128)(2,1)S(1)}, u32[]{:S(2)}, u32[]{:S(2)}) collective-permute-start(bf16[512,512]{1,0:T(8,128)(2,1)S(1)} %collective-permute-done.k.pair_k), channel_id=1, source_target_pairs={{0,8},{8,16},{16,24},{1,9},{9,17},{17,25},{2,10},{10,18},{18,26},{... | collective-permute-start | bytes 1572872 | tf_op jit(solution)/shard_map/ppermute | solution.py:423
  23.3 1.7 %own_gradients.1.acc = f32[3,256,512]{2,1,0:T(8,128)S(1)} custom-call(s32[12]{0:T(128)S(1)} %dynamic-slice_bitcast_fusion.place, bf16[512,512]{1,0:T(8,128)(2,1)S(1)} %copy-done.3, bf16[512,512]{1,0:T(8,128)(2,1)S(1)} %multiply_convert_fusion.e, bf16[512,512]{1,0:T(8,128)(2,1)S(1)} %get-tuple-element.32.gated, f32[256,512]{1,0:T(8,128)S(1)} %get-tuple-element.41.gate, ...), custom_call_target="tpu_custom_call" | custom-call | flops 1 | bytes 1 | tf_op jit(solution)/shard_map/own_gradients/pallas_call | solution.py:144
  25.1 1.7 %keys_part.3 = (bf16[512,512]{1,0:T(8,128)(2,1)S(1)}, f32[256,512]{1,0:T(8,128)S(1)}, f32[256,512]{1,0:T(8,128)S(1)}, bf16[256,512]{1,0:T(8,128)(2,1)S(1)}) custom-call(s32[12]{0:T(128)S(1)} %dynamic-slice_bitcast_fusion.place, bf16[512,512]{1,0:T(8,128)(2,1)S(1)} %collective-permute-done.k.pair_k, bf16[1,3,512,512]{3,2,1,0:T(8,128)(2,1)S(1)} %copy-done.1), custom_call_target="tpu_custom_call" | custom-call | flops 1 | bytes 1 | tf_op jit(solution)/shard_map/keys_part/pallas_call | solution.py:82
  27.5 1.1 %collective-permute-done.5.e = bf16[512,512]{1,0:T(8,128)(2,1)S(1)} collective-permute-done((bf16[512,512]{1,0:T(8,128)(2,1)S(1)}, bf16[512,512]{1,0:T(8,128)(2,1)S(1)}, u32[]{:S(2)}, u32[]{:S(2)}) %collective-permute-start.5) | collective-permute-done | bytes 524320 | tf_op jit(solution)/shard_map/ppermute | solution.py:41
  28.5 3.3 %collective-permute-done.3.up_k = bf16[512,512]{1,0:T(8,128)(2,1)S(1)} collective-permute-done((bf16[512,512]{1,0:T(8,128)(2,1)S(1)}, bf16[512,512]{1,0:T(8,128)(2,1)S(1)}, u32[]{:S(2)}, u32[]{:S(2)}) %collective-permute-start.3) | collective-permute-done | bytes 524320 | tf_op jit(solution)/shard_map/ppermute | solution.py:423
  31.9 1.8 %both_gradients.1 = (f32[3,64,512]{2,1,0:T(8,128)S(1)}, bf16[3,64,512]{2,1,0:T(8,128)(2,1)S(1)}, bf16[3,64,512]{2,1,0:T(8,128)(2,1)S(1)}, bf16[3,64,512]{2,1,0:T(8,128)(2,1)S(1)}) custom-call(s32[12]{0:T(128)S(1)} %dynamic-slice_bitcast_fusion.place, bf16[512,512]{1,0:T(8,128)(2,1)S(1)} %collective-permute-done.k.pair_k, ...), custom_call_target="tpu_custom_call" | custom-call | flops 1 | bytes 1 | tf_op jit(solution)/shard_map/both_gradients/pallas_call | solution.py:159
  33.7 5.0 %collective-permute-start.9 = (bf16[3,64,512]{2,1,0:T(8,128)(2,1)S(1)}, bf16[3,64,512]{2,1,0:T(8,128)(2,1)S(1)}, u32[]{:S(2)}, u32[]{:S(2)}) collective-permute-start(bf16[3,64,512]{2,1,0:T(8,128)(2,1)S(1)} %get-tuple-element.48), channel_id=1, source_target_pairs={{0,24},{4,28},{8,16},{12,20},{16,8},{20,12},{24,0},{28,4},{1,25},{... | collective-permute-start | bytes 589832 | tf_op jit(solution)/shard_map/ppermute | solution.py:41
  39.3 5.2 %collective-permute-done.9.rest_2_ = bf16[3,64,512]{2,1,0:T(8,128)(2,1)S(1)} collective-permute-done((bf16[3,64,512]{2,1,0:T(8,128)(2,1)S(1)}, bf16[3,64,512]{2,1,0:T(8,128)(2,1)S(1)}, u32[]{:S(2)}, u32[]{:S(2)}) %collective-permute-start.9) | collective-permute-done | bytes 196640 | tf_op jit(solution)/shard_map/ppermute | solution.py:41
  44.5 5.0 %collective-permute-done.6.early_v.rest_7_ = bf16[768,512]{1,0:T(8,128)(2,1)S(1)} collective-permute-done((bf16[768,512]{1,0:T(8,128)(2,1)S(1)}, bf16[768,512]{1,0:T(8,128)(2,1)S(1)}, u32[]{:S(2)}, u32[]{:S(2)}) %collective-permute-start.6) | collective-permute-done | bytes 786464 | tf_op jit(solution)/shard_map/ppermute | solution.py:41
  49.5 4.2 %collective-permute-done.8.rest_1_ = bf16[3,64,512]{2,1,0:T(8,128)(2,1)S(1)} collective-permute-done((bf16[3,64,512]{2,1,0:T(8,128)(2,1)S(1)}, bf16[3,64,512]{2,1,0:T(8,128)(2,1)S(1)}, u32[]{:S(2)}, u32[]{:S(2)}) %collective-permute-start.8) | collective-permute-done | bytes 196640 | tf_op jit(solution)/shard_map/ppermute | solution.py:41
  55.6 3.1 %collective-permute-start.13 = (bf16[3,64,512]{2,1,0:T(8,128)(2,1)S(1)}, bf16[3,64,512]{2,1,0:T(8,128)(2,1)S(1)}, u32[]{:S(2)}, u32[]{:S(2)}) collective-permute-start(bf16[3,64,512]{2,1,0:T(8,128)(2,1)S(1)} %renew.1.rest_0_), channel_id=1, source_target_pairs={{0,24},{4,28},{8,16},{12,20},{16,8},{20,12},{24,0},{28,4},{1,25},{... | collective-permute-start | bytes 589832 | tf_op jit(solution)/shard_map/ppermute | solution.py:41
  59.2 3.0 %collective-permute-done.10.rest_1_ = bf16[3,64,512]{2,1,0:T(8,128)(2,1)S(1)} collective-permute-done((bf16[3,64,512]{2,1,0:T(8,128)(2,1)S(1)}, bf16[3,64,512]{2,1,0:T(8,128)(2,1)S(1)}, u32[]{:S(2)}, u32[]{:S(2)}) %collective-permute-start.10) | collective-permute-done | bytes 196640 | tf_op jit(solution)/shard_map/ppermute | solution.py:41
  62.2 2.0 %collective-permute-start.17 = (bf16[256,512]{1,0:T(8,128)(2,1)S(1)}, bf16[256,512]{1,0:T(8,128)(2,1)S(1)}, u32[]{:S(2)}, u32[]{:S(2)}) collective-permute-start(bf16[256,512]{1,0:T(8,128)(2,1)S(1)} %collective-permute-done.1.rest_4_), channel_id=1, source_target_pairs={{0,4},{4,0},{8,12},{12,8},{16,20},{20,16},{24,28},{28,24},{1,5},{5... | collective-permute-start | bytes 786440 | tf_op jit(solution)/shard_map/ppermute | solution.py:41
  65.1 2.3 %window_attention.1.attended = f32[512,512]{1,0:T(8,128)S(1)} custom-call(s32[12]{0:T(128)S(1)} %dynamic-slice_bitcast_fusion.place, bf16[512,512]{1,0:T(8,128)(2,1)S(1)} %copy-done.5, bf16[512,512]{1,0:T(8,128)(2,1)S(1)} %copy-done.3, bf16[512,512]{1,0:T(8,128)(2,1)S(1)} %copy-done.4, bf16[512,512]{1,0:T(8,128)(2,1)S(1)} %collective-permute-done.k.pair_k, ...), custom_call_target="tpu_custom_call" | custom-call | flops 1 | bytes 1 | tf_op jit(solution)/shard_map/window_attention/pallas_call | solution.py:201
  67.4 1.2 %collective-permute-start.16 = (bf16[3,64,512]{2,1,0:T(8,128)(2,1)S(1)}, bf16[3,64,512]{2,1,0:T(8,128)(2,1)S(1)}, u32[]{:S(2)}, u32[]{:S(2)}) collective-permute-start(bf16[3,64,512]{2,1,0:T(8,128)(2,1)S(1)} %collective-permute-done.13.rest_3_), channel_id=1, source_target_pairs={{0,4},{4,0},{8,12},{12,8},{16,20},{20,16},{24,28},{28,24},{1,5},{5... | collective-permute-start | bytes 589832 | tf_op jit(solution)/shard_map/ppermute | solution.py:41
  68.6 6.2 %collective-permute-done.12.rest_2_ = bf16[3,64,512]{2,1,0:T(8,128)(2,1)S(1)} collective-permute-done((bf16[3,64,512]{2,1,0:T(8,128)(2,1)S(1)}, bf16[3,64,512]{2,1,0:T(8,128)(2,1)S(1)}, u32[]{:S(2)}, u32[]{:S(2)}) %collective-permute-start.12) | collective-permute-done | bytes 196640 | tf_op jit(solution)/shard_map/ppermute | solution.py:41
  75.4 5.5 %collective-permute-done.15.rest_6_ = bf16[3,64,512]{2,1,0:T(8,128)(2,1)S(1)} collective-permute-done((bf16[3,64,512]{2,1,0:T(8,128)(2,1)S(1)}, bf16[3,64,512]{2,1,0:T(8,128)(2,1)S(1)}, u32[]{:S(2)}, u32[]{:S(2)}) %collective-permute-start.15) | collective-permute-done | bytes 196640 | tf_op jit(solution)/shard_map/ppermute | solution.py:41
  81.1 1.7 %apply_fast.1.rest_0_ = bf16[512,512]{1,0:T(8,128)(2,1)S(1)} custom-call(s32[12]{0:T(128)S(1)} %dynamic-slice_bitcast_fusion.place, bf16[512,512]{1,0:T(8,128)(2,1)S(1)} %copy-done.5, f32[512,512]{1,0:T(8,128)S(1)} %window_attention.1.attended, bf16[3,64,512]{2,1,0:T(8,128)(2,1)S(1)} %renew.1.rest_0_, ...), custom_call_target="tpu_custom_call" | custom-call | flops 1 | bytes 1 | tf_op jit(solution)/shard_map/apply_fast/pallas_call | solution.py:280
  82.8 1.6 %collective-permute-start.19 = (bf16[512,512]{1,0:T(8,128)(2,1)S(1)}, bf16[512,512]{1,0:T(8,128)(2,1)S(1)}, u32[]{:S(2)}, u32[]{:S(2)}) collective-permute-start(bf16[512,512]{1,0:T(8,128)(2,1)S(1)} %apply_fast.1.rest_0_), channel_id=1, source_target_pairs={{0,2},{1,3},{2,0},{3,1},{4,6},{5,7},{6,4},{7,5},{8,10},{9,11},{10,... | collective-permute-start | bytes 1572872 | tf_op jit(solution)/shard_map/ppermute | solution.py:41
  84.4 3.0 %collective-permute-done.20.rest_9_ = bf16[256,512]{1,0:T(8,128)(2,1)S(1)} collective-permute-done((bf16[256,512]{1,0:T(8,128)(2,1)S(1)}, bf16[256,512]{1,0:T(8,128)(2,1)S(1)}, u32[]{:S(2)}, u32[]{:S(2)}) %collective-permute-start.20) | collective-permute-done | bytes 262176 | tf_op jit(solution)/shard_map/ppermute | solution.py:41
  87.6 6.1 %collective-permute-done.22.rest_10_ = bf16[256,512]{1,0:T(8,128)(2,1)S(1)} collective-permute-done((bf16[256,512]{1,0:T(8,128)(2,1)S(1)}, bf16[256,512]{1,0:T(8,128)(2,1)S(1)}, u32[]{:S(2)}, u32[]{:S(2)}) %collective-permute-start.22) | collective-permute-done | bytes 262176 | tf_op jit(solution)/shard_map/ppermute | solution.py:41
  93.7 1.0 %collective-permute-done.19.rest_2_ = bf16[512,512]{1,0:T(8,128)(2,1)S(1)} collective-permute-done((bf16[512,512]{1,0:T(8,128)(2,1)S(1)}, bf16[512,512]{1,0:T(8,128)(2,1)S(1)}, u32[]{:S(2)}, u32[]{:S(2)}) %collective-permute-start.19) | collective-permute-done | bytes 524320 | tf_op jit(solution)/shard_map/ppermute | solution.py:41
  94.7 1.7 %project_most.1 = (f32[512,512]{1,0:T(8,128)S(1)}, bf16[512,512]{1,0:T(8,128)(2,1)S(1)}) custom-call(s32[12]{0:T(128)S(1)} %dynamic-slice_bitcast_fusion.place, bf16[512,512]{1,0:T(8,128)(2,1)S(1)} %apply_fast.1.rest_0_, bf16[512,512]{1,0:T(8,128)(2,1)S(1)} %collective-permute-done.18.rest_1_, bf16[512,512]{1,0:T(8,128)(2,1)S(1)} %collective-permute-done.19.rest_2_, ...), custom_call_target="tpu_custom_call" | custom-call | flops 1 | bytes 1 | tf_op jit(solution)/shard_map/project_most/pallas_call | solution.py:316
  96.6 1.2 %project_last.1 = bf16[512,512]{1,0:T(8,128)(2,1)} custom-call(f32[512,512]{1,0:T(8,128)S(1)} %get-tuple-element.60.partial, bf16[512,512]{1,0:T(8,128)(2,1)S(1)} %collective-permute-done.23.block, bf16[512,512]{1,0:T(8,128)(2,1)S(1)} %get-tuple-element.61.rows), custom_call_target="tpu_custom_call" | custom-call | flops 1 | bytes 1 | tf_op jit(solution)/shard_map/project_last/pallas_call | solution.py:337
  (48 shorter events, 8.5 us)
Async XLA Ops:
  0.6 12.2 %copy-start.8 = (f32[512,1]{0,1:T(1,128)S(1)}, f32[512,1]{0,1:T(1,128)}, u32[]{:S(2)}) copy-start(f32[512,1]{0,1:T(1,128)} %param.11) | copy-start | bytes 6148
  0.6 10.6 %collective-permute-start.1 = (bf16[256,512]{1,0:T(8,128)(2,1)}, bf16[256,512]{1,0:T(8,128)(2,1)S(1)}, u32[]{:S(2)}, u32[]{:S(2)}) collective-permute-start(bf16[256,512]{1,0:T(8,128)(2,1)} %rest_3_.1), channel_id=1, source_target_pairs={{0,8},{4,12},{8,24},{12,28},{24,16},{28,20},{16,0},{20,4},{1,9},{5... | collective-permute-start | bytes 786440 | tf_op jit(solution)/shard_map/ppermute | solution.py:358
  3.7 15.9 %collective-permute-start = (bf16[512,512]{1,0:T(8,128)(2,1)}, bf16[512,512]{1,0:T(8,128)(2,1)S(1)}, u32[]{:S(2)}, u32[]{:S(2)}) collective-permute-start(bf16[512,512]{1,0:T(8,128)(2,1)} %k.5), channel_id=1, source_target_pairs={{0,4},{4,0},{8,12},{12,8},{16,20},{20,16},{24,28},{28,24},{1,5},{5... | collective-permute-start | bytes 1572872 | tf_op jit(solution)/shard_map/ppermute | solution.py:41
  5.9 1.4 %copy-start = (bf16[1,3,512,512]{3,2,1,0:T(8,128)(2,1)S(1)}, bf16[1,3,512,512]{3,2,1,0:T(8,128)(2,1)}, u32[]{:S(2)}) copy-start(bf16[1,3,512,512]{3,2,1,0:T(8,128)(2,1)} %w.5) | copy-start | bytes 4718596
  8.4 4.4 %copy-start.4 = (bf16[512,512]{1,0:T(8,128)(2,1)S(1)}, bf16[512,512]{1,0:T(8,128)(2,1)}, u32[]{:S(2)}) copy-start(bf16[512,512]{1,0:T(8,128)(2,1)} %v.1) | copy-start | bytes 1572868
  8.4 14.9 %copy-start.3 = (bf16[512,512]{1,0:T(8,128)(2,1)S(1)}, bf16[512,512]{1,0:T(8,128)(2,1)}, u32[]{:S(2)}) copy-start(bf16[512,512]{1,0:T(8,128)(2,1)} %k.5) | copy-start | bytes 1572868
  11.2 8.4 %collective-permute-start.2 = (bf16[256,512]{1,0:T(8,128)(2,1)S(1)}, bf16[256,512]{1,0:T(8,128)(2,1)S(1)}, u32[]{:S(2)}, u32[]{:S(2)}) collective-permute-start(bf16[256,512]{1,0:T(8,128)(2,1)S(1)} %collective-permute-done.1.rest_4_), channel_id=1, source_target_pairs={{0,8},{4,12},{8,24},{12,28},{24,16},{28,20},{16,0},{20,4},{1,9},{5... | collective-permute-start | bytes 786440 | tf_op jit(solution)/shard_map/ppermute | solution.py:358
  13.0 15.6 %collective-permute-start.5 = (bf16[512,512]{1,0:T(8,128)(2,1)S(1)}, bf16[512,512]{1,0:T(8,128)(2,1)S(1)}, u32[]{:S(2)}, u32[]{:S(2)}) collective-permute-start(bf16[512,512]{1,0:T(8,128)(2,1)S(1)} %multiply_convert_fusion.e), channel_id=1, source_target_pairs={{0,4},{4,0},{8,12},{12,8},{16,20},{20,16},{24,28},{28,24},{1,5},{5... | collective-permute-start | bytes 1572872 | tf_op jit(solution)/shard_map/ppermute | solution.py:41
  14.0 12.9 %collective-permute-start.4 = (bf16[512,512]{1,0:T(8,128)(2,1)S(1)}, bf16[512,512]{1,0:T(8,128)(2,1)S(1)}, u32[]{:S(2)}, u32[]{:S(2)}) collective-permute-start(bf16[512,512]{1,0:T(8,128)(2,1)S(1)} %copy-done.4), channel_id=1, source_target_pairs={{4,12},{12,20},{20,28},{5,13},{13,21},{21,29},{6,14},{14,22},{22,3... | collective-permute-start | bytes 1572872 | tf_op jit(solution)/shard_map/ppermute | solution.py:421
  19.6 12.2 %collective-permute-start.3 = (bf16[512,512]{1,0:T(8,128)(2,1)S(1)}, bf16[512,512]{1,0:T(8,128)(2,1)S(1)}, u32[]{:S(2)}, u32[]{:S(2)}) collective-permute-start(bf16[512,512]{1,0:T(8,128)(2,1)S(1)} %collective-permute-done.k.pair_k), channel_id=1, source_target_pairs={{0,8},{8,16},{16,24},{1,9},{9,17},{17,25},{2,10},{10,18},{18,26},{... | collective-permute-start | bytes 1572872 | tf_op jit(solution)/shard_map/ppermute | solution.py:423
  23.3 1.7 %copy-start.1 = (bf16[1,3,512,512]{3,2,1,0:T(8,128)(2,1)S(1)}, bf16[1,3,512,512]{3,2,1,0:T(8,128)(2,1)}, u32[]{:S(2)}) copy-start(bf16[1,3,512,512]{3,2,1,0:T(8,128)(2,1)} %w.5) | copy-start | bytes 4718596
  25.1 1.8 %copy-start.7 = (bf16[256,512]{1,0:T(8,128)(2,1)S(1)}, bf16[256,512]{1,0:T(8,128)(2,1)}, u32[]{:S(2)}) copy-start(bf16[256,512]{1,0:T(8,128)(2,1)} %rest_3_.1) | copy-start | bytes 786436
  31.9 21.9 %copy-start.6 = (f32[1,3,64,512]{3,2,1,0:T(8,128)S(1)}, f32[1,3,64,512]{3,2,1,0:T(8,128)}, u32[]{:S(2)}) copy-start(f32[1,3,64,512]{3,2,1,0:T(8,128)} %momentum.1) | copy-start | bytes 1179652
  33.6 15.9 %collective-permute-start.6 = (bf16[768,512]{1,0:T(8,128)(2,1)S(1)}, bf16[768,512]{1,0:T(8,128)(2,1)S(1)}, u32[]{:S(2)}, u32[]{:S(2)}) collective-permute-start(bf16[768,512]{1,0:T(8,128)(2,1)S(1)} %crossing.1), channel_id=1, source_target_pairs={{0,4},{4,0},{8,12},{12,8},{16,20},{20,16},{24,28},{28,24},{1,5},{5... | collective-permute-start | bytes 2359304 | tf_op jit(solution)/shard_map/ppermute | solution.py:41
  33.7 10.8 %collective-permute-start.9 = (bf16[3,64,512]{2,1,0:T(8,128)(2,1)S(1)}, bf16[3,64,512]{2,1,0:T(8,128)(2,1)S(1)}, u32[]{:S(2)}, u32[]{:S(2)}) collective-permute-start(bf16[3,64,512]{2,1,0:T(8,128)(2,1)S(1)} %get-tuple-element.48), channel_id=1, source_target_pairs={{0,24},{4,28},{8,16},{12,20},{16,8},{20,12},{24,0},{28,4},{1,25},{... | collective-permute-start | bytes 589832 | tf_op jit(solution)/shard_map/ppermute | solution.py:41
  38.7 10.8 %collective-permute-start.7 = (bf16[3,64,512]{2,1,0:T(8,128)(2,1)S(1)}, bf16[3,64,512]{2,1,0:T(8,128)(2,1)S(1)}, u32[]{:S(2)}, u32[]{:S(2)}) collective-permute-start(bf16[3,64,512]{2,1,0:T(8,128)(2,1)S(1)} %get-tuple-element.44), channel_id=1, source_target_pairs={{0,8},{4,12},{8,0},{12,4},{16,24},{20,28},{24,16},{28,20},{1,9},{5... | collective-permute-start | bytes 589832 | tf_op jit(solution)/shard_map/ppermute | solution.py:41
  38.7 15.0 %collective-permute-start.8 = (bf16[3,64,512]{2,1,0:T(8,128)(2,1)S(1)}, bf16[3,64,512]{2,1,0:T(8,128)(2,1)S(1)}, u32[]{:S(2)}, u32[]{:S(2)}) collective-permute-start(bf16[3,64,512]{2,1,0:T(8,128)(2,1)S(1)} %get-tuple-element.47), channel_id=1, source_target_pairs={{0,16},{4,20},{8,24},{12,28},{16,0},{20,4},{24,8},{28,12},{1,17},{... | collective-permute-start | bytes 589832 | tf_op jit(solution)/shard_map/ppermute | solution.py:41
  54.6 10.5 %copy-start.5 = (bf16[512,512]{1,0:T(8,128)(2,1)S(1)}, bf16[512,512]{1,0:T(8,128)(2,1)}, u32[]{:S(2)}) copy-start(bf16[512,512]{1,0:T(8,128)(2,1)} %q.3) | copy-start | bytes 1572868
  54.6 7.6 %collective-permute-start.10 = (bf16[3,64,512]{2,1,0:T(8,128)(2,1)S(1)}, bf16[3,64,512]{2,1,0:T(8,128)(2,1)S(1)}, u32[]{:S(2)}, u32[]{:S(2)}) collective-permute-start(bf16[3,64,512]{2,1,0:T(8,128)(2,1)S(1)} %renew.1.rest_0_), channel_id=1, source_target_pairs={{0,8},{4,12},{8,0},{12,4},{16,24},{20,28},{24,16},{28,20},{1,9},{5... | collective-permute-start | bytes 589832 | tf_op jit(solution)/shard_map/ppermute | solution.py:41
  54.7 7.5 %collective-permute-start.11 = (bf16[3,64,512]{2,1,0:T(8,128)(2,1)S(1)}, bf16[3,64,512]{2,1,0:T(8,128)(2,1)S(1)}, u32[]{:S(2)}, u32[]{:S(2)}) collective-permute-start(bf16[3,64,512]{2,1,0:T(8,128)(2,1)S(1)} %renew.1.rest_0_), channel_id=1, source_target_pairs={{0,4},{4,0},{8,12},{12,8},{16,20},{20,16},{24,28},{28,24},{1,5},{5... | collective-permute-start | bytes 589832 | tf_op jit(solution)/shard_map/ppermute | solution.py:41
  55.6 11.8 %collective-permute-start.13 = (bf16[3,64,512]{2,1,0:T(8,128)(2,1)S(1)}, bf16[3,64,512]{2,1,0:T(8,128)(2,1)S(1)}, u32[]{:S(2)}, u32[]{:S(2)}) collective-permute-start(bf16[3,64,512]{2,1,0:T(8,128)(2,1)S(1)} %renew.1.rest_0_), channel_id=1, source_target_pairs={{0,24},{4,28},{8,16},{12,20},{16,8},{20,12},{24,0},{28,4},{1,25},{... | collective-permute-start | bytes 589832 | tf_op jit(solution)/shard_map/ppermute | solution.py:41
  58.7 16.1 %collective-permute-start.12 = (bf16[3,64,512]{2,1,0:T(8,128)(2,1)S(1)}, bf16[3,64,512]{2,1,0:T(8,128)(2,1)S(1)}, u32[]{:S(2)}, u32[]{:S(2)}) collective-permute-start(bf16[3,64,512]{2,1,0:T(8,128)(2,1)S(1)} %renew.1.rest_0_), channel_id=1, source_target_pairs={{0,16},{4,20},{8,24},{12,28},{16,0},{20,4},{24,8},{28,12},{1,17},{... | collective-permute-start | bytes 589832 | tf_op jit(solution)/shard_map/ppermute | solution.py:41
  62.2 13.2 %collective-permute-start.14 = (bf16[3,64,512]{2,1,0:T(8,128)(2,1)S(1)}, bf16[3,64,512]{2,1,0:T(8,128)(2,1)S(1)}, u32[]{:S(2)}, u32[]{:S(2)}) collective-permute-start(bf16[3,64,512]{2,1,0:T(8,128)(2,1)S(1)} %collective-permute-done.10.rest_1_), channel_id=1, source_target_pairs={{0,4},{4,0},{8,12},{12,8},{16,20},{20,16},{24,28},{28,24},{1,5},{5... | collective-permute-start | bytes 589832 | tf_op jit(solution)/shard_map/ppermute | solution.py:41
  62.2 18.9 %collective-permute-start.17 = (bf16[256,512]{1,0:T(8,128)(2,1)S(1)}, bf16[256,512]{1,0:T(8,128)(2,1)S(1)}, u32[]{:S(2)}, u32[]{:S(2)}) collective-permute-start(bf16[256,512]{1,0:T(8,128)(2,1)S(1)} %collective-permute-done.1.rest_4_), channel_id=1, source_target_pairs={{0,4},{4,0},{8,12},{12,8},{16,20},{20,16},{24,28},{28,24},{1,5},{5... | collective-permute-start | bytes 786440 | tf_op jit(solution)/shard_map/ppermute | solution.py:41
  67.4 7.9 %collective-permute-start.16 = (bf16[3,64,512]{2,1,0:T(8,128)(2,1)S(1)}, bf16[3,64,512]{2,1,0:T(8,128)(2,1)S(1)}, u32[]{:S(2)}, u32[]{:S(2)}) collective-permute-start(bf16[3,64,512]{2,1,0:T(8,128)(2,1)S(1)} %collective-permute-done.13.rest_3_), channel_id=1, source_target_pairs={{0,4},{4,0},{8,12},{12,8},{16,20},{20,16},{24,28},{28,24},{1,5},{5... | collective-permute-start | bytes 589832 | tf_op jit(solution)/shard_map/ppermute | solution.py:41
  74.8 6.0 %collective-permute-start.15 = (bf16[3,64,512]{2,1,0:T(8,128)(2,1)S(1)}, bf16[3,64,512]{2,1,0:T(8,128)(2,1)S(1)}, u32[]{:S(2)}, u32[]{:S(2)}) collective-permute-start(bf16[3,64,512]{2,1,0:T(8,128)(2,1)S(1)} %collective-permute-done.12.rest_2_), channel_id=1, source_target_pairs={{0,4},{4,0},{8,12},{12,8},{16,20},{20,16},{24,28},{28,24},{1,5},{5... | collective-permute-start | bytes 589832 | tf_op jit(solution)/shard_map/ppermute | solution.py:41
  75.4 9.0 %collective-permute-start.21 = (bf16[256,512]{1,0:T(8,128)(2,1)S(1)}, bf16[256,512]{1,0:T(8,128)(2,1)S(1)}, u32[]{:S(2)}, u32[]{:S(2)}) collective-permute-start(bf16[256,512]{1,0:T(8,128)(2,1)S(1)} %collective-permute-done.2.rest_5_), channel_id=1, source_target_pairs={{0,8},{4,12},{8,24},{12,28},{24,16},{28,20},{16,0},{20,4},{1,9},{5... | collective-permute-start | bytes 786440 | tf_op jit(solution)/shard_map/ppermute | solution.py:358
  80.8 6.5 %collective-permute-start.20 = (bf16[256,512]{1,0:T(8,128)(2,1)S(1)}, bf16[256,512]{1,0:T(8,128)(2,1)S(1)}, u32[]{:S(2)}, u32[]{:S(2)}) collective-permute-start(bf16[256,512]{1,0:T(8,128)(2,1)S(1)} %collective-permute-done.2.rest_5_), channel_id=1, source_target_pairs={{0,4},{4,0},{8,12},{12,8},{16,20},{20,16},{24,28},{28,24},{1,5},{5... | collective-permute-start | bytes 786440 | tf_op jit(solution)/shard_map/ppermute | solution.py:41
  82.8 11.9 %collective-permute-start.19 = (bf16[512,512]{1,0:T(8,128)(2,1)S(1)}, bf16[512,512]{1,0:T(8,128)(2,1)S(1)}, u32[]{:S(2)}, u32[]{:S(2)}) collective-permute-start(bf16[512,512]{1,0:T(8,128)(2,1)S(1)} %apply_fast.1.rest_0_), channel_id=1, source_target_pairs={{0,2},{1,3},{2,0},{3,1},{4,6},{5,7},{6,4},{7,5},{8,10},{9,11},{10,... | collective-permute-start | bytes 1572872 | tf_op jit(solution)/shard_map/ppermute | solution.py:41
  87.4 6.4 %collective-permute-start.22 = (bf16[256,512]{1,0:T(8,128)(2,1)S(1)}, bf16[256,512]{1,0:T(8,128)(2,1)S(1)}, u32[]{:S(2)}, u32[]{:S(2)}) collective-permute-start(bf16[256,512]{1,0:T(8,128)(2,1)S(1)} %collective-permute-done.21.rest_6_), channel_id=1, source_target_pairs={{0,4},{4,0},{8,12},{12,8},{16,20},{20,16},{24,28},{28,24},{1,5},{5... | collective-permute-start | bytes 786440 | tf_op jit(solution)/shard_map/ppermute | solution.py:41
  87.6 7.1 %collective-permute-start.18 = (bf16[512,512]{1,0:T(8,128)(2,1)S(1)}, bf16[512,512]{1,0:T(8,128)(2,1)S(1)}, u32[]{:S(2)}, u32[]{:S(2)}) collective-permute-start(bf16[512,512]{1,0:T(8,128)(2,1)S(1)} %apply_fast.1.rest_0_), channel_id=1, source_target_pairs={{0,1},{1,0},{2,3},{3,2},{4,5},{5,4},{6,7},{7,6},{8,9},{9,8},{10,11... | collective-permute-start | bytes 1572872 | tf_op jit(solution)/shard_map/ppermute | solution.py:41
  94.7 1.9 %collective-permute-start.23 = (bf16[512,512]{1,0:T(8,128)(2,1)S(1)}, bf16[512,512]{1,0:T(8,128)(2,1)S(1)}, u32[]{:S(2)}, u32[]{:S(2)}) collective-permute-start(bf16[512,512]{1,0:T(8,128)(2,1)S(1)} %collective-permute-done.19.rest_2_), channel_id=1, source_target_pairs={{0,1},{1,0},{2,3},{3,2},{4,5},{5,4},{6,7},{7,6},{8,9},{9,8},{10,11... | collective-permute-start | bytes 1572872 | tf_op jit(solution)/shard_map/ppermute | solution.py:41
  (1 other events, 1.0 us)

commit v14 on v11

--- a/solution.py
+++ b/solution.py
@@ -438,19 +438,19 @@
     far = [swap(renewed, "seq", 1)]
     wide_far = [crossed, swap(after(wide[1], near[1]), "seq", 1)]
     near[1] = after(near[1], far[0])
+    total = after(summed[0], near[1])
+    for piece in pieces:
+        total = total + piece.astype(jnp.float32)
+    moment = MOMENTUM_DECAY * momentum + total[None]
+    near[3] = after(near[3], moment)
     far += [swap(unit, "seq", 1) for unit in near[1:]]
     attended = window_attention(
         place, queries, keys, values, pair_keys, up_keys, after(crossed, near[1])
     )
     wide.append(ring_step(after(wide[2], far[1], near[2], near[3]), outer))
 
-    total = after(summed[0], near[1])
-    for piece in pieces:
-        total = total + piece.astype(jnp.float32)
-    moment = MOMENTUM_DECAY * momentum + total[None]
-
     forwarded = far[-1]
-    far[-1] = after(far[-1], attended, wide_far[1], moment)
+    far[-1] = after(far[-1], attended, wide_far[1])
     wide_far.append(swap(after(wide[2], forwarded), "seq", 1))
     wide_far.append(swap(after(wide[3], wide_far[2]), "seq", 1))
 

time: 98.1 us -> 98.1 us (level)
    ppermute x19, waiting for transfers between devices: 35.4 us -> 37.6 us  [swap(): return lax.ppermute(array, axis, [(i, i ^ mask) for i in range(devices)])]
    ppermute x3, waiting for transfers between devices: 7.53 us -> 6.11 us  [ring_step(): return lax.ppermute(unit, 'seq', pairs)]
  transfers between devices with their start and end apart: 24 -> 24, of which waited for: 16 -> 15; matrix products, arithmetic and copies ran while one was open for 2% -> 2% of each run, Pallas kernels for 12% -> 12%
where the time goes in v14:
time: 98.1 us; the launch traced here: 97.8 us
  waiting for transfers between devices  47.1 us (48%)
  starting transfers between devices  30.4 us (31%)
  Pallas kernels  15.3 us (16%)
  local copies, waits for them, and re-layouts  3.17 us (3%)
  other arithmetic  1.07 us (1%)
    ppermute x19, waiting for transfers between devices, swap(): return lax.ppermute(array, axis, [(i, i ^ mask) for i in range(devices)])  37.6 us
    ppermute x19, starting transfers between devices, swap(): return lax.ppermute(array, axis, [(i, i ^ mask) for i in range(devices)])  21.4 us
    ppermute x3, waiting for transfers between devices, ring_step(): return lax.ppermute(unit, 'seq', pairs)  6.11 us
    ppermute x3, starting transfers between devices, ring_step(): return lax.ppermute(unit, 'seq', pairs)  4.68 us
    ppermute x1, starting transfers between devices, shards(): lax.ppermute(up_keys, 'seq', [(s, s + 2) for s in range(0, ranks - 2, 2)])  3.65 us
    pallas_call x2, Pallas kernels, keys_part(): pl.pallas_call(functools.partial(keys_kernel, outer), out_shape=[jax.Shap...  3.49 us
    ppermute x1, waiting for transfers between devices, shards(): lax.ppermute(up_keys, 'seq', [(s, s + 2) for s in range(0, ranks - 2, 2)])  3.31 us
    unnamed x18, local copies, waits for them, and re-layouts  2.48 us
  transfers between devices with their start and end apart: 24, of which 15 were waited for; matrix products, arithmetic and copies ran while one was open for 2% of the time, Pallas kernels for 12%

profile of v14, /device:TPU:0, one launch (start us, length us, event | category | flops | bytes accessed | tf_op | source)
XLA Modules:
  0.0 97.8 jit_solution(8950517811970678599)
XLA Ops:
  0.6 3.1 %collective-permute-start.1 = (bf16[256,512]{1,0:T(8,128)(2,1)}, bf16[256,512]{1,0:T(8,128)(2,1)S(1)}, u32[]{:S(2)}, u32[]{:S(2)}) collective-permute-start(bf16[256,512]{1,0:T(8,128)(2,1)} %rest_3_.1), channel_id=1, source_target_pairs={{0,8},{4,12},{8,24},{12,28},{24,16},{28,20},{16,0},{20,4},{1,9},{5... | collective-permute-start | bytes 786440 | tf_op jit(solution)/shard_map/ppermute | solution.py:358
  3.7 1.5 %collective-permute-start = (bf16[512,512]{1,0:T(8,128)(2,1)}, bf16[512,512]{1,0:T(8,128)(2,1)S(1)}, u32[]{:S(2)}, u32[]{:S(2)}) collective-permute-start(bf16[512,512]{1,0:T(8,128)(2,1)} %k.5), channel_id=1, source_target_pairs={{0,4},{4,0},{8,12},{12,8},{16,20},{20,16},{24,28},{28,24},{1,5},{5... | collective-permute-start | bytes 1572872 | tf_op jit(solution)/shard_map/ppermute | solution.py:41
  5.9 1.4 %copy-done = bf16[1,3,512,512]{3,2,1,0:T(8,128)(2,1)S(1)} copy-done((bf16[1,3,512,512]{3,2,1,0:T(8,128)(2,1)S(1)}, bf16[1,3,512,512]{3,2,1,0:T(8,128)(2,1)}, u32[]{:S(2)}) %copy-start) | copy-done | bytes 1572888
  8.4 1.7 %keys_part.2 = (bf16[512,512]{1,0:T(8,128)(2,1)S(1)}, f32[256,512]{1,0:T(8,128)S(1)}, f32[256,512]{1,0:T(8,128)S(1)}, bf16[256,512]{1,0:T(8,128)(2,1)S(1)}) custom-call(s32[12]{0:T(128)S(1)} %dynamic-slice_bitcast_fusion.place, bf16[512,512]{1,0:T(8,128)(2,1)S(1)} %copy-done.2, bf16[1,3,512,512]{3,2,1,0:T(8,128)(2,1)S(1)} %copy-done), custom_call_target="tpu_custom_call" | custom-call | flops 1 | bytes 1 | tf_op jit(solution)/shard_map/keys_part/pallas_call | solution.py:82
  10.1 1.1 %collective-permute-done.1.rest_4_ = bf16[256,512]{1,0:T(8,128)(2,1)S(1)} collective-permute-done((bf16[256,512]{1,0:T(8,128)(2,1)}, bf16[256,512]{1,0:T(8,128)(2,1)S(1)}, u32[]{:S(2)}, u32[]{:S(2)}) %collective-permute-start.1) | collective-permute-done | bytes 262176 | tf_op jit(solution)/shard_map/ppermute | solution.py:358
  11.2 1.5 %collective-permute-start.2 = (bf16[256,512]{1,0:T(8,128)(2,1)S(1)}, bf16[256,512]{1,0:T(8,128)(2,1)S(1)}, u32[]{:S(2)}, u32[]{:S(2)}) collective-permute-start(bf16[256,512]{1,0:T(8,128)(2,1)S(1)} %collective-permute-done.1.rest_4_), channel_id=1, source_target_pairs={{0,8},{4,12},{8,24},{12,28},{24,16},{28,20},{16,0},{20,4},{1,9},{5... | collective-permute-start | bytes 786440 | tf_op jit(solution)/shard_map/ppermute | solution.py:358
  14.6 5.0 %collective-permute-done.2.rest_5_ = bf16[256,512]{1,0:T(8,128)(2,1)S(1)} collective-permute-done((bf16[256,512]{1,0:T(8,128)(2,1)S(1)}, bf16[256,512]{1,0:T(8,128)(2,1)S(1)}, u32[]{:S(2)}, u32[]{:S(2)}) %collective-permute-start.2) | collective-permute-done | bytes 262176 | tf_op jit(solution)/shard_map/ppermute | solution.py:358
  19.6 3.6 %collective-permute-start.3 = (bf16[512,512]{1,0:T(8,128)(2,1)S(1)}, bf16[512,512]{1,0:T(8,128)(2,1)S(1)}, u32[]{:S(2)}, u32[]{:S(2)}) collective-permute-start(bf16[512,512]{1,0:T(8,128)(2,1)S(1)} %collective-permute-done.k.pair_k), channel_id=1, source_target_pairs={{0,8},{8,16},{16,24},{1,9},{9,17},{17,25},{2,10},{10,18},{18,26},{... | collective-permute-start | bytes 1572872 | tf_op jit(solution)/shard_map/ppermute | solution.py:423
  23.3 1.7 %own_gradients.1.acc = f32[3,256,512]{2,1,0:T(8,128)S(1)} custom-call(s32[12]{0:T(128)S(1)} %dynamic-slice_bitcast_fusion.place, bf16[512,512]{1,0:T(8,128)(2,1)S(1)} %copy-done.3, bf16[512,512]{1,0:T(8,128)(2,1)S(1)} %multiply_convert_fusion.e, bf16[512,512]{1,0:T(8,128)(2,1)S(1)} %get-tuple-element.32.gated, f32[256,512]{1,0:T(8,128)S(1)} %get-tuple-element.41.gate, ...), custom_call_target="tpu_custom_call" | custom-call | flops 1 | bytes 1 | tf_op jit(solution)/shard_map/own_gradients/pallas_call | solution.py:144
  25.1 1.7 %keys_part.3 = (bf16[512,512]{1,0:T(8,128)(2,1)S(1)}, f32[256,512]{1,0:T(8,128)S(1)}, f32[256,512]{1,0:T(8,128)S(1)}, bf16[256,512]{1,0:T(8,128)(2,1)S(1)}) custom-call(s32[12]{0:T(128)S(1)} %dynamic-slice_bitcast_fusion.place, bf16[512,512]{1,0:T(8,128)(2,1)S(1)} %collective-permute-done.k.pair_k, bf16[1,3,512,512]{3,2,1,0:T(8,128)(2,1)S(1)} %copy-done.1), custom_call_target="tpu_custom_call" | custom-call | flops 1 | bytes 1 | tf_op jit(solution)/shard_map/keys_part/pallas_call | solution.py:82
  27.5 1.1 %collective-permute-done.5.e = bf16[512,512]{1,0:T(8,128)(2,1)S(1)} collective-permute-done((bf16[512,512]{1,0:T(8,128)(2,1)S(1)}, bf16[512,512]{1,0:T(8,128)(2,1)S(1)}, u32[]{:S(2)}, u32[]{:S(2)}) %collective-permute-start.5) | collective-permute-done | bytes 524320 | tf_op jit(solution)/shard_map/ppermute | solution.py:41
  28.5 3.3 %collective-permute-done.3.up_k = bf16[512,512]{1,0:T(8,128)(2,1)S(1)} collective-permute-done((bf16[512,512]{1,0:T(8,128)(2,1)S(1)}, bf16[512,512]{1,0:T(8,128)(2,1)S(1)}, u32[]{:S(2)}, u32[]{:S(2)}) %collective-permute-start.3) | collective-permute-done | bytes 524320 | tf_op jit(solution)/shard_map/ppermute | solution.py:423
  31.9 1.8 %both_gradients.1 = (f32[3,64,512]{2,1,0:T(8,128)S(1)}, bf16[3,64,512]{2,1,0:T(8,128)(2,1)S(1)}, bf16[3,64,512]{2,1,0:T(8,128)(2,1)S(1)}, bf16[3,64,512]{2,1,0:T(8,128)(2,1)S(1)}) custom-call(s32[12]{0:T(128)S(1)} %dynamic-slice_bitcast_fusion.place, bf16[512,512]{1,0:T(8,128)(2,1)S(1)} %collective-permute-done.k.pair_k, ...), custom_call_target="tpu_custom_call" | custom-call | flops 1 | bytes 1 | tf_op jit(solution)/shard_map/both_gradients/pallas_call | solution.py:159
  33.7 5.0 %collective-permute-start.9 = (bf16[3,64,512]{2,1,0:T(8,128)(2,1)S(1)}, bf16[3,64,512]{2,1,0:T(8,128)(2,1)S(1)}, u32[]{:S(2)}, u32[]{:S(2)}) collective-permute-start(bf16[3,64,512]{2,1,0:T(8,128)(2,1)S(1)} %get-tuple-element.48), channel_id=1, source_target_pairs={{0,24},{4,28},{8,16},{12,20},{16,8},{20,12},{24,0},{28,4},{1,25},{... | collective-permute-start | bytes 589832 | tf_op jit(solution)/shard_map/ppermute | solution.py:41
  39.3 5.2 %collective-permute-done.9.rest_2_ = bf16[3,64,512]{2,1,0:T(8,128)(2,1)S(1)} collective-permute-done((bf16[3,64,512]{2,1,0:T(8,128)(2,1)S(1)}, bf16[3,64,512]{2,1,0:T(8,128)(2,1)S(1)}, u32[]{:S(2)}, u32[]{:S(2)}) %collective-permute-start.9) | collective-permute-done | bytes 196640 | tf_op jit(solution)/shard_map/ppermute | solution.py:41
  44.5 5.0 %collective-permute-done.6.early_v.rest_7_ = bf16[768,512]{1,0:T(8,128)(2,1)S(1)} collective-permute-done((bf16[768,512]{1,0:T(8,128)(2,1)S(1)}, bf16[768,512]{1,0:T(8,128)(2,1)S(1)}, u32[]{:S(2)}, u32[]{:S(2)}) %collective-permute-start.6) | collective-permute-done | bytes 786464 | tf_op jit(solution)/shard_map/ppermute | solution.py:41
  49.5 4.2 %collective-permute-done.8.rest_1_ = bf16[3,64,512]{2,1,0:T(8,128)(2,1)S(1)} collective-permute-done((bf16[3,64,512]{2,1,0:T(8,128)(2,1)S(1)}, bf16[3,64,512]{2,1,0:T(8,128)(2,1)S(1)}, u32[]{:S(2)}, u32[]{:S(2)}) %collective-permute-start.8) | collective-permute-done | bytes 196640 | tf_op jit(solution)/shard_map/ppermute | solution.py:41
  55.6 3.1 %collective-permute-start.13 = (bf16[3,64,512]{2,1,0:T(8,128)(2,1)S(1)}, bf16[3,64,512]{2,1,0:T(8,128)(2,1)S(1)}, u32[]{:S(2)}, u32[]{:S(2)}) collective-permute-start(bf16[3,64,512]{2,1,0:T(8,128)(2,1)S(1)} %renew.1.rest_0_), channel_id=1, source_target_pairs={{0,24},{4,28},{8,16},{12,20},{16,8},{20,12},{24,0},{28,4},{1,25},{... | collective-permute-start | bytes 589832 | tf_op jit(solution)/shard_map/ppermute | solution.py:41
  59.2 3.0 %collective-permute-done.10.rest_1_ = bf16[3,64,512]{2,1,0:T(8,128)(2,1)S(1)} collective-permute-done((bf16[3,64,512]{2,1,0:T(8,128)(2,1)S(1)}, bf16[3,64,512]{2,1,0:T(8,128)(2,1)S(1)}, u32[]{:S(2)}, u32[]{:S(2)}) %collective-permute-start.10) | collective-permute-done | bytes 196640 | tf_op jit(solution)/shard_map/ppermute | solution.py:41
  62.2 2.0 %collective-permute-start.17 = (bf16[256,512]{1,0:T(8,128)(2,1)S(1)}, bf16[256,512]{1,0:T(8,128)(2,1)S(1)}, u32[]{:S(2)}, u32[]{:S(2)}) collective-permute-start(bf16[256,512]{1,0:T(8,128)(2,1)S(1)} %collective-permute-done.1.rest_4_), channel_id=1, source_target_pairs={{0,4},{4,0},{8,12},{12,8},{16,20},{20,16},{24,28},{28,24},{1,5},{5... | collective-permute-start | bytes 786440 | tf_op jit(solution)/shard_map/ppermute | solution.py:41
  65.1 1.3 %collective-permute-done.13.rest_3_ = bf16[3,64,512]{2,1,0:T(8,128)(2,1)S(1)} collective-permute-done((bf16[3,64,512]{2,1,0:T(8,128)(2,1)S(1)}, bf16[3,64,512]{2,1,0:T(8,128)(2,1)S(1)}, u32[]{:S(2)}, u32[]{:S(2)}) %collective-permute-start.13) | collective-permute-done | bytes 196640 | tf_op jit(solution)/shard_map/ppermute | solution.py:41
  66.4 2.2 %collective-permute-start.16 = (bf16[3,64,512]{2,1,0:T(8,128)(2,1)S(1)}, bf16[3,64,512]{2,1,0:T(8,128)(2,1)S(1)}, u32[]{:S(2)}, u32[]{:S(2)}) collective-permute-start(bf16[3,64,512]{2,1,0:T(8,128)(2,1)S(1)} %collective-permute-done.13.rest_3_), channel_id=1, source_target_pairs={{0,4},{4,0},{8,12},{12,8},{16,20},{20,16},{24,28},{28,24},{1,5},{5... | collective-permute-start | bytes 589832 | tf_op jit(solution)/shard_map/ppermute | solution.py:41
  68.6 6.2 %collective-permute-done.12.rest_2_ = bf16[3,64,512]{2,1,0:T(8,128)(2,1)S(1)} collective-permute-done((bf16[3,64,512]{2,1,0:T(8,128)(2,1)S(1)}, bf16[3,64,512]{2,1,0:T(8,128)(2,1)S(1)}, u32[]{:S(2)}, u32[]{:S(2)}) %collective-permute-start.12) | collective-permute-done | bytes 196640 | tf_op jit(solution)/shard_map/ppermute | solution.py:41
  75.4 2.3 %window_attention.1.attended = f32[512,512]{1,0:T(8,128)S(1)} custom-call(s32[12]{0:T(128)S(1)} %dynamic-slice_bitcast_fusion.place, bf16[512,512]{1,0:T(8,128)(2,1)S(1)} %copy-done.5, bf16[512,512]{1,0:T(8,128)(2,1)S(1)} %copy-done.3, bf16[512,512]{1,0:T(8,128)(2,1)S(1)} %copy-done.4, bf16[512,512]{1,0:T(8,128)(2,1)S(1)} %collective-permute-done.k.pair_k, ...), custom_call_target="tpu_custom_call" | custom-call | flops 1 | bytes 1 | tf_op jit(solution)/shard_map/window_attention/pallas_call | solution.py:201
  77.7 1.6 %collective-permute-start.20 = (bf16[256,512]{1,0:T(8,128)(2,1)S(1)}, bf16[256,512]{1,0:T(8,128)(2,1)S(1)}, u32[]{:S(2)}, u32[]{:S(2)}) collective-permute-start(bf16[256,512]{1,0:T(8,128)(2,1)S(1)} %collective-permute-done.2.rest_5_), channel_id=1, source_target_pairs={{0,4},{4,0},{8,12},{12,8},{16,20},{20,16},{24,28},{28,24},{1,5},{5... | collective-permute-start | bytes 786440 | tf_op jit(solution)/shard_map/ppermute | solution.py:41
  79.3 3.3 %collective-permute-done.15.rest_6_ = bf16[3,64,512]{2,1,0:T(8,128)(2,1)S(1)} collective-permute-done((bf16[3,64,512]{2,1,0:T(8,128)(2,1)S(1)}, bf16[3,64,512]{2,1,0:T(8,128)(2,1)S(1)}, u32[]{:S(2)}, u32[]{:S(2)}) %collective-permute-start.15) | collective-permute-done | bytes 196640 | tf_op jit(solution)/shard_map/ppermute | solution.py:41
  82.6 1.7 %apply_fast.1.rest_0_ = bf16[512,512]{1,0:T(8,128)(2,1)S(1)} custom-call(s32[12]{0:T(128)S(1)} %dynamic-slice_bitcast_fusion.place, bf16[512,512]{1,0:T(8,128)(2,1)S(1)} %copy-done.5, f32[512,512]{1,0:T(8,128)S(1)} %window_attention.1.attended, bf16[3,64,512]{2,1,0:T(8,128)(2,1)S(1)} %renew.1.rest_0_, ...), custom_call_target="tpu_custom_call" | custom-call | flops 1 | bytes 1 | tf_op jit(solution)/shard_map/apply_fast/pallas_call | solution.py:280
  84.3 1.6 %collective-permute-start.19 = (bf16[512,512]{1,0:T(8,128)(2,1)S(1)}, bf16[512,512]{1,0:T(8,128)(2,1)S(1)}, u32[]{:S(2)}, u32[]{:S(2)}) collective-permute-start(bf16[512,512]{1,0:T(8,128)(2,1)S(1)} %apply_fast.1.rest_0_), channel_id=1, source_target_pairs={{0,2},{1,3},{2,0},{3,1},{4,6},{5,7},{6,4},{7,5},{8,10},{9,11},{10,... | collective-permute-start | bytes 1572872 | tf_op jit(solution)/shard_map/ppermute | solution.py:41
  87.3 5.7 %collective-permute-done.22.rest_10_ = bf16[256,512]{1,0:T(8,128)(2,1)S(1)} collective-permute-done((bf16[256,512]{1,0:T(8,128)(2,1)S(1)}, bf16[256,512]{1,0:T(8,128)(2,1)S(1)}, u32[]{:S(2)}, u32[]{:S(2)}) %collective-permute-start.22) | collective-permute-done | bytes 262176 | tf_op jit(solution)/shard_map/ppermute | solution.py:41
  93.0 1.7 %collective-permute-done.19.rest_2_ = bf16[512,512]{1,0:T(8,128)(2,1)S(1)} collective-permute-done((bf16[512,512]{1,0:T(8,128)(2,1)S(1)}, bf16[512,512]{1,0:T(8,128)(2,1)S(1)}, u32[]{:S(2)}, u32[]{:S(2)}) %collective-permute-start.19) | collective-permute-done | bytes 524320 | tf_op jit(solution)/shard_map/ppermute | solution.py:41
  94.7 1.7 %project_most.1 = (f32[512,512]{1,0:T(8,128)S(1)}, bf16[512,512]{1,0:T(8,128)(2,1)S(1)}) custom-call(s32[12]{0:T(128)S(1)} %dynamic-slice_bitcast_fusion.place, bf16[512,512]{1,0:T(8,128)(2,1)S(1)} %apply_fast.1.rest_0_, bf16[512,512]{1,0:T(8,128)(2,1)S(1)} %collective-permute-done.18.rest_1_, bf16[512,512]{1,0:T(8,128)(2,1)S(1)} %collective-permute-done.19.rest_2_, ...), custom_call_target="tpu_custom_call" | custom-call | flops 1 | bytes 1 | tf_op jit(solution)/shard_map/project_most/pallas_call | solution.py:316
  96.6 1.2 %project_last.1 = bf16[512,512]{1,0:T(8,128)(2,1)} custom-call(f32[512,512]{1,0:T(8,128)S(1)} %get-tuple-element.60.partial, bf16[512,512]{1,0:T(8,128)(2,1)S(1)} %collective-permute-done.23.block, bf16[512,512]{1,0:T(8,128)(2,1)S(1)} %get-tuple-element.61.rows), custom_call_target="tpu_custom_call" | custom-call | flops 1 | bytes 1 | tf_op jit(solution)/shard_map/project_last/pallas_call | solution.py:337
  (48 shorter events, 10.4 us)
Async XLA Ops:
  0.6 12.2 %copy-start.8 = (f32[512,1]{0,1:T(1,128)S(1)}, f32[512,1]{0,1:T(1,128)}, u32[]{:S(2)}) copy-start(f32[512,1]{0,1:T(1,128)} %param.11) | copy-start | bytes 6148
  0.6 10.6 %collective-permute-start.1 = (bf16[256,512]{1,0:T(8,128)(2,1)}, bf16[256,512]{1,0:T(8,128)(2,1)S(1)}, u32[]{:S(2)}, u32[]{:S(2)}) collective-permute-start(bf16[256,512]{1,0:T(8,128)(2,1)} %rest_3_.1), channel_id=1, source_target_pairs={{0,8},{4,12},{8,24},{12,28},{24,16},{28,20},{16,0},{20,4},{1,9},{5... | collective-permute-start | bytes 786440 | tf_op jit(solution)/shard_map/ppermute | solution.py:358
  3.7 15.9 %collective-permute-start = (bf16[512,512]{1,0:T(8,128)(2,1)}, bf16[512,512]{1,0:T(8,128)(2,1)S(1)}, u32[]{:S(2)}, u32[]{:S(2)}) collective-permute-start(bf16[512,512]{1,0:T(8,128)(2,1)} %k.5), channel_id=1, source_target_pairs={{0,4},{4,0},{8,12},{12,8},{16,20},{20,16},{24,28},{28,24},{1,5},{5... | collective-permute-start | bytes 1572872 | tf_op jit(solution)/shard_map/ppermute | solution.py:41
  5.9 1.4 %copy-start = (bf16[1,3,512,512]{3,2,1,0:T(8,128)(2,1)S(1)}, bf16[1,3,512,512]{3,2,1,0:T(8,128)(2,1)}, u32[]{:S(2)}) copy-start(bf16[1,3,512,512]{3,2,1,0:T(8,128)(2,1)} %w.5) | copy-start | bytes 4718596
  8.4 4.4 %copy-start.4 = (bf16[512,512]{1,0:T(8,128)(2,1)S(1)}, bf16[512,512]{1,0:T(8,128)(2,1)}, u32[]{:S(2)}) copy-start(bf16[512,512]{1,0:T(8,128)(2,1)} %v.1) | copy-start | bytes 1572868
  8.4 14.9 %copy-start.3 = (bf16[512,512]{1,0:T(8,128)(2,1)S(1)}, bf16[512,512]{1,0:T(8,128)(2,1)}, u32[]{:S(2)}) copy-start(bf16[512,512]{1,0:T(8,128)(2,1)} %k.5) | copy-start | bytes 1572868
  11.2 8.4 %collective-permute-start.2 = (bf16[256,512]{1,0:T(8,128)(2,1)S(1)}, bf16[256,512]{1,0:T(8,128)(2,1)S(1)}, u32[]{:S(2)}, u32[]{:S(2)}) collective-permute-start(bf16[256,512]{1,0:T(8,128)(2,1)S(1)} %collective-permute-done.1.rest_4_), channel_id=1, source_target_pairs={{0,8},{4,12},{8,24},{12,28},{24,16},{28,20},{16,0},{20,4},{1,9},{5... | collective-permute-start | bytes 786440 | tf_op jit(solution)/shard_map/ppermute | solution.py:358
  13.0 15.6 %collective-permute-start.5 = (bf16[512,512]{1,0:T(8,128)(2,1)S(1)}, bf16[512,512]{1,0:T(8,128)(2,1)S(1)}, u32[]{:S(2)}, u32[]{:S(2)}) collective-permute-start(bf16[512,512]{1,0:T(8,128)(2,1)S(1)} %multiply_convert_fusion.e), channel_id=1, source_target_pairs={{0,4},{4,0},{8,12},{12,8},{16,20},{20,16},{24,28},{28,24},{1,5},{5... | collective-permute-start | bytes 1572872 | tf_op jit(solution)/shard_map/ppermute | solution.py:41
  14.0 12.9 %collective-permute-start.4 = (bf16[512,512]{1,0:T(8,128)(2,1)S(1)}, bf16[512,512]{1,0:T(8,128)(2,1)S(1)}, u32[]{:S(2)}, u32[]{:S(2)}) collective-permute-start(bf16[512,512]{1,0:T(8,128)(2,1)S(1)} %copy-done.4), channel_id=1, source_target_pairs={{4,12},{12,20},{20,28},{5,13},{13,21},{21,29},{6,14},{14,22},{22,3... | collective-permute-start | bytes 1572872 | tf_op jit(solution)/shard_map/ppermute | solution.py:421
  19.6 12.2 %collective-permute-start.3 = (bf16[512,512]{1,0:T(8,128)(2,1)S(1)}, bf16[512,512]{1,0:T(8,128)(2,1)S(1)}, u32[]{:S(2)}, u32[]{:S(2)}) collective-permute-start(bf16[512,512]{1,0:T(8,128)(2,1)S(1)} %collective-permute-done.k.pair_k), channel_id=1, source_target_pairs={{0,8},{8,16},{16,24},{1,9},{9,17},{17,25},{2,10},{10,18},{18,26},{... | collective-permute-start | bytes 1572872 | tf_op jit(solution)/shard_map/ppermute | solution.py:423
  23.3 1.7 %copy-start.1 = (bf16[1,3,512,512]{3,2,1,0:T(8,128)(2,1)S(1)}, bf16[1,3,512,512]{3,2,1,0:T(8,128)(2,1)}, u32[]{:S(2)}) copy-start(bf16[1,3,512,512]{3,2,1,0:T(8,128)(2,1)} %w.5) | copy-start | bytes 4718596
  25.1 1.8 %copy-start.7 = (bf16[256,512]{1,0:T(8,128)(2,1)S(1)}, bf16[256,512]{1,0:T(8,128)(2,1)}, u32[]{:S(2)}) copy-start(bf16[256,512]{1,0:T(8,128)(2,1)} %rest_3_.1) | copy-start | bytes 786436
  31.9 21.9 %copy-start.6 = (f32[1,3,64,512]{3,2,1,0:T(8,128)S(1)}, f32[1,3,64,512]{3,2,1,0:T(8,128)}, u32[]{:S(2)}) copy-start(f32[1,3,64,512]{3,2,1,0:T(8,128)} %momentum.1) | copy-start | bytes 1179652
  33.6 15.9 %collective-permute-start.6 = (bf16[768,512]{1,0:T(8,128)(2,1)S(1)}, bf16[768,512]{1,0:T(8,128)(2,1)S(1)}, u32[]{:S(2)}, u32[]{:S(2)}) collective-permute-start(bf16[768,512]{1,0:T(8,128)(2,1)S(1)} %crossing.1), channel_id=1, source_target_pairs={{0,4},{4,0},{8,12},{12,8},{16,20},{20,16},{24,28},{28,24},{1,5},{5... | collective-permute-start | bytes 2359304 | tf_op jit(solution)/shard_map/ppermute | solution.py:41
  33.7 10.8 %collective-permute-start.9 = (bf16[3,64,512]{2,1,0:T(8,128)(2,1)S(1)}, bf16[3,64,512]{2,1,0:T(8,128)(2,1)S(1)}, u32[]{:S(2)}, u32[]{:S(2)}) collective-permute-start(bf16[3,64,512]{2,1,0:T(8,128)(2,1)S(1)} %get-tuple-element.48), channel_id=1, source_target_pairs={{0,24},{4,28},{8,16},{12,20},{16,8},{20,12},{24,0},{28,4},{1,25},{... | collective-permute-start | bytes 589832 | tf_op jit(solution)/shard_map/ppermute | solution.py:41
  38.7 10.8 %collective-permute-start.7 = (bf16[3,64,512]{2,1,0:T(8,128)(2,1)S(1)}, bf16[3,64,512]{2,1,0:T(8,128)(2,1)S(1)}, u32[]{:S(2)}, u32[]{:S(2)}) collective-permute-start(bf16[3,64,512]{2,1,0:T(8,128)(2,1)S(1)} %get-tuple-element.44), channel_id=1, source_target_pairs={{0,8},{4,12},{8,0},{12,4},{16,24},{20,28},{24,16},{28,20},{1,9},{5... | collective-permute-start | bytes 589832 | tf_op jit(solution)/shard_map/ppermute | solution.py:41
  38.7 15.0 %collective-permute-start.8 = (bf16[3,64,512]{2,1,0:T(8,128)(2,1)S(1)}, bf16[3,64,512]{2,1,0:T(8,128)(2,1)S(1)}, u32[]{:S(2)}, u32[]{:S(2)}) collective-permute-start(bf16[3,64,512]{2,1,0:T(8,128)(2,1)S(1)} %get-tuple-element.47), channel_id=1, source_target_pairs={{0,16},{4,20},{8,24},{12,28},{16,0},{20,4},{24,8},{28,12},{1,17},{... | collective-permute-start | bytes 589832 | tf_op jit(solution)/shard_map/ppermute | solution.py:41
  54.6 20.8 %copy-start.5 = (bf16[512,512]{1,0:T(8,128)(2,1)S(1)}, bf16[512,512]{1,0:T(8,128)(2,1)}, u32[]{:S(2)}) copy-start(bf16[512,512]{1,0:T(8,128)(2,1)} %q.3) | copy-start | bytes 1572868
  54.6 7.6 %collective-permute-start.10 = (bf16[3,64,512]{2,1,0:T(8,128)(2,1)S(1)}, bf16[3,64,512]{2,1,0:T(8,128)(2,1)S(1)}, u32[]{:S(2)}, u32[]{:S(2)}) collective-permute-start(bf16[3,64,512]{2,1,0:T(8,128)(2,1)S(1)} %renew.1.rest_0_), channel_id=1, source_target_pairs={{0,8},{4,12},{8,0},{12,4},{16,24},{20,28},{24,16},{28,20},{1,9},{5... | collective-permute-start | bytes 589832 | tf_op jit(solution)/shard_map/ppermute | solution.py:41
  54.7 7.5 %collective-permute-start.11 = (bf16[3,64,512]{2,1,0:T(8,128)(2,1)S(1)}, bf16[3,64,512]{2,1,0:T(8,128)(2,1)S(1)}, u32[]{:S(2)}, u32[]{:S(2)}) collective-permute-start(bf16[3,64,512]{2,1,0:T(8,128)(2,1)S(1)} %renew.1.rest_0_), channel_id=1, source_target_pairs={{0,4},{4,0},{8,12},{12,8},{16,20},{20,16},{24,28},{28,24},{1,5},{5... | collective-permute-start | bytes 589832 | tf_op jit(solution)/shard_map/ppermute | solution.py:41
  55.6 10.9 %collective-permute-start.13 = (bf16[3,64,512]{2,1,0:T(8,128)(2,1)S(1)}, bf16[3,64,512]{2,1,0:T(8,128)(2,1)S(1)}, u32[]{:S(2)}, u32[]{:S(2)}) collective-permute-start(bf16[3,64,512]{2,1,0:T(8,128)(2,1)S(1)} %renew.1.rest_0_), channel_id=1, source_target_pairs={{0,24},{4,28},{8,16},{12,20},{16,8},{20,12},{24,0},{28,4},{1,25},{... | collective-permute-start | bytes 589832 | tf_op jit(solution)/shard_map/ppermute | solution.py:41
  58.7 16.1 %collective-permute-start.12 = (bf16[3,64,512]{2,1,0:T(8,128)(2,1)S(1)}, bf16[3,64,512]{2,1,0:T(8,128)(2,1)S(1)}, u32[]{:S(2)}, u32[]{:S(2)}) collective-permute-start(bf16[3,64,512]{2,1,0:T(8,128)(2,1)S(1)} %renew.1.rest_0_), channel_id=1, source_target_pairs={{0,16},{4,20},{8,24},{12,28},{16,0},{20,4},{24,8},{28,12},{1,17},{... | collective-permute-start | bytes 589832 | tf_op jit(solution)/shard_map/ppermute | solution.py:41
  62.2 15.5 %collective-permute-start.14 = (bf16[3,64,512]{2,1,0:T(8,128)(2,1)S(1)}, bf16[3,64,512]{2,1,0:T(8,128)(2,1)S(1)}, u32[]{:S(2)}, u32[]{:S(2)}) collective-permute-start(bf16[3,64,512]{2,1,0:T(8,128)(2,1)S(1)} %collective-permute-done.10.rest_1_), channel_id=1, source_target_pairs={{0,4},{4,0},{8,12},{12,8},{16,20},{20,16},{24,28},{28,24},{1,5},{5... | collective-permute-start | bytes 589832 | tf_op jit(solution)/shard_map/ppermute | solution.py:41
  62.2 17.1 %collective-permute-start.17 = (bf16[256,512]{1,0:T(8,128)(2,1)S(1)}, bf16[256,512]{1,0:T(8,128)(2,1)S(1)}, u32[]{:S(2)}, u32[]{:S(2)}) collective-permute-start(bf16[256,512]{1,0:T(8,128)(2,1)S(1)} %collective-permute-done.1.rest_4_), channel_id=1, source_target_pairs={{0,4},{4,0},{8,12},{12,8},{16,20},{20,16},{24,28},{28,24},{1,5},{5... | collective-permute-start | bytes 786440 | tf_op jit(solution)/shard_map/ppermute | solution.py:41
  66.4 11.3 %collective-permute-start.16 = (bf16[3,64,512]{2,1,0:T(8,128)(2,1)S(1)}, bf16[3,64,512]{2,1,0:T(8,128)(2,1)S(1)}, u32[]{:S(2)}, u32[]{:S(2)}) collective-permute-start(bf16[3,64,512]{2,1,0:T(8,128)(2,1)S(1)} %collective-permute-done.13.rest_3_), channel_id=1, source_target_pairs={{0,4},{4,0},{8,12},{12,8},{16,20},{20,16},{24,28},{28,24},{1,5},{5... | collective-permute-start | bytes 589832 | tf_op jit(solution)/shard_map/ppermute | solution.py:41
  74.8 7.8 %collective-permute-start.15 = (bf16[3,64,512]{2,1,0:T(8,128)(2,1)S(1)}, bf16[3,64,512]{2,1,0:T(8,128)(2,1)S(1)}, u32[]{:S(2)}, u32[]{:S(2)}) collective-permute-start(bf16[3,64,512]{2,1,0:T(8,128)(2,1)S(1)} %collective-permute-done.12.rest_2_), channel_id=1, source_target_pairs={{0,4},{4,0},{8,12},{12,8},{16,20},{20,16},{24,28},{28,24},{1,5},{5... | collective-permute-start | bytes 589832 | tf_op jit(solution)/shard_map/ppermute | solution.py:41
  77.7 8.2 %collective-permute-start.21 = (bf16[256,512]{1,0:T(8,128)(2,1)S(1)}, bf16[256,512]{1,0:T(8,128)(2,1)S(1)}, u32[]{:S(2)}, u32[]{:S(2)}) collective-permute-start(bf16[256,512]{1,0:T(8,128)(2,1)S(1)} %collective-permute-done.2.rest_5_), channel_id=1, source_target_pairs={{0,8},{4,12},{8,24},{12,28},{24,16},{28,20},{16,0},{20,4},{1,9},{5... | collective-permute-start | bytes 786440 | tf_op jit(solution)/shard_map/ppermute | solution.py:358
  77.7 8.7 %collective-permute-start.20 = (bf16[256,512]{1,0:T(8,128)(2,1)S(1)}, bf16[256,512]{1,0:T(8,128)(2,1)S(1)}, u32[]{:S(2)}, u32[]{:S(2)}) collective-permute-start(bf16[256,512]{1,0:T(8,128)(2,1)S(1)} %collective-permute-done.2.rest_5_), channel_id=1, source_target_pairs={{0,4},{4,0},{8,12},{12,8},{16,20},{20,16},{24,28},{28,24},{1,5},{5... | collective-permute-start | bytes 786440 | tf_op jit(solution)/shard_map/ppermute | solution.py:41
  84.3 10.4 %collective-permute-start.19 = (bf16[512,512]{1,0:T(8,128)(2,1)S(1)}, bf16[512,512]{1,0:T(8,128)(2,1)S(1)}, u32[]{:S(2)}, u32[]{:S(2)}) collective-permute-start(bf16[512,512]{1,0:T(8,128)(2,1)S(1)} %apply_fast.1.rest_0_), channel_id=1, source_target_pairs={{0,2},{1,3},{2,0},{3,1},{4,6},{5,7},{6,4},{7,5},{8,10},{9,11},{10,... | collective-permute-start | bytes 1572872 | tf_op jit(solution)/shard_map/ppermute | solution.py:41
  86.5 6.5 %collective-permute-start.22 = (bf16[256,512]{1,0:T(8,128)(2,1)S(1)}, bf16[256,512]{1,0:T(8,128)(2,1)S(1)}, u32[]{:S(2)}, u32[]{:S(2)}) collective-permute-start(bf16[256,512]{1,0:T(8,128)(2,1)S(1)} %collective-permute-done.21.rest_6_), channel_id=1, source_target_pairs={{0,4},{4,0},{8,12},{12,8},{16,20},{20,16},{24,28},{28,24},{1,5},{5... | collective-permute-start | bytes 786440 | tf_op jit(solution)/shard_map/ppermute | solution.py:41
  87.3 7.5 %collective-permute-start.18 = (bf16[512,512]{1,0:T(8,128)(2,1)S(1)}, bf16[512,512]{1,0:T(8,128)(2,1)S(1)}, u32[]{:S(2)}, u32[]{:S(2)}) collective-permute-start(bf16[512,512]{1,0:T(8,128)(2,1)S(1)} %apply_fast.1.rest_0_), channel_id=1, source_target_pairs={{0,1},{1,0},{2,3},{3,2},{4,5},{5,4},{6,7},{7,6},{8,9},{9,8},{10,11... | collective-permute-start | bytes 1572872 | tf_op jit(solution)/shard_map/ppermute | solution.py:41
  94.7 1.9 %collective-permute-start.23 = (bf16[512,512]{1,0:T(8,128)(2,1)S(1)}, bf16[512,512]{1,0:T(8,128)(2,1)S(1)}, u32[]{:S(2)}, u32[]{:S(2)}) collective-permute-start(bf16[512,512]{1,0:T(8,128)(2,1)S(1)} %collective-permute-done.19.rest_2_), channel_id=1, source_target_pairs={{0,1},{1,0},{2,3},{3,2},{4,5},{5,4},{6,7},{7,6},{8,9},{9,8},{10,11... | collective-permute-start | bytes 1572872 | tf_op jit(solution)/shard_map/ppermute | solution.py:41
  (1 other events, 1.0 us)
